TPU v7x, 128 devices: a whole 4x4x4 slice. The times are simulated.
128 devices in a mesh: dp: 8 (over x, core), seq: 16 (over z, y).
Axes of the slice: x: 4, y: 4, z: 4, core: 2. Of those that a mesh axis runs over, the one named last changes fastest.
Arguments:
- trunk: bfloat16 [8, 4096, 1536], P('dp', 'seq'), may hold values from -34 to 34
- skip: bfloat16 [8, 8192, 1536], P('dp', 'seq'), may hold values from -6 to 6
- valid_bins: int32 [8], P('dp'), may hold values from 2048 to 4096, as said below
- query_weight: bfloat16 [1536, 256], replicated
- key_weight: bfloat16 [1536, 256], replicated
- value_weight: bfloat16 [1536, 768], replicated, may hold values from -0.15625 to 0.15625
- out_weight: bfloat16 [768, 1536], replicated, may hold values from -0.21875 to 0.21875
- depth_weight: float32 [3, 1536], replicated, may hold values from -3 to 3
- point_weight: bfloat16 [1536, 1536], replicated, may hold values from -0.15625 to 0.15625
- cotangent: bfloat16 [8, 8192, 1536], P('dp', 'seq'), may hold values from -6 to 6
Outputs:
- grad_pointwise: bfloat16 [1536, 1536], replicated
- grad_depthwise: float32 [3, 1536], replicated
- grad_skip: bfloat16 [8, 8192, 1536], P('dp', 'seq')
Inputs may be any that keep to these rules, and one draw needn't show every extreme that they name: Bins at or past a window's valid_bins are padding; in every draw some window is whole.
All inputs are finite; a program needn't handle non-finite values.
Results may differ from a plain program's by a relative error of at most 0.017.
Values may be sent and summed in bfloat16 or wider, within the bound.
No kernel may reach another device: no remote copies, remote signals or barrier semaphores. Data moves between devices by JAX's collectives and lax.ppermute only.
A program may use at most 128 MiB of HBM per device.

v0:
```python
from functools import partial
import math

import jax
import jax.numpy as jnp
from jax import lax
from jax.sharding import PartitionSpec as P

H = 4
DH = 64
DV = 192


def padded_2(cells, sides, width):
    for axis, dim in sides:
        count = lax.axis_size(axis)
        ends = count - 1
        head = lax.slice_in_dim(cells, 0, width, axis=dim)
        tail = lax.slice_in_dim(cells, cells.shape[dim] - width, cells.shape[dim], axis=dim)
        cells = jnp.concatenate(
            [
                lax.ppermute(tail, axis, [(i, (i + 1) % count) for i in range(ends)]),
                cells,
                lax.ppermute(head, axis, [((i + 1) % count, i) for i in range(ends)]),
            ],
            axis=dim,
        )
    return cells


def local(
    trunk,
    skip,
    valid_bins,
    query_weight,
    key_weight,
    value_weight,
    out_weight,
    depth_weight,
    point_weight,
    cotangent,
):
    tokens = trunk[0]
    row_count = tokens.shape[0]
    score_scale = 1.0 / math.sqrt(DH)
    queries = (
        jnp.dot(tokens, query_weight, preferred_element_type=jnp.float32)
        .astype(jnp.bfloat16)
        .reshape(row_count, H, DH)
    )
    keys = jnp.dot(tokens, key_weight, preferred_element_type=jnp.float32).astype(jnp.bfloat16)
    values = jnp.dot(tokens, value_weight, preferred_element_type=jnp.float32).astype(jnp.bfloat16)
    limit = valid_bins[0]
    running_max = jnp.full((H, row_count), -1e30, jnp.float32)
    weighted = jnp.zeros((row_count, H, DV), jnp.float32)
    key_piece = lax.all_gather(keys, "seq", axis=0, tiled=True)
    value_piece = lax.all_gather(values, "seq", axis=0, tiled=True)
    width = key_piece.shape[0]
    key_heads = key_piece.reshape(width, H, DH)
    value_heads = value_piece.reshape(width, H, DV)
    scores = (
        jnp.einsum("qhd,khd->hqk", queries, key_heads, preferred_element_type=jnp.float32)
        * score_scale
    )
    places = jnp.arange(width, dtype=jnp.int32)
    scores = jnp.where(places[None, None, :] < limit, scores, -1e30)
    fresh_max = jnp.maximum(running_max, jnp.max(scores, axis=2))
    shrink = jnp.exp(running_max - fresh_max)
    weights_raw = jnp.exp(scores - fresh_max[:, :, None])
    running_total = jnp.sum(weights_raw, axis=2)
    update = jnp.einsum(
        "hqk,khd->qhd",
        weights_raw.astype(jnp.bfloat16),
        value_heads,
        preferred_element_type=jnp.float32,
    )
    weighted = weighted * shrink.T[:, :, None] + update
    running_max, running_total, weighted = (fresh_max, running_total, weighted)
    mixed = (weighted / running_total.T[:, :, None]).reshape(row_count, H * DV)
    attended = (mixed * lax.rsqrt(jnp.mean(mixed * mixed, axis=1, keepdims=True) + 1e-05)).astype(
        jnp.bfloat16
    )
    hidden = (
        tokens.astype(jnp.float32)
        + jnp.dot(attended, out_weight, preferred_element_type=jnp.float32)
    ).astype(jnp.bfloat16)
    upsampled = (
        jnp.repeat(hidden, 2, axis=0).astype(jnp.float32) + skip[0].astype(jnp.float32)
    ).astype(jnp.bfloat16)
    padded = padded_2(upsampled, (("seq", 0),), 1)
    pre_act = (
        depth_weight[0] * padded[:-2]
        + depth_weight[1] * padded[1:-1]
        + depth_weight[2] * padded[2:]
    )
    act_value, pullback = jax.vjp(partial(jax.nn.gelu, approximate=True), pre_act)
    activated = act_value.astype(jnp.bfloat16)
    upstream = cotangent[0]
    grad_act = lax.dot_general(
        upstream, point_weight, (((1,), (1,)), ((), ())), preferred_element_type=jnp.float32
    )
    grad_pre = pullback(grad_act)[0].astype(jnp.bfloat16)
    fine_rows = grad_pre.shape[0]
    grad_wide = grad_pre.astype(jnp.float32)
    depth_term = jnp.stack(
        [
            jnp.sum(padded[offset : offset + fine_rows].astype(jnp.float32) * grad_wide, axis=0)
            for offset in range(3)
        ]
    )
    grad_padded = padded_2(grad_pre, (("seq", 0),), 1)
    grad_skip = (
        depth_weight[0] * grad_padded[2:]
        + depth_weight[1] * grad_padded[1:-1]
        + depth_weight[2] * grad_padded[:-2]
    ).astype(jnp.bfloat16)
    norm_scale = 1.0 / math.sqrt(lax.axis_size("dp") * lax.axis_size("seq") * fine_rows)
    point_term = lax.dot_general(
        activated, upstream, (((0,), (0,)), ((), ())), preferred_element_type=jnp.float32
    )
    point_total, depth_total = lax.psum((point_term, depth_term), ("dp", "seq"))
    grad_pointwise = (point_total * norm_scale).astype(jnp.bfloat16)
    return (grad_pointwise, depth_total * norm_scale, grad_skip[None])


def solution(mesh):
    return jax.shard_map(
        local,
        mesh=mesh,
        in_specs=(
            P("dp", "seq", None),
            P("dp", "seq", None),
            P("dp"),
            P(),
            P(),
            P(),
            P(),
            P(),
            P(),
            P("dp", "seq", None),
        ),
        out_specs=(P(), P(), P("dp", "seq", None)),
        check_vma=False,
    )
```

profile of v0, /device:TPU:1, one launch (start us, length us, event | category | flops | bytes accessed | tf_op | source)
XLA Modules:
  0.0 349.5 jit_solution(12524377417579679030)
XLA Ops:
  7.2 2.6 convolution_convert_fusion.1
  9.8 0.0 all-gather.5.cloned.1.call-start
  9.9 3.4 convolution_convert_fusion
  13.4 0.0 all-reduce.2.cloned.1.call-start
  14.1 1.6 convolution_convert_fusion.2
  15.7 42.6 %all-gather.3.cloned.1.call-done = bf16[4096,256]{1,0:T(8,128)(2,1)} async-done(((bf16[256,256]{1,0:T(8,128)(2,1)}), bf16[4096,256]{1,0:T(8,128)(2,1)}) %all-gather.3.cloned.1.call-update) | async-done | bytes 2097168 | tf_op jit(solution)/shard_map/all_gather | solution.py:56
  58.2 4.1 %copy.15 = bf16[4096,256]{0,1:T(8,128)(2,1)} copy(bf16[4096,256]{1,0:T(8,128)(2,1)} %all-gather.3.cloned.1.call-done) | data formatting | bytes 4194304 | tf_op jit(solution)/shard_map/all_gather | solution.py:56
  62.3 4.1 %fusion = (f32[4,256]{1,0:T(4,128)S(1)}, f32[4,256,4096]{2,1,0:T(8,128)S(1)}) fusion(pred[4096]{0:T(1024)(128)(4,1)S(1)} %iota_compare_fusion, bf16[256,4,64]{0,2,1:T(8,128)(2,1)S(1)} %bitcast.49, bf16[4096,4,64]{0,2,1:T(8,128)(2,1)} %bitcast.47), kind=kOutput, calls=%fused_computation.2 | convolution fusion | flops 549452800 | bytes 19013632 | tf_op jit(solution)/shard_map/qhd,khd->hqk/dot_general | solution.py:62
  66.4 5.9 %copy-done.2 = f32[4,256,4096]{2,1,0:T(8,128)} copy-done((f32[4,256,4096]{2,1,0:T(8,128)}, f32[4,256,4096]{2,1,0:T(8,128)S(1)}, u32[]{:S(2)}) %copy-start.2) | copy-done | bytes 16777240
  72.4 4.0 %fusion.1 = f32[4,256]{1,0:T(4,128)S(1)} fusion(f32[4,256,4096]{2,1,0:T(8,128)S(1)} %get-tuple-element.17, f32[4,256]{1,0:T(4,128)S(1)} %get-tuple-element.15, pred[4096]{0:T(1024)(128)(4,1)S(1)} %iota_compare_fusion), kind=kLoop, calls=%fused_computation.3 | loop fusion | flops 16776192 | bytes 16789504 | tf_op jit(solution)/shard_map/reduce_sum | solution.py:70
  76.4 46.3 %all-gather.5.cloned.1.call-done = bf16[4096,768]{1,0:T(8,128)(2,1)} async-done(((bf16[256,768]{1,0:T(8,128)(2,1)}), bf16[4096,768]{1,0:T(8,128)(2,1)}) %all-gather.5.cloned.1.call-update) | async-done | bytes 6291472 | tf_op jit(solution)/shard_map/all_gather | solution.py:57
  122.7 8.6 %copy.16 = bf16[4096,768]{0,1:T(8,128)(2,1)} copy(bf16[4096,768]{1,0:T(8,128)(2,1)} %all-gather.5.cloned.1.call-done) | data formatting | bytes 12582912 | tf_op jit(solution)/shard_map/all_gather | solution.py:57
  131.3 10.3 %multiply_reduce_fusion = (f32[256]{0:T(256)S(1)}, f32[256,4,192]{0,2,1:T(8,128)S(1)}) fusion(f32[256,4]{0,1:T(4,128)S(1)} %bitcast.50, bf16[4096,4,192]{0,2,1:T(8,128)(2,1)} %bitcast.48, f32[4,256,4096]{2,1,0:T(8,128)} %copy-done.2, f32[4,256]{1,0:T(4,128)S(1)} %get-tuple-element.15, pred[4096]{0:T(1024)(128)(4,1)S(1)} %iota_compare_fusion, ...), kind=kOutput, calls=%fused_computation.68 | convolution fusion | flops 1628176128 | bytes 23872512 | tf_op jit(solution)/shard_map/hqk,khd->qhd/dot_general | solution.py:71
  141.6 0.1 fusion.51
  141.7 0.8 fusion.26
  142.5 2.7 broadcast_in_dim.33
  145.2 5.2 %convert_element_type.79 = f32[512,1536]{1,0:T(8,128)} reshape(f32[256,2,1536]{2,1,0:T(2,128)} %broadcast_in_dim.33) | data formatting | bytes 6291456 | tf_op jit(solution)/shard_map/convert_element_type | solution.py:88
  150.5 2.9 fusion.24
  153.4 3.1 collective-permute-start
  156.6 1.5 collective-permute-start.1
  158.0 0.1 slice_reduce_fusion.2
  158.1 2.8 collective-permute-done.1
  160.9 6.6 %fusion.27 = f32[1536,1536]{1,0:T(8,128)} fusion(bf16[512,1536]{1,0:T(8,128)(2,1)S(1)} %fusion.24, bf16[1,1536]{1,0:T(2,128)(2,1)S(1)} %collective-permute-done.1, bf16[1,1536]{1,0:T(2,128)(2,1)S(1)} %collective-permute-done, bf16[1,512,1536]{2,1,0:T(8,128)(2,1)S(1)} %copy-done.5, f32[1536]{0:T(1024)S(1)} %get-tuple-element.7, ...), kind=kOutput, calls=%fused_computation.41 | convolution fusion | flops 2434007040 | bytes 12607488 | tf_op jit(solution)/shard_map/dot_general | solution.py:118
  167.5 7.5 %fusion.17 = bf16[512,1536]{1,0:T(8,128)(2,1)S(1)} fusion(bf16[1,1536]{1,0:T(2,128)(2,1)S(1)} %collective-permute-done.1, bf16[512,1536]{1,0:T(8,128)(2,1)S(1)} %fusion.24, bf16[1,1536]{1,0:T(2,128)(2,1)S(1)} %collective-permute-done, bf16[1536,1536]{1,0:T(8,128)(2,1)} %param.18, bf16[1,512,1536]{2,1,0:T(8,128)(2,1)} %param.19, ...), kind=kOutput, calls=%fused_computation.28 | convolution fusion | flops 2442657792 | bytes 9461760 | tf_op jit(solution)/shard_map/dot_general | solution.py:99
  175.1 1.3 collective-permute-start.2
  176.4 4.0 %collective-permute-start.3 = (bf16[1,1536]{1,0:T(2,128)(2,1)S(1)}, bf16[1,1536]{1,0:T(2,128)(2,1)S(1)}, u32[]{:S(2)}, u32[]{:S(2)}) collective-permute-start(bf16[1,1536]{1,0:T(2,128)(2,1)S(1)} %get-tuple-element.11), channel_id=1, source_target_pairs={{0,1},{1,2},{2,3},{3,4},{4,5},{5,6},{6,7},{7,8},{8,9},{9,10},{10,1... | collective-permute-start | bytes 9224 | tf_op jit(solution)/shard_map/ppermute | solution.py:22
  180.4 0.7 collective-permute-done.3
  181.1 3.5 %fusion.18 = (f32[1536]{0:T(1024)S(1)}, f32[1536]{0:T(1024)S(1)}, f32[1536]{0:T(1024)S(1)}, bf16[1,512,1536]{2,1,0:T(8,128)(2,1)}) fusion(bf16[512,1536]{1,0:T(8,128)(2,1)S(1)} %fusion.17, bf16[512,1536]{1,0:T(8,128)(2,1)S(1)} %fusion.24, bf16[1,1536]{1,0:T(2,128)(2,1)S(1)} %collective-permute-done, bf16[1,1536]{1,0:T(2,128)(2,1)S(1)} %collective-permute-done.1, ...), kind=kLoop, calls=%fused_computation.29 | loop fusion | flops 23588352 | bytes 4767744 | tf_op jit(solution)/shard_map/reduce_sum | solution.py:107
  184.7 74.9 %psum.15 = f32[3,1536]{1,0:T(4,128)S(1)} all-reduce(f32[3,1536]{1,0:T(4,128)S(1)} %pad_maximum_fusion.5), channel_id=1, replica_groups=mesh['dp'=8,'seq'=16] {'dp','seq'}, use_global_device_ids=true, to_apply=%region_7.8 | all-reduce | flops 4608 | bytes 36864 | tf_op jit(solution)/shard_map/psum | solution.py:121
  259.6 0.6 broadcast_multiply_fusion
  260.2 75.5 %all-reduce.2.cloned.1.call-done = f32[1536,1536]{1,0:T(8,128)} async-done(((f32[1536,1536]{1,0:T(8,128)}), f32[1536,1536]{1,0:T(8,128)}) %all-reduce.2.cloned.1.call-update) | async-done | bytes 9437200 | tf_op jit(solution)/shard_map/psum | solution.py:121
  335.7 7.2 %multiply_convert_fusion = bf16[1536,1536]{1,0:T(8,128)(2,1)} fusion(f32[1536,1536]{1,0:T(8,128)} %all-reduce.2.cloned.1.call-done), kind=kLoop, calls=%fused_computation.5 | loop fusion | flops 4718592 | bytes 14155776 | tf_op jit(solution)/shard_map/convert_element_type | solution.py:122
  (26 shorter events, 0.2 us)
Async XLA Ops:
  7.2 134.5 %copy-start = (bf16[768,1536]{1,0:T(8,128)(2,1)S(1)}, bf16[768,1536]{1,0:T(8,128)(2,1)}, u32[]{:S(2)}) copy-start(bf16[768,1536]{1,0:T(8,128)(2,1)} %param.16) | copy-start | bytes 7077892
  7.2 6.9 %copy-start.3 = (bf16[1,256,1536]{2,1,0:T(8,128)(2,1)S(1)}, bf16[1,256,1536]{2,1,0:T(8,128)(2,1)}, u32[]{:S(2)}) copy-start(bf16[1,256,1536]{2,1,0:T(8,128)(2,1)} %param.10) | copy-start | bytes 2359300
  7.2 51.0 %all-gather.3.cloned.1.call-start = ((), (), s32[]{:S(2)}) async-start(), calls=%async_computation | async-start | bytes 2228224 | tf_op jit(solution)/shard_map/all_gather | solution.py:56
  9.8 112.8 %all-gather.5.cloned.1.call-start = ((), (), s32[]{:S(2)}) async-start(), calls=%async_computation.1 | async-start | bytes 6684672 | tf_op jit(solution)/shard_map/all_gather | solution.py:57
  13.4 322.4 %all-reduce.2.cloned.1.call-start = ((), (), s32[]{:S(2)}) async-start(), calls=%async_computation.2 | async-start | bytes 18874368 | tf_op jit(solution)/shard_map/psum | solution.py:121
  66.4 6.0 %copy-start.2 = (f32[4,256,4096]{2,1,0:T(8,128)}, f32[4,256,4096]{2,1,0:T(8,128)S(1)}, u32[]{:S(2)}) copy-start(f32[4,256,4096]{2,1,0:T(8,128)S(1)} %get-tuple-element.17) | copy-start | bytes 50331652
  150.5 7.6 %copy-start.4 = (f32[3,1536]{1,0:T(4,128)S(1)}, f32[3,1536]{1,0:T(4,128)}, u32[]{:S(2)}) copy-start(f32[3,1536]{1,0:T(4,128)} %param.17) | copy-start | bytes 55300
  150.5 10.4 %copy-start.5 = (bf16[1,512,1536]{2,1,0:T(8,128)(2,1)S(1)}, bf16[1,512,1536]{2,1,0:T(8,128)(2,1)}, u32[]{:S(2)}) copy-start(bf16[1,512,1536]{2,1,0:T(8,128)(2,1)} %param.19) | copy-start | bytes 4718596
  153.4 4.7 %collective-permute-start = (bf16[1,1536]{1,0:T(2,128)(2,1)S(1)}, bf16[1,1536]{1,0:T(2,128)(2,1)S(1)}, u32[]{:S(2)}, u32[]{:S(2)}) collective-permute-start(bf16[1,1536]{1,0:T(2,128)(2,1)S(1)} %get-tuple-element.12), channel_id=1, source_target_pairs={{0,1},{1,2},{2,3},{3,4},{4,5},{5,6},{6,7},{7,8},{8,9},{9,10},{10,1... | collective-permute-start | bytes 9224 | tf_op jit(solution)/shard_map/ppermute | solution.py:22
  156.6 4.4 %collective-permute-start.1 = (bf16[1,1536]{1,0:T(2,128)(2,1)S(1)}, bf16[1,1536]{1,0:T(2,128)(2,1)S(1)}, u32[]{:S(2)}, u32[]{:S(2)}) collective-permute-start(bf16[1,1536]{1,0:T(2,128)(2,1)S(1)} %get-tuple-element.13), channel_id=1, source_target_pairs={{1,0},{2,1},{3,2},{4,3},{5,4},{6,5},{7,6},{8,7},{9,8},{10,9},{11,1... | collective-permute-start | bytes 9224 | tf_op jit(solution)/shard_map/ppermute | solution.py:24
  175.1 5.3 %collective-permute-start.2 = (bf16[1,1536]{1,0:T(2,128)(2,1)S(1)}, bf16[1,1536]{1,0:T(2,128)(2,1)S(1)}, u32[]{:S(2)}, u32[]{:S(2)}) collective-permute-start(bf16[1,1536]{1,0:T(2,128)(2,1)S(1)} %get-tuple-element.10), channel_id=1, source_target_pairs={{1,0},{2,1},{3,2},{4,3},{5,4},{6,5},{7,6},{8,7},{9,8},{10,9},{11,1... | collective-permute-start | bytes 9224 | tf_op jit(solution)/shard_map/ppermute | solution.py:24
  176.4 4.8 %collective-permute-start.3 = (bf16[1,1536]{1,0:T(2,128)(2,1)S(1)}, bf16[1,1536]{1,0:T(2,128)(2,1)S(1)}, u32[]{:S(2)}, u32[]{:S(2)}) collective-permute-start(bf16[1,1536]{1,0:T(2,128)(2,1)S(1)} %get-tuple-element.11), channel_id=1, source_target_pairs={{0,1},{1,2},{2,3},{3,4},{4,5},{5,6},{6,7},{7,8},{8,9},{9,10},{10,1... | collective-permute-start | bytes 9224 | tf_op jit(solution)/shard_map/ppermute | solution.py:22
  335.7 7.2 %copy-start.1 = (bf16[768,1536]{1,0:T(8,128)(2,1)S(1)}, bf16[768,1536]{1,0:T(8,128)(2,1)}, u32[]{:S(2)}) copy-start(bf16[768,1536]{1,0:T(8,128)(2,1)} %param.16) | copy-start | bytes 7077892
Sparse Core Ops, SparseCore 0:
  10.7 47.4 all-gather.2
  60.9 61.6 all-gather.4
  167.6 168.0 all-reduce.1
where the time goes:
time: 350 us
  waiting for transfers between devices  168 us (48%)
  blocking collectives  74.9 us (21%)
  matrix products  36.9 us (11%)
  local copies, waits for them, and re-layouts  26.7 us (8%)
  other arithmetic  18.4 us (5%)
  between operations  14.6 us (4%)
  starting transfers between devices  9.98 us (3%)
    psum x1, waiting for transfers between devices, local(): point_total, depth_total = lax.psum((point_term, depth_term), ('dp', 'seq'))  75.5 us
    psum x1, blocking collectives, local(): point_total, depth_total = lax.psum((point_term, depth_term), ('dp', 'seq'))  74.9 us
    all_gather x1, waiting for transfers between devices, local(): value_piece = lax.all_gather(values, 'seq', axis=0, tiled=True)  46.3 us
    all_gather x1, waiting for transfers between devices, local(): key_piece = lax.all_gather(keys, 'seq', axis=0, tiled=True)  42.6 us
    dot_general x1, matrix products, local(): jnp.einsum('hqk,khd->qhd', weights_raw.astype(jnp.bfloat16), value_heads,...  10.3 us
    all_gather x1, local copies, waits for them, and re-layouts, local(): value_piece = lax.all_gather(values, 'seq', axis=0, tiled=True)  8.63 us
    dot_general x1, matrix products, local(): lax.dot_general(upstream, point_weight, (((1,), (1,)), ((), ())), preferr...  7.54 us
    convert_element_type x1, other arithmetic, local(): grad_pointwise = (point_total * norm_scale).astype(jnp.bfloat16)  7.24 us
  transfers between devices with their start and end apart: 7, of which 5 were waited for; matrix products, arithmetic and copies ran while one was open for 8% of the time, Pallas kernels for 0%

commit v1 on v0

v1 whole, which is shorter than its diff:
```python
from functools import partial
import math

import jax
import jax.numpy as jnp
from jax import lax
from jax.experimental import pallas as pl
from jax.experimental.pallas import tpu as pltpu
from jax.sharding import Mesh, PartitionSpec as P

H = 4
DH = 64
DV = 192
AXES = ("x", "c", "z", "y")
SIZES = (4, 2, 4, 4)
EXTRA = 16
BF = jnp.bfloat16
F32 = jnp.float32


def flat(x, c, z, y):
    return ((x * 2 + c) * 4 + z) * 4 + y


def turn(phase, step):
    pairs = []
    for x in range(4):
        for c in range(2):
            for z in range(4):
                for y in range(4):
                    at = {"x": x, "z": z, "y": y}
                    axis = ("x", "y", "z")[(phase + c) % 3]
                    to = dict(at)
                    to[axis] = (at[axis] + step) % 4
                    pairs.append((flat(x, c, z, y), flat(to["x"], c, to["z"], to["y"])))
    return pairs


def ring(step):
    return [(i, (i + step) % 4) for i in range(4)]


def exchange(pieces, phase):
    got = [pieces[0], None, None, None]
    for d in (2, 1, 3):
        got[d] = lax.ppermute(pieces[d], AXES, turn(phase, d))
    return got


def total_of(got):
    a, b, c, d = (g.astype(F32) for g in got)
    return (a + c) + (b + d)


def attend(bases, q, kv, state, last):
    rows = q[0].shape[0]
    width = kv.shape[0]
    part = width // 4
    first = state is None

    def kernel(bases_ref, *refs):
        q_refs, refs = refs[:4], refs[4:]
        kv_ref, refs = refs[0], refs[1:]
        if not first:
            max_in, sum_in, refs = refs[:4], refs[4:8], refs[8:]
        if last:
            out_refs = refs
        else:
            max_out, sum_out = refs[:4], refs[4:8]
        lane = lax.broadcasted_iota(jnp.int32, (width, 256), 1)
        pair = kv_ref[...]
        keys = pair[:, 128:]
        values = jnp.where(lane == DV, jnp.ones((), BF), pair)
        place = lax.broadcasted_iota(jnp.int32, (1, part), 1)
        keep = jnp.concatenate([place + bases_ref[i] < bases_ref[4] for i in range(4)], axis=1)
        for i in range(4):
            scores = lax.dot_general(
                q_refs[i][...], keys, (((1,), (1,)), ((), ())), preferred_element_type=F32
            )
            scores = jnp.where(keep, scores * (1.0 / math.sqrt(DH)), -1e30)
            high = jnp.max(scores, axis=1, keepdims=True)
            if not first:
                before = max_in[i][:, :1]
                high = jnp.maximum(high, before)
            probs = jnp.exp(scores - high).astype(BF)
            update = jnp.dot(probs, values, preferred_element_type=F32)
            if not first:
                update = update + sum_in[i][...] * jnp.exp(before - high)
            if last:
                out_refs[i][...] = (update / update[:, DV : DV + 1]).astype(BF)
            else:
                max_out[i][...] = jnp.broadcast_to(high, (rows, 128))
                sum_out[i][...] = update

    vmem = pl.BlockSpec(memory_space=pltpu.VMEM)
    ins = [*q, kv]
    if not first:
        ins += [*state[0], *state[1]]
    if last:
        outs = [jax.ShapeDtypeStruct((rows, 256), BF)] * 4
    else:
        outs = [jax.ShapeDtypeStruct((rows, 128), F32)] * 4
        outs += [jax.ShapeDtypeStruct((rows, 256), F32)] * 4
    got = pl.pallas_call(
        kernel,
        out_shape=outs,
        in_specs=[pl.BlockSpec(memory_space=pltpu.SMEM)] + [vmem] * len(ins),
        out_specs=[vmem] * len(outs),
        compiler_params=pltpu.CompilerParams(vmem_limit_bytes=40 << 20),
        cost_estimate=pl.CostEstimate(
            flops=4 * 2 * rows * width * 512, bytes_accessed=4 << 20, transcendentals=4 * rows * width
        ),
    )(bases, *ins)
    return got if last else (got[:4], got[4:])


def local(
    trunk,
    skip,
    valid_bins,
    query_weight,
    key_weight,
    value_weight,
    out_weight,
    depth_weight,
    point_weight,
    cotangent,
):
    tokens, skipped, upstream = trunk[0], skip[0], cotangent[0]
    rows = tokens.shape[0]
    fine = skipped.shape[0]
    ix, ic, iz, iy = (lax.axis_index(a) for a in AXES)
    place = iz * 4 + iy

    down = jnp.concatenate([tokens[-1:], skipped[-2:], upstream[-1:]], axis=0)
    up = jnp.concatenate([tokens[:1], skipped[:2], upstream[:1]], axis=0)
    before = lax.ppermute(down, ("z", "y"), [(i, i + 1) for i in range(15)])
    after = lax.ppermute(up, ("z", "y"), [(i + 1, i) for i in range(15)])

    keys = jnp.dot(tokens, key_weight, preferred_element_type=F32).astype(BF)
    values = jnp.dot(tokens, value_weight, preferred_element_type=F32).astype(BF)
    key_heads = keys.reshape(rows, H, DH).transpose(1, 0, 2)
    value_heads = values.reshape(rows, H, DV).transpose(1, 0, 2)
    pairs = jnp.concatenate([value_heads, key_heads], axis=2)
    own = [lax.dynamic_index_in_dim(pairs, (iy + d) % 4, 0, keepdims=False) for d in range(4)]
    kv = [own[0], None, None, None]
    for d in (2, 1, 3):
        kv[d] = lax.ppermute(own[d], "y", ring(d))
    kv_own = jnp.concatenate(kv, axis=0)
    kv_far = {d: lax.ppermute(kv_own, "z", ring(d)) for d in (1, 3, 2)}

    tail = jnp.concatenate([before[:1], after[:1], jnp.zeros((EXTRA - 2, tokens.shape[1]), BF)], axis=0)
    queries = jnp.dot(
        jnp.concatenate([tokens, tail], axis=0), query_weight, preferred_element_type=F32
    ).astype(BF)
    query_heads = queries.reshape(rows + EXTRA, H, DH).transpose(1, 0, 2)
    query_heads = jnp.pad(query_heads, ((0, 0), (0, 0), (64, 0)))
    own = [lax.dynamic_index_in_dim(query_heads, (iy + d) % 4, 0, keepdims=False) for d in range(4)]
    q = [own[0], None, None, None]
    for d in (2, 1, 3):
        q[d] = lax.ppermute(own[d], "y", ring(d))

    def bases(far):
        depth = (iz - far) % 4
        return jnp.stack([(depth * 4 + (iy - d) % 4) * rows for d in range(4)] + [valid_bins[0]]).astype(jnp.int32)

    state = attend(bases(0), q, kv_own, None, False)
    state = attend(bases(1), q, kv_far[1], state, False)
    state = attend(bases(3), q, kv_far[3], state, False)
    mixed = attend(bases(2), q, kv_far[2], state, True)
    back = [mixed[0], None, None, None]
    for d in (2, 1, 3):
        back[d] = lax.ppermute(mixed[d], "y", ring(4 - d))
    squares = sum(jnp.sum(jnp.square(b[:, :DV].astype(F32)), axis=1, keepdims=True) for b in back)
    scale = lax.rsqrt(squares * (1.0 / (H * DV)) + 1e-05)
    out_heads = out_weight.reshape(H, DV, -1)
    attended = jnp.concatenate([(b[:, :DV].astype(F32) * scale).astype(BF) for b in back], axis=1)
    weights = jnp.concatenate(
        [lax.dynamic_index_in_dim(out_heads, (iy + d) % 4, 0, keepdims=False) for d in range(4)], axis=0
    )
    hidden = (
        jnp.concatenate([tokens, tail], axis=0).astype(F32)
        + jnp.dot(attended, weights, preferred_element_type=F32)
    ).astype(BF)

    def raised(hid, skp):
        return (jnp.repeat(hid, 2, axis=0).astype(F32) + skp.astype(F32)).astype(BF)

    zero = jnp.zeros((2, tokens.shape[1]), BF)
    padded = jnp.concatenate(
        [
            jnp.where(place > 0, raised(hidden[rows : rows + 1], before[1:3]), zero),
            raised(hidden[:rows], skipped),
            jnp.where(place < 15, raised(hidden[rows + 1 : rows + 2], after[1:3]), zero),
        ],
        axis=0,
    )
    pre_act = depth_weight[0] * padded[:-2] + depth_weight[1] * padded[1:-1] + depth_weight[2] * padded[2:]
    act_value, pullback = jax.vjp(partial(jax.nn.gelu, approximate=True), pre_act)
    activated = act_value.astype(BF)[1:-1]
    point_term = lax.dot_general(
        activated, upstream, (((0,), (0,)), ((), ())), preferred_element_type=F32
    ).astype(BF)
    wide = jnp.concatenate([before[3:4], upstream, after[3:4]], axis=0)
    grad_act = lax.dot_general(wide, point_weight, (((1,), (1,)), ((), ())), preferred_element_type=F32)
    grad_pre = pullback(grad_act)[0].astype(BF)
    grad_mid = grad_pre[1:-1].astype(F32)
    depth_term = jnp.stack(
        [jnp.sum(padded[1 + t : 1 + t + fine].astype(F32) * grad_mid, axis=0) for t in range(3)]
    )
    grad_skip = (
        depth_weight[0] * grad_pre[2:] + depth_weight[1] * grad_pre[1:-1] + depth_weight[2] * grad_pre[:-2]
    ).astype(BF)

    norm_scale = 1.0 / math.sqrt(128 * fine)
    half = point_term.shape[0] // 2
    swap = [(0, 1), (1, 0)]
    theirs = lax.dynamic_slice_in_dim(point_term, (1 - ic) * half, half, axis=0)
    mine = lax.dynamic_slice_in_dim(point_term, ic * half, half, axis=0)
    pair_sum = (mine.astype(F32) + lax.ppermute(theirs, "c", swap).astype(F32)).astype(BF)
    first_at = jnp.where(ic == 0, ix, iy)
    second_at = jnp.where(ic == 0, iy, iz)
    quarter = half // 4
    got = exchange(
        [lax.dynamic_slice_in_dim(pair_sum, (first_at + d) % 4 * quarter, quarter, axis=0) for d in range(4)], 0
    )
    sum_one = total_of(got).astype(BF)

    half_c = depth_term.shape[1] // 2
    d_theirs = lax.dynamic_slice_in_dim(depth_term, (1 - ic) * half_c, half_c, axis=1)
    d_mine = lax.dynamic_slice_in_dim(depth_term, ic * half_c, half_c, axis=1)
    d_sum = d_mine + lax.ppermute(d_theirs, "c", swap)
    d_sum = total_of(exchange([d_sum] * 4, 0))
    rider = jnp.pad(d_sum.astype(BF), ((0, 5), (0, half_c)))

    slim = quarter // 4
    got = exchange(
        [
            jnp.concatenate(
                [lax.dynamic_slice_in_dim(sum_one, (second_at + d) % 4 * slim, slim, axis=0), rider], axis=0
            )
            for d in range(4)
        ],
        1,
    )
    sum_two = total_of(got).astype(BF)
    sum_three = total_of(exchange([sum_two] * 4, 2)) * norm_scale
    d_half = sum_three[slim : slim + 3, :half_c]
    final = sum_three[:slim].astype(BF)

    def gathered(piece, phase, at):
        got = exchange([piece] * 4, phase)
        whole = jnp.zeros((4, *piece.shape), piece.dtype)
        for d in range(4):
            whole = lax.dynamic_update_index_in_dim(whole, got[d], (at - d) % 4, 0)
        return whole.reshape(4 * piece.shape[0], piece.shape[1])

    final = gathered(final, 1, second_at)
    final = gathered(final, 0, first_at)
    other = lax.ppermute(final, "c", swap)
    low = jnp.where(ic == 0, final, other)
    high = jnp.where(ic == 0, other, final)
    d_other = lax.ppermute(d_half, "c", swap)
    d_all = jnp.concatenate(
        [jnp.where(ic == 0, d_half, d_other), jnp.where(ic == 0, d_other, d_half)], axis=1
    )
    return (jnp.concatenate([low, high], axis=0), d_all, grad_skip[None])


def solution(mesh):
    fine_mesh = Mesh(mesh.devices.reshape(SIZES), AXES)
    rows = P(("x", "c"), ("z", "y"), None)
    return jax.shard_map(
        local,
        mesh=fine_mesh,
        in_specs=(rows, rows, P(("x", "c")), P(), P(), P(), P(), P(), P(), rows),
        out_specs=(P(), P(), rows),
        check_vma=False,
    )
```

time: 350 us -> 195 us (0.56)
  the two profiles are of different devices: /device:TPU:1 before, /device:TPU:41 now
where the time goes in v1:
time: 195 us; the launch traced here: 194 us
  starting transfers between devices  71.7 us (37%)
  waiting for transfers between devices  54.7 us (28%)
  local copies, waits for them, and re-layouts  19.6 us (10%)
  other arithmetic  17.9 us (9%)
  matrix products  17.4 us (9%)
  Pallas kernels  10.5 us (5%)
  between operations  2.09 us (1%)
    ppermute x18, waiting for transfers between devices, exchange(): got[d] = lax.ppermute(pieces[d], AXES, turn(phase, d))  36.3 us
    ppermute x18, starting transfers between devices, exchange(): got[d] = lax.ppermute(pieces[d], AXES, turn(phase, d))  19.7 us
    ppermute x1, starting transfers between devices, local(): other = lax.ppermute(final, 'c', swap)  16.8 us
    pallas_call x4, Pallas kernels, attend(): pl.pallas_call(kernel, out_shape=outs, in_specs=[pl.BlockSpec(memory_spac...  10.5 us
    ppermute x1, starting transfers between devices, local(): lax.ppermute(theirs, 'c', swap).astype(F32)  9.07 us
    ppermute x3, starting transfers between devices, local(): q[d] = lax.ppermute(own[d], 'y', ring(d))  8.01 us
    dot_general x1, matrix products, local(): lax.dot_general(wide, point_weight, (((1,), (1,)), ((), ())), preferred_e...  7.47 us
    ppermute x3, waiting for transfers between devices, local(): kv_far = {d: lax.ppermute(kv_own, 'z', ring(d)) for d in (1, 3, 2)}  7.35 us
  transfers between devices with their start and end apart: 36, of which 19 were waited for; matrix products, arithmetic and copies ran while one was open for 10% of the time, Pallas kernels for 4%

profile of v1, /device:TPU:41, one launch (start us, length us, event | category | flops | bytes accessed | tf_op | source)
XLA Modules:
  0.0 194.0 jit_solution(10599527156212657735)
XLA Ops:
  2.3 2.7 %convolution_convert_fusion.1 = bf16[256,768]{1,0:T(8,128)(2,1)} fusion(bf16[1536,768]{1,0:T(8,128)(2,1)S(1)} %copy-done, bf16[1,256,1536]{2,1,0:T(8,128)(2,1)} %param.10), kind=kOutput, calls=%fused_computation.54 | convolution fusion | flops 604176384 | bytes 3538944 | tf_op jit(solution)/shard_map/dot_general | solution.py:141
  16.0 3.4 %collective-permute-start.1 = (bf16[4,1536]{1,0:T(4,128)(2,1)S(1)}, bf16[4,1536]{1,0:T(4,128)(2,1)S(1)}, u32[]{:S(2)}, u32[]{:S(2)}) collective-permute-start(bf16[4,1536]{1,0:T(4,128)(2,1)S(1)} %pad_maximum_fusion.9), channel_id=1, source_target_pairs={{1,0},{2,1},{3,2},{4,3},{5,4},{6,5},{7,6},{8,7},{9,8},{10,9},{11,1... | collective-permute-start | bytes 36872 | tf_op jit(solution)/shard_map/ppermute | solution.py:138
  23.3 2.5 %collective-permute-start.2 = (bf16[272,128]{1,0:T(8,128)(2,1)S(1)}, bf16[272,128]{1,0:T(8,128)(2,1)S(1)}, u32[]{:S(2)}, u32[]{:S(2)}) collective-permute-start(bf16[272,128]{1,0:T(8,128)(2,1)S(1)} %bitcast.113), channel_id=1, source_target_pairs={{0,1},{1,2},{2,3},{3,0},{4,5},{5,6},{6,7},{7,4},{8,9},{9,10},{10,1... | collective-permute-start | bytes 208904 | tf_op jit(solution)/shard_map/ppermute | solution.py:161
  26.0 3.4 %collective-permute-start.3 = (bf16[272,128]{1,0:T(8,128)(2,1)S(1)}, bf16[272,128]{1,0:T(8,128)(2,1)S(1)}, u32[]{:S(2)}, u32[]{:S(2)}) collective-permute-start(bf16[272,128]{1,0:T(8,128)(2,1)S(1)} %bitcast.111), channel_id=1, source_target_pairs={{0,2},{1,3},{2,0},{3,1},{4,6},{5,7},{6,4},{7,5},{8,10},{9,11},{10,... | collective-permute-start | bytes 208904 | tf_op jit(solution)/shard_map/ppermute | solution.py:161
  32.8 3.0 %dynamic-slice_bitcast_fusion.3 = (bf16[192,1536]{1,0:T(8,128)(2,1)}, bf16[192,1536]{1,0:T(8,128)(2,1)}, bf16[192,1536]{1,0:T(8,128)(2,1)}, bf16[192,1536]{1,0:T(8,128)(2,1)}) fusion(bf16[4,192,1536]{2,1,0:T(8,128)(2,1)} %bitcast.97, s32[]{:T(128)S(6)} %select_n.281, s32[]{:T(128)S(6)} %select_n.287, s32[]{:T(128)S(6)} %select_n.285, s32[]{:T(128)S(6)} %select_n.283), kind=kLoop, calls=%fused_computation.71 | loop fusion | bytes 4718608 | tf_op jit(solution)/shard_map/jit(dynamic_index_in_dim)/squeeze | solution.py:179
  37.0 2.5 %shard_map.121 = (f32[272,128]{1,0:T(8,128)S(1)}, f32[272,128]{1,0:T(8,128)S(1)}, f32[272,128]{1,0:T(8,128)S(1)}, f32[272,128]{1,0:T(8,128)S(1)}, f32[272,256]{1...) custom-call(s32[5]{0:T(128)S(1)} %stack.91.bases_ref, ...), custom_call_target="tpu_custom_call" | custom-call | flops 1140850688 | bytes 4194304 | tf_op jit(solution)/shard_map/pallas_call | solution.py:104
  39.5 2.7 %shard_map.122 = (f32[272,128]{1,0:T(8,128)S(1)}, f32[272,128]{1,0:T(8,128)S(1)}, f32[272,128]{1,0:T(8,128)S(1)}, f32[272,128]{1,0:T(8,128)S(1)}, f32[272,256]{1...) custom-call(s32[5]{0:T(128)S(1)} %stack.86.bases_ref, ...), custom_call_target="tpu_custom_call" | custom-call | flops 1140850688 | bytes 4194304 | tf_op jit(solution)/shard_map/pallas_call | solution.py:104
  42.2 2.7 %shard_map.123 = (f32[272,128]{1,0:T(8,128)S(1)}, f32[272,128]{1,0:T(8,128)S(1)}, f32[272,128]{1,0:T(8,128)S(1)}, f32[272,128]{1,0:T(8,128)S(1)}, f32[272,256]{1...) custom-call(s32[5]{0:T(128)S(1)} %stack.81.bases_ref, ...), custom_call_target="tpu_custom_call" | custom-call | flops 1140850688 | bytes 4194304 | tf_op jit(solution)/shard_map/pallas_call | solution.py:104
  44.9 7.3 %collective-permute-done.8.refs_4_ = bf16[1024,256]{1,0:T(8,128)(2,1)S(1)} collective-permute-done((bf16[1024,256]{1,0:T(8,128)(2,1)S(1)}, bf16[1024,256]{1,0:T(8,128)(2,1)S(1)}, u32[]{:S(2)}, u32[]{:S(2)}) %collective-permute-start.8) | collective-permute-done | bytes 524320 | tf_op jit(solution)/shard_map/ppermute | solution.py:150
  52.3 2.7 %shard_map.124 = (bf16[272,256]{1,0:T(8,128)(2,1)S(1)}, bf16[272,256]{1,0:T(8,128)(2,1)S(1)}, bf16[272,256]{1,0:T(8,128)(2,1)S(1)}, bf16[272,256]{1,0:T(8,128)(2,1)S(1)}) custom-call(s32[5]{0:T(128)S(1)} %stack.76.bases_ref, bf16[272,128]{1,0:T(8,128)(2,1)S(1)} %bitcast.95, bf16[272,128]{1,0:T(8,128)(2,1)S(1)} %collective-permute-done.2.refs_1_, ...), custom_call_target="tpu_custom_call" | custom-call | flops 1140850688 | bytes 4194304 | tf_op jit(solution)/shard_map/pallas_call | solution.py:104
  62.8 2.3 %add_convert_fusion.1 = bf16[272,1536]{1,0:T(8,128)(2,1)S(1)} fusion(bf16[192,1536]{1,0:T(8,128)(2,1)} %get-tuple-element.75, bf16[192,1536]{1,0:T(8,128)(2,1)} %get-tuple-element.76, bf16[192,1536]{1,0:T(8,128)(2,1)} %get-tuple-element.77, bf16[192,1536]{1,0:T(8,128)(2,1)S(1)} %copy-done.5, bf16[272,192]{1,0:T(8,128)(2,1)S(1)} %get-tuple-element.111, ...), kind=kOutput, calls=%fused_computation.42 | convolution fusion | flops 657014784 | bytes 4405792 | tf_op jit(solution)/shard_map/dot_general | solution.py:183
  66.4 3.3 %convert_element_type.202 = f32[512,1536]{1,0:T(8,128)} reshape(f32[256,2,1536]{2,1,0:T(2,128)S(1)} %broadcast_in_dim.54) | data formatting | bytes 6291456 | tf_op jit(solution)/shard_map/convert_element_type | solution.py:187
  69.7 2.8 %fusion.14 = bf16[512,1536]{1,0:T(8,128)(2,1)S(1)} fusion(f32[512,1536]{1,0:T(8,128)} %convert_element_type.202, bf16[1,512,1536]{2,1,0:T(8,128)(2,1)} %param.11), kind=kLoop, calls=%fused_computation.26 | loop fusion | flops 2359296 | bytes 6291456 | tf_op jit(solution)/shard_map/convert_element_type | solution.py:187
  74.8 3.0 %convolution_convert_fusion = bf16[1536,1536]{1,0:T(8,128)(2,1)S(1)} fusion(f32[514,1536]{1,0:T(8,128)S(1)} %get-tuple-element.79, f32[514,1536]{1,0:T(8,128)S(1)} %get-tuple-element.78, bf16[1,512,1536]{2,1,0:T(8,128)(2,1)S(1)} %copy-done.8), kind=kOutput, calls=%fused_computation | convolution fusion | flops 2419851264 | bytes 12582912 | tf_op jit(solution)/shard_map/dot_general | solution.py:201
  77.8 2.2 %copy-done.2 = bf16[1536,1536]{1,0:T(8,128)(2,1)} copy-done((bf16[1536,1536]{1,0:T(8,128)(2,1)}, bf16[1536,1536]{1,0:T(8,128)(2,1)S(1)}, u32[]{:S(2)}) %copy-start.2) | copy-done | bytes 4718616
  81.6 9.1 %collective-permute-start.14 = (bf16[768,1536]{1,0:T(8,128)(2,1)}, bf16[768,1536]{1,0:T(8,128)(2,1)}, u32[]{:S(2)}, u32[]{:S(2)}) collective-permute-start(bf16[768,1536]{1,0:T(8,128)(2,1)} %constant_dynamic-slice_fusion.8), channel_id=1, source_target_pairs={{0,16},{16,0},{1,17},{17,1},{2,18},{18,2},{3,19},{19,3},{4,20},{20... | collective-permute-start | bytes 7077896 | tf_op jit(solution)/shard_map/ppermute | solution.py:220
  90.6 7.5 %fusion.6 = bf16[514,1536]{1,0:T(8,128)(2,1)S(1)} fusion(bf16[1536,1536]{1,0:T(8,128)(2,1)} %param.18, bf16[1,1536]{1,0:T(2,128)(2,1)S(1)} %get-tuple-element.103, bf16[512,1536]{1,0:T(8,128)(2,1)S(1)} %bitcast.114, bf16[1,1536]{1,0:T(2,128)(2,1)S(1)} %get-tuple-element.101, bf16[2,1536]{1,0:T(2,128)(2,1)S(1)} %broadcast_select_fusion.2, ...), kind=kOutput, calls=%fused_computation.15 | convolution fusion | flops 2460883968 | bytes 9480192 | tf_op jit(solution)/shard_map/dot_general | solution.py:205
  98.1 3.4 %fusion.7 = (f32[1536]{0:T(1024)S(1)}, f32[1536]{0:T(1024)S(1)}, f32[1536]{0:T(1024)S(1)}, bf16[1,512,1536]{2,1,0:T(8,128)(2,1)}) fusion(bf16[2,1536]{1,0:T(2,128)(2,1)S(1)} %broadcast_select_fusion.3, bf16[512,1536]{1,0:T(8,128)(2,1)S(1)} %fusion.14, bf16[514,1536]{1,0:T(8,128)(2,1)S(1)} %fusion.6, bf16[2,1536]{1,0:T(2,128)(2,1)S(1)} %broadcast_select_fusion.2, ...), kind=kLoop, calls=%fused_computation.17 | loop fusion | flops 18869760 | bytes 7913472 | tf_op jit(solution)/shard_map/reduce_sum | solution.py:209
  101.6 2.3 %add_convert_fusion = bf16[768,1536]{1,0:T(8,128)(2,1)S(1)} fusion(bf16[768,1536]{1,0:T(8,128)(2,1)} %collective-permute-done.14, bf16[1536,1536]{1,0:T(8,128)(2,1)S(1)} %copy-done.3, s32[]{:T(128)S(6)} %select_n.294), kind=kLoop, calls=%fused_computation.6 | loop fusion | flops 4718592 | bytes 7077892 | tf_op jit(solution)/shard_map/convert_element_type | solution.py:220
  105.0 2.6 %collective-permute-start.16 = (bf16[192,1536]{1,0:T(8,128)(2,1)}, bf16[192,1536]{1,0:T(8,128)(2,1)}, u32[]{:S(2)}, u32[]{:S(2)}) collective-permute-start(bf16[192,1536]{1,0:T(8,128)(2,1)} %get-tuple-element.73), channel_id=1, source_target_pairs={{0,32},{1,33},{2,34},{3,35},{4,36},{5,37},{6,38},{7,39},{8,40},{9,... | collective-permute-start | bytes 1769480 | tf_op jit(solution)/shard_map/ppermute | solution.py:46
  107.6 3.7 %collective-permute-start.18 = (f32[3,768]{1,0:T(4,128)S(1)}, f32[3,768]{1,0:T(4,128)S(1)}, u32[]{:S(2)}, u32[]{:S(2)}) collective-permute-start(f32[3,768]{1,0:T(4,128)S(1)} %constant_dynamic-slice_fusion.3), channel_id=1, source_target_pairs={{0,16},{16,0},{1,17},{17,1},{2,18},{18,2},{3,19},{19,3},{4,20},{20... | collective-permute-start | bytes 27656 | tf_op jit(solution)/shard_map/ppermute | solution.py:232
  112.1 2.6 %collective-permute-start.20 = (f32[3,768]{1,0:T(4,128)S(1)}, f32[3,768]{1,0:T(4,128)}, u32[]{:S(2)}, u32[]{:S(2)}) collective-permute-start(f32[3,768]{1,0:T(4,128)S(1)} %dynamic-slice_add_fusion), channel_id=1, source_target_pairs={{0,32},{1,33},{2,34},{3,35},{4,36},{5,37},{6,38},{7,39},{8,40},{9,... | collective-permute-start | bytes 27656 | tf_op jit(solution)/shard_map/ppermute | solution.py:46
  114.7 7.6 %collective-permute-done.19 = f32[3,768]{1,0:T(4,128)S(1)} collective-permute-done((f32[3,768]{1,0:T(4,128)S(1)}, f32[3,768]{1,0:T(4,128)S(1)}, u32[]{:S(2)}, u32[]{:S(2)}) %collective-permute-start.19) | collective-permute-done | bytes 9248 | tf_op jit(solution)/shard_map/ppermute | solution.py:46
  129.7 4.3 %collective-permute-done.22 = bf16[56,1536]{1,0:T(8,128)(2,1)S(1)} collective-permute-done((bf16[56,1536]{1,0:T(8,128)(2,1)S(1)}, bf16[56,1536]{1,0:T(8,128)(2,1)S(1)}, u32[]{:S(2)}, u32[]{:S(2)}) %collective-permute-start.22) | collective-permute-done | bytes 172064 | tf_op jit(solution)/shard_map/ppermute | solution.py:46
  136.1 2.4 %collective-permute-start.25 = (bf16[56,1536]{1,0:T(8,128)(2,1)S(1)}, bf16[56,1536]{1,0:T(8,128)(2,1)S(1)}, u32[]{:S(2)}, u32[]{:S(2)}) collective-permute-start(bf16[56,1536]{1,0:T(8,128)(2,1)S(1)} %add_convert_fusion.3), channel_id=1, source_target_pairs={{0,8},{1,9},{2,10},{3,11},{4,12},{5,13},{6,14},{7,15},{8,0},{9,1},... | collective-permute-start | bytes 516104 | tf_op jit(solution)/shard_map/ppermute | solution.py:46
  142.0 2.2 %collective-permute-done.26 = bf16[56,1536]{1,0:T(8,128)(2,1)S(1)} collective-permute-done((bf16[56,1536]{1,0:T(8,128)(2,1)S(1)}, bf16[56,1536]{1,0:T(8,128)(2,1)S(1)}, u32[]{:S(2)}, u32[]{:S(2)}) %collective-permute-start.26) | collective-permute-done | bytes 172064 | tf_op jit(solution)/shard_map/ppermute | solution.py:46
  151.4 3.2 %collective-permute-start.32 = (bf16[192,1536]{1,0:T(8,128)(2,1)S(1)}, bf16[192,1536]{1,0:T(8,128)(2,1)S(1)}, u32[]{:S(2)}, u32[]{:S(2)}) collective-permute-start(bf16[192,1536]{1,0:T(8,128)(2,1)S(1)} %bitcast.99), channel_id=1, source_target_pairs={{0,64},{1,65},{2,66},{3,67},{4,68},{5,69},{6,70},{7,71},{8,72},{9,... | collective-permute-start | bytes 1769480 | tf_op jit(solution)/shard_map/ppermute | solution.py:46
  155.4 6.5 %collective-permute-done.31 = bf16[192,1536]{1,0:T(8,128)(2,1)S(1)} collective-permute-done((bf16[192,1536]{1,0:T(8,128)(2,1)S(1)}, bf16[192,1536]{1,0:T(8,128)(2,1)S(1)}, u32[]{:S(2)}, u32[]{:S(2)}) %collective-permute-start.31) | collective-permute-done | bytes 589856 | tf_op jit(solution)/shard_map/ppermute | solution.py:46
  163.1 6.2 %collective-permute-done.33 = bf16[192,1536]{1,0:T(8,128)(2,1)S(1)} collective-permute-done((bf16[192,1536]{1,0:T(8,128)(2,1)S(1)}, bf16[192,1536]{1,0:T(8,128)(2,1)S(1)}, u32[]{:S(2)}, u32[]{:S(2)}) %collective-permute-start.33) | collective-permute-done | bytes 589856 | tf_op jit(solution)/shard_map/ppermute | solution.py:46
  169.3 16.8 %collective-permute-start.34 = (bf16[768,1536]{1,0:T(8,128)(2,1)S(1)}, bf16[768,1536]{1,0:T(8,128)(2,1)S(1)}, u32[]{:S(2)}, u32[]{:S(2)}) collective-permute-start(bf16[768,1536]{1,0:T(8,128)(2,1)S(1)} %bitcast.96), channel_id=1, source_target_pairs={{0,16},{16,0},{1,17},{17,1},{2,18},{18,2},{3,19},{19,3},{4,20},{20... | collective-permute-start | bytes 7077896 | tf_op jit(solution)/shard_map/ppermute | solution.py:260
  186.2 4.1 %collective-permute-done.35 = f32[3,768]{1,0:T(4,128)S(1)} collective-permute-done((f32[3,768]{1,0:T(4,128)S(1)}, f32[3,768]{1,0:T(4,128)S(1)}, u32[]{:S(2)}, u32[]{:S(2)}) %collective-permute-start.35) | collective-permute-done | bytes 9248 | tf_op jit(solution)/shard_map/ppermute | solution.py:263
  191.4 2.5 %pad_maximum_fusion = bf16[1536,1536]{1,0:T(8,128)(2,1)} fusion(bf16[768,1536]{1,0:T(8,128)(2,1)S(1)} %get-tuple-element.70, bf16[768,1536]{1,0:T(8,128)(2,1)S(1)} %get-tuple-element.69), kind=kLoop, calls=%fused_computation.5 | loop fusion | flops 9437184 | bytes 9437184 | tf_op jit(solution)/shard_map/concatenate | solution.py:267
  (142 shorter events, 58.6 us)
Async XLA Ops:
  8.0 13.4 %collective-permute-start.5 = (bf16[256,256]{1,0:T(8,128)(2,1)S(1)}, bf16[256,256]{1,0:T(8,128)(2,1)S(1)}, u32[]{:S(2)}, u32[]{:S(2)}) collective-permute-start(bf16[256,256]{1,0:T(8,128)(2,1)S(1)} %bitcast.108), channel_id=1, source_target_pairs={{0,1},{1,2},{2,3},{3,0},{4,5},{5,6},{6,7},{7,4},{8,9},{9,10},{10,1... | collective-permute-start | bytes 393224 | tf_op jit(solution)/shard_map/ppermute | solution.py:148
  9.4 12.0 %collective-permute-start.6 = (bf16[256,256]{1,0:T(8,128)(2,1)S(1)}, bf16[256,256]{1,0:T(8,128)(2,1)S(1)}, u32[]{:S(2)}, u32[]{:S(2)}) collective-permute-start(bf16[256,256]{1,0:T(8,128)(2,1)S(1)} %bitcast.109), channel_id=1, source_target_pairs={{0,2},{1,3},{2,0},{3,1},{4,6},{5,7},{6,4},{7,5},{8,10},{9,11},{10,... | collective-permute-start | bytes 393224 | tf_op jit(solution)/shard_map/ppermute | solution.py:148
  10.3 11.1 %collective-permute-start.7 = (bf16[256,256]{1,0:T(8,128)(2,1)S(1)}, bf16[256,256]{1,0:T(8,128)(2,1)S(1)}, u32[]{:S(2)}, u32[]{:S(2)}) collective-permute-start(bf16[256,256]{1,0:T(8,128)(2,1)S(1)} %bitcast.110), channel_id=1, source_target_pairs={{0,3},{1,0},{2,1},{3,2},{4,7},{5,4},{6,5},{7,6},{8,11},{9,8},{10,9... | collective-permute-start | bytes 393224 | tf_op jit(solution)/shard_map/ppermute | solution.py:148
  14.1 5.5 %collective-permute-start = (bf16[4,1536]{1,0:T(4,128)(2,1)S(1)}, bf16[4,1536]{1,0:T(4,128)(2,1)S(1)}, u32[]{:S(2)}, u32[]{:S(2)}) collective-permute-start(bf16[4,1536]{1,0:T(4,128)(2,1)S(1)} %pad_maximum_fusion.8), channel_id=1, source_target_pairs={{0,1},{1,2},{2,3},{3,4},{4,5},{5,6},{6,7},{7,8},{8,9},{9,10},{10,1... | collective-permute-start | bytes 36872 | tf_op jit(solution)/shard_map/ppermute | solution.py:137
  16.0 4.7 %collective-permute-start.1 = (bf16[4,1536]{1,0:T(4,128)(2,1)S(1)}, bf16[4,1536]{1,0:T(4,128)(2,1)S(1)}, u32[]{:S(2)}, u32[]{:S(2)}) collective-permute-start(bf16[4,1536]{1,0:T(4,128)(2,1)S(1)} %pad_maximum_fusion.9), channel_id=1, source_target_pairs={{1,0},{2,1},{3,2},{4,3},{5,4},{6,5},{7,6},{8,7},{9,8},{10,9},{11,1... | collective-permute-start | bytes 36872 | tf_op jit(solution)/shard_map/ppermute | solution.py:138
  21.5 18.0 %collective-permute-start.10 = (bf16[1024,256]{1,0:T(8,128)(2,1)S(1)}, bf16[1024,256]{1,0:T(8,128)(2,1)S(1)}, u32[]{:S(2)}, u32[]{:S(2)}) collective-permute-start(bf16[1024,256]{1,0:T(8,128)(2,1)S(1)} %pad_maximum_fusion.5.refs_4_), channel_id=1, source_target_pairs={{0,4},{4,8},{8,12},{12,0},{1,5},{5,9},{9,13},{13,1},{2,6},{6,10},{... | collective-permute-start | bytes 1572872 | tf_op jit(solution)/shard_map/ppermute | solution.py:150
  23.3 8.4 %collective-permute-start.2 = (bf16[272,128]{1,0:T(8,128)(2,1)S(1)}, bf16[272,128]{1,0:T(8,128)(2,1)S(1)}, u32[]{:S(2)}, u32[]{:S(2)}) collective-permute-start(bf16[272,128]{1,0:T(8,128)(2,1)S(1)} %bitcast.113), channel_id=1, source_target_pairs={{0,1},{1,2},{2,3},{3,0},{4,5},{5,6},{6,7},{7,4},{8,9},{9,10},{10,1... | collective-permute-start | bytes 208904 | tf_op jit(solution)/shard_map/ppermute | solution.py:161
  26.0 11.0 %collective-permute-start.3 = (bf16[272,128]{1,0:T(8,128)(2,1)S(1)}, bf16[272,128]{1,0:T(8,128)(2,1)S(1)}, u32[]{:S(2)}, u32[]{:S(2)}) collective-permute-start(bf16[272,128]{1,0:T(8,128)(2,1)S(1)} %bitcast.111), channel_id=1, source_target_pairs={{0,2},{1,3},{2,0},{3,1},{4,6},{5,7},{6,4},{7,5},{8,10},{9,11},{10,... | collective-permute-start | bytes 208904 | tf_op jit(solution)/shard_map/ppermute | solution.py:161
  29.5 7.5 %collective-permute-start.4 = (bf16[272,128]{1,0:T(8,128)(2,1)S(1)}, bf16[272,128]{1,0:T(8,128)(2,1)S(1)}, u32[]{:S(2)}, u32[]{:S(2)}) collective-permute-start(bf16[272,128]{1,0:T(8,128)(2,1)S(1)} %bitcast.112), channel_id=1, source_target_pairs={{0,3},{1,0},{2,1},{3,2},{4,7},{5,4},{6,5},{7,6},{8,11},{9,8},{10,9... | collective-permute-start | bytes 208904 | tf_op jit(solution)/shard_map/ppermute | solution.py:161
  31.6 10.6 %collective-permute-start.9 = (bf16[1024,256]{1,0:T(8,128)(2,1)S(1)}, bf16[1024,256]{1,0:T(8,128)(2,1)S(1)}, u32[]{:S(2)}, u32[]{:S(2)}) collective-permute-start(bf16[1024,256]{1,0:T(8,128)(2,1)S(1)} %pad_maximum_fusion.5.refs_4_), channel_id=1, source_target_pairs={{0,12},{4,0},{8,4},{12,8},{1,13},{5,1},{9,5},{13,9},{2,14},{6,2},{... | collective-permute-start | bytes 1572872 | tf_op jit(solution)/shard_map/ppermute | solution.py:150
  31.7 20.5 %collective-permute-start.8 = (bf16[1024,256]{1,0:T(8,128)(2,1)S(1)}, bf16[1024,256]{1,0:T(8,128)(2,1)S(1)}, u32[]{:S(2)}, u32[]{:S(2)}) collective-permute-start(bf16[1024,256]{1,0:T(8,128)(2,1)S(1)} %pad_maximum_fusion.5.refs_4_), channel_id=1, source_target_pairs={{0,8},{4,12},{8,0},{12,4},{1,9},{5,13},{9,1},{13,5},{2,10},{6,14},... | collective-permute-start | bytes 1572872 | tf_op jit(solution)/shard_map/ppermute | solution.py:150
  55.5 5.5 %collective-permute-start.12 = (bf16[272,256]{1,0:T(8,128)(2,1)S(1)}, bf16[272,256]{1,0:T(8,128)(2,1)S(1)}, u32[]{:S(2)}, u32[]{:S(2)}) collective-permute-start(bf16[272,256]{1,0:T(8,128)(2,1)S(1)} %get-tuple-element.57), channel_id=1, source_target_pairs={{0,2},{1,3},{2,0},{3,1},{4,6},{5,7},{6,4},{7,5},{8,10},{9,11},{10,... | collective-permute-start | bytes 417800 | tf_op jit(solution)/shard_map/ppermute | solution.py:173
  55.8 6.6 %collective-permute-start.13 = (bf16[272,256]{1,0:T(8,128)(2,1)S(1)}, bf16[272,256]{1,0:T(8,128)(2,1)S(1)}, u32[]{:S(2)}, u32[]{:S(2)}) collective-permute-start(bf16[272,256]{1,0:T(8,128)(2,1)S(1)} %get-tuple-element.58), channel_id=1, source_target_pairs={{0,1},{1,2},{2,3},{3,0},{4,5},{5,6},{6,7},{7,4},{8,9},{9,10},{10,1... | collective-permute-start | bytes 417800 | tf_op jit(solution)/shard_map/ppermute | solution.py:173
  81.6 20.0 %collective-permute-start.14 = (bf16[768,1536]{1,0:T(8,128)(2,1)}, bf16[768,1536]{1,0:T(8,128)(2,1)}, u32[]{:S(2)}, u32[]{:S(2)}) collective-permute-start(bf16[768,1536]{1,0:T(8,128)(2,1)} %constant_dynamic-slice_fusion.8), channel_id=1, source_target_pairs={{0,16},{16,0},{1,17},{17,1},{2,18},{18,2},{3,19},{19,3},{4,20},{20... | collective-permute-start | bytes 7077896 | tf_op jit(solution)/shard_map/ppermute | solution.py:220
  105.0 21.4 %collective-permute-start.15 = (bf16[192,1536]{1,0:T(8,128)(2,1)}, bf16[192,1536]{1,0:T(8,128)(2,1)S(1)}, u32[]{:S(2)}, u32[]{:S(2)}) collective-permute-start(bf16[192,1536]{1,0:T(8,128)(2,1)} %get-tuple-element.71), channel_id=1, source_target_pairs={{0,64},{1,65},{2,66},{3,67},{4,68},{5,69},{6,70},{7,71},{8,72},{9,... | collective-permute-start | bytes 1769480 | tf_op jit(solution)/shard_map/ppermute | solution.py:46
  105.0 21.4 %collective-permute-start.16 = (bf16[192,1536]{1,0:T(8,128)(2,1)}, bf16[192,1536]{1,0:T(8,128)(2,1)}, u32[]{:S(2)}, u32[]{:S(2)}) collective-permute-start(bf16[192,1536]{1,0:T(8,128)(2,1)} %get-tuple-element.73), channel_id=1, source_target_pairs={{0,32},{1,33},{2,34},{3,35},{4,36},{5,37},{6,38},{7,39},{8,40},{9,... | collective-permute-start | bytes 1769480 | tf_op jit(solution)/shard_map/ppermute | solution.py:46
  107.6 18.8 %collective-permute-start.17 = (bf16[192,1536]{1,0:T(8,128)(2,1)S(1)}, bf16[192,1536]{1,0:T(8,128)(2,1)}, u32[]{:S(2)}, u32[]{:S(2)}) collective-permute-start(bf16[192,1536]{1,0:T(8,128)(2,1)S(1)} %get-tuple-element.72), channel_id=1, source_target_pairs={{0,96},{1,97},{2,98},{3,99},{4,100},{5,101},{6,102},{7,103},{8,104... | collective-permute-start | bytes 1769480 | tf_op jit(solution)/shard_map/ppermute | solution.py:46
  107.6 4.5 %collective-permute-start.18 = (f32[3,768]{1,0:T(4,128)S(1)}, f32[3,768]{1,0:T(4,128)S(1)}, u32[]{:S(2)}, u32[]{:S(2)}) collective-permute-start(f32[3,768]{1,0:T(4,128)S(1)} %constant_dynamic-slice_fusion.3), channel_id=1, source_target_pairs={{0,16},{16,0},{1,17},{17,1},{2,18},{18,2},{3,19},{19,3},{4,20},{20... | collective-permute-start | bytes 27656 | tf_op jit(solution)/shard_map/ppermute | solution.py:232
  112.1 10.2 %collective-permute-start.19 = (f32[3,768]{1,0:T(4,128)S(1)}, f32[3,768]{1,0:T(4,128)S(1)}, u32[]{:S(2)}, u32[]{:S(2)}) collective-permute-start(f32[3,768]{1,0:T(4,128)S(1)} %dynamic-slice_add_fusion), channel_id=1, source_target_pairs={{0,64},{1,65},{2,66},{3,67},{4,68},{5,69},{6,70},{7,71},{8,72},{9,... | collective-permute-start | bytes 27656 | tf_op jit(solution)/shard_map/ppermute | solution.py:46
  112.1 11.9 %collective-permute-start.20 = (f32[3,768]{1,0:T(4,128)S(1)}, f32[3,768]{1,0:T(4,128)}, u32[]{:S(2)}, u32[]{:S(2)}) collective-permute-start(f32[3,768]{1,0:T(4,128)S(1)} %dynamic-slice_add_fusion), channel_id=1, source_target_pairs={{0,32},{1,33},{2,34},{3,35},{4,36},{5,37},{6,38},{7,39},{8,40},{9,... | collective-permute-start | bytes 27656 | tf_op jit(solution)/shard_map/ppermute | solution.py:46
  128.1 5.9 %collective-permute-start.22 = (bf16[56,1536]{1,0:T(8,128)(2,1)S(1)}, bf16[56,1536]{1,0:T(8,128)(2,1)S(1)}, u32[]{:S(2)}, u32[]{:S(2)}) collective-permute-start(bf16[56,1536]{1,0:T(8,128)(2,1)S(1)} %get-tuple-element.105), channel_id=1, source_target_pairs={{0,2},{1,3},{2,0},{3,1},{4,6},{5,7},{6,4},{7,5},{8,10},{9,11},{10,... | collective-permute-start | bytes 516104 | tf_op jit(solution)/shard_map/ppermute | solution.py:46
  128.2 5.9 %collective-permute-start.23 = (bf16[56,1536]{1,0:T(8,128)(2,1)S(1)}, bf16[56,1536]{1,0:T(8,128)(2,1)S(1)}, u32[]{:S(2)}, u32[]{:S(2)}) collective-permute-start(bf16[56,1536]{1,0:T(8,128)(2,1)S(1)} %get-tuple-element.106), channel_id=1, source_target_pairs={{0,1},{1,2},{2,3},{3,0},{4,5},{5,6},{6,7},{7,4},{8,9},{9,10},{10,1... | collective-permute-start | bytes 516104 | tf_op jit(solution)/shard_map/ppermute | solution.py:46
  128.2 7.8 %collective-permute-start.24 = (bf16[56,1536]{1,0:T(8,128)(2,1)S(1)}, bf16[56,1536]{1,0:T(8,128)(2,1)S(1)}, u32[]{:S(2)}, u32[]{:S(2)}) collective-permute-start(bf16[56,1536]{1,0:T(8,128)(2,1)S(1)} %get-tuple-element.107), channel_id=1, source_target_pairs={{0,3},{1,0},{2,1},{3,2},{4,7},{5,4},{6,5},{7,6},{8,11},{9,8},{10,9... | collective-permute-start | bytes 516104 | tf_op jit(solution)/shard_map/ppermute | solution.py:46
  136.1 5.8 %collective-permute-start.25 = (bf16[56,1536]{1,0:T(8,128)(2,1)S(1)}, bf16[56,1536]{1,0:T(8,128)(2,1)S(1)}, u32[]{:S(2)}, u32[]{:S(2)}) collective-permute-start(bf16[56,1536]{1,0:T(8,128)(2,1)S(1)} %add_convert_fusion.3), channel_id=1, source_target_pairs={{0,8},{1,9},{2,10},{3,11},{4,12},{5,13},{6,14},{7,15},{8,0},{9,1},... | collective-permute-start | bytes 516104 | tf_op jit(solution)/shard_map/ppermute | solution.py:46
  138.6 5.6 %collective-permute-start.26 = (bf16[56,1536]{1,0:T(8,128)(2,1)S(1)}, bf16[56,1536]{1,0:T(8,128)(2,1)S(1)}, u32[]{:S(2)}, u32[]{:S(2)}) collective-permute-start(bf16[56,1536]{1,0:T(8,128)(2,1)S(1)} %add_convert_fusion.3), channel_id=1, source_target_pairs={{0,4},{1,5},{2,6},{3,7},{4,8},{5,9},{6,10},{7,11},{8,12},{9,13},{1... | collective-permute-start | bytes 516104 | tf_op jit(solution)/shard_map/ppermute | solution.py:46
  139.3 4.9 %collective-permute-start.27 = (bf16[56,1536]{1,0:T(8,128)(2,1)S(1)}, bf16[56,1536]{1,0:T(8,128)(2,1)S(1)}, u32[]{:S(2)}, u32[]{:S(2)}) collective-permute-start(bf16[56,1536]{1,0:T(8,128)(2,1)S(1)} %add_convert_fusion.3), channel_id=1, source_target_pairs={{0,12},{1,13},{2,14},{3,15},{4,0},{5,1},{6,2},{7,3},{8,4},{9,5},{1... | collective-permute-start | bytes 516104 | tf_op jit(solution)/shard_map/ppermute | solution.py:46
  144.7 5.6 %collective-permute-start.29 = (bf16[48,1536]{1,0:T(8,128)(2,1)S(1)}, bf16[48,1536]{1,0:T(8,128)(2,1)S(1)}, u32[]{:S(2)}, u32[]{:S(2)}) collective-permute-start(bf16[48,1536]{1,0:T(8,128)(2,1)S(1)} %get-tuple-element.68), channel_id=1, source_target_pairs={{0,2},{1,3},{2,0},{3,1},{4,6},{5,7},{6,4},{7,5},{8,10},{9,11},{10,... | collective-permute-start | bytes 442376 | tf_op jit(solution)/shard_map/ppermute | solution.py:46
  145.3 5.9 %collective-permute-start.30 = (bf16[48,1536]{1,0:T(8,128)(2,1)S(1)}, bf16[48,1536]{1,0:T(8,128)(2,1)S(1)}, u32[]{:S(2)}, u32[]{:S(2)}) collective-permute-start(bf16[48,1536]{1,0:T(8,128)(2,1)S(1)} %get-tuple-element.68), channel_id=1, source_target_pairs={{0,3},{1,0},{2,1},{3,2},{4,7},{5,4},{6,5},{7,6},{8,11},{9,8},{10,9... | collective-permute-start | bytes 442376 | tf_op jit(solution)/shard_map/ppermute | solution.py:46
  151.2 10.7 %collective-permute-start.31 = (bf16[192,1536]{1,0:T(8,128)(2,1)S(1)}, bf16[192,1536]{1,0:T(8,128)(2,1)S(1)}, u32[]{:S(2)}, u32[]{:S(2)}) collective-permute-start(bf16[192,1536]{1,0:T(8,128)(2,1)S(1)} %bitcast.98), channel_id=1, source_target_pairs={{0,32},{1,33},{2,34},{3,35},{4,36},{5,37},{6,38},{7,39},{8,40},{9,... | collective-permute-start | bytes 1769480 | tf_op jit(solution)/shard_map/ppermute | solution.py:46
  151.4 11.7 %collective-permute-start.32 = (bf16[192,1536]{1,0:T(8,128)(2,1)S(1)}, bf16[192,1536]{1,0:T(8,128)(2,1)S(1)}, u32[]{:S(2)}, u32[]{:S(2)}) collective-permute-start(bf16[192,1536]{1,0:T(8,128)(2,1)S(1)} %bitcast.99), channel_id=1, source_target_pairs={{0,64},{1,65},{2,66},{3,67},{4,68},{5,69},{6,70},{7,71},{8,72},{9,... | collective-permute-start | bytes 1769480 | tf_op jit(solution)/shard_map/ppermute | solution.py:46
  154.6 14.7 %collective-permute-start.33 = (bf16[192,1536]{1,0:T(8,128)(2,1)S(1)}, bf16[192,1536]{1,0:T(8,128)(2,1)S(1)}, u32[]{:S(2)}, u32[]{:S(2)}) collective-permute-start(bf16[192,1536]{1,0:T(8,128)(2,1)S(1)} %bitcast.100), channel_id=1, source_target_pairs={{0,96},{1,97},{2,98},{3,99},{4,100},{5,101},{6,102},{7,103},{8,104... | collective-permute-start | bytes 1769480 | tf_op jit(solution)/shard_map/ppermute | solution.py:46
  169.3 21.6 %collective-permute-start.34 = (bf16[768,1536]{1,0:T(8,128)(2,1)S(1)}, bf16[768,1536]{1,0:T(8,128)(2,1)S(1)}, u32[]{:S(2)}, u32[]{:S(2)}) collective-permute-start(bf16[768,1536]{1,0:T(8,128)(2,1)S(1)} %bitcast.96), channel_id=1, source_target_pairs={{0,16},{16,0},{1,17},{17,1},{2,18},{18,2},{3,19},{19,3},{4,20},{20... | collective-permute-start | bytes 7077896 | tf_op jit(solution)/shard_map/ppermute | solution.py:260
  (14 other events, 77.3 us)

commit v2 on v1

v2 whole, which is shorter than its diff:
```python
import math

import jax
import jax.numpy as jnp
from jax import lax
from jax.experimental import pallas as pl
from jax.experimental.pallas import tpu as pltpu
from jax.sharding import Mesh, PartitionSpec as P

H = 4
DH = 64
DV = 192
AXES = ("x", "c", "z", "y")
SIZES = (4, 2, 4, 4)
BF = jnp.bfloat16
F32 = jnp.float32
TAIL = 16
VMEM = pl.BlockSpec(memory_space=pltpu.VMEM)
SMEM = pl.BlockSpec(memory_space=pltpu.SMEM)
ANY = pl.BlockSpec(memory_space=pl.ANY)
SUM_RINGS = (("x", "y"), ("y", "z"), ("z", "x"))
HEAD_RING = ("y", "z")
ROW_RING = ("z", "y")


def params(mib):
    return pltpu.CompilerParams(vmem_limit_bytes=mib << 20)


def turn(axes, step):
    pairs = []
    for x in range(4):
        for c in range(2):
            for z in range(4):
                for y in range(4):
                    at = {"x": x, "z": z, "y": y}
                    to = dict(at)
                    to[axes[c]] = (at[axes[c]] + step) % 4
                    flat = [((p["x"] * 2 + c) * 4 + p["z"]) * 4 + p["y"] for p in (at, to)]
                    pairs.append(tuple(flat))
    return pairs


def exchange(pieces, axes, sign=1):
    got = [pieces[0], None, None, None]
    for d in (2, 1, 3):
        got[d] = lax.ppermute(pieces[d], AXES, turn(axes, sign * d))
    return got


def total_of(got):
    a, b, c, d = (g.astype(F32) for g in got)
    return (a + c) + (b + d)


def project(at, tokens, query_weight, key_weight, value_weight):
    rows = tokens.shape[0]

    def kernel(at_ref, tok_ref, wq_ref, wk_ref, wv_ref, *refs):
        outs, held = refs[:4], refs[4]
        tok = tok_ref[...]
        v = jnp.dot(tok, wv_ref[...], preferred_element_type=F32)
        k = jnp.dot(tok, wk_ref[...], preferred_element_type=F32)
        q = jnp.dot(tok, wq_ref[...], preferred_element_type=F32)
        zero = jnp.zeros((rows, DH), F32)
        for h in range(H):
            held[h] = jnp.concatenate(
                [
                    v[:, h * DV : (h + 1) * DV],
                    k[:, h * DH : (h + 1) * DH],
                    zero,
                    q[:, h * DH : (h + 1) * DH],
                ],
                axis=1,
            ).astype(BF)
        for d in range(4):
            outs[d][...] = held[(at_ref[0] + d) % 4]

    return pl.pallas_call(
        kernel,
        out_shape=[jax.ShapeDtypeStruct((rows, 384), BF)] * 4,
        in_specs=[SMEM] + [VMEM] * 4,
        out_specs=[VMEM] * 4,
        scratch_shapes=[pltpu.VMEM((4, rows, 384), BF)],
        compiler_params=params(40),
        name="project",
    )(at, tokens, query_weight, key_weight, value_weight)


def stack_rows(parts):
    rows = parts[0].shape[0]

    def kernel(*refs):
        ins, out = refs[:4], refs[4]
        row = lax.broadcasted_iota(jnp.int32, (TAIL, 128), 0)
        tail = jnp.zeros((TAIL, 128), F32)
        for d in range(4):
            out[d * rows : (d + 1) * rows, :] = ins[d][:, :256]
            first = ins[d][:TAIL, 256:].astype(F32)[:1]
            final = ins[d][rows - TAIL :, 256:].astype(F32)[TAIL - 1 :]
            tail = jnp.where(row == d, first, tail)
            tail = jnp.where(row == 4 + d, final, tail)
        out[4 * rows :, :128] = jnp.zeros((TAIL, 128), BF)
        out[4 * rows :, 128:] = tail.astype(BF)

    return pl.pallas_call(
        kernel,
        out_shape=jax.ShapeDtypeStruct((4 * rows + TAIL, 256), BF),
        in_specs=[VMEM] * 4,
        out_specs=VMEM,
        compiler_params=params(16),
        name="stack_rows",
    )(*parts)


def attend(bases, q, pairs, state, flags=None):
    rows = q[0].shape[0]
    width = 4 * rows
    first = state is None
    last = flags is not None

    def kernel(bases_ref, *refs):
        if last:
            flags_ref, refs = refs[0], refs[1:]
        q_refs, refs = refs[:4], refs[4:]
        pair_refs, refs = refs[: len(pairs)], refs[len(pairs) :]
        if not first:
            max_in, sum_in, refs = refs[:4], refs[4:8], refs[8:]
        lane = lax.broadcasted_iota(jnp.int32, (width, 256), 1)
        place = lax.broadcasted_iota(jnp.int32, (1, rows), 1)

        def masks(n):
            return jnp.concatenate(
                [place + bases_ref[4 * n + i] < bases_ref[16] for i in range(4)], axis=1
            )

        def values_of(ref):
            return jnp.where(lane == DV, jnp.ones((), BF), ref[:width, :])

        def scores_of(query, ref, keep):
            scores = lax.dot_general(
                query, ref[:width, 128:], (((1,), (1,)), ((), ())), preferred_element_type=F32
            )
            return jnp.where(keep, scores * (1.0 / math.sqrt(DH)), -1e30)

        def shares(sums):
            return sums / sums[:, DV : DV + 1]

        if last:
            tails = [r[width:, 128:].astype(F32) for r in pair_refs]
            own, low, high = tails[0], tails[1], tails[2]
            row = lax.broadcasted_iota(jnp.int32, (TAIL, 128), 0)
            edge = jnp.zeros((TAIL, 128), F32)
            for d in range(4):
                n, m = (d + 1) % 4, (d + 3) % 4
                other = jnp.where(flags_ref[0] == 0, own[4 + n : 5 + n], low[4 + d : 5 + d])
                prev = jnp.where(flags_ref[1 + d] == 1, low[4 + n : 5 + n], other)
                other = jnp.where(flags_ref[0] == 0, own[m : m + 1], high[d : d + 1])
                nxt = jnp.where(flags_ref[5 + d] == 1, high[m : m + 1], other)
                edge = jnp.where(row == d, prev, edge)
                edge = jnp.where(row == 4 + d, nxt, edge)
            edge = edge.astype(BF)
            parts = [scores_of(edge, r, masks(n)) for n, r in enumerate(pair_refs)]
            peak = jnp.max(parts[0], axis=1, keepdims=True)
            for s in parts[1:]:
                peak = jnp.maximum(peak, jnp.max(s, axis=1, keepdims=True))
            edge_sums = jnp.zeros((TAIL, 256), F32)
            for s, r in zip(parts, pair_refs):
                edge_sums += jnp.dot(jnp.exp(s - peak).astype(BF), values_of(r), preferred_element_type=F32)
            edge_out = shares(edge_sums)
            row = lax.broadcasted_iota(jnp.int32, (TAIL, 256), 0)

        near = len(pairs) - 1
        keep = masks(near)
        values = values_of(pair_refs[near])
        for i in range(4):
            scores = scores_of(q_refs[i][:, 256:], pair_refs[near], keep)
            peak = jnp.max(scores, axis=1, keepdims=True)
            if not first:
                before = max_in[i][:, :1]
                peak = jnp.maximum(peak, before)
            probs = jnp.exp(scores - peak).astype(BF)
            update = jnp.dot(probs, values, preferred_element_type=F32)
            if not first:
                update = update + sum_in[i][...] * jnp.exp(before - peak)
            if last:
                refs[i][:rows, :] = shares(update).astype(BF)
                ends = jnp.where(row == 0, edge_out[i : i + 1], jnp.zeros((TAIL, 256), F32))
                ends = jnp.where(row == 1, edge_out[4 + i : 5 + i], ends)
                refs[i][rows:, :] = ends.astype(BF)
            else:
                refs[i][...] = jnp.broadcast_to(peak, (rows, 128))
                refs[4 + i][...] = update

    ins = [*q, *pairs]
    if not first:
        ins += [*state[0], *state[1]]
    if last:
        outs = [jax.ShapeDtypeStruct((rows + TAIL, 256), BF)] * 4
    else:
        outs = [jax.ShapeDtypeStruct((rows, 128), F32)] * 4
        outs += [jax.ShapeDtypeStruct((rows, 256), F32)] * 4
    scalars = [bases, flags] if last else [bases]
    got = pl.pallas_call(
        kernel,
        out_shape=outs,
        in_specs=[SMEM] * len(scalars) + [VMEM] * len(ins),
        out_specs=[VMEM] * len(outs),
        compiler_params=params(40),
        cost_estimate=pl.CostEstimate(
            flops=4 * 2 * rows * width * 512, bytes_accessed=4 << 20, transcendentals=4 * rows * width
        ),
        name="attend",
    )(*scalars, *ins)
    return got if last else (got[:4], got[4:])


def gelu_parts(pre):
    slope = math.sqrt(2.0 / math.pi)
    square = pre * pre
    bend = jnp.tanh(slope * (pre + 0.044715 * (square * pre)))
    return bend, square, slope


def forward(scalars, back, tokens, halo, skipped, out_heads, depth_weight):
    rows, columns = tokens.shape
    fine = 2 * rows
    wide = 256

    def kernel(s_ref, b0, b1, b2, b3, tok_ref, halo_ref, skip_ref, ow_ref, dw_ref, up_ref, act_ref, att, held):
        @pl.when(pl.program_id(0) == 0)
        def _():
            mixed = [b[:, :DV].astype(F32) for b in (b0, b1, b2, b3)]
            squares = sum(jnp.sum(m * m, axis=1, keepdims=True) for m in mixed)
            scale = lax.rsqrt(squares * (1.0 / (H * DV)) + 1e-05)
            for d in range(4):
                att[d] = (mixed[d] * scale).astype(BF)

        grown = jnp.zeros((rows + TAIL, wide), F32)
        for d in range(4):
            grown += jnp.dot(att[d], ow_ref[(s_ref[0] + d) % 4], preferred_element_type=F32)
        hidden = (tok_ref[...].astype(F32) + grown[:rows]).astype(BF)
        ends = (halo_ref[:TAIL, :] + grown[rows:]).astype(BF).astype(F32)
        twice = lax.broadcasted_iota(jnp.int32, (fine, rows), 0) // 2
        twice = jnp.where(twice == lax.broadcasted_iota(jnp.int32, (fine, rows), 1), 1.0, 0.0).astype(BF)
        up = jnp.dot(twice, hidden, preferred_element_type=F32) + skip_ref[...].astype(F32)
        held[8 : 8 + fine, :] = up.astype(BF).astype(F32)
        row = lax.broadcasted_iota(jnp.int32, (8, wide), 0)
        low = (ends[:1] + halo_ref[16:24, :]).astype(BF).astype(F32)
        held[:8, :] = jnp.where((row >= 6) & (s_ref[1] > 0), low, 0.0)
        high = (ends[1:2] + halo_ref[24:32, :]).astype(BF).astype(F32)
        held[8 + fine :, :] = jnp.where((row < 2) & (s_ref[2] > 0), high, 0.0)
        up_ref[...] = held[...].astype(BF)
        pre = (
            dw_ref[0:1, :] * held[7 : 7 + fine, :]
            + dw_ref[1:2, :] * held[8 : 8 + fine, :]
            + dw_ref[2:3, :] * held[9 : 9 + fine, :]
        )
        bend, _, _ = gelu_parts(pre)
        act_ref[...] = (pre * (0.5 * (1.0 + bend))).astype(BF)

    def cols(count):
        return pl.BlockSpec((count, wide), lambda j: (0, j))

    whole = pl.BlockSpec((rows + TAIL, 256), lambda j: (0, 0))
    return pl.pallas_call(
        kernel,
        grid=(columns // wide,),
        out_shape=[
            jax.ShapeDtypeStruct((fine + 16, columns), BF),
            jax.ShapeDtypeStruct((fine, columns), BF),
        ],
        in_specs=[SMEM]
        + [whole] * 4
        + [
            cols(rows),
            cols(32),
            cols(fine),
            pl.BlockSpec((H, DV, wide), lambda j: (0, 0, j)),
            cols(3),
        ],
        out_specs=[cols(fine + 16), cols(fine)],
        scratch_shapes=[pltpu.VMEM((4, rows + TAIL, DV), BF), pltpu.VMEM((fine + 16, wide), F32)],
        compiler_params=params(40),
        name="forward",
    )(scalars, *back, tokens, halo, skipped, out_heads, depth_weight)


def backward(up, grad_act, grad_act_ends, depth_weight):
    fine, columns = grad_act.shape
    wide = 256

    def kernel(up_ref, ga_ref, ge_ref, dw_ref, gs_ref, gd_ref, held, grad):
        held[:8, :] = jnp.zeros((8, wide), F32)
        held[8 : fine + 24, :] = up_ref[...].astype(F32)
        held[fine + 24 :, :] = jnp.zeros((8, wide), F32)

        def grad_of(start, count, upstream):
            pre = (
                dw_ref[0:1, :] * held[start - 1 : start - 1 + count, :]
                + dw_ref[1:2, :] * held[start : start + count, :]
                + dw_ref[2:3, :] * held[start + 1 : start + 1 + count, :]
            )
            bend, square, slope = gelu_parts(pre)
            rate = 0.5 * (1.0 + bend) + (0.5 * slope) * pre * (1.0 - bend * bend) * (
                1.0 + (3 * 0.044715) * square
            )
            return (upstream * rate).astype(BF).astype(F32)

        grad[:8, :] = grad_of(8, 8, ge_ref[:8, :])
        mid = grad_of(16, fine, ga_ref[...])
        grad[8 : 8 + fine, :] = mid
        grad[8 + fine :, :] = grad_of(16 + fine, 8, ge_ref[8:, :])
        gs_ref[...] = (
            dw_ref[0:1, :] * grad[9 : 9 + fine, :]
            + dw_ref[1:2, :] * mid
            + dw_ref[2:3, :] * grad[7 : 7 + fine, :]
        ).astype(BF)
        for t in range(3):
            gd_ref[t : t + 1, :] = jnp.sum(held[15 + t : 15 + t + fine, :] * mid, axis=0, keepdims=True)

    def cols(count):
        return pl.BlockSpec((count, wide), lambda j: (0, j))

    return pl.pallas_call(
        kernel,
        grid=(columns // wide,),
        out_shape=[jax.ShapeDtypeStruct((fine, columns), BF), jax.ShapeDtypeStruct((3, columns), F32)],
        in_specs=[cols(fine + 16), cols(fine), cols(16), cols(3)],
        out_specs=[cols(fine), cols(3)],
        scratch_shapes=[pltpu.VMEM((fine + 32, wide), F32), pltpu.VMEM((fine + 16, wide), F32)],
        compiler_params=params(40),
        cost_estimate=pl.CostEstimate(flops=60 * fine * columns, bytes_accessed=9 << 20, transcendentals=fine * columns),
        name="backward",
    )(up, grad_act, grad_act_ends, depth_weight)


def product(scalars, act, upstream, steps, arrived=None):
    half, quarter = act.shape[1] // 2, upstream.shape[1] // 4
    joint = arrived is None

    def kernel(s_ref, a_ref, g_ref, *refs):
        left = a_ref[:, pl.ds(pl.multiple_of(s_ref[0] * half, 128), half)]
        for n, d in enumerate(steps):
            at = pl.multiple_of((s_ref[1] + d) % 4 * quarter, 128)
            block = lax.dot_general(
                left, g_ref[:, pl.ds(at, quarter)], (((0,), (0,)), ((), ())), preferred_element_type=F32
            )
            if joint:
                refs[0][n] = block.astype(BF)
            else:
                refs[1 + n][...] = (block + refs[0][n].astype(F32)).astype(BF)

    if joint:
        outs = jax.ShapeDtypeStruct((len(steps), half, quarter), BF)
        out_specs = VMEM
    else:
        outs = [jax.ShapeDtypeStruct((half, quarter), BF)] * len(steps)
        out_specs = [VMEM] * len(steps)
    ins = [act, upstream] if joint else [act, upstream, arrived]
    return pl.pallas_call(
        kernel,
        out_shape=outs,
        in_specs=[SMEM] + [VMEM] * len(ins),
        out_specs=out_specs,
        compiler_params=params(40),
        cost_estimate=pl.CostEstimate(
            flops=2 * act.shape[0] * half * quarter * len(steps), bytes_accessed=6 << 20, transcendentals=0
        ),
        name="product",
    )(scalars, *ins)


def split_rows(at, got, rider):
    rows, columns = got[0].shape
    slim = rows // 4

    def kernel(at_ref, *refs):
        ins, rider_ref, outs = refs[:4], refs[4], refs[5:]
        for d in range(4):
            take = pl.ds(pl.multiple_of((at_ref[0] + d) % 4 * slim, 16), slim)
            outs[d][:slim, :] = total_of([r[take, :] for r in ins]).astype(BF)
            outs[d][slim:, :] = rider_ref[...]

    return pl.pallas_call(
        kernel,
        out_shape=[jax.ShapeDtypeStruct((slim + TAIL, columns), BF)] * 4,
        in_specs=[SMEM] + [VMEM] * 5,
        out_specs=[VMEM] * 4,
        compiler_params=params(24),
        name="split_rows",
    )(at, *got, rider)


def join_rows(at, got, rider):
    slim, columns = got[0].shape

    def kernel(at_ref, *refs):
        ins, rider_ref, out = refs[:4], refs[4], refs[5]
        for d in range(4):
            put = pl.ds(pl.multiple_of((at_ref[0] + 4 - d) % 4 * slim, 16), slim)
            out[put, :] = ins[d][...]
        out[4 * slim :, :] = rider_ref[...]

    return pl.pallas_call(
        kernel,
        out_shape=jax.ShapeDtypeStruct((4 * slim + TAIL, columns), BF),
        in_specs=[SMEM] + [VMEM] * 5,
        out_specs=VMEM,
        compiler_params=params(24),
        name="join_rows",
    )(at, *got, rider)


def lay_out(scalars, own, other):
    half, quarter = own[0].shape[0] - TAIL, own[0].shape[1]

    def kernel(s_ref, *refs):
        blocks, out, sems = refs[:8], refs[8], refs[9]
        copies = []
        for n in range(8):
            mine = n < 4
            side = s_ref[0] if mine else 1 - s_ref[0]
            at = s_ref[1] if mine else s_ref[2]
            down = pl.multiple_of(side * half, 16)
            over = pl.multiple_of((at + 4 - n % 4) % 4 * quarter, 128)
            copies.append(
                pltpu.make_async_copy(
                    blocks[n].at[pl.ds(0, half), :],
                    out.at[pl.ds(down, half), pl.ds(over, quarter)],
                    sems.at[n],
                )
            )
        for copy in copies:
            copy.start()
        for copy in copies:
            copy.wait()

    return pl.pallas_call(
        kernel,
        out_shape=jax.ShapeDtypeStruct((2 * half, 4 * quarter), BF),
        in_specs=[SMEM] + [ANY] * 8,
        out_specs=ANY,
        scratch_shapes=[pltpu.SemaphoreType.DMA((8,))],
        name="lay_out",
    )(scalars, *own, *other)


def local(
    trunk,
    skip,
    valid_bins,
    query_weight,
    key_weight,
    value_weight,
    out_weight,
    depth_weight,
    point_weight,
    cotangent,
):
    tokens, skipped, upstream = trunk[0], skip[0], cotangent[0]
    rows, columns = tokens.shape
    fine = skipped.shape[0]
    ix, ic, iz, iy = (lax.axis_index(a) for a in AXES)
    index = {"x": ix, "z": iz, "y": iy}
    place = iz * 4 + iy

    def at(axes, swap=False):
        a, b = axes[::-1] if swap else axes
        return jnp.where(ic == 0, index[a], index[b])

    def ints(*values):
        return jnp.stack([jnp.asarray(v, jnp.int32) for v in values])

    head_at, row_at = at(HEAD_RING), at(ROW_RING)

    blocks = project(ints(head_at), tokens, query_weight, key_weight, value_weight)
    q = exchange(blocks, HEAD_RING)
    own = stack_rows(q)
    far = {d: lax.ppermute(own, AXES, turn(ROW_RING, d)) for d in (1, 3, 2)}

    def bases(*steps):
        values = []
        for far_by in steps:
            for d in range(4):
                h, r = (head_at - d) % 4, (row_at - far_by) % 4
                values.append(jnp.where(ic == 0, r * 4 + h, h * 4 + r) * rows)
        values += [jnp.int32(0)] * (16 - len(values)) + [valid_bins[0]]
        return ints(*values)

    state = attend(bases(0), q, [own], None)

    (tokens_l, skipped_l, upstream_l), _ = lax.optimization_barrier(
        ((tokens, skipped, upstream), state[0][0])
    )
    down = jnp.concatenate([tokens_l[-1:], skipped_l[-2:], upstream_l[-1:]], axis=0)
    up = jnp.concatenate([tokens_l[:1], skipped_l[:2], upstream_l[:1]], axis=0)
    before = lax.ppermute(down, ("z", "y"), [(i, i + 1) for i in range(15)])
    after = lax.ppermute(up, ("z", "y"), [(i + 1, i) for i in range(15)])

    def blank(count):
        return jnp.zeros((count, columns), BF)

    halo = jnp.concatenate(
        [before[:1], after[:1], blank(20), before[1:3], after[1:3], blank(6)], axis=0
    ).astype(F32)
    ends = jnp.concatenate([blank(7), before[3:4], after[3:4], blank(7)], axis=0)
    dims = (((1,), (1,)), ((), ()))
    grad_act = lax.dot_general(upstream_l, point_weight, dims, preferred_element_type=F32)
    grad_act_ends = lax.dot_general(ends, point_weight, dims, preferred_element_type=F32)

    state = attend(bases(1), q, [far[1]], state)
    state = attend(bases(3), q, [far[3]], state)
    flags = [ic]
    for d in range(4):
        flags.append(jnp.where(ic == 0, (iy - d) % 4, iy) == 0)
    for d in range(4):
        flags.append(jnp.where(ic == 0, (iy - d) % 4, iy) == 3)
    mixed = attend(bases(0, 1, 3, 2), q, [own, far[1], far[3], far[2]], state, ints(*flags))
    back = exchange(mixed, HEAD_RING, -1)
    up_rows, act = forward(
        ints(head_at, place > 0, place < 15), back, tokens, halo, skipped, out_weight.reshape(H, DV, -1), depth_weight
    )

    swap = [(0, 1), (1, 0)]
    theirs = ints(1 - ic, at(SUM_RINGS[0], True))
    mine = ints(ic, at(SUM_RINGS[0]))
    sent = [product(theirs, act, upstream, steps) for steps in ((2, 1), (3, 0))]
    arrived = [lax.ppermute(s, "c", swap) for s in sent]
    piece_2, piece_1 = product(mine, act, upstream, (2, 1), arrived[0])
    piece_3, piece_0 = product(mine, act, upstream, (3, 0), arrived[1])
    got = exchange([piece_0, piece_1, piece_2, piece_3], SUM_RINGS[0])

    (up_rows, grad_act), _ = lax.optimization_barrier(((up_rows, grad_act), (piece_0, piece_1)))
    grad_skip, depth_term = backward(up_rows, grad_act, grad_act_ends, depth_weight)
    half = columns // 2
    d_theirs = lax.dynamic_slice_in_dim(depth_term, (1 - ic) * half, half, axis=1)
    d_mine = lax.dynamic_slice_in_dim(depth_term, ic * half, half, axis=1)
    d_sum = d_mine + lax.ppermute(d_theirs, "c", swap)
    rider = jnp.pad(d_sum.reshape(6, half // 2).astype(BF), ((0, TAIL - 6), (0, 0)))

    slim = half // 4
    second_at = at(SUM_RINGS[1])
    got = exchange(split_rows(ints(second_at), got, rider), SUM_RINGS[1])
    got = exchange([total_of(got).astype(BF)] * 4, SUM_RINGS[2])
    norm_scale = 1.0 / math.sqrt(128 * fine)
    summed = (total_of(got) * norm_scale).astype(BF)
    piece, rider = summed[:slim], summed[slim:]
    joined = join_rows(ints(second_at), exchange([piece] * 4, SUM_RINGS[1]), rider)
    got = exchange([joined] * 4, SUM_RINGS[0])
    other = [lax.ppermute(g, "c", swap) for g in got]
    grad_pointwise = lay_out(ints(ic, at(SUM_RINGS[0]), at(SUM_RINGS[0], True)), got, other)

    def depth_of(blocks):
        return total_of([b[half : half + 6] for b in blocks]).reshape(3, half)

    d_own, d_other = depth_of(got), depth_of(other)
    grad_depth = jnp.concatenate(
        [jnp.where(ic == 0, d_own, d_other), jnp.where(ic == 0, d_other, d_own)], axis=1
    )
    return (grad_pointwise, grad_depth, grad_skip[None])


def solution(mesh):
    fine_mesh = Mesh(mesh.devices.reshape(SIZES), AXES)
    rows = P(("x", "c"), ("z", "y"), None)
    return jax.shard_map(
        local,
        mesh=fine_mesh,
        in_specs=(rows, rows, P(("x", "c")), P(), P(), P(), P(), P(), P(), rows),
        out_specs=(P(), P(), rows),
        check_vma=False,
    )
```

time: 195 us -> 311 us (1.59)
  the two profiles are of different devices: /device:TPU:41 before, /device:TPU:1 now
where the time goes in v2:
time: 311 us; the launch traced here: 306 us
  Pallas kernels  187 us (60%)
  starting transfers between devices  56.4 us (18%)
  waiting for transfers between devices  34.1 us (11%)
  local copies, waits for them, and re-layouts  16.5 us (5%)
  matrix products  8.3 us (3%)
    pallas_call x1, Pallas kernels, lay_out(): pl.pallas_call(kernel, out_shape=jax.ShapeDtypeStruct((2 * half, 4 * quar...  145 us
    ppermute x21, waiting for transfers between devices, exchange(): got[d] = lax.ppermute(pieces[d], AXES, turn(axes, sign * d))  28.4 us
    ppermute x21, starting transfers between devices, exchange(): got[d] = lax.ppermute(pieces[d], AXES, turn(axes, sign * d))  26.1 us
    ppermute x4, starting transfers between devices, local(): other = [lax.ppermute(g, 'c', swap) for g in got]  16.3 us
    unnamed x50, local copies, waits for them, and re-layouts  14.1 us
    pallas_call x4, Pallas kernels, product(): pl.pallas_call(kernel, out_shape=outs, in_specs=[SMEM] + [VMEM] * len(ins...  11 us
    pallas_call x4, Pallas kernels, attend(): pl.pallas_call(kernel, out_shape=outs, in_specs=[SMEM] * len(scalars) + [...  10.9 us
    pallas_call x1, Pallas kernels, backward(): pl.pallas_call(kernel, grid=(columns // wide,), out_shape=[jax.ShapeDtype...  10.5 us
  transfers between devices with their start and end apart: 33, of which 18 were waited for; matrix products, arithmetic and copies ran while one was open for 4% of the time, Pallas kernels for 10%

profile of v2, /device:TPU:1, one launch (start us, length us, event | category | flops | bytes accessed | tf_op | source)
XLA Modules:
  0.0 306.0 jit_solution(13281106110617572075)
XLA Ops:
  7.1 2.5 collective-permute-start
  9.6 3.3 %collective-permute-start.1 = (bf16[256,384]{1,0:T(8,128)(2,1)S(1)}, bf16[256,384]{1,0:T(8,128)(2,1)S(1)}, u32[]{:S(2)}, u32[]{:S(2)}) collective-permute-start(bf16[256,384]{1,0:T(8,128)(2,1)S(1)} %get-tuple-element.54), channel_id=1, source_target_pairs={{0,2},{1,3},{2,0},{3,1},{4,6},{5,7},{6,4},{7,5},{8,10},{9,11},{10,... | collective-permute-start | bytes 589832 | tf_op jit(solution)/shard_map/ppermute | solution.py:47
  15.0 3.3 %collective-permute-done.1.refs_2_.refs_3_ = bf16[256,384]{1,0:T(8,128)(2,1)S(1)} collective-permute-done((bf16[256,384]{1,0:T(8,128)(2,1)S(1)}, bf16[256,384]{1,0:T(8,128)(2,1)S(1)}, u32[]{:S(2)}, u32[]{:S(2)}) %collective-permute-start.1) | collective-permute-done | bytes 196640 | tf_op jit(solution)/shard_map/ppermute | solution.py:47
  18.4 2.7 collective-permute-start.5
  22.6 2.4 attend.4
  26.6 2.3 collective-permute-start.9
  30.3 2.9 collective-permute-done.9
  34.1 2.6 attend.5
  36.7 2.5 attend.6
  39.3 3.4 %attend.7 = (bf16[272,256]{1,0:T(8,128)(2,1)S(1)}, bf16[272,256]{1,0:T(8,128)(2,1)S(1)}, bf16[272,256]{1,0:T(8,128)(2,1)S(1)}, bf16[272,256]{1,0:T(8,128)(2,1)S(1)}) custom-call(s32[17]{0:T(128)S(1)} %stack.196.bases_ref, s32[9]{0:T(128)S(1)} %stack.213.refs_0_, bf16[256,384]{1,0:T(8,128)(2,1)S(1)} %get-tuple-element.52.refs_0_.refs_1_, ...), custom_call_target="tpu_custom_call" | custom-call | flops 1073741824 | bytes 4194304 | tf_op jit(solution)/shard_map/attend/pallas_call | solution.py:204
  58.8 7.2 %forward.1 = (bf16[528,1536]{1,0:T(8,128)(2,1)S(1)}, bf16[512,1536]{1,0:T(8,128)(2,1)S(1)}) custom-call(s32[3]{0:T(128)S(1)} %pad_add_fusion.2.s_ref, bf16[272,256]{1,0:T(8,128)(2,1)S(1)} %get-tuple-element.80.b0, bf16[272,256]{1,0:T(8,128)(2,1)S(1)} %collective-permute-done.6.b1, bf16[272,256]{1,0:T(8,128)(2,1)S(1)} %copy-done.14, ...), custom_call_target="tpu_custom_call" | custom-call | tf_op jit(solution)/shard_map/forward/pallas_call | solution.py:266
  66.0 2.6 product.4
  68.6 3.0 collective-permute-start.11
  71.6 2.6 product.6
  74.3 4.5 %fusion.14.ga_ref = f32[512,1536]{1,0:T(8,128)S(1)} fusion(bf16[512,1536]{1,0:T(8,128)(2,1)S(1)} %bitcast.42, bf16[1536,1536]{1,0:T(8,128)(2,1)} %param.18), kind=kOutput, calls=%fused_computation.29 | convolution fusion | flops 2415919104 | bytes 9437184 | tf_op jit(solution)/shard_map/dot_general | solution.py:509
  78.8 2.7 product.5
  82.6 3.1 %product.7 = (bf16[768,384]{1,0:T(8,128)(2,1)}, bf16[768,384]{1,0:T(8,128)(2,1)}) custom-call(s32[2]{0:T(128)S(1)} %pad_add_fusion.1.s_ref, bf16[512,1536]{1,0:T(8,128)(2,1)S(1)} %get-tuple-element.87.a_ref, bf16[512,1536]{1,0:T(8,128)(2,1)S(1)} %bitcast.44, bf16[2,768,384]{2,1,0:T(8,128)(2,1)} %collective-permute-done.12.refs_0_), custom_call_target="tpu_custom_call" | custom-call | flops 603979776 | bytes 6291456 | tf_op jit(solution)/shard_map/product/pallas_call | solution.py:361
  87.3 3.8 %fusion.ge_ref = f32[16,1536]{1,0:T(8,128)S(1)} fusion(bf16[1536,1536]{1,0:T(8,128)(2,1)} %param.18, bf16[7,1536]{1,0:T(8,128)(2,1)S(1)} %broadcast.28, bf16[1,1536]{1,0:T(2,128)(2,1)S(1)} %get-tuple-element.111, bf16[1,1536]{1,0:T(2,128)(2,1)S(1)} %get-tuple-element.109), kind=kOutput, calls=%fused_computation.2 | convolution fusion | flops 75694080 | bytes 4844544 | tf_op jit(solution)/shard_map/dot_general | solution.py:510
  91.1 10.5 %backward.1 = (bf16[512,1536]{1,0:T(8,128)(2,1)}, f32[3,1536]{1,0:T(4,128)S(1)}) custom-call(bf16[528,1536]{1,0:T(8,128)(2,1)S(1)} %copy-done.7, f32[512,1536]{1,0:T(8,128)S(1)} %fusion.14.ga_ref, f32[16,1536]{1,0:T(8,128)S(1)} %fusion.ge_ref, f32[3,1536]{1,0:T(4,128)S(1)} %copy-done.17), custom_call_target="tpu_custom_call" | custom-call | flops 47185920 | bytes 9437184 | tf_op jit(solution)/shard_map/backward/pallas_call | solution.py:325
  101.6 3.1 %collective-permute-start.16 = (f32[3,768]{1,0:T(4,128)S(1)}, f32[3,768]{1,0:T(4,128)S(1)}, u32[]{:S(2)}, u32[]{:S(2)}) collective-permute-start(f32[3,768]{1,0:T(4,128)S(1)} %constant_dynamic-slice_fusion), channel_id=1, source_target_pairs={{0,16},{16,0},{1,17},{17,1},{2,18},{18,2},{3,19},{19,3},{4,20},{20... | collective-permute-start | bytes 27656 | tf_op jit(solution)/shard_map/ppermute | solution.py:539
  107.0 3.3 %collective-permute-start.17 = (bf16[208,384]{1,0:T(8,128)(2,1)S(1)}, bf16[208,384]{1,0:T(8,128)(2,1)S(1)}, u32[]{:S(2)}, u32[]{:S(2)}) collective-permute-start(bf16[208,384]{1,0:T(8,128)(2,1)S(1)} %get-tuple-element.97), channel_id=1, source_target_pairs={{0,2},{1,3},{2,0},{3,1},{4,6},{5,7},{6,4},{7,5},{8,10},{9,11},{10,... | collective-permute-start | bytes 479240 | tf_op jit(solution)/shard_map/ppermute | solution.py:47
  110.3 2.7 collective-permute-start.19
  113.3 2.7 collective-permute-done.18
  120.7 4.7 %collective-permute-done.21 = bf16[208,384]{1,0:T(8,128)(2,1)S(1)} collective-permute-done((bf16[208,384]{1,0:T(8,128)(2,1)S(1)}, bf16[208,384]{1,0:T(8,128)(2,1)S(1)}, u32[]{:S(2)}, u32[]{:S(2)}) %collective-permute-start.21) | collective-permute-done | bytes 159776 | tf_op jit(solution)/shard_map/ppermute | solution.py:47
  125.6 2.4 collective-permute-start.25
  128.7 3.0 collective-permute-done.25.refs_3_
  137.0 4.4 %collective-permute-start.29 = (bf16[784,384]{1,0:T(8,128)(2,1)S(1)}, bf16[784,384]{1,0:T(8,128)(2,1)S(1)}, u32[]{:S(2)}, u32[]{:S(2)}) collective-permute-start(bf16[784,384]{1,0:T(8,128)(2,1)S(1)} %join_rows.1.refs_0_), channel_id=1, source_target_pairs={{0,16},{16,0},{1,17},{17,1},{2,18},{18,2},{3,19},{19,3},{4,20},{20... | collective-permute-start | bytes 1806344 | tf_op jit(solution)/shard_map/ppermute | solution.py:551
  141.4 3.1 %collective-permute-done.28.refs_3_ = bf16[784,384]{1,0:T(8,128)(2,1)S(1)} collective-permute-done((bf16[784,384]{1,0:T(8,128)(2,1)S(1)}, bf16[784,384]{1,0:T(8,128)(2,1)S(1)}, u32[]{:S(2)}, u32[]{:S(2)}) %collective-permute-start.28) | collective-permute-done | bytes 602144 | tf_op jit(solution)/shard_map/ppermute | solution.py:47
  144.5 3.7 %collective-permute-start.32 = (bf16[784,384]{1,0:T(8,128)(2,1)S(1)}, bf16[784,384]{1,0:T(8,128)(2,1)S(1)}, u32[]{:S(2)}, u32[]{:S(2)}) collective-permute-start(bf16[784,384]{1,0:T(8,128)(2,1)S(1)} %collective-permute-done.28.refs_3_), channel_id=1, source_target_pairs={{0,16},{16,0},{1,17},{17,1},{2,18},{18,2},{3,19},{19,3},{4,20},{20... | collective-permute-start | bytes 1806344 | tf_op jit(solution)/shard_map/ppermute | solution.py:551
  148.3 3.3 %collective-permute-start.31 = (bf16[784,384]{1,0:T(8,128)(2,1)S(1)}, bf16[784,384]{1,0:T(8,128)(2,1)S(1)}, u32[]{:S(2)}, u32[]{:S(2)}) collective-permute-start(bf16[784,384]{1,0:T(8,128)(2,1)S(1)} %collective-permute-done.27.refs_2_), channel_id=1, source_target_pairs={{0,16},{16,0},{1,17},{17,1},{2,18},{18,2},{3,19},{19,3},{4,20},{20... | collective-permute-start | bytes 1806344 | tf_op jit(solution)/shard_map/ppermute | solution.py:551
  152.9 4.9 %collective-permute-start.30 = (bf16[784,384]{1,0:T(8,128)(2,1)S(1)}, bf16[784,384]{1,0:T(8,128)(2,1)S(1)}, u32[]{:S(2)}, u32[]{:S(2)}) collective-permute-start(bf16[784,384]{1,0:T(8,128)(2,1)S(1)} %collective-permute-done.26.refs_1_), channel_id=1, source_target_pairs={{0,16},{16,0},{1,17},{17,1},{2,18},{18,2},{3,19},{19,3},{4,20},{20... | collective-permute-start | bytes 1806344 | tf_op jit(solution)/shard_map/ppermute | solution.py:551
  161.0 144.8 %lay_out.1 = bf16[1536,1536]{1,0:T(8,128)(2,1)} custom-call(s32[3]{0:T(128)} %pad_add_fusion.s_ref, bf16[784,384]{1,0:T(8,128)(2,1)} %copy-done.3, bf16[784,384]{1,0:T(8,128)(2,1)} %copy-done.20, bf16[784,384]{1,0:T(8,128)(2,1)} %copy-done.19, bf16[784,384]{1,0:T(8,128)(2,1)} %copy-done.18, bf16[784,384]{1,0:T(8,128)(2,1)} %copy-done.21, ...), custom_call_target="tpu_custom_call" | custom-call | tf_op jit(solution)/shard_map/lay_out/pallas_call | solution.py:439
  (137 shorter events, 50.0 us)
Async XLA Ops:
  7.1 8.0 %collective-permute-start = (bf16[256,384]{1,0:T(8,128)(2,1)S(1)}, bf16[256,384]{1,0:T(8,128)(2,1)S(1)}, u32[]{:S(2)}, u32[]{:S(2)}) collective-permute-start(bf16[256,384]{1,0:T(8,128)(2,1)S(1)} %get-tuple-element.53), channel_id=1, source_target_pairs={{0,1},{1,2},{2,3},{3,0},{4,5},{5,6},{6,7},{7,4},{8,9},{9,10},{10,1... | collective-permute-start | bytes 589832 | tf_op jit(solution)/shard_map/ppermute | solution.py:47
  9.6 8.8 %collective-permute-start.1 = (bf16[256,384]{1,0:T(8,128)(2,1)S(1)}, bf16[256,384]{1,0:T(8,128)(2,1)S(1)}, u32[]{:S(2)}, u32[]{:S(2)}) collective-permute-start(bf16[256,384]{1,0:T(8,128)(2,1)S(1)} %get-tuple-element.54), channel_id=1, source_target_pairs={{0,2},{1,3},{2,0},{3,1},{4,6},{5,7},{6,4},{7,5},{8,10},{9,11},{10,... | collective-permute-start | bytes 589832 | tf_op jit(solution)/shard_map/ppermute | solution.py:47
  12.9 5.5 %collective-permute-start.2 = (bf16[256,384]{1,0:T(8,128)(2,1)S(1)}, bf16[256,384]{1,0:T(8,128)(2,1)S(1)}, u32[]{:S(2)}, u32[]{:S(2)}) collective-permute-start(bf16[256,384]{1,0:T(8,128)(2,1)S(1)} %get-tuple-element.55), channel_id=1, source_target_pairs={{0,3},{1,0},{2,1},{3,2},{4,7},{5,4},{6,5},{7,6},{8,11},{9,8},{10,9... | collective-permute-start | bytes 589832 | tf_op jit(solution)/shard_map/ppermute | solution.py:47
  18.4 20.9 %collective-permute-start.5 = (bf16[1040,256]{1,0:T(8,128)(2,1)S(1)}, bf16[1040,256]{1,0:T(8,128)(2,1)S(1)}, u32[]{:S(2)}, u32[]{:S(2)}) collective-permute-start(bf16[1040,256]{1,0:T(8,128)(2,1)S(1)} %stack_rows.1.refs_4_.refs_5_), channel_id=1, source_target_pairs={{0,8},{1,9},{2,10},{3,11},{4,12},{5,13},{6,14},{7,15},{8,0},{9,1},... | collective-permute-start | bytes 1597448 | tf_op jit(solution)/shard_map/ppermute | solution.py:480
  21.1 15.6 %collective-permute-start.4 = (bf16[1040,256]{1,0:T(8,128)(2,1)S(1)}, bf16[1040,256]{1,0:T(8,128)(2,1)S(1)}, u32[]{:S(2)}, u32[]{:S(2)}) collective-permute-start(bf16[1040,256]{1,0:T(8,128)(2,1)S(1)} %stack_rows.1.refs_4_.refs_5_), channel_id=1, source_target_pairs={{0,12},{1,13},{2,14},{3,15},{4,0},{5,1},{6,2},{7,3},{8,4},{9,5},{1... | collective-permute-start | bytes 1597448 | tf_op jit(solution)/shard_map/ppermute | solution.py:480
  21.9 12.2 %collective-permute-start.3 = (bf16[1040,256]{1,0:T(8,128)(2,1)S(1)}, bf16[1040,256]{1,0:T(8,128)(2,1)S(1)}, u32[]{:S(2)}, u32[]{:S(2)}) collective-permute-start(bf16[1040,256]{1,0:T(8,128)(2,1)S(1)} %stack_rows.1.refs_4_.refs_5_), channel_id=1, source_target_pairs={{0,4},{1,5},{2,6},{3,7},{4,8},{5,9},{6,10},{7,11},{8,12},{9,13},{1... | collective-permute-start | bytes 1597448 | tf_op jit(solution)/shard_map/ppermute | solution.py:480
  26.6 6.6 %collective-permute-start.9 = (bf16[4,1536]{1,0:T(4,128)(2,1)S(1)}, bf16[4,1536]{1,0:T(4,128)(2,1)S(1)}, u32[]{:S(2)}, u32[]{:S(2)}) collective-permute-start(bf16[4,1536]{1,0:T(4,128)(2,1)S(1)} %pad_maximum_fusion.1), channel_id=1, source_target_pairs={{0,1},{1,2},{2,3},{3,4},{4,5},{5,6},{6,7},{7,8},{8,9},{9,10},{10,1... | collective-permute-start | bytes 36872 | tf_op jit(solution)/shard_map/ppermute | solution.py:498
  29.0 17.2 %collective-permute-start.10 = (bf16[4,1536]{1,0:T(4,128)(2,1)S(1)}, bf16[4,1536]{1,0:T(4,128)(2,1)S(1)}, u32[]{:S(2)}, u32[]{:S(2)}) collective-permute-start(bf16[4,1536]{1,0:T(4,128)(2,1)S(1)} %pad_maximum_fusion.2), channel_id=1, source_target_pairs={{1,0},{2,1},{3,2},{4,3},{5,4},{6,5},{7,6},{8,7},{9,8},{10,9},{11,1... | collective-permute-start | bytes 36872 | tf_op jit(solution)/shard_map/ppermute | solution.py:499
  42.6 5.8 %collective-permute-start.6 = (bf16[272,256]{1,0:T(8,128)(2,1)S(1)}, bf16[272,256]{1,0:T(8,128)(2,1)S(1)}, u32[]{:S(2)}, u32[]{:S(2)}) collective-permute-start(bf16[272,256]{1,0:T(8,128)(2,1)S(1)} %get-tuple-element.81), channel_id=1, source_target_pairs={{0,3},{1,0},{2,1},{3,2},{4,7},{5,4},{6,5},{7,6},{8,11},{9,8},{10,9... | collective-permute-start | bytes 417800 | tf_op jit(solution)/shard_map/ppermute | solution.py:47
  44.9 5.5 %collective-permute-start.7 = (bf16[272,256]{1,0:T(8,128)(2,1)S(1)}, bf16[272,256]{1,0:T(8,128)(2,1)S(1)}, u32[]{:S(2)}, u32[]{:S(2)}) collective-permute-start(bf16[272,256]{1,0:T(8,128)(2,1)S(1)} %get-tuple-element.82), channel_id=1, source_target_pairs={{0,2},{1,3},{2,0},{3,1},{4,6},{5,7},{6,4},{7,5},{8,10},{9,11},{10,... | collective-permute-start | bytes 417800 | tf_op jit(solution)/shard_map/ppermute | solution.py:47
  45.9 6.2 %collective-permute-start.8 = (bf16[272,256]{1,0:T(8,128)(2,1)S(1)}, bf16[272,256]{1,0:T(8,128)(2,1)S(1)}, u32[]{:S(2)}, u32[]{:S(2)}) collective-permute-start(bf16[272,256]{1,0:T(8,128)(2,1)S(1)} %get-tuple-element.83), channel_id=1, source_target_pairs={{0,1},{1,2},{2,3},{3,0},{4,5},{5,6},{6,7},{7,4},{8,9},{9,10},{10,1... | collective-permute-start | bytes 417800 | tf_op jit(solution)/shard_map/ppermute | solution.py:47
  68.6 10.2 %collective-permute-start.11 = (bf16[2,768,384]{2,1,0:T(8,128)(2,1)}, bf16[2,768,384]{2,1,0:T(8,128)(2,1)}, u32[]{:S(2)}, u32[]{:S(2)}) collective-permute-start(bf16[2,768,384]{2,1,0:T(8,128)(2,1)} %product.4), channel_id=1, source_target_pairs={{0,16},{16,0},{1,17},{17,1},{2,18},{18,2},{3,19},{19,3},{4,20},{20... | collective-permute-start | bytes 3538952 | tf_op jit(solution)/shard_map/ppermute | solution.py:529
  74.2 8.5 %collective-permute-start.12 = (bf16[2,768,384]{2,1,0:T(8,128)(2,1)}, bf16[2,768,384]{2,1,0:T(8,128)(2,1)}, u32[]{:S(2)}, u32[]{:S(2)}) collective-permute-start(bf16[2,768,384]{2,1,0:T(8,128)(2,1)} %product.6), channel_id=1, source_target_pairs={{0,16},{16,0},{1,17},{17,1},{2,18},{18,2},{3,19},{19,3},{4,20},{20... | collective-permute-start | bytes 3538952 | tf_op jit(solution)/shard_map/ppermute | solution.py:529
  82.4 23.2 %collective-permute-start.15 = (bf16[768,384]{1,0:T(8,128)(2,1)}, bf16[768,384]{1,0:T(8,128)(2,1)}, u32[]{:S(2)}, u32[]{:S(2)}) collective-permute-start(bf16[768,384]{1,0:T(8,128)(2,1)} %get-tuple-element.91), channel_id=1, source_target_pairs={{0,96},{1,97},{2,98},{3,99},{4,100},{5,101},{6,102},{7,103},{8,104... | collective-permute-start | bytes 1769480 | tf_op jit(solution)/shard_map/ppermute | solution.py:47
  85.7 19.8 %collective-permute-start.14 = (bf16[768,384]{1,0:T(8,128)(2,1)}, bf16[768,384]{1,0:T(8,128)(2,1)S(1)}, u32[]{:S(2)}, u32[]{:S(2)}) collective-permute-start(bf16[768,384]{1,0:T(8,128)(2,1)} %get-tuple-element.90), channel_id=1, source_target_pairs={{0,64},{1,65},{2,66},{3,67},{4,68},{5,69},{6,70},{7,71},{8,72},{9,... | collective-permute-start | bytes 1769480 | tf_op jit(solution)/shard_map/ppermute | solution.py:47
  86.7 18.9 %collective-permute-start.13 = (bf16[768,384]{1,0:T(8,128)(2,1)}, bf16[768,384]{1,0:T(8,128)(2,1)S(1)}, u32[]{:S(2)}, u32[]{:S(2)}) collective-permute-start(bf16[768,384]{1,0:T(8,128)(2,1)} %get-tuple-element.89), channel_id=1, source_target_pairs={{0,32},{1,33},{2,34},{3,35},{4,36},{5,37},{6,38},{7,39},{8,40},{9,... | collective-permute-start | bytes 1769480 | tf_op jit(solution)/shard_map/ppermute | solution.py:47
  107.0 6.3 %collective-permute-start.17 = (bf16[208,384]{1,0:T(8,128)(2,1)S(1)}, bf16[208,384]{1,0:T(8,128)(2,1)S(1)}, u32[]{:S(2)}, u32[]{:S(2)}) collective-permute-start(bf16[208,384]{1,0:T(8,128)(2,1)S(1)} %get-tuple-element.97), channel_id=1, source_target_pairs={{0,2},{1,3},{2,0},{3,1},{4,6},{5,7},{6,4},{7,5},{8,10},{9,11},{10,... | collective-permute-start | bytes 479240 | tf_op jit(solution)/shard_map/ppermute | solution.py:47
  110.3 5.6 %collective-permute-start.18 = (bf16[208,384]{1,0:T(8,128)(2,1)S(1)}, bf16[208,384]{1,0:T(8,128)(2,1)S(1)}, u32[]{:S(2)}, u32[]{:S(2)}) collective-permute-start(bf16[208,384]{1,0:T(8,128)(2,1)S(1)} %get-tuple-element.98), channel_id=1, source_target_pairs={{0,1},{1,2},{2,3},{3,0},{4,5},{5,6},{6,7},{7,4},{8,9},{9,10},{10,1... | collective-permute-start | bytes 479240 | tf_op jit(solution)/shard_map/ppermute | solution.py:47
  110.3 5.6 %collective-permute-start.19 = (bf16[208,384]{1,0:T(8,128)(2,1)S(1)}, bf16[208,384]{1,0:T(8,128)(2,1)S(1)}, u32[]{:S(2)}, u32[]{:S(2)}) collective-permute-start(bf16[208,384]{1,0:T(8,128)(2,1)S(1)} %get-tuple-element.99), channel_id=1, source_target_pairs={{0,3},{1,0},{2,1},{3,2},{4,7},{5,4},{6,5},{7,6},{8,11},{9,8},{10,9... | collective-permute-start | bytes 479240 | tf_op jit(solution)/shard_map/ppermute | solution.py:47
  116.0 4.7 %collective-permute-start.22 = (bf16[208,384]{1,0:T(8,128)(2,1)S(1)}, bf16[208,384]{1,0:T(8,128)(2,1)S(1)}, u32[]{:S(2)}, u32[]{:S(2)}) collective-permute-start(bf16[208,384]{1,0:T(8,128)(2,1)S(1)} %add_convert_fusion), channel_id=1, source_target_pairs={{0,12},{1,13},{2,14},{3,15},{4,0},{5,1},{6,2},{7,3},{8,4},{9,5},{1... | collective-permute-start | bytes 479240 | tf_op jit(solution)/shard_map/ppermute | solution.py:47
  118.1 7.3 %collective-permute-start.21 = (bf16[208,384]{1,0:T(8,128)(2,1)S(1)}, bf16[208,384]{1,0:T(8,128)(2,1)S(1)}, u32[]{:S(2)}, u32[]{:S(2)}) collective-permute-start(bf16[208,384]{1,0:T(8,128)(2,1)S(1)} %add_convert_fusion), channel_id=1, source_target_pairs={{0,4},{1,5},{2,6},{3,7},{4,8},{5,9},{6,10},{7,11},{8,12},{9,13},{1... | collective-permute-start | bytes 479240 | tf_op jit(solution)/shard_map/ppermute | solution.py:47
  118.1 7.3 %collective-permute-start.20 = (bf16[208,384]{1,0:T(8,128)(2,1)S(1)}, bf16[208,384]{1,0:T(8,128)(2,1)S(1)}, u32[]{:S(2)}, u32[]{:S(2)}) collective-permute-start(bf16[208,384]{1,0:T(8,128)(2,1)S(1)} %add_convert_fusion), channel_id=1, source_target_pairs={{0,8},{1,9},{2,10},{3,11},{4,12},{5,13},{6,14},{7,15},{8,0},{9,1},... | collective-permute-start | bytes 479240 | tf_op jit(solution)/shard_map/ppermute | solution.py:47
  125.6 6.1 %collective-permute-start.25 = (bf16[192,384]{1,0:T(8,128)(2,1)S(1)}, bf16[192,384]{1,0:T(8,128)(2,1)S(1)}, u32[]{:S(2)}, u32[]{:S(2)}) collective-permute-start(bf16[192,384]{1,0:T(8,128)(2,1)S(1)} %slice.94.refs_0_), channel_id=1, source_target_pairs={{0,3},{1,0},{2,1},{3,2},{4,7},{5,4},{6,5},{7,6},{8,11},{9,8},{10,9... | collective-permute-start | bytes 442376 | tf_op jit(solution)/shard_map/ppermute | solution.py:47
  128.0 5.6 %collective-permute-start.24 = (bf16[192,384]{1,0:T(8,128)(2,1)S(1)}, bf16[192,384]{1,0:T(8,128)(2,1)S(1)}, u32[]{:S(2)}, u32[]{:S(2)}) collective-permute-start(bf16[192,384]{1,0:T(8,128)(2,1)S(1)} %slice.94.refs_0_), channel_id=1, source_target_pairs={{0,2},{1,3},{2,0},{3,1},{4,6},{5,7},{6,4},{7,5},{8,10},{9,11},{10,... | collective-permute-start | bytes 442376 | tf_op jit(solution)/shard_map/ppermute | solution.py:47
  128.1 7.1 %collective-permute-start.23 = (bf16[192,384]{1,0:T(8,128)(2,1)S(1)}, bf16[192,384]{1,0:T(8,128)(2,1)S(1)}, u32[]{:S(2)}, u32[]{:S(2)}) collective-permute-start(bf16[192,384]{1,0:T(8,128)(2,1)S(1)} %slice.94.refs_0_), channel_id=1, source_target_pairs={{0,1},{1,2},{2,3},{3,0},{4,5},{5,6},{6,7},{7,4},{8,9},{9,10},{10,1... | collective-permute-start | bytes 442376 | tf_op jit(solution)/shard_map/ppermute | solution.py:47
  135.3 9.2 %collective-permute-start.28 = (bf16[784,384]{1,0:T(8,128)(2,1)S(1)}, bf16[784,384]{1,0:T(8,128)(2,1)S(1)}, u32[]{:S(2)}, u32[]{:S(2)}) collective-permute-start(bf16[784,384]{1,0:T(8,128)(2,1)S(1)} %join_rows.1.refs_0_), channel_id=1, source_target_pairs={{0,96},{1,97},{2,98},{3,99},{4,100},{5,101},{6,102},{7,103},{8,104... | collective-permute-start | bytes 1806344 | tf_op jit(solution)/shard_map/ppermute | solution.py:47
  135.8 12.4 %collective-permute-start.27 = (bf16[784,384]{1,0:T(8,128)(2,1)S(1)}, bf16[784,384]{1,0:T(8,128)(2,1)S(1)}, u32[]{:S(2)}, u32[]{:S(2)}) collective-permute-start(bf16[784,384]{1,0:T(8,128)(2,1)S(1)} %join_rows.1.refs_0_), channel_id=1, source_target_pairs={{0,64},{1,65},{2,66},{3,67},{4,68},{5,69},{6,70},{7,71},{8,72},{9,... | collective-permute-start | bytes 1806344 | tf_op jit(solution)/shard_map/ppermute | solution.py:47
  136.6 16.3 %collective-permute-start.26 = (bf16[784,384]{1,0:T(8,128)(2,1)S(1)}, bf16[784,384]{1,0:T(8,128)(2,1)S(1)}, u32[]{:S(2)}, u32[]{:S(2)}) collective-permute-start(bf16[784,384]{1,0:T(8,128)(2,1)S(1)} %join_rows.1.refs_0_), channel_id=1, source_target_pairs={{0,32},{1,33},{2,34},{3,35},{4,36},{5,37},{6,38},{7,39},{8,40},{9,... | collective-permute-start | bytes 1806344 | tf_op jit(solution)/shard_map/ppermute | solution.py:47
  137.0 21.5 %collective-permute-start.29 = (bf16[784,384]{1,0:T(8,128)(2,1)S(1)}, bf16[784,384]{1,0:T(8,128)(2,1)S(1)}, u32[]{:S(2)}, u32[]{:S(2)}) collective-permute-start(bf16[784,384]{1,0:T(8,128)(2,1)S(1)} %join_rows.1.refs_0_), channel_id=1, source_target_pairs={{0,16},{16,0},{1,17},{17,1},{2,18},{18,2},{3,19},{19,3},{4,20},{20... | collective-permute-start | bytes 1806344 | tf_op jit(solution)/shard_map/ppermute | solution.py:551
  144.5 14.0 %collective-permute-start.32 = (bf16[784,384]{1,0:T(8,128)(2,1)S(1)}, bf16[784,384]{1,0:T(8,128)(2,1)S(1)}, u32[]{:S(2)}, u32[]{:S(2)}) collective-permute-start(bf16[784,384]{1,0:T(8,128)(2,1)S(1)} %collective-permute-done.28.refs_3_), channel_id=1, source_target_pairs={{0,16},{16,0},{1,17},{17,1},{2,18},{18,2},{3,19},{19,3},{4,20},{20... | collective-permute-start | bytes 1806344 | tf_op jit(solution)/shard_map/ppermute | solution.py:551
  148.3 10.2 %collective-permute-start.31 = (bf16[784,384]{1,0:T(8,128)(2,1)S(1)}, bf16[784,384]{1,0:T(8,128)(2,1)S(1)}, u32[]{:S(2)}, u32[]{:S(2)}) collective-permute-start(bf16[784,384]{1,0:T(8,128)(2,1)S(1)} %collective-permute-done.27.refs_2_), channel_id=1, source_target_pairs={{0,16},{16,0},{1,17},{17,1},{2,18},{18,2},{3,19},{19,3},{4,20},{20... | collective-permute-start | bytes 1806344 | tf_op jit(solution)/shard_map/ppermute | solution.py:551
  152.9 6.6 %collective-permute-start.30 = (bf16[784,384]{1,0:T(8,128)(2,1)S(1)}, bf16[784,384]{1,0:T(8,128)(2,1)S(1)}, u32[]{:S(2)}, u32[]{:S(2)}) collective-permute-start(bf16[784,384]{1,0:T(8,128)(2,1)S(1)} %collective-permute-done.26.refs_1_), channel_id=1, source_target_pairs={{0,16},{16,0},{1,17},{17,1},{2,18},{18,2},{3,19},{19,3},{4,20},{20... | collective-permute-start | bytes 1806344 | tf_op jit(solution)/shard_map/ppermute | solution.py:551
  (26 other events, 127.4 us)

commit v3 on v2

--- a/solution.py
+++ b/solution.py
@@ -54,35 +54,63 @@
 
 
 def project(at, tokens, query_weight, key_weight, value_weight):
-    rows = tokens.shape[0]
+    rows, depth = tokens.shape
+    step = 384
+    count = depth // step
 
     def kernel(at_ref, tok_ref, wq_ref, wk_ref, wv_ref, *refs):
-        outs, held = refs[:4], refs[4]
+        outs, q_sum, k_sum, v_sum, held = refs[:4], refs[4], refs[5], refs[6], refs[7]
+        j = pl.program_id(0)
         tok = tok_ref[...]
-        v = jnp.dot(tok, wv_ref[...], preferred_element_type=F32)
-        k = jnp.dot(tok, wk_ref[...], preferred_element_type=F32)
-        q = jnp.dot(tok, wq_ref[...], preferred_element_type=F32)
-        zero = jnp.zeros((rows, DH), F32)
-        for h in range(H):
-            held[h] = jnp.concatenate(
-                [
-                    v[:, h * DV : (h + 1) * DV],
-                    k[:, h * DH : (h + 1) * DH],
-                    zero,
-                    q[:, h * DH : (h + 1) * DH],
-                ],
-                axis=1,
-            ).astype(BF)
-        for d in range(4):
-            outs[d][...] = held[(at_ref[0] + d) % 4]
-
-    return pl.pallas_call(
-        kernel,
+        for total, w_ref in ((v_sum, wv_ref), (k_sum, wk_ref), (q_sum, wq_ref)):
+            term = jnp.dot(tok, w_ref[...], preferred_element_type=F32)
+
+            @pl.when(j == 0)
+            def _():
+                total[...] = term
+
+            @pl.when(j > 0)
+            def _():
+                total[...] += term
+
+        @pl.when(j == count - 1)
+        def _():
+            zero = jnp.zeros((rows, DH), F32)
+            for h in range(H):
+                held[h] = jnp.concatenate(
+                    [
+                        v_sum[:, h * DV : (h + 1) * DV],
+                        k_sum[:, h * DH : (h + 1) * DH],
+                        zero,
+                        q_sum[:, h * DH : (h + 1) * DH] * (1.0 / math.sqrt(DH)),
+                    ],
+                    axis=1,
+                ).astype(BF)
+            for d in range(4):
+                outs[d][...] = held[(at_ref[0] + d) % 4]
+
+    def deep(width):
+        return pl.BlockSpec((step, width), lambda j: (j, 0))
+
+    return pl.pallas_call(
+        kernel,
+        grid=(count,),
         out_shape=[jax.ShapeDtypeStruct((rows, 384), BF)] * 4,
-        in_specs=[SMEM] + [VMEM] * 4,
-        out_specs=[VMEM] * 4,
-        scratch_shapes=[pltpu.VMEM((4, rows, 384), BF)],
-        compiler_params=params(40),
+        in_specs=[
+            SMEM,
+            pl.BlockSpec((rows, step), lambda j: (0, j)),
+            deep(H * DH),
+            deep(H * DH),
+            deep(H * DV),
+        ],
+        out_specs=[pl.BlockSpec((rows, 384), lambda j: (0, 0))] * 4,
+        scratch_shapes=[
+            pltpu.VMEM((rows, H * DH), F32),
+            pltpu.VMEM((rows, H * DH), F32),
+            pltpu.VMEM((rows, H * DV), F32),
+            pltpu.VMEM((4, rows, 384), BF),
+        ],
+        compiler_params=params(60),
         name="project",
     )(at, tokens, query_weight, key_weight, value_weight)
 
@@ -141,7 +169,7 @@
             scores = lax.dot_general(
                 query, ref[:width, 128:], (((1,), (1,)), ((), ())), preferred_element_type=F32
             )
-            return jnp.where(keep, scores * (1.0 / math.sqrt(DH)), -1e30)
+            return jnp.where(keep, scores, -1e30)
 
         def shares(sums):
             return sums / sums[:, DV : DV + 1]
@@ -281,16 +309,19 @@
         ],
         out_specs=[cols(fine + 16), cols(fine)],
         scratch_shapes=[pltpu.VMEM((4, rows + TAIL, DV), BF), pltpu.VMEM((fine + 16, wide), F32)],
-        compiler_params=params(40),
+        compiler_params=params(60),
         name="forward",
     )(scalars, *back, tokens, halo, skipped, out_heads, depth_weight)
 
 
-def backward(up, grad_act, grad_act_ends, depth_weight):
-    fine, columns = grad_act.shape
+def backward(up, upstream, ends, point_weight, depth_weight):
+    fine, columns = upstream.shape
     wide = 256
 
-    def kernel(up_ref, ga_ref, ge_ref, dw_ref, gs_ref, gd_ref, held, grad):
+    def kernel(up_ref, g_ref, e_ref, pw_ref, dw_ref, gs_ref, gd_ref, held, grad):
+        dims = (((1,), (1,)), ((), ()))
+        upper = lax.dot_general(g_ref[...], pw_ref[...], dims, preferred_element_type=F32)
+        edges = lax.dot_general(e_ref[...], pw_ref[...], dims, preferred_element_type=F32)
         held[:8, :] = jnp.zeros((8, wide), F32)
         held[8 : fine + 24, :] = up_ref[...].astype(F32)
         held[fine + 24 :, :] = jnp.zeros((8, wide), F32)
@@ -307,10 +338,10 @@
             )
             return (upstream * rate).astype(BF).astype(F32)
 
-        grad[:8, :] = grad_of(8, 8, ge_ref[:8, :])
-        mid = grad_of(16, fine, ga_ref[...])
+        grad[:8, :] = grad_of(8, 8, edges[:8])
+        mid = grad_of(16, fine, upper)
         grad[8 : 8 + fine, :] = mid
-        grad[8 + fine :, :] = grad_of(16 + fine, 8, ge_ref[8:, :])
+        grad[8 + fine :, :] = grad_of(16 + fine, 8, edges[8:])
         gs_ref[...] = (
             dw_ref[0:1, :] * grad[9 : 9 + fine, :]
             + dw_ref[1:2, :] * mid
@@ -326,38 +357,44 @@
         kernel,
         grid=(columns // wide,),
         out_shape=[jax.ShapeDtypeStruct((fine, columns), BF), jax.ShapeDtypeStruct((3, columns), F32)],
-        in_specs=[cols(fine + 16), cols(fine), cols(16), cols(3)],
+        in_specs=[
+            cols(fine + 16),
+            pl.BlockSpec((fine, columns), lambda j: (0, 0)),
+            pl.BlockSpec((16, columns), lambda j: (0, 0)),
+            pl.BlockSpec((wide, columns), lambda j: (j, 0)),
+            cols(3),
+        ],
         out_specs=[cols(fine), cols(3)],
         scratch_shapes=[pltpu.VMEM((fine + 32, wide), F32), pltpu.VMEM((fine + 16, wide), F32)],
         compiler_params=params(40),
-        cost_estimate=pl.CostEstimate(flops=60 * fine * columns, bytes_accessed=9 << 20, transcendentals=fine * columns),
+        cost_estimate=pl.CostEstimate(
+            flops=2 * fine * columns * columns, bytes_accessed=11 << 20, transcendentals=fine * columns
+        ),
         name="backward",
-    )(up, grad_act, grad_act_ends, depth_weight)
-
-
-def product(scalars, act, upstream, steps, arrived=None):
-    half, quarter = act.shape[1] // 2, upstream.shape[1] // 4
+    )(up, upstream, ends, point_weight, depth_weight)
+
+
+def product(scalars, act, turned, steps, arrived=None):
+    half, quarter = act.shape[1] // 2, turned.shape[0] // 4
     joint = arrived is None
 
     def kernel(s_ref, a_ref, g_ref, *refs):
-        left = a_ref[:, pl.ds(pl.multiple_of(s_ref[0] * half, 128), half)]
+        right = a_ref[:, pl.ds(pl.multiple_of(s_ref[0] * half, 128), half)]
         for n, d in enumerate(steps):
-            at = pl.multiple_of((s_ref[1] + d) % 4 * quarter, 128)
-            block = lax.dot_general(
-                left, g_ref[:, pl.ds(at, quarter)], (((0,), (0,)), ((), ())), preferred_element_type=F32
-            )
+            at = pl.multiple_of((s_ref[1] + d) % 4 * quarter, 16)
+            block = jnp.dot(g_ref[pl.ds(at, quarter), :], right, preferred_element_type=F32)
             if joint:
                 refs[0][n] = block.astype(BF)
             else:
                 refs[1 + n][...] = (block + refs[0][n].astype(F32)).astype(BF)
 
     if joint:
-        outs = jax.ShapeDtypeStruct((len(steps), half, quarter), BF)
+        outs = jax.ShapeDtypeStruct((len(steps), quarter, half), BF)
         out_specs = VMEM
     else:
-        outs = [jax.ShapeDtypeStruct((half, quarter), BF)] * len(steps)
+        outs = [jax.ShapeDtypeStruct((quarter, half), BF)] * len(steps)
         out_specs = [VMEM] * len(steps)
-    ins = [act, upstream] if joint else [act, upstream, arrived]
+    ins = [act, turned] if joint else [act, turned, arrived]
     return pl.pallas_call(
         kernel,
         out_shape=outs,
@@ -396,17 +433,20 @@
     slim, columns = got[0].shape
 
     def kernel(at_ref, *refs):
-        ins, rider_ref, out = refs[:4], refs[4], refs[5]
+        ins, rider_ref, out, held = refs[:4], refs[4], refs[5], refs[6]
         for d in range(4):
             put = pl.ds(pl.multiple_of((at_ref[0] + 4 - d) % 4 * slim, 16), slim)
-            out[put, :] = ins[d][...]
-        out[4 * slim :, :] = rider_ref[...]
-
-    return pl.pallas_call(
-        kernel,
-        out_shape=jax.ShapeDtypeStruct((4 * slim + TAIL, columns), BF),
+            held[put, :] = ins[d][...]
+        out[:columns, :] = held[...].T
+        last = rider_ref[...].astype(F32)[:8]
+        out[columns:, :] = jnp.concatenate([last[:, : 4 * slim], last[:, 4 * slim :]], axis=0).astype(BF)
+
+    return pl.pallas_call(
+        kernel,
+        out_shape=jax.ShapeDtypeStruct((columns + TAIL, 4 * slim), BF),
         in_specs=[SMEM] + [VMEM] * 5,
         out_specs=VMEM,
+        scratch_shapes=[pltpu.VMEM((4 * slim, columns), BF)],
         compiler_params=params(24),
         name="join_rows",
     )(at, *got, rider)
@@ -416,32 +456,29 @@
     half, quarter = own[0].shape[0] - TAIL, own[0].shape[1]
 
     def kernel(s_ref, *refs):
-        blocks, out, sems = refs[:8], refs[8], refs[9]
-        copies = []
+        blocks, out = refs[:8], refs[8]
         for n in range(8):
-            mine = n < 4
-            side = s_ref[0] if mine else 1 - s_ref[0]
-            at = s_ref[1] if mine else s_ref[2]
-            down = pl.multiple_of(side * half, 16)
-            over = pl.multiple_of((at + 4 - n % 4) % 4 * quarter, 128)
-            copies.append(
-                pltpu.make_async_copy(
-                    blocks[n].at[pl.ds(0, half), :],
-                    out.at[pl.ds(down, half), pl.ds(over, quarter)],
-                    sems.at[n],
-                )
-            )
-        for copy in copies:
-            copy.start()
-        for copy in copies:
-            copy.wait()
+
+            @pl.when(pl.program_id(0) == n)
+            def _():
+                out[...] = blocks[n][:half, :]
+
+    def place(n, s_ref):
+        mine = n < 4
+        side = jnp.where(mine, s_ref[0], 1 - s_ref[0])
+        at = jnp.where(mine, s_ref[1], s_ref[2])
+        return side, (at + 8 - n) % 4
 
     return pl.pallas_call(
         kernel,
         out_shape=jax.ShapeDtypeStruct((2 * half, 4 * quarter), BF),
-        in_specs=[SMEM] + [ANY] * 8,
-        out_specs=ANY,
-        scratch_shapes=[pltpu.SemaphoreType.DMA((8,))],
+        grid_spec=pltpu.PrefetchScalarGridSpec(
+            num_scalar_prefetch=1,
+            grid=(8,),
+            in_specs=[pl.BlockSpec((half + TAIL, quarter), lambda n, s_ref: (0, 0))] * 8,
+            out_specs=pl.BlockSpec((half, quarter), place),
+        ),
+        compiler_params=params(24),
         name="lay_out",
     )(scalars, *own, *other)
 
@@ -477,7 +514,7 @@
     blocks = project(ints(head_at), tokens, query_weight, key_weight, value_weight)
     q = exchange(blocks, HEAD_RING)
     own = stack_rows(q)
-    far = {d: lax.ppermute(own, AXES, turn(ROW_RING, d)) for d in (1, 3, 2)}
+    far = {d: lax.ppermute(own, AXES, turn(ROW_RING, d)) for d in (1, 3)}
 
     def bases(*steps):
         values = []
@@ -489,6 +526,8 @@
         return ints(*values)
 
     state = attend(bases(0), q, [own], None)
+    own_2, _ = lax.optimization_barrier((own, state[0][0]))
+    far[2] = lax.ppermute(own_2, AXES, turn(ROW_RING, 2))
 
     (tokens_l, skipped_l, upstream_l), _ = lax.optimization_barrier(
         ((tokens, skipped, upstream), state[0][0])
@@ -505,9 +544,7 @@
         [before[:1], after[:1], blank(20), before[1:3], after[1:3], blank(6)], axis=0
     ).astype(F32)
     ends = jnp.concatenate([blank(7), before[3:4], after[3:4], blank(7)], axis=0)
-    dims = (((1,), (1,)), ((), ()))
-    grad_act = lax.dot_general(upstream_l, point_weight, dims, preferred_element_type=F32)
-    grad_act_ends = lax.dot_general(ends, point_weight, dims, preferred_element_type=F32)
+    turned = upstream_l.T
 
     state = attend(bases(1), q, [far[1]], state)
     state = attend(bases(3), q, [far[3]], state)
@@ -525,21 +562,21 @@
     swap = [(0, 1), (1, 0)]
     theirs = ints(1 - ic, at(SUM_RINGS[0], True))
     mine = ints(ic, at(SUM_RINGS[0]))
-    sent = [product(theirs, act, upstream, steps) for steps in ((2, 1), (3, 0))]
+    sent = [product(theirs, act, turned, steps) for steps in ((2, 1), (3, 0))]
     arrived = [lax.ppermute(s, "c", swap) for s in sent]
-    piece_2, piece_1 = product(mine, act, upstream, (2, 1), arrived[0])
-    piece_3, piece_0 = product(mine, act, upstream, (3, 0), arrived[1])
+    piece_2, piece_1 = product(mine, act, turned, (2, 1), arrived[0])
+    piece_3, piece_0 = product(mine, act, turned, (3, 0), arrived[1])
     got = exchange([piece_0, piece_1, piece_2, piece_3], SUM_RINGS[0])
 
-    (up_rows, grad_act), _ = lax.optimization_barrier(((up_rows, grad_act), (piece_0, piece_1)))
-    grad_skip, depth_term = backward(up_rows, grad_act, grad_act_ends, depth_weight)
+    up_rows, _ = lax.optimization_barrier((up_rows, (piece_0, piece_1)))
+    grad_skip, depth_term = backward(up_rows, upstream, ends, point_weight, depth_weight)
     half = columns // 2
     d_theirs = lax.dynamic_slice_in_dim(depth_term, (1 - ic) * half, half, axis=1)
     d_mine = lax.dynamic_slice_in_dim(depth_term, ic * half, half, axis=1)
     d_sum = d_mine + lax.ppermute(d_theirs, "c", swap)
-    rider = jnp.pad(d_sum.reshape(6, half // 2).astype(BF), ((0, TAIL - 6), (0, 0)))
-
-    slim = half // 4
+    rider = jnp.pad(d_sum.astype(BF), ((0, TAIL - 3), (0, 0)))
+
+    slim = columns // 16
     second_at = at(SUM_RINGS[1])
     got = exchange(split_rows(ints(second_at), got, rider), SUM_RINGS[1])
     got = exchange([total_of(got).astype(BF)] * 4, SUM_RINGS[2])
@@ -552,7 +589,8 @@
     grad_pointwise = lay_out(ints(ic, at(SUM_RINGS[0]), at(SUM_RINGS[0], True)), got, other)
 
     def depth_of(blocks):
-        return total_of([b[half : half + 6] for b in blocks]).reshape(3, half)
+        rows = total_of([b[half:] for b in blocks])
+        return jnp.concatenate([rows[:3], rows[8:11]], axis=1)
 
     d_own, d_other = depth_of(got), depth_of(other)
     grad_depth = jnp.concatenate(

time: 311 us -> 175 us (0.56); the launches traced: 306 us -> 174 us
  Pallas kernels: 187 us -> 56.9 us
  matrix products: 8.3 us -> 0 us
  local copies, waits for them, and re-layouts: 16.5 us -> 23.2 us
    pallas_call x1, Pallas kernels: 145 us -> 4.35 us  [lay_out(): pl.pallas_call(kernel, out_shape=jax.ShapeDtypeStruct((2 * half, 4 * quar...]
    dot_general x2 -> x0, matrix products: 8.3 us -> none  [the longest x1 4.53 us: local(): lax.dot_general(upstream_l, point_weight, dims, preferred_element_type=F32)]
    ppermute x4, starting transfers between devices: 16.3 us -> 10.4 us  [local(): other = [lax.ppermute(g, 'c', swap) for g in got]]
    pallas_call x2, Pallas kernels: 1.39 us -> 7.26 us  [the longest x1 7.02 us: project(): pl.pallas_call(kernel, grid=(count,), out_shape=[jax.ShapeDtypeStruct((ro...]
    unnamed x50 -> x60, local copies, waits for them, and re-layouts: 14.1 us -> 19 us
    ppermute x2, starting transfers between devices: 3.02 us -> 6.31 us  [local(): arrived = [lax.ppermute(s, 'c', swap) for s in sent]]
  transfers between devices with their start and end apart: 33 -> 33, of which waited for: 18 -> 17; matrix products, arithmetic and copies ran while one was open for 4% -> 3% of each run, Pallas kernels for 10% -> 18%
where the time goes in v3:
time: 175 us; the launch traced here: 174 us
  Pallas kernels  56.9 us (33%)
  starting transfers between devices  56.9 us (33%)
  waiting for transfers between devices  32.8 us (19%)
  local copies, waits for them, and re-layouts  23.2 us (13%)
  other arithmetic  2.53 us (1%)
    ppermute x21, waiting for transfers between devices, exchange(): got[d] = lax.ppermute(pieces[d], AXES, turn(axes, sign * d))  29.2 us
    ppermute x21, starting transfers between devices, exchange(): got[d] = lax.ppermute(pieces[d], AXES, turn(axes, sign * d))  27.3 us
    unnamed x60, local copies, waits for them, and re-layouts  19 us
    pallas_call x4, Pallas kernels, attend(): pl.pallas_call(kernel, out_shape=outs, in_specs=[SMEM] * len(scalars) + [...  12.8 us
    pallas_call x1, Pallas kernels, backward(): pl.pallas_call(kernel, grid=(columns // wide,), out_shape=[jax.ShapeDtype...  11.3 us
    ppermute x4, starting transfers between devices, local(): other = [lax.ppermute(g, 'c', swap) for g in got]  10.4 us
    pallas_call x4, Pallas kernels, product(): pl.pallas_call(kernel, out_shape=outs, in_specs=[SMEM] + [VMEM] * len(ins...  10.4 us
    pallas_call x1, Pallas kernels, forward(): pl.pallas_call(kernel, grid=(columns // wide,), out_shape=[jax.ShapeDtype...  9.19 us
  transfers between devices with their start and end apart: 33, of which 17 were waited for; matrix products, arithmetic and copies ran while one was open for 3% of the time, Pallas kernels for 18%

profile of v3, /device:TPU:1, one launch (start us, length us, event | category | flops | bytes accessed | tf_op | source)
XLA Modules:
  0.0 174.0 jit_solution(5603173675777040897)
XLA Ops:
  0.6 7.0 %project.1 = (bf16[256,384]{1,0:T(8,128)(2,1)}, bf16[256,384]{1,0:T(8,128)(2,1)}, bf16[256,384]{1,0:T(8,128)(2,1)}, bf16[256,384]{1,0:T(8,128)(2,1)}) custom-call(s32[1]{0:T(128)} %bitcast.3.at_ref, bf16[256,1536]{1,0:T(8,128)(2,1)} %bitcast.40, bf16[1536,256]{1,0:T(8,128)(2,1)} %wq_ref.1, bf16[1536,256]{1,0:T(8,128)(2,1)} %wk_ref.1, bf16[1536,768]{1,0:T(8,128)(2,1)} %wv_ref.1), custom_call_target="tpu_custom_call" | custom-call | tf_op jit(solution)/shard_map/project/pallas_call | solution.py:95
  7.7 2.5 %collective-permute-start = (bf16[256,384]{1,0:T(8,128)(2,1)}, bf16[256,384]{1,0:T(8,128)(2,1)S(1)}, u32[]{:S(2)}, u32[]{:S(2)}) collective-permute-start(bf16[256,384]{1,0:T(8,128)(2,1)} %get-tuple-element.53), channel_id=1, source_target_pairs={{0,1},{1,2},{2,3},{3,0},{4,5},{5,6},{6,7},{7,4},{8,9},{9,10},{10,1... | collective-permute-start | bytes 589832 | tf_op jit(solution)/shard_map/ppermute | solution.py:47
  10.1 3.3 %collective-permute-start.1 = (bf16[256,384]{1,0:T(8,128)(2,1)}, bf16[256,384]{1,0:T(8,128)(2,1)S(1)}, u32[]{:S(2)}, u32[]{:S(2)}) collective-permute-start(bf16[256,384]{1,0:T(8,128)(2,1)} %get-tuple-element.54), channel_id=1, source_target_pairs={{0,2},{1,3},{2,0},{3,1},{4,6},{5,7},{6,4},{7,5},{8,10},{9,11},{10,... | collective-permute-start | bytes 589832 | tf_op jit(solution)/shard_map/ppermute | solution.py:47
  16.1 3.0 %collective-permute-done.1.refs_2_.refs_3_ = bf16[256,384]{1,0:T(8,128)(2,1)S(1)} collective-permute-done((bf16[256,384]{1,0:T(8,128)(2,1)}, bf16[256,384]{1,0:T(8,128)(2,1)S(1)}, u32[]{:S(2)}, u32[]{:S(2)}) %collective-permute-start.1) | collective-permute-done | bytes 196640 | tf_op jit(solution)/shard_map/ppermute | solution.py:47
  22.8 2.3 %attend.4 = (f32[256,128]{1,0:T(8,128)S(1)}, f32[256,128]{1,0:T(8,128)S(1)}, f32[256,128]{1,0:T(8,128)S(1)}, f32[256,128]{1,0:T(8,128)S(1)}, f32[256,256]{1,0:T(...) custom-call(s32[17]{0:T(128)S(1)} %stack.214.bases_ref, ...), custom_call_target="tpu_custom_call" | custom-call | flops 1073741824 | bytes 4194304 | tf_op jit(solution)/shard_map/attend/pallas_call | solution.py:232
  33.0 4.0 %collective-permute-start.9 = (bf16[4,1536]{1,0:T(4,128)(2,1)S(1)}, bf16[4,1536]{1,0:T(4,128)(2,1)S(1)}, u32[]{:S(2)}, u32[]{:S(2)}) collective-permute-start(bf16[4,1536]{1,0:T(4,128)(2,1)S(1)} %pad_maximum_fusion.2), channel_id=1, source_target_pairs={{0,1},{1,2},{2,3},{3,4},{4,5},{5,6},{6,7},{7,8},{8,9},{9,10},{10,1... | collective-permute-start | bytes 36872 | tf_op jit(solution)/shard_map/ppermute | solution.py:537
  47.8 2.6 %attend.5 = (f32[256,128]{1,0:T(8,128)S(1)}, f32[256,128]{1,0:T(8,128)S(1)}, f32[256,128]{1,0:T(8,128)S(1)}, f32[256,128]{1,0:T(8,128)S(1)}, f32[256,256]{1,0:T(...) custom-call(s32[17]{0:T(128)S(1)} %stack.216.bases_ref, ...), custom_call_target="tpu_custom_call" | custom-call | flops 1073741824 | bytes 4194304 | tf_op jit(solution)/shard_map/attend/pallas_call | solution.py:232
  50.5 3.1 %attend.6 = (f32[256,128]{1,0:T(8,128)S(1)}, f32[256,128]{1,0:T(8,128)S(1)}, f32[256,128]{1,0:T(8,128)S(1)}, f32[256,128]{1,0:T(8,128)S(1)}, f32[256,256]{1,0:T(...) custom-call(s32[17]{0:T(128)S(1)} %stack.215.bases_ref, ...), custom_call_target="tpu_custom_call" | custom-call | flops 1073741824 | bytes 4194304 | tf_op jit(solution)/shard_map/attend/pallas_call | solution.py:232
  53.7 4.7 %attend.7 = (bf16[272,256]{1,0:T(8,128)(2,1)S(1)}, bf16[272,256]{1,0:T(8,128)(2,1)}, bf16[272,256]{1,0:T(8,128)(2,1)}, bf16[272,256]{1,0:T(8,128)(2,1)}) custom-call(s32[17]{0:T(128)S(1)} %stack.196.bases_ref, s32[9]{0:T(128)S(1)} %stack.213.refs_0_, bf16[256,384]{1,0:T(8,128)(2,1)S(1)} %copy-done.4, ...), custom_call_target="tpu_custom_call" | custom-call | flops 1073741824 | bytes 4194304 | tf_op jit(solution)/shard_map/attend/pallas_call | solution.py:232
  59.0 2.0 %collective-permute-start.6 = (bf16[272,256]{1,0:T(8,128)(2,1)}, bf16[272,256]{1,0:T(8,128)(2,1)S(1)}, u32[]{:S(2)}, u32[]{:S(2)}) collective-permute-start(bf16[272,256]{1,0:T(8,128)(2,1)} %get-tuple-element.82), channel_id=1, source_target_pairs={{0,3},{1,0},{2,1},{3,2},{4,7},{5,4},{6,5},{7,6},{8,11},{9,8},{10,9... | collective-permute-start | bytes 417800 | tf_op jit(solution)/shard_map/ppermute | solution.py:47
  64.9 1.9 %collective-permute-done.7.b2 = bf16[272,256]{1,0:T(8,128)(2,1)S(1)} collective-permute-done((bf16[272,256]{1,0:T(8,128)(2,1)}, bf16[272,256]{1,0:T(8,128)(2,1)S(1)}, u32[]{:S(2)}, u32[]{:S(2)}) %collective-permute-start.7) | collective-permute-done | bytes 139296 | tf_op jit(solution)/shard_map/ppermute | solution.py:47
  68.8 9.2 %forward.1 = (bf16[528,1536]{1,0:T(8,128)(2,1)}, bf16[512,1536]{1,0:T(8,128)(2,1)}) custom-call(s32[3]{0:T(128)} %pad_add_fusion.2.s_ref, bf16[272,256]{1,0:T(8,128)(2,1)} %copy-done.7, bf16[272,256]{1,0:T(8,128)(2,1)} %copy-done.27, bf16[272,256]{1,0:T(8,128)(2,1)} %copy-done.28, bf16[272,256]{1,0:T(8,128)(2,1)} %copy-done.29, bf16[256,1536]{1,0:T(8,128)(2,1)} %bitcast.42, ...), custom_call_target="tpu_custom_call" | custom-call | tf_op jit(solution)/shard_map/forward/pallas_call | solution.py:294
  79.4 2.4 %product.6 = bf16[2,384,768]{2,1,0:T(8,128)(2,1)} custom-call(s32[2]{0:T(128)S(1)} %pad_add_fusion.3.s_ref, bf16[512,1536]{1,0:T(8,128)(2,1)S(1)} %copy-done, bf16[1536,512]{1,0:T(8,128)(2,1)S(1)} %copy.14.g_ref), custom_call_target="tpu_custom_call" | custom-call | flops 603979776 | bytes 6291456 | tf_op jit(solution)/shard_map/product/pallas_call | solution.py:398
  81.8 6.3 %collective-permute-start.12 = (bf16[2,384,768]{2,1,0:T(8,128)(2,1)}, bf16[2,384,768]{2,1,0:T(8,128)(2,1)}, u32[]{:S(2)}, u32[]{:S(2)}) collective-permute-start(bf16[2,384,768]{2,1,0:T(8,128)(2,1)} %product.6), channel_id=1, source_target_pairs={{0,16},{16,0},{1,17},{17,1},{2,18},{18,2},{3,19},{19,3},{4,20},{20... | collective-permute-start | bytes 3538952 | tf_op jit(solution)/shard_map/ppermute | solution.py:566
  88.1 2.4 %product.4 = bf16[2,384,768]{2,1,0:T(8,128)(2,1)} custom-call(s32[2]{0:T(128)S(1)} %pad_add_fusion.3.s_ref, bf16[512,1536]{1,0:T(8,128)(2,1)S(1)} %copy-done, bf16[1536,512]{1,0:T(8,128)(2,1)S(1)} %copy.14.g_ref), custom_call_target="tpu_custom_call" | custom-call | flops 603979776 | bytes 6291456 | tf_op jit(solution)/shard_map/product/pallas_call | solution.py:398
  91.0 2.9 %product.7 = (bf16[384,768]{1,0:T(8,128)(2,1)}, bf16[384,768]{1,0:T(8,128)(2,1)}) custom-call(s32[2]{0:T(128)S(1)} %pad_add_fusion.1.s_ref, bf16[512,1536]{1,0:T(8,128)(2,1)S(1)} %copy-done.1, bf16[1536,512]{1,0:T(8,128)(2,1)S(1)} %copy.14.g_ref, bf16[2,384,768]{2,1,0:T(8,128)(2,1)} %collective-permute-done.12.refs_0_), custom_call_target="tpu_custom_call" | custom-call | flops 603979776 | bytes 6291456 | tf_op jit(solution)/shard_map/product/pallas_call | solution.py:398
  95.7 2.7 %product.5 = (bf16[384,768]{1,0:T(8,128)(2,1)}, bf16[384,768]{1,0:T(8,128)(2,1)S(1)}) custom-call(s32[2]{0:T(128)S(1)} %pad_add_fusion.1.s_ref, bf16[512,1536]{1,0:T(8,128)(2,1)S(1)} %copy-done.1, bf16[1536,512]{1,0:T(8,128)(2,1)S(1)} %copy.14.g_ref, bf16[2,384,768]{2,1,0:T(8,128)(2,1)} %collective-permute-done.11.refs_0_), custom_call_target="tpu_custom_call" | custom-call | flops 603979776 | bytes 6291456 | tf_op jit(solution)/shard_map/product/pallas_call | solution.py:398
  100.3 2.3 %copy-done.9 = bf16[1536,1536]{1,0:T(8,128)(2,1)S(1)} copy-done((bf16[1536,1536]{1,0:T(8,128)(2,1)S(1)}, bf16[1536,1536]{1,0:T(8,128)(2,1)}, u32[]{:S(2)}) %copy-start.9) | copy-done | bytes 4718616
  102.7 11.3 %backward.1 = (bf16[512,1536]{1,0:T(8,128)(2,1)}, f32[3,1536]{1,0:T(4,128)S(1)}) custom-call(bf16[528,1536]{1,0:T(8,128)(2,1)S(1)} %copy-done.10, bf16[512,1536]{1,0:T(8,128)(2,1)S(1)} %bitcast.39, bf16[16,1536]{1,0:T(8,128)(2,1)S(1)} %pad_maximum_fusion.e_ref, bf16[1536,1536]{1,0:T(8,128)(2,1)S(1)} %copy-done.9, f32[3,1536]{1,0:T(4,128)S(1)} %copy-done.8), custom_call_target="tpu_custom_call" | custom-call | flops 2415919104 | bytes 11534336 | tf_op jit(solution)/shard_map/backward/pallas_call | solution.py:356
  114.0 3.2 %collective-permute-start.16 = (f32[3,768]{1,0:T(4,128)S(1)}, f32[3,768]{1,0:T(4,128)S(1)}, u32[]{:S(2)}, u32[]{:S(2)}) collective-permute-start(f32[3,768]{1,0:T(4,128)S(1)} %constant_dynamic-slice_fusion), channel_id=1, source_target_pairs={{0,16},{16,0},{1,17},{17,1},{2,18},{18,2},{3,19},{19,3},{4,20},{20... | collective-permute-start | bytes 27656 | tf_op jit(solution)/shard_map/ppermute | solution.py:576
  119.6 2.8 %collective-permute-start.17 = (bf16[112,768]{1,0:T(8,128)(2,1)S(1)}, bf16[112,768]{1,0:T(8,128)(2,1)S(1)}, u32[]{:S(2)}, u32[]{:S(2)}) collective-permute-start(bf16[112,768]{1,0:T(8,128)(2,1)S(1)} %get-tuple-element.97), channel_id=1, source_target_pairs={{0,2},{1,3},{2,0},{3,1},{4,6},{5,7},{6,4},{7,5},{8,10},{9,11},{10,... | collective-permute-start | bytes 516104 | tf_op jit(solution)/shard_map/ppermute | solution.py:47
  122.4 2.7 %collective-permute-start.19 = (bf16[112,768]{1,0:T(8,128)(2,1)S(1)}, bf16[112,768]{1,0:T(8,128)(2,1)S(1)}, u32[]{:S(2)}, u32[]{:S(2)}) collective-permute-start(bf16[112,768]{1,0:T(8,128)(2,1)S(1)} %get-tuple-element.99), channel_id=1, source_target_pairs={{0,3},{1,0},{2,1},{3,2},{4,7},{5,4},{6,5},{7,6},{8,11},{9,8},{10,9... | collective-permute-start | bytes 516104 | tf_op jit(solution)/shard_map/ppermute | solution.py:47
  125.8 2.4 %collective-permute-done.18 = bf16[112,768]{1,0:T(8,128)(2,1)S(1)} collective-permute-done((bf16[112,768]{1,0:T(8,128)(2,1)S(1)}, bf16[112,768]{1,0:T(8,128)(2,1)S(1)}, u32[]{:S(2)}, u32[]{:S(2)}) %collective-permute-start.18) | collective-permute-done | bytes 172064 | tf_op jit(solution)/shard_map/ppermute | solution.py:47
  128.8 2.5 %collective-permute-start.22 = (bf16[112,768]{1,0:T(8,128)(2,1)S(1)}, bf16[112,768]{1,0:T(8,128)(2,1)S(1)}, u32[]{:S(2)}, u32[]{:S(2)}) collective-permute-start(bf16[112,768]{1,0:T(8,128)(2,1)S(1)} %add_convert_fusion), channel_id=1, source_target_pairs={{0,12},{1,13},{2,14},{3,15},{4,0},{5,1},{6,2},{7,3},{8,4},{9,5},{1... | collective-permute-start | bytes 516104 | tf_op jit(solution)/shard_map/ppermute | solution.py:47
  131.3 3.2 %collective-permute-done.20 = bf16[112,768]{1,0:T(8,128)(2,1)S(1)} collective-permute-done((bf16[112,768]{1,0:T(8,128)(2,1)S(1)}, bf16[112,768]{1,0:T(8,128)(2,1)S(1)}, u32[]{:S(2)}, u32[]{:S(2)}) %collective-permute-start.20) | collective-permute-done | bytes 172064 | tf_op jit(solution)/shard_map/ppermute | solution.py:47
  136.5 3.2 %collective-permute-start.24 = (bf16[96,768]{1,0:T(8,128)(2,1)S(1)}, bf16[96,768]{1,0:T(8,128)(2,1)S(1)}, u32[]{:S(2)}, u32[]{:S(2)}) collective-permute-start(bf16[96,768]{1,0:T(8,128)(2,1)S(1)} %slice.110.refs_0_), channel_id=1, source_target_pairs={{0,2},{1,3},{2,0},{3,1},{4,6},{5,7},{6,4},{7,5},{8,10},{9,11},{10,... | collective-permute-start | bytes 442376 | tf_op jit(solution)/shard_map/ppermute | solution.py:47
  141.3 2.5 %collective-permute-done.24.refs_2_ = bf16[96,768]{1,0:T(8,128)(2,1)S(1)} collective-permute-done((bf16[96,768]{1,0:T(8,128)(2,1)S(1)}, bf16[96,768]{1,0:T(8,128)(2,1)S(1)}, u32[]{:S(2)}, u32[]{:S(2)}) %collective-permute-start.24) | collective-permute-done | bytes 147488 | tf_op jit(solution)/shard_map/ppermute | solution.py:47
  144.3 1.9 %collective-permute-start.27 = (bf16[784,384]{1,0:T(8,128)(2,1)S(1)}, bf16[784,384]{1,0:T(8,128)(2,1)S(1)}, u32[]{:S(2)}, u32[]{:S(2)}) collective-permute-start(bf16[784,384]{1,0:T(8,128)(2,1)S(1)} %join_rows.1.refs_0_), channel_id=1, source_target_pairs={{0,64},{1,65},{2,66},{3,67},{4,68},{5,69},{6,70},{7,71},{8,72},{9,... | collective-permute-start | bytes 1806344 | tf_op jit(solution)/shard_map/ppermute | solution.py:47
  147.0 5.0 %collective-permute-start.29 = (bf16[784,384]{1,0:T(8,128)(2,1)S(1)}, bf16[784,384]{1,0:T(8,128)(2,1)S(1)}, u32[]{:S(2)}, u32[]{:S(2)}) collective-permute-start(bf16[784,384]{1,0:T(8,128)(2,1)S(1)} %join_rows.1.refs_0_), channel_id=1, source_target_pairs={{0,16},{16,0},{1,17},{17,1},{2,18},{18,2},{3,19},{19,3},{4,20},{20... | collective-permute-start | bytes 1806344 | tf_op jit(solution)/shard_map/ppermute | solution.py:588
  151.9 9.2 %collective-permute-done.26.refs_1_ = bf16[784,384]{1,0:T(8,128)(2,1)S(1)} collective-permute-done((bf16[784,384]{1,0:T(8,128)(2,1)S(1)}, bf16[784,384]{1,0:T(8,128)(2,1)S(1)}, u32[]{:S(2)}, u32[]{:S(2)}) %collective-permute-start.26) | collective-permute-done | bytes 602144 | tf_op jit(solution)/shard_map/ppermute | solution.py:47
  161.1 4.5 %collective-permute-start.30 = (bf16[784,384]{1,0:T(8,128)(2,1)S(1)}, bf16[784,384]{1,0:T(8,128)(2,1)S(1)}, u32[]{:S(2)}, u32[]{:S(2)}) collective-permute-start(bf16[784,384]{1,0:T(8,128)(2,1)S(1)} %collective-permute-done.26.refs_1_), channel_id=1, source_target_pairs={{0,16},{16,0},{1,17},{17,1},{2,18},{18,2},{3,19},{19,3},{4,20},{20... | collective-permute-start | bytes 1806344 | tf_op jit(solution)/shard_map/ppermute | solution.py:588
  169.7 4.3 %lay_out.1 = bf16[1536,1536]{1,0:T(8,128)(2,1)} custom-call(s32[3]{0:T(128)S(1)} %pad_add_fusion.s_ref, bf16[784,384]{1,0:T(8,128)(2,1)S(1)} %join_rows.1.refs_0_, bf16[784,384]{1,0:T(8,128)(2,1)S(1)} %collective-permute-done.26.refs_1_, bf16[784,384]{1,0:T(8,128)(2,1)S(1)} %collective-permute-done.27.refs_2_, ...), custom_call_target="tpu_custom_call" | custom-call | tf_op jit(solution)/shard_map/lay_out/pallas_call | solution.py:472
  (148 shorter events, 48.9 us)
Async XLA Ops:
  7.7 8.4 %collective-permute-start = (bf16[256,384]{1,0:T(8,128)(2,1)}, bf16[256,384]{1,0:T(8,128)(2,1)S(1)}, u32[]{:S(2)}, u32[]{:S(2)}) collective-permute-start(bf16[256,384]{1,0:T(8,128)(2,1)} %get-tuple-element.53), channel_id=1, source_target_pairs={{0,1},{1,2},{2,3},{3,0},{4,5},{5,6},{6,7},{7,4},{8,9},{9,10},{10,1... | collective-permute-start | bytes 589832 | tf_op jit(solution)/shard_map/ppermute | solution.py:47
  10.1 9.0 %collective-permute-start.1 = (bf16[256,384]{1,0:T(8,128)(2,1)}, bf16[256,384]{1,0:T(8,128)(2,1)S(1)}, u32[]{:S(2)}, u32[]{:S(2)}) collective-permute-start(bf16[256,384]{1,0:T(8,128)(2,1)} %get-tuple-element.54), channel_id=1, source_target_pairs={{0,2},{1,3},{2,0},{3,1},{4,6},{5,7},{6,4},{7,5},{8,10},{9,11},{10,... | collective-permute-start | bytes 589832 | tf_op jit(solution)/shard_map/ppermute | solution.py:47
  13.4 5.7 %collective-permute-start.2 = (bf16[256,384]{1,0:T(8,128)(2,1)}, bf16[256,384]{1,0:T(8,128)(2,1)S(1)}, u32[]{:S(2)}, u32[]{:S(2)}) collective-permute-start(bf16[256,384]{1,0:T(8,128)(2,1)} %get-tuple-element.55), channel_id=1, source_target_pairs={{0,3},{1,0},{2,1},{3,2},{4,7},{5,4},{6,5},{7,6},{8,11},{9,8},{10,9... | collective-permute-start | bytes 589832 | tf_op jit(solution)/shard_map/ppermute | solution.py:47
  20.1 20.3 %collective-permute-start.3 = (bf16[1040,256]{1,0:T(8,128)(2,1)S(1)}, bf16[1040,256]{1,0:T(8,128)(2,1)S(1)}, u32[]{:S(2)}, u32[]{:S(2)}) collective-permute-start(bf16[1040,256]{1,0:T(8,128)(2,1)S(1)} %stack_rows.1.refs_4_.refs_5_), channel_id=1, source_target_pairs={{0,4},{1,5},{2,6},{3,7},{4,8},{5,9},{6,10},{7,11},{8,12},{9,13},{1... | collective-permute-start | bytes 1597448 | tf_op jit(solution)/shard_map/ppermute | solution.py:517
  21.2 29.3 %collective-permute-start.4 = (bf16[1040,256]{1,0:T(8,128)(2,1)S(1)}, bf16[1040,256]{1,0:T(8,128)(2,1)}, u32[]{:S(2)}, u32[]{:S(2)}) collective-permute-start(bf16[1040,256]{1,0:T(8,128)(2,1)S(1)} %stack_rows.1.refs_4_.refs_5_), channel_id=1, source_target_pairs={{0,12},{1,13},{2,14},{3,15},{4,0},{5,1},{6,2},{7,3},{8,4},{9,5},{1... | collective-permute-start | bytes 1597448 | tf_op jit(solution)/shard_map/ppermute | solution.py:517
  31.6 8.7 %collective-permute-start.10 = (bf16[4,1536]{1,0:T(4,128)(2,1)S(1)}, bf16[4,1536]{1,0:T(4,128)(2,1)S(1)}, u32[]{:S(2)}, u32[]{:S(2)}) collective-permute-start(bf16[4,1536]{1,0:T(4,128)(2,1)S(1)} %pad_maximum_fusion.3), channel_id=1, source_target_pairs={{1,0},{2,1},{3,2},{4,3},{5,4},{6,5},{7,6},{8,7},{9,8},{10,9},{11,1... | collective-permute-start | bytes 36872 | tf_op jit(solution)/shard_map/ppermute | solution.py:538
  33.0 29.2 %collective-permute-start.9 = (bf16[4,1536]{1,0:T(4,128)(2,1)S(1)}, bf16[4,1536]{1,0:T(4,128)(2,1)S(1)}, u32[]{:S(2)}, u32[]{:S(2)}) collective-permute-start(bf16[4,1536]{1,0:T(4,128)(2,1)S(1)} %pad_maximum_fusion.2), channel_id=1, source_target_pairs={{0,1},{1,2},{2,3},{3,4},{4,5},{5,6},{6,7},{7,8},{8,9},{9,10},{10,1... | collective-permute-start | bytes 36872 | tf_op jit(solution)/shard_map/ppermute | solution.py:537
  37.0 16.7 %collective-permute-start.5 = (bf16[1040,256]{1,0:T(8,128)(2,1)S(1)}, bf16[1040,256]{1,0:T(8,128)(2,1)}, u32[]{:S(2)}, u32[]{:S(2)}) collective-permute-start(bf16[1040,256]{1,0:T(8,128)(2,1)S(1)} %stack_rows.1.refs_4_.refs_5_), channel_id=1, source_target_pairs={{0,8},{1,9},{2,10},{3,11},{4,12},{5,13},{6,14},{7,15},{8,0},{9,1},... | collective-permute-start | bytes 1597448 | tf_op jit(solution)/shard_map/ppermute | solution.py:530
  59.0 5.9 %collective-permute-start.6 = (bf16[272,256]{1,0:T(8,128)(2,1)}, bf16[272,256]{1,0:T(8,128)(2,1)S(1)}, u32[]{:S(2)}, u32[]{:S(2)}) collective-permute-start(bf16[272,256]{1,0:T(8,128)(2,1)} %get-tuple-element.82), channel_id=1, source_target_pairs={{0,3},{1,0},{2,1},{3,2},{4,7},{5,4},{6,5},{7,6},{8,11},{9,8},{10,9... | collective-permute-start | bytes 417800 | tf_op jit(solution)/shard_map/ppermute | solution.py:47
  61.0 5.7 %collective-permute-start.7 = (bf16[272,256]{1,0:T(8,128)(2,1)}, bf16[272,256]{1,0:T(8,128)(2,1)S(1)}, u32[]{:S(2)}, u32[]{:S(2)}) collective-permute-start(bf16[272,256]{1,0:T(8,128)(2,1)} %get-tuple-element.83), channel_id=1, source_target_pairs={{0,2},{1,3},{2,0},{3,1},{4,6},{5,7},{6,4},{7,5},{8,10},{9,11},{10,... | collective-permute-start | bytes 417800 | tf_op jit(solution)/shard_map/ppermute | solution.py:47
  62.1 6.1 %collective-permute-start.8 = (bf16[272,256]{1,0:T(8,128)(2,1)}, bf16[272,256]{1,0:T(8,128)(2,1)S(1)}, u32[]{:S(2)}, u32[]{:S(2)}) collective-permute-start(bf16[272,256]{1,0:T(8,128)(2,1)} %get-tuple-element.84), channel_id=1, source_target_pairs={{0,1},{1,2},{2,3},{3,0},{4,5},{5,6},{6,7},{7,4},{8,9},{9,10},{10,1... | collective-permute-start | bytes 417800 | tf_op jit(solution)/shard_map/ppermute | solution.py:47
  81.8 9.1 %collective-permute-start.12 = (bf16[2,384,768]{2,1,0:T(8,128)(2,1)}, bf16[2,384,768]{2,1,0:T(8,128)(2,1)}, u32[]{:S(2)}, u32[]{:S(2)}) collective-permute-start(bf16[2,384,768]{2,1,0:T(8,128)(2,1)} %product.6), channel_id=1, source_target_pairs={{0,16},{16,0},{1,17},{17,1},{2,18},{18,2},{3,19},{19,3},{4,20},{20... | collective-permute-start | bytes 3538952 | tf_op jit(solution)/shard_map/ppermute | solution.py:566
  90.5 5.2 %collective-permute-start.11 = (bf16[2,384,768]{2,1,0:T(8,128)(2,1)}, bf16[2,384,768]{2,1,0:T(8,128)(2,1)}, u32[]{:S(2)}, u32[]{:S(2)}) collective-permute-start(bf16[2,384,768]{2,1,0:T(8,128)(2,1)} %product.4), channel_id=1, source_target_pairs={{0,16},{16,0},{1,17},{17,1},{2,18},{18,2},{3,19},{19,3},{4,20},{20... | collective-permute-start | bytes 3538952 | tf_op jit(solution)/shard_map/ppermute | solution.py:566
  93.9 24.2 %collective-permute-start.13 = (bf16[384,768]{1,0:T(8,128)(2,1)}, bf16[384,768]{1,0:T(8,128)(2,1)}, u32[]{:S(2)}, u32[]{:S(2)}) collective-permute-start(bf16[384,768]{1,0:T(8,128)(2,1)} %get-tuple-element.90), channel_id=1, source_target_pairs={{0,32},{1,33},{2,34},{3,35},{4,36},{5,37},{6,38},{7,39},{8,40},{9,... | collective-permute-start | bytes 1769480 | tf_op jit(solution)/shard_map/ppermute | solution.py:47
  93.9 24.2 %collective-permute-start.14 = (bf16[384,768]{1,0:T(8,128)(2,1)}, bf16[384,768]{1,0:T(8,128)(2,1)}, u32[]{:S(2)}, u32[]{:S(2)}) collective-permute-start(bf16[384,768]{1,0:T(8,128)(2,1)} %get-tuple-element.91), channel_id=1, source_target_pairs={{0,64},{1,65},{2,66},{3,67},{4,68},{5,69},{6,70},{7,71},{8,72},{9,... | collective-permute-start | bytes 1769480 | tf_op jit(solution)/shard_map/ppermute | solution.py:47
  99.2 18.9 %collective-permute-start.15 = (bf16[384,768]{1,0:T(8,128)(2,1)}, bf16[384,768]{1,0:T(8,128)(2,1)S(1)}, u32[]{:S(2)}, u32[]{:S(2)}) collective-permute-start(bf16[384,768]{1,0:T(8,128)(2,1)} %get-tuple-element.92), channel_id=1, source_target_pairs={{0,96},{1,97},{2,98},{3,99},{4,100},{5,101},{6,102},{7,103},{8,104... | collective-permute-start | bytes 1769480 | tf_op jit(solution)/shard_map/ppermute | solution.py:47
  114.0 4.0 %collective-permute-start.16 = (f32[3,768]{1,0:T(4,128)S(1)}, f32[3,768]{1,0:T(4,128)S(1)}, u32[]{:S(2)}, u32[]{:S(2)}) collective-permute-start(f32[3,768]{1,0:T(4,128)S(1)} %constant_dynamic-slice_fusion), channel_id=1, source_target_pairs={{0,16},{16,0},{1,17},{17,1},{2,18},{18,2},{3,19},{19,3},{4,20},{20... | collective-permute-start | bytes 27656 | tf_op jit(solution)/shard_map/ppermute | solution.py:576
  119.6 6.1 %collective-permute-start.17 = (bf16[112,768]{1,0:T(8,128)(2,1)S(1)}, bf16[112,768]{1,0:T(8,128)(2,1)S(1)}, u32[]{:S(2)}, u32[]{:S(2)}) collective-permute-start(bf16[112,768]{1,0:T(8,128)(2,1)S(1)} %get-tuple-element.97), channel_id=1, source_target_pairs={{0,2},{1,3},{2,0},{3,1},{4,6},{5,7},{6,4},{7,5},{8,10},{9,11},{10,... | collective-permute-start | bytes 516104 | tf_op jit(solution)/shard_map/ppermute | solution.py:47
  122.4 5.8 %collective-permute-start.18 = (bf16[112,768]{1,0:T(8,128)(2,1)S(1)}, bf16[112,768]{1,0:T(8,128)(2,1)S(1)}, u32[]{:S(2)}, u32[]{:S(2)}) collective-permute-start(bf16[112,768]{1,0:T(8,128)(2,1)S(1)} %get-tuple-element.98), channel_id=1, source_target_pairs={{0,1},{1,2},{2,3},{3,0},{4,5},{5,6},{6,7},{7,4},{8,9},{9,10},{10,1... | collective-permute-start | bytes 516104 | tf_op jit(solution)/shard_map/ppermute | solution.py:47
  122.4 5.8 %collective-permute-start.19 = (bf16[112,768]{1,0:T(8,128)(2,1)S(1)}, bf16[112,768]{1,0:T(8,128)(2,1)S(1)}, u32[]{:S(2)}, u32[]{:S(2)}) collective-permute-start(bf16[112,768]{1,0:T(8,128)(2,1)S(1)} %get-tuple-element.99), channel_id=1, source_target_pairs={{0,3},{1,0},{2,1},{3,2},{4,7},{5,4},{6,5},{7,6},{8,11},{9,8},{10,9... | collective-permute-start | bytes 516104 | tf_op jit(solution)/shard_map/ppermute | solution.py:47
  128.3 6.2 %collective-permute-start.20 = (bf16[112,768]{1,0:T(8,128)(2,1)S(1)}, bf16[112,768]{1,0:T(8,128)(2,1)S(1)}, u32[]{:S(2)}, u32[]{:S(2)}) collective-permute-start(bf16[112,768]{1,0:T(8,128)(2,1)S(1)} %add_convert_fusion), channel_id=1, source_target_pairs={{0,8},{1,9},{2,10},{3,11},{4,12},{5,13},{6,14},{7,15},{8,0},{9,1},... | collective-permute-start | bytes 516104 | tf_op jit(solution)/shard_map/ppermute | solution.py:47
  128.6 7.3 %collective-permute-start.21 = (bf16[112,768]{1,0:T(8,128)(2,1)S(1)}, bf16[112,768]{1,0:T(8,128)(2,1)S(1)}, u32[]{:S(2)}, u32[]{:S(2)}) collective-permute-start(bf16[112,768]{1,0:T(8,128)(2,1)S(1)} %add_convert_fusion), channel_id=1, source_target_pairs={{0,4},{1,5},{2,6},{3,7},{4,8},{5,9},{6,10},{7,11},{8,12},{9,13},{1... | collective-permute-start | bytes 516104 | tf_op jit(solution)/shard_map/ppermute | solution.py:47
  128.8 7.1 %collective-permute-start.22 = (bf16[112,768]{1,0:T(8,128)(2,1)S(1)}, bf16[112,768]{1,0:T(8,128)(2,1)S(1)}, u32[]{:S(2)}, u32[]{:S(2)}) collective-permute-start(bf16[112,768]{1,0:T(8,128)(2,1)S(1)} %add_convert_fusion), channel_id=1, source_target_pairs={{0,12},{1,13},{2,14},{3,15},{4,0},{5,1},{6,2},{7,3},{8,4},{9,5},{1... | collective-permute-start | bytes 516104 | tf_op jit(solution)/shard_map/ppermute | solution.py:47
  136.1 5.3 %collective-permute-start.23 = (bf16[96,768]{1,0:T(8,128)(2,1)S(1)}, bf16[96,768]{1,0:T(8,128)(2,1)S(1)}, u32[]{:S(2)}, u32[]{:S(2)}) collective-permute-start(bf16[96,768]{1,0:T(8,128)(2,1)S(1)} %slice.110.refs_0_), channel_id=1, source_target_pairs={{0,1},{1,2},{2,3},{3,0},{4,5},{5,6},{6,7},{7,4},{8,9},{9,10},{10,1... | collective-permute-start | bytes 442376 | tf_op jit(solution)/shard_map/ppermute | solution.py:47
  136.5 7.3 %collective-permute-start.24 = (bf16[96,768]{1,0:T(8,128)(2,1)S(1)}, bf16[96,768]{1,0:T(8,128)(2,1)S(1)}, u32[]{:S(2)}, u32[]{:S(2)}) collective-permute-start(bf16[96,768]{1,0:T(8,128)(2,1)S(1)} %slice.110.refs_0_), channel_id=1, source_target_pairs={{0,2},{1,3},{2,0},{3,1},{4,6},{5,7},{6,4},{7,5},{8,10},{9,11},{10,... | collective-permute-start | bytes 442376 | tf_op jit(solution)/shard_map/ppermute | solution.py:47
  139.7 4.3 %collective-permute-start.25 = (bf16[96,768]{1,0:T(8,128)(2,1)S(1)}, bf16[96,768]{1,0:T(8,128)(2,1)S(1)}, u32[]{:S(2)}, u32[]{:S(2)}) collective-permute-start(bf16[96,768]{1,0:T(8,128)(2,1)S(1)} %slice.110.refs_0_), channel_id=1, source_target_pairs={{0,3},{1,0},{2,1},{3,2},{4,7},{5,4},{6,5},{7,6},{8,11},{9,8},{10,9... | collective-permute-start | bytes 442376 | tf_op jit(solution)/shard_map/ppermute | solution.py:47
  144.2 16.9 %collective-permute-start.26 = (bf16[784,384]{1,0:T(8,128)(2,1)S(1)}, bf16[784,384]{1,0:T(8,128)(2,1)S(1)}, u32[]{:S(2)}, u32[]{:S(2)}) collective-permute-start(bf16[784,384]{1,0:T(8,128)(2,1)S(1)} %join_rows.1.refs_0_), channel_id=1, source_target_pairs={{0,32},{1,33},{2,34},{3,35},{4,36},{5,37},{6,38},{7,39},{8,40},{9,... | collective-permute-start | bytes 1806344 | tf_op jit(solution)/shard_map/ppermute | solution.py:47
  144.3 21.3 %collective-permute-start.27 = (bf16[784,384]{1,0:T(8,128)(2,1)S(1)}, bf16[784,384]{1,0:T(8,128)(2,1)S(1)}, u32[]{:S(2)}, u32[]{:S(2)}) collective-permute-start(bf16[784,384]{1,0:T(8,128)(2,1)S(1)} %join_rows.1.refs_0_), channel_id=1, source_target_pairs={{0,64},{1,65},{2,66},{3,67},{4,68},{5,69},{6,70},{7,71},{8,72},{9,... | collective-permute-start | bytes 1806344 | tf_op jit(solution)/shard_map/ppermute | solution.py:47
  146.2 19.5 %collective-permute-start.28 = (bf16[784,384]{1,0:T(8,128)(2,1)S(1)}, bf16[784,384]{1,0:T(8,128)(2,1)S(1)}, u32[]{:S(2)}, u32[]{:S(2)}) collective-permute-start(bf16[784,384]{1,0:T(8,128)(2,1)S(1)} %join_rows.1.refs_0_), channel_id=1, source_target_pairs={{0,96},{1,97},{2,98},{3,99},{4,100},{5,101},{6,102},{7,103},{8,104... | collective-permute-start | bytes 1806344 | tf_op jit(solution)/shard_map/ppermute | solution.py:47
  147.0 19.7 %collective-permute-start.29 = (bf16[784,384]{1,0:T(8,128)(2,1)S(1)}, bf16[784,384]{1,0:T(8,128)(2,1)S(1)}, u32[]{:S(2)}, u32[]{:S(2)}) collective-permute-start(bf16[784,384]{1,0:T(8,128)(2,1)S(1)} %join_rows.1.refs_0_), channel_id=1, source_target_pairs={{0,16},{16,0},{1,17},{17,1},{2,18},{18,2},{3,19},{19,3},{4,20},{20... | collective-permute-start | bytes 1806344 | tf_op jit(solution)/shard_map/ppermute | solution.py:588
  161.1 6.2 %collective-permute-start.30 = (bf16[784,384]{1,0:T(8,128)(2,1)S(1)}, bf16[784,384]{1,0:T(8,128)(2,1)S(1)}, u32[]{:S(2)}, u32[]{:S(2)}) collective-permute-start(bf16[784,384]{1,0:T(8,128)(2,1)S(1)} %collective-permute-done.26.refs_1_), channel_id=1, source_target_pairs={{0,16},{16,0},{1,17},{17,1},{2,18},{18,2},{3,19},{19,3},{4,20},{20... | collective-permute-start | bytes 1806344 | tf_op jit(solution)/shard_map/ppermute | solution.py:588
  165.7 3.4 %collective-permute-start.32 = (bf16[784,384]{1,0:T(8,128)(2,1)S(1)}, bf16[784,384]{1,0:T(8,128)(2,1)S(1)}, u32[]{:S(2)}, u32[]{:S(2)}) collective-permute-start(bf16[784,384]{1,0:T(8,128)(2,1)S(1)} %collective-permute-done.28.refs_3_), channel_id=1, source_target_pairs={{0,16},{16,0},{1,17},{17,1},{2,18},{18,2},{3,19},{19,3},{4,20},{20... | collective-permute-start | bytes 1806344 | tf_op jit(solution)/shard_map/ppermute | solution.py:588
  (31 other events, 93.8 us)

commit v4 on v2

v4 whole, which is shorter than its diff:
```python
import math

import jax
import jax.numpy as jnp
from jax import lax
from jax.experimental import pallas as pl
from jax.experimental.pallas import tpu as pltpu
from jax.sharding import Mesh, PartitionSpec as P

H = 4
DH = 64
DV = 192
AXES = ("x", "c", "z", "y")
SIZES = (4, 2, 4, 4)
BF = jnp.bfloat16
F32 = jnp.float32
TAIL = 16
VMEM = pl.BlockSpec(memory_space=pltpu.VMEM)
SMEM = pl.BlockSpec(memory_space=pltpu.SMEM)
ANY = pl.BlockSpec(memory_space=pl.ANY)
SUM_RINGS = (("x", "y"), ("y", "z"), ("z", "x"))
HEAD_RING = ("y", "z")
CORE, HEAD_AT, HAS_LOW, HAS_HIGH, FIRST_AT, THEIR_FIRST, SECOND_AT, FLAGS, BASES, VALID = 0, 1, 2, 3, 4, 5, 6, 8, 17, 33
ROW_RING = ("z", "y")


def params(mib):
    return pltpu.CompilerParams(vmem_limit_bytes=mib << 20)


def turn(axes, step):
    pairs = []
    for x in range(4):
        for c in range(2):
            for z in range(4):
                for y in range(4):
                    at = {"x": x, "z": z, "y": y}
                    to = dict(at)
                    to[axes[c]] = (at[axes[c]] + step) % 4
                    flat = [((p["x"] * 2 + c) * 4 + p["z"]) * 4 + p["y"] for p in (at, to)]
                    pairs.append(tuple(flat))
    return pairs


def exchange(pieces, axes, sign=1):
    got = [pieces[0], None, None, None]
    for d in (2, 1, 3):
        got[d] = lax.ppermute(pieces[d], AXES, turn(axes, sign * d))
    return got


def total_of(got):
    a, b, c, d = (g.astype(F32) for g in got)
    return (a + c) + (b + d)


def project(at, tokens, query_weight, key_weight, value_weight):
    rows, depth = tokens.shape
    cut = depth // 2

    def kernel(at_ref, tok_hbm, wq_hbm, wk_hbm, wv_hbm, *refs):
        outs, (tok_ref, wq_ref, wk_ref, wv_ref, held, sems) = refs[:4], refs[4:]
        low, high = pl.ds(0, cut), pl.ds(cut, depth - cut)
        copies = [
            pltpu.make_async_copy(tok_hbm, tok_ref, sems.at[0]),
            pltpu.make_async_copy(wv_hbm.at[low, :], wv_ref.at[low, :], sems.at[1]),
            pltpu.make_async_copy(wv_hbm.at[high, :], wv_ref.at[high, :], sems.at[2]),
            pltpu.make_async_copy(wk_hbm, wk_ref, sems.at[3]),
            pltpu.make_async_copy(wq_hbm, wq_ref, sems.at[4]),
        ]
        for copy in copies:
            copy.start()
        copies[0].wait()
        tok = tok_ref[...]
        copies[1].wait()
        v = jnp.dot(tok[:, :cut], wv_ref[:cut, :], preferred_element_type=F32)
        copies[2].wait()
        v += jnp.dot(tok[:, cut:], wv_ref[cut:, :], preferred_element_type=F32)
        copies[3].wait()
        k = jnp.dot(tok, wk_ref[...], preferred_element_type=F32)
        copies[4].wait()
        q = jnp.dot(tok, wq_ref[...], preferred_element_type=F32) * (1.0 / math.sqrt(DH))
        zero = jnp.zeros((rows, DH), F32)
        for h in range(H):
            held[h] = jnp.concatenate(
                [
                    v[:, h * DV : (h + 1) * DV],
                    k[:, h * DH : (h + 1) * DH],
                    zero,
                    q[:, h * DH : (h + 1) * DH],
                ],
                axis=1,
            ).astype(BF)
        for d in range(4):
            outs[d][...] = held[(at_ref[HEAD_AT] + d) % 4]

    return pl.pallas_call(
        kernel,
        out_shape=[jax.ShapeDtypeStruct((rows, 384), BF)] * 4,
        in_specs=[SMEM] + [ANY] * 4,
        out_specs=[VMEM] * 4,
        scratch_shapes=[
            pltpu.VMEM((rows, depth), BF),
            pltpu.VMEM((depth, H * DH), BF),
            pltpu.VMEM((depth, H * DH), BF),
            pltpu.VMEM((depth, H * DV), BF),
            pltpu.VMEM((4, rows, 384), BF),
            pltpu.SemaphoreType.DMA((5,)),
        ],
        compiler_params=params(53),
        name="project",
    )(at, tokens, query_weight, key_weight, value_weight)


def stack_rows(parts):
    rows = parts[0].shape[0]

    def kernel(*refs):
        ins, out = refs[:4], refs[4]
        row = lax.broadcasted_iota(jnp.int32, (TAIL, 128), 0)
        tail = jnp.zeros((TAIL, 128), F32)
        for d in range(4):
            out[d * rows : (d + 1) * rows, :] = ins[d][:, :256]
            first = ins[d][:TAIL, 256:].astype(F32)[:1]
            final = ins[d][rows - TAIL :, 256:].astype(F32)[TAIL - 1 :]
            tail = jnp.where(row == d, first, tail)
            tail = jnp.where(row == 4 + d, final, tail)
        out[4 * rows :, :128] = jnp.zeros((TAIL, 128), BF)
        out[4 * rows :, 128:] = tail.astype(BF)

    return pl.pallas_call(
        kernel,
        out_shape=jax.ShapeDtypeStruct((4 * rows + TAIL, 256), BF),
        in_specs=[VMEM] * 4,
        out_specs=VMEM,
        compiler_params=params(8),
        name="stack_rows",
    )(*parts)


def attend(scalars, near, q, pairs, state):
    rows = q[0].shape[0]
    width = 4 * rows
    first = state is None
    last = len(pairs) == 4

    def kernel(s_ref, *refs):
        q_refs, refs = refs[:4], refs[4:]
        pair_refs, refs = refs[: len(pairs)], refs[len(pairs) :]
        if not first:
            old, refs = refs[0], refs[1:]
        lane = lax.broadcasted_iota(jnp.int32, (width, 256), 1)
        place = lax.broadcasted_iota(jnp.int32, (1, rows), 1)

        def masks(n):
            return jnp.concatenate(
                [place + s_ref[BASES + 4 * n + i] < s_ref[VALID] for i in range(4)], axis=1
            )

        def values_of(ref):
            return jnp.where(lane == DV, jnp.ones((), BF), ref[:width, :])

        def scores_of(query, ref, keep):
            scores = lax.dot_general(
                query, ref[:width, 128:], (((1,), (1,)), ((), ())), preferred_element_type=F32
            )
            return jnp.where(keep, scores, -1e30)

        def shares(sums):
            return sums / sums[:, DV : DV + 1]

        if last:
            tails = [r[width:, 128:].astype(F32) for r in pair_refs]
            own, low, high = tails[0], tails[1], tails[2]
            row = lax.broadcasted_iota(jnp.int32, (TAIL, 128), 0)
            edge = jnp.zeros((TAIL, 128), F32)
            for d in range(4):
                n, m = (d + 1) % 4, (d + 3) % 4
                other = jnp.where(s_ref[FLAGS] == 0, own[4 + n : 5 + n], low[4 + d : 5 + d])
                prev = jnp.where(s_ref[FLAGS + 1 + d] == 1, low[4 + n : 5 + n], other)
                other = jnp.where(s_ref[FLAGS] == 0, own[m : m + 1], high[d : d + 1])
                nxt = jnp.where(s_ref[FLAGS + 5 + d] == 1, high[m : m + 1], other)
                edge = jnp.where(row == d, prev, edge)
                edge = jnp.where(row == 4 + d, nxt, edge)
            edge = edge.astype(BF)
            parts = [scores_of(edge, r, masks(n)) for n, r in enumerate(pair_refs)]
            peak = jnp.max(parts[0], axis=1, keepdims=True)
            for s in parts[1:]:
                peak = jnp.maximum(peak, jnp.max(s, axis=1, keepdims=True))
            edge_sums = jnp.zeros((TAIL, 256), F32)
            for s, r in zip(parts, pair_refs):
                edge_sums += jnp.dot(jnp.exp(s - peak).astype(BF), values_of(r), preferred_element_type=F32)
            edge_out = shares(edge_sums)
            row = lax.broadcasted_iota(jnp.int32, (TAIL, 256), 0)

        spot = lax.broadcasted_iota(jnp.int32, (rows, 256), 1)
        if not last:
            refs[1][...] = jnp.zeros((8, 128), F32)
        pair_ref = pair_refs[-1]
        keep = masks(near)
        values = values_of(pair_ref)
        for i in range(4):
            scores = scores_of(q_refs[i][:, 256:], pair_ref, keep)
            peak = jnp.max(scores, axis=1, keepdims=True)
            if not first:
                sums = old[i * rows : (i + 1) * rows, :]
                before = sums[:, DV + 1 : DV + 2]
                peak = jnp.maximum(peak, before)
            probs = jnp.exp(scores - peak).astype(BF)
            update = jnp.dot(probs, values, preferred_element_type=F32)
            if not first:
                update = update + sums * jnp.exp(before - peak)
            if last:
                refs[i][:rows, :] = shares(update).astype(BF)
                ends = jnp.where(row == 0, edge_out[i : i + 1], jnp.zeros((TAIL, 256), F32))
                ends = jnp.where(row == 1, edge_out[4 + i : 5 + i], ends)
                refs[i][rows:, :] = ends.astype(BF)
            else:
                refs[0][i * rows : (i + 1) * rows, :] = jnp.where(spot == DV + 1, peak, update)

    ins = [*q, *pairs]
    if not first:
        ins += [state]
    if last:
        outs = [jax.ShapeDtypeStruct((rows + TAIL, 256), BF)] * 4
    else:
        outs = [jax.ShapeDtypeStruct((4 * rows, 256), F32), jax.ShapeDtypeStruct((8, 128), F32)]
    got = pl.pallas_call(
        kernel,
        out_shape=outs,
        in_specs=[SMEM] + [VMEM] * len(ins),
        out_specs=[VMEM] * len(outs),
        compiler_params=params(16),
        cost_estimate=pl.CostEstimate(
            flops=4 * 2 * rows * width * 512, bytes_accessed=4 << 20, transcendentals=4 * rows * width
        ),
        name="attend",
    )(scalars, *ins)
    return got


def gelu_parts(pre):
    slope = math.sqrt(2.0 / math.pi)
    square = pre * pre
    bend = jnp.tanh(slope * (pre + 0.044715 * (square * pre)))
    return bend, square, slope


def edges(mark, trunk, skip, cotangent):
    columns = trunk.shape[1]

    def kernel(mark_ref, t_ref, s_ref, c_ref, down, up, buffer, sems):
        copies = []
        for n, ref in enumerate((t_ref, s_ref, c_ref)):
            for end in range(2):
                start = end * (ref.shape[0] - TAIL)
                copies.append(
                    pltpu.make_async_copy(
                        ref.at[pl.ds(start, TAIL), :], buffer.at[2 * n + end], sems.at[2 * n + end]
                    )
                )
        for copy in copies:
            copy.start()
        for copy in copies:
            copy.wait()
        t_first, t_last, s_first, s_last, c_first, c_last = (buffer[n].astype(F32) for n in range(6))
        row = lax.broadcasted_iota(jnp.int32, (TAIL, columns), 0)

        def four(a, b, c, d):
            rest = jnp.where(row == 2, c, jnp.where(row == 3, d, 0.0))
            return jnp.where(row == 0, a, jnp.where(row == 1, b, rest)).astype(BF)

        up[...] = four(t_first[:1], s_first[:1], s_first[1:2], c_first[:1])
        e = TAIL - 1
        down[...] = four(t_last[e:], s_last[e - 1 : e], s_last[e:], c_last[e:])

    return pl.pallas_call(
        kernel,
        out_shape=[jax.ShapeDtypeStruct((TAIL, columns), BF)] * 2,
        in_specs=[VMEM, ANY, ANY, ANY],
        out_specs=[VMEM] * 2,
        scratch_shapes=[pltpu.VMEM((6, TAIL, columns), BF), pltpu.SemaphoreType.DMA((6,))],
        compiler_params=params(8),
        name="edges",
    )(mark, trunk, skip, cotangent)


def gelu_parts(pre):
    slope = math.sqrt(2.0 / math.pi)
    square = pre * pre
    bend = jnp.tanh(slope * (pre + 0.044715 * (square * pre)))
    return bend, square, slope


WIDE = 256


def forward(scalars, ours, back, tokens, skipped, out_heads, before, after, depth_weight, turned):
    rows, columns = tokens.shape
    fine = 2 * rows
    half = columns // 2
    steps = half // WIDE
    quarter = columns // 4

    def side(s_ref):
        return s_ref[CORE] if ours else 1 - s_ref[CORE]

    def kernel(s_ref, b0, b1, b2, b3, low_ref, high_ref, dw_ref, tok_hbm, skip_hbm, ow_hbm, g_hbm, *refs):
        if ours:
            up_ref, act_ref = refs[:2]
            refs = refs[2:]
        else:
            up_ref, prod_ref, act_ref, g_ref = refs[:4]
            refs = refs[4:]
        att, held, tok, skp, ow, sems = refs
        j = pl.program_id(0)

        def copies(n):
            put = pl.ds(n * WIDE, WIDE)
            take = pl.ds(pl.multiple_of(side(s_ref) * half + n * WIDE, 128), WIDE)
            return [
                pltpu.make_async_copy(ow_hbm.at[:, :, take], ow.at[n], sems.at[3 * n]),
                pltpu.make_async_copy(tok_hbm.at[:, take], tok.at[n], sems.at[3 * n + 1]),
                pltpu.make_async_copy(skip_hbm.at[:, take], skp.at[n], sems.at[3 * n + 2]),
            ]

        turned_copy = None if ours else pltpu.make_async_copy(g_hbm, g_ref, sems.at[3 * steps])

        @pl.when(j == 0)
        def _():
            for n in range(steps):
                for copy in copies(n):
                    copy.start()
            if not ours:
                turned_copy.start()
            mixed = [b[:, :DV].astype(F32) for b in (b0, b1, b2, b3)]
            squares = sum(jnp.sum(m * m, axis=1, keepdims=True) for m in mixed)
            scale = lax.rsqrt(squares * (1.0 / (H * DV)) + 1e-05)
            for d in range(4):
                att[d] = (mixed[d] * scale).astype(BF)

        def chunk(n):
            for copy in copies(n):
                copy.wait()
            cut = pl.ds(n * WIDE, WIDE)
            low, high = low_ref[...].astype(F32), high_ref[...].astype(F32)
            grown = jnp.zeros((rows + TAIL, WIDE), F32)
            for d in range(4):
                grown += jnp.dot(att[d], ow[n, (s_ref[HEAD_AT] + d) % 4], preferred_element_type=F32)
            hidden = (tok[n].astype(F32) + grown[:rows]).astype(BF)
            low_hid = (low[:1] + grown[rows : rows + 1]).astype(BF).astype(F32)
            high_hid = (high[:1] + grown[rows + 1 : rows + 2]).astype(BF).astype(F32)
            twice = lax.broadcasted_iota(jnp.int32, (fine, rows), 0) // 2
            twice = jnp.where(twice == lax.broadcasted_iota(jnp.int32, (fine, rows), 1), 1.0, 0.0).astype(BF)
            up = jnp.dot(twice, hidden, preferred_element_type=F32) + skp[n].astype(F32)
            held[8 : 8 + fine, :] = up.astype(BF).astype(F32)
            row = lax.broadcasted_iota(jnp.int32, (8, WIDE), 0)
            edge = (low_hid + jnp.where(row == 6, low[1:2], low[2:3])).astype(BF).astype(F32)
            held[:8, :] = jnp.where((row >= 6) & (s_ref[HAS_LOW] > 0), edge, 0.0)
            edge = (high_hid + jnp.where(row == 0, high[1:2], high[2:3])).astype(BF).astype(F32)
            held[8 + fine :, :] = jnp.where((row < 2) & (s_ref[HAS_HIGH] > 0), edge, 0.0)
            up_ref[...] = held[...].astype(BF)
            pre = (
                dw_ref[0:1, :] * held[7 : 7 + fine, :]
                + dw_ref[1:2, :] * held[8 : 8 + fine, :]
                + dw_ref[2:3, :] * held[9 : 9 + fine, :]
            )
            bend, _, _ = gelu_parts(pre)
            value = (pre * (0.5 * (1.0 + bend))).astype(BF)
            if ours:
                act_ref[...] = value
            else:
                act_ref[:, n * WIDE : (n + 1) * WIDE] = value

        for n in range(steps):
            pl.when(j == n)(lambda n=n: chunk(n))

        if not ours:

            @pl.when(j == steps)
            def _():
                turned_copy.wait()

            @pl.when(j >= steps)
            def _():
                at = pl.multiple_of((s_ref[THEIR_FIRST] + j - steps) % 4 * quarter, 16)
                prod_ref[0] = jnp.dot(
                    g_ref[pl.ds(at, quarter), :], act_ref[...], preferred_element_type=F32
                ).astype(BF)

    def cols(count, full):
        def place(j, s_ref):
            n = jnp.minimum(j, steps - 1)
            return 0, (side(s_ref) * steps + n if full else n)

        return pl.BlockSpec((count, WIDE), place)

    def flat(count, width):
        return pl.BlockSpec((count, width), lambda j, s_ref: (0, 0))

    outs = [jax.ShapeDtypeStruct((fine + 16, half), BF)]
    out_specs = [cols(fine + 16, False)]
    scratch = []
    if ours:
        outs += [jax.ShapeDtypeStruct((fine, half), BF)]
        out_specs += [cols(fine, False)]
    else:
        outs += [jax.ShapeDtypeStruct((4, quarter, half), BF)]
        out_specs += [
            pl.BlockSpec((1, quarter, half), lambda j, s_ref: (jnp.maximum(j - steps, 0), 0, 0))
        ]
        scratch += [pltpu.VMEM((fine, half), BF), pltpu.VMEM((columns, fine), BF)]
    scratch += [
        pltpu.VMEM((4, rows + TAIL, DV), BF),
        pltpu.VMEM((fine + 16, WIDE), F32),
        pltpu.VMEM((steps, rows, WIDE), BF),
        pltpu.VMEM((steps, fine, WIDE), BF),
        pltpu.VMEM((steps, H, DV, WIDE), BF),
        pltpu.SemaphoreType.DMA((3 * steps + 1,)),
    ]
    return pl.pallas_call(
        kernel,
        out_shape=outs,
        grid_spec=pltpu.PrefetchScalarGridSpec(
            num_scalar_prefetch=1,
            grid=(steps if ours else steps + 4,),
            in_specs=[flat(rows + TAIL, 256)] * 4
            + [cols(TAIL, True), cols(TAIL, True), cols(3, True)]
            + [ANY] * 4,
            out_specs=out_specs,
            scratch_shapes=scratch,
        ),
        compiler_params=params(48),
        cost_estimate=pl.CostEstimate(
            flops=2 * fine * columns * columns, bytes_accessed=9 << 20, transcendentals=fine * half
        ),
        name="forward",
    )(scalars, *back, before, after, depth_weight, tokens, skipped, out_heads, turned)


def backward(scalars, ours, up, upstream, before, after, point_weight, depth_weight, behind, whole=None):
    fine, columns = upstream.shape
    half = columns // 2
    steps = half // WIDE

    def side(s_ref):
        return s_ref[CORE] if ours else 1 - s_ref[CORE]

    def kernel(s_ref, up_ref, g_ref, low_ref, high_ref, pw_ref, dw_ref, *refs):
        gs_ref, gd_ref, held, grad, ends = refs[-5:]
        dims = (((1,), (1,)), ((), ()))

        @pl.when(pl.program_id(0) == 0)
        def _():
            row = lax.broadcasted_iota(jnp.int32, (TAIL, columns), 0)
            low, high = low_ref[...].astype(F32), high_ref[...].astype(F32)
            ends[...] = jnp.where(row == 7, low[3:4], jnp.where(row == 8, high[3:4], 0.0)).astype(BF)

        upper = lax.dot_general(g_ref[...], pw_ref[...], dims, preferred_element_type=F32)
        outer = lax.dot_general(ends[...], pw_ref[...], dims, preferred_element_type=F32)
        held[:8, :] = jnp.zeros((8, WIDE), F32)
        held[8 : fine + 24, :] = up_ref[...].astype(F32)
        held[fine + 24 :, :] = jnp.zeros((8, WIDE), F32)

        def grad_of(start, count, coming):
            pre = (
                dw_ref[0:1, :] * held[start - 1 : start - 1 + count, :]
                + dw_ref[1:2, :] * held[start : start + count, :]
                + dw_ref[2:3, :] * held[start + 1 : start + 1 + count, :]
            )
            bend, square, slope = gelu_parts(pre)
            rate = 0.5 * (1.0 + bend) + (0.5 * slope) * pre * (1.0 - bend * bend) * (
                1.0 + (3 * 0.044715) * square
            )
            return (coming * rate).astype(BF).astype(F32)

        grad[:8, :] = grad_of(8, 8, outer[:8])
        mid = grad_of(16, fine, upper)
        grad[8 : 8 + fine, :] = mid
        grad[8 + fine :, :] = grad_of(16 + fine, 8, outer[8:])
        gs_ref[...] = (
            dw_ref[0:1, :] * grad[9 : 9 + fine, :]
            + dw_ref[1:2, :] * mid
            + dw_ref[2:3, :] * grad[7 : 7 + fine, :]
        ).astype(BF)
        for t in range(3):
            gd_ref[t : t + 1, :] = jnp.sum(held[15 + t : 15 + t + fine, :] * mid, axis=0, keepdims=True)

    def cols(count, full):
        return pl.BlockSpec((count, WIDE), lambda j, s_ref: (0, (side(s_ref) * steps if full else 0) + j))

    def flat(count):
        return pl.BlockSpec((count, columns), lambda j, s_ref: (0, 0))

    ins = [up, upstream, before, after, point_weight, depth_weight, behind]
    if whole is not None:
        ins.append(whole)
    return pl.pallas_call(
        kernel,
        out_shape=[jax.ShapeDtypeStruct((fine, columns), BF), jax.ShapeDtypeStruct((3, half), F32)],
        grid_spec=pltpu.PrefetchScalarGridSpec(
            num_scalar_prefetch=1,
            grid=(steps,),
            in_specs=[
                cols(fine + 16, False),
                flat(fine),
                flat(TAIL),
                flat(TAIL),
                pl.BlockSpec((WIDE, columns), lambda j, s_ref: (side(s_ref) * steps + j, 0)),
                cols(3, True),
            ]
            + [ANY] * (len(ins) - 6),
            out_specs=[cols(fine, True), cols(3, False)],
            scratch_shapes=[
                pltpu.VMEM((fine + 32, WIDE), F32),
                pltpu.VMEM((fine + 16, WIDE), F32),
                pltpu.VMEM((TAIL, columns), BF),
            ],
        ),
        input_output_aliases={} if whole is None else {8: 0},
        compiler_params=params(48),
        cost_estimate=pl.CostEstimate(
            flops=fine * columns * columns, bytes_accessed=6 << 20, transcendentals=fine * half
        ),
        name="backward",
    )(scalars, *ins)


def product(scalars, act, turned, steps, arrived):
    half, quarter = act.shape[1], turned.shape[0] // 4

    def kernel(s_ref, a_ref, g_ref, arrived_ref, *outs):
        for out, d in zip(outs, steps):
            at = pl.multiple_of((s_ref[FIRST_AT] + d) % 4 * quarter, 16)
            block = jnp.dot(g_ref[pl.ds(at, quarter), :], a_ref[...], preferred_element_type=F32)
            out[...] = (block + arrived_ref[d].astype(F32)).astype(BF)

    return pl.pallas_call(
        kernel,
        out_shape=[jax.ShapeDtypeStruct((quarter, half), BF)] * len(steps),
        in_specs=[SMEM] + [VMEM] * 3,
        out_specs=[VMEM] * len(steps),
        compiler_params=params(14),
        cost_estimate=pl.CostEstimate(
            flops=2 * act.shape[0] * half * quarter * len(steps), bytes_accessed=6 << 20, transcendentals=0
        ),
        name="product",
    )(scalars, act, turned, arrived)


def split_rows(at, got, rider):
    rows, columns = got[0].shape
    slim = rows // 4

    def kernel(at_ref, *refs):
        ins, rider_ref, outs = refs[:4], refs[4], refs[5:]
        for d in range(4):
            take = pl.ds(pl.multiple_of((at_ref[SECOND_AT] + d) % 4 * slim, 16), slim)
            outs[d][:slim, :] = total_of([r[take, :] for r in ins]).astype(BF)
            outs[d][slim:, :] = rider_ref[...]

    return pl.pallas_call(
        kernel,
        out_shape=[jax.ShapeDtypeStruct((slim + TAIL, columns), BF)] * 4,
        in_specs=[SMEM] + [VMEM] * 5,
        out_specs=[VMEM] * 4,
        compiler_params=params(10),
        name="split_rows",
    )(at, *got, rider)


def join_rows(at, got, rider):
    slim, columns = got[0].shape

    def kernel(at_ref, *refs):
        ins, rider_ref, out, held = refs[:4], refs[4], refs[5], refs[6]
        for d in range(4):
            put = pl.ds(pl.multiple_of((at_ref[SECOND_AT] + 4 - d) % 4 * slim, 16), slim)
            held[put, :] = ins[d][...]
        out[:columns, :] = held[...].T
        last = rider_ref[...].astype(F32)[:8]
        out[columns:, :] = jnp.concatenate([last[:, : 4 * slim], last[:, 4 * slim :]], axis=0).astype(BF)

    return pl.pallas_call(
        kernel,
        out_shape=jax.ShapeDtypeStruct((columns + TAIL, 4 * slim), BF),
        in_specs=[SMEM] + [VMEM] * 5,
        out_specs=VMEM,
        scratch_shapes=[pltpu.VMEM((4 * slim, columns), BF)],
        compiler_params=params(10),
        name="join_rows",
    )(at, *got, rider)


def lay_out(scalars, step, own, other, whole=None):
    half, quarter = own.shape[0] - TAIL, own.shape[1]

    def kernel(s_ref, own_ref, other_ref, *refs):
        out = refs[-1]
        for n, ref in enumerate((own_ref, other_ref)):

            @pl.when(pl.program_id(0) == n)
            def _():
                out[...] = ref[:half, :]

    def place(n, s_ref):
        side = jnp.where(n == 0, s_ref[CORE], 1 - s_ref[CORE])
        at = jnp.where(n == 0, s_ref[FIRST_AT], s_ref[THEIR_FIRST])
        return side, (at + 4 - step) % 4

    block = pl.BlockSpec((half + TAIL, quarter), lambda n, s_ref: (0, 0))
    extra = [] if whole is None else [whole]
    return pl.pallas_call(
        kernel,
        out_shape=jax.ShapeDtypeStruct((2 * half, 4 * quarter), BF),
        grid_spec=pltpu.PrefetchScalarGridSpec(
            num_scalar_prefetch=1,
            grid=(2,),
            in_specs=[block] * 2 + [ANY] * len(extra),
            out_specs=pl.BlockSpec((half, quarter), place),
        ),
        input_output_aliases={} if whole is None else {3: 0},
        compiler_params=params(12),
        name="lay_out",
    )(scalars, own, other, *extra)


def local(
    trunk,
    skip,
    valid_bins,
    query_weight,
    key_weight,
    value_weight,
    out_weight,
    depth_weight,
    point_weight,
    cotangent,
):
    tokens, skipped, upstream = trunk[0], skip[0], cotangent[0]
    rows, columns = tokens.shape
    fine = skipped.shape[0]
    ix, ic, iz, iy = (lax.axis_index(a) for a in AXES)
    index = {"x": ix, "z": iz, "y": iy}
    place = iz * 4 + iy

    def at(axes, swap=False):
        a, b = axes[::-1] if swap else axes
        return jnp.where(ic == 0, index[a], index[b])

    def ints(*values):
        return jnp.stack([jnp.asarray(v, jnp.int32) for v in values])

    head_at, row_at = at(HEAD_RING), at(ROW_RING)
    values = [ic, head_at, place > 0, place < 15, at(SUM_RINGS[0]), at(SUM_RINGS[0], True), at(SUM_RINGS[1]), 0, ic]
    start_at = [jnp.where(ic == 0, (iy - d) % 4, iy) for d in range(4)]
    values += [v == 0 for v in start_at] + [v == 3 for v in start_at]
    for far_by in (0, 1, 3, 2):
        for d in range(4):
            h, r = (head_at - d) % 4, (row_at - far_by) % 4
            values.append(jnp.where(ic == 0, r * 4 + h, h * 4 + r) * rows)
    scalars = ints(*values, valid_bins[0])

    blocks = project(scalars, tokens, query_weight, key_weight, value_weight)
    q = exchange(blocks, HEAD_RING)
    own = stack_rows(q)
    far = {d: lax.ppermute(own, AXES, turn(ROW_RING, d)) for d in (1, 3, 2)}
    state, mark = attend(scalars, 0, q, [own], None)

    down, up = edges(mark, tokens, skipped, upstream)
    before = lax.ppermute(down, ("z", "y"), [(i, i + 1) for i in range(15)])
    after = lax.ppermute(up, ("z", "y"), [(i + 1, i) for i in range(15)])
    turned = upstream.T

    state, _ = attend(scalars, 1, q, [far[1]], state)
    state, _ = attend(scalars, 2, q, [far[3]], state)
    mixed = attend(scalars, 3, q, [own, far[1], far[3], far[2]], state)
    back = exchange(mixed, HEAD_RING, -1)
    swap = [(0, 1), (1, 0)]
    given = (back, tokens, skipped, out_weight.reshape(H, DV, -1), before, after, depth_weight, turned)
    up_theirs, sent = forward(scalars, False, *given)
    arrived = lax.ppermute(sent, "c", swap)
    up_ours, act = forward(scalars, True, *given)
    piece_2, piece_1 = product(scalars, act, turned, (2, 1), arrived)
    piece_3, piece_0 = product(scalars, act, turned, (3, 0), arrived)
    got = exchange([piece_0, piece_1, piece_2, piece_3], SUM_RINGS[0])

    given = (upstream, before, after, point_weight, depth_weight, piece_0)
    grad_skip, d_theirs = backward(scalars, False, up_theirs, *given)
    d_arrived = lax.ppermute(d_theirs, "c", swap)
    grad_skip, d_mine = backward(scalars, True, up_ours, *given, grad_skip)
    d_sum = d_mine + d_arrived
    half = columns // 2
    rider = jnp.pad(d_sum.astype(BF), ((0, TAIL - 3), (0, 0)))

    slim = columns // 16
    got = exchange(split_rows(scalars, got, rider), SUM_RINGS[1])
    got = exchange([total_of(got).astype(BF)] * 4, SUM_RINGS[2])
    norm_scale = 1.0 / math.sqrt(128 * fine)
    summed = (total_of(got) * norm_scale).astype(BF)
    piece, rider = summed[:slim], summed[slim:]
    joined = join_rows(scalars, exchange([piece] * 4, SUM_RINGS[1]), rider)
    got = exchange([joined] * 4, SUM_RINGS[0])
    other = [lax.ppermute(g, "c", swap) for g in got]
    grad_pointwise = None
    for d in (0, 1, 3, 2):
        grad_pointwise = lay_out(scalars, d, got[d], other[d], grad_pointwise)

    def depth_of(blocks):
        rows = total_of([b[half:] for b in blocks])
        return jnp.concatenate([rows[:3], rows[8:11]], axis=1)

    d_own, d_other = depth_of(got), depth_of(other)
    grad_depth = jnp.concatenate(
        [jnp.where(ic == 0, d_own, d_other), jnp.where(ic == 0, d_other, d_own)], axis=1
    )
    return (grad_pointwise, grad_depth, grad_skip[None])


def solution(mesh):
    fine_mesh = Mesh(mesh.devices.reshape(SIZES), AXES)
    rows = P(("x", "c"), ("z", "y"), None)
    return jax.shard_map(
        local,
        mesh=fine_mesh,
        in_specs=(rows, rows, P(("x", "c")), P(), P(), P(), P(), P(), P(), rows),
        out_specs=(P(), P(), rows),
        check_vma=False,
    )
```

time: 311 us -> 161 us (0.52); the launches traced: 306 us -> 161 us
  Pallas kernels: 187 us -> 59.1 us
  local copies, waits for them, and re-layouts: 16.5 us -> 4.32 us
  matrix products: 8.3 us -> 0 us
    pallas_call x1 -> x4, Pallas kernels: 145 us -> 6.62 us  [lay_out(): pl.pallas_call(kernel, out_shape=jax.ShapeDtypeStruct((2 * half, 4 * quar...]
    unnamed x50 -> x16, local copies, waits for them, and re-layouts: 14.1 us -> 3.46 us
    dot_general x2 -> x0, matrix products: 8.3 us -> none  [the longest x1 4.53 us: local(): lax.dot_general(upstream_l, point_weight, dims, preferred_element_type=F32)]
    pallas_call x11 -> x12, Pallas kernels: 39.6 us -> 47.1 us  [the longest x2 15.4 us: backward(): pl.pallas_call(kernel, out_shape=[jax.ShapeDtypeStruct((fine, columns), B...]
    ppermute x21, starting transfers between devices: 26.1 us -> 33.4 us  [exchange(): got[d] = lax.ppermute(pieces[d], AXES, turn(axes, sign * d))]
    ppermute x1, waiting for transfers between devices: 0.01 us -> 6.84 us  [local(): after = lax.ppermute(up, ('z', 'y'), [(i + 1, i) for i in range(15)])]
    ppermute x21, waiting for transfers between devices: 28.4 us -> 22.2 us  [exchange(): got[d] = lax.ppermute(pieces[d], AXES, turn(axes, sign * d))]
    ppermute x3, waiting for transfers between devices: 0.9 us -> 5.18 us  [local(): far = {d: lax.ppermute(own, AXES, turn(ROW_RING, d)) for d in (1, 3, 2)}]
  transfers between devices with their start and end apart: 33 -> 32, of which waited for: 18 -> 15; matrix products, arithmetic and copies ran while one was open for 4% -> 0% of each run, Pallas kernels for 10% -> 21%
where the time goes in v4:
time: 161 us
  starting transfers between devices  59.3 us (37%)
  Pallas kernels  59.1 us (37%)
  waiting for transfers between devices  35.4 us (22%)
  local copies, waits for them, and re-layouts  4.32 us (3%)
  between operations  1.83 us (1%)
    ppermute x21, starting transfers between devices, exchange(): got[d] = lax.ppermute(pieces[d], AXES, turn(axes, sign * d))  33.4 us
    ppermute x21, waiting for transfers between devices, exchange(): got[d] = lax.ppermute(pieces[d], AXES, turn(axes, sign * d))  22.2 us
    ppermute x4, starting transfers between devices, local(): other = [lax.ppermute(g, 'c', swap) for g in got]  15.6 us
    pallas_call x2, Pallas kernels, backward(): pl.pallas_call(kernel, out_shape=[jax.ShapeDtypeStruct((fine, columns), B...  15.4 us
    pallas_call x2, Pallas kernels, forward(): pl.pallas_call(kernel, out_shape=outs, grid_spec=pltpu.PrefetchScalarGrid...  14.8 us
    pallas_call x4, Pallas kernels, attend(): pl.pallas_call(kernel, out_shape=outs, in_specs=[SMEM] + [VMEM] * len(ins...  12.4 us
    ppermute x1, waiting for transfers between devices, local(): after = lax.ppermute(up, ('z', 'y'), [(i + 1, i) for i in range(15)])  6.84 us
    pallas_call x4, Pallas kernels, lay_out(): pl.pallas_call(kernel, out_shape=jax.ShapeDtypeStruct((2 * half, 4 * quar...  6.62 us
  transfers between devices with their start and end apart: 32, of which 15 were waited for; matrix products, arithmetic and copies ran while one was open for 0% of the time, Pallas kernels for 21%

profile of v4, /device:TPU:1, one launch (start us, length us, event | category | flops | bytes accessed | tf_op | source)
XLA Modules:
  0.0 160.8 jit_solution(18276807406632165320)
XLA Ops:
  1.7 4.5 %project.1 = (bf16[256,384]{1,0:T(8,128)(2,1)S(1)}, bf16[256,384]{1,0:T(8,128)(2,1)S(1)}, bf16[256,384]{1,0:T(8,128)(2,1)S(1)}, bf16[256,384]{1,0:T(8,128)(2,1)S(1)}) custom-call(s32[34]{0:T(128)S(1)} %stack.165.at_ref.s_ref, bf16[256,1536]{1,0:T(8,128)(2,1)} %bitcast.41, bf16[1536,256]{1,0:T(8,128)(2,1)} %wq_hbm.1, bf16[1536,256]{1,0:T(8,128)(2,1)} %wk_hbm.1, ...), custom_call_target="tpu_custom_call" | custom-call | tf_op jit(solution)/shard_map/project/pallas_call | solution.py:97
  6.2 2.5 %collective-permute-start = (bf16[256,384]{1,0:T(8,128)(2,1)S(1)}, bf16[256,384]{1,0:T(8,128)(2,1)S(1)}, u32[]{:S(2)}, u32[]{:S(2)}) collective-permute-start(bf16[256,384]{1,0:T(8,128)(2,1)S(1)} %get-tuple-element.34), channel_id=1, source_target_pairs={{0,1},{1,2},{2,3},{3,0},{4,5},{5,6},{6,7},{7,4},{8,9},{9,10},{10,1... | collective-permute-start | bytes 589832 | tf_op jit(solution)/shard_map/ppermute | solution.py:48
  8.7 3.3 %collective-permute-start.1 = (bf16[256,384]{1,0:T(8,128)(2,1)S(1)}, bf16[256,384]{1,0:T(8,128)(2,1)S(1)}, u32[]{:S(2)}, u32[]{:S(2)}) collective-permute-start(bf16[256,384]{1,0:T(8,128)(2,1)S(1)} %get-tuple-element.35), channel_id=1, source_target_pairs={{0,2},{1,3},{2,0},{3,1},{4,6},{5,7},{6,4},{7,5},{8,10},{9,11},{10,... | collective-permute-start | bytes 589832 | tf_op jit(solution)/shard_map/ppermute | solution.py:48
  14.1 3.3 %collective-permute-done.1.refs_2_ = bf16[256,384]{1,0:T(8,128)(2,1)S(1)} collective-permute-done((bf16[256,384]{1,0:T(8,128)(2,1)S(1)}, bf16[256,384]{1,0:T(8,128)(2,1)S(1)}, u32[]{:S(2)}, u32[]{:S(2)}) %collective-permute-start.1) | collective-permute-done | bytes 196640 | tf_op jit(solution)/shard_map/ppermute | solution.py:48
  18.6 1.7 %collective-permute-start.4 = (bf16[1040,256]{1,0:T(8,128)(2,1)S(1)}, bf16[1040,256]{1,0:T(8,128)(2,1)S(1)}, u32[]{:S(2)}, u32[]{:S(2)}) collective-permute-start(bf16[1040,256]{1,0:T(8,128)(2,1)S(1)} %stack_rows.1.refs_4_), channel_id=1, source_target_pairs={{0,12},{1,13},{2,14},{3,15},{4,0},{5,1},{6,2},{7,3},{8,4},{9,5},{1... | collective-permute-start | bytes 1597448 | tf_op jit(solution)/shard_map/ppermute | solution.py:667
  21.7 2.4 %attend.4 = (f32[1024,256]{1,0:T(8,128)S(1)}, f32[8,128]{1,0:T(8,128)S(1)}) custom-call(s32[34]{0:T(128)S(1)} %stack.165.at_ref.s_ref, bf16[256,384]{1,0:T(8,128)(2,1)S(1)} %get-tuple-element.33.refs_0_, bf16[256,384]{1,0:T(8,128)(2,1)S(1)} %collective-permute-done.refs_1_, bf16[256,384]{1,0:T(8,128)(2,1)S(1)} %collective-permute-done.1.refs_2_, ...), custom_call_target="tpu_custom_call" | custom-call | flops 1073741824 | bytes 4194304 | tf_op jit(solution)/shard_map/attend/pallas_call | solution.py:228
  24.0 3.2 %collective-permute-done.3.refs_4_.refs_5_ = bf16[1040,256]{1,0:T(8,128)(2,1)S(1)} collective-permute-done((bf16[1040,256]{1,0:T(8,128)(2,1)S(1)}, bf16[1040,256]{1,0:T(8,128)(2,1)S(1)}, u32[]{:S(2)}, u32[]{:S(2)}) %collective-permute-start.3) | collective-permute-done | bytes 532512 | tf_op jit(solution)/shard_map/ppermute | solution.py:667
  27.2 3.0 %attend.5 = (f32[1024,256]{1,0:T(8,128)S(1)}, f32[8,128]{1,0:T(8,128)}) custom-call(s32[34]{0:T(128)S(1)} %stack.165.at_ref.s_ref, bf16[256,384]{1,0:T(8,128)(2,1)S(1)} %get-tuple-element.33.refs_0_, bf16[256,384]{1,0:T(8,128)(2,1)S(1)} %collective-permute-done.refs_1_, bf16[256,384]{1,0:T(8,128)(2,1)S(1)} %collective-permute-done.1.refs_2_, ...), custom_call_target="tpu_custom_call" | custom-call | flops 1073741824 | bytes 4194304 | tf_op jit(solution)/shard_map/attend/pallas_call | solution.py:228
  30.2 2.0 %collective-permute-done.4.refs_4_.refs_6_ = bf16[1040,256]{1,0:T(8,128)(2,1)S(1)} collective-permute-done((bf16[1040,256]{1,0:T(8,128)(2,1)S(1)}, bf16[1040,256]{1,0:T(8,128)(2,1)S(1)}, u32[]{:S(2)}, u32[]{:S(2)}) %collective-permute-start.4) | collective-permute-done | bytes 532512 | tf_op jit(solution)/shard_map/ppermute | solution.py:667
  32.2 3.0 %attend.6 = (f32[1024,256]{1,0:T(8,128)S(1)}, f32[8,128]{1,0:T(8,128)}) custom-call(s32[34]{0:T(128)S(1)} %stack.165.at_ref.s_ref, bf16[256,384]{1,0:T(8,128)(2,1)S(1)} %get-tuple-element.33.refs_0_, bf16[256,384]{1,0:T(8,128)(2,1)S(1)} %collective-permute-done.refs_1_, bf16[256,384]{1,0:T(8,128)(2,1)S(1)} %collective-permute-done.1.refs_2_, ...), custom_call_target="tpu_custom_call" | custom-call | flops 1073741824 | bytes 4194304 | tf_op jit(solution)/shard_map/attend/pallas_call | solution.py:228
  35.2 4.0 %attend.7 = (bf16[272,256]{1,0:T(8,128)(2,1)S(1)}, bf16[272,256]{1,0:T(8,128)(2,1)}, bf16[272,256]{1,0:T(8,128)(2,1)}, bf16[272,256]{1,0:T(8,128)(2,1)S(1)}) custom-call(s32[34]{0:T(128)S(1)} %stack.165.at_ref.s_ref, bf16[256,384]{1,0:T(8,128)(2,1)S(1)} %get-tuple-element.33.refs_0_, bf16[256,384]{1,0:T(8,128)(2,1)S(1)} %collective-permute-done.refs_1_, ...), custom_call_target="tpu_custom_call" | custom-call | flops 1073741824 | bytes 4194304 | tf_op jit(solution)/shard_map/attend/pallas_call | solution.py:228
  39.2 2.0 %collective-permute-start.6 = (bf16[272,256]{1,0:T(8,128)(2,1)}, bf16[272,256]{1,0:T(8,128)(2,1)S(1)}, u32[]{:S(2)}, u32[]{:S(2)}) collective-permute-start(bf16[272,256]{1,0:T(8,128)(2,1)} %get-tuple-element.41), channel_id=1, source_target_pairs={{0,3},{1,0},{2,1},{3,2},{4,7},{5,4},{6,5},{7,6},{8,11},{9,8},{10,9... | collective-permute-start | bytes 417800 | tf_op jit(solution)/shard_map/ppermute | solution.py:48
  47.0 6.8 %collective-permute-done.10.high_ref = bf16[16,1536]{1,0:T(8,128)(2,1)S(1)} collective-permute-done((bf16[16,1536]{1,0:T(8,128)(2,1)}, bf16[16,1536]{1,0:T(8,128)(2,1)S(1)}, u32[]{:S(2)}, u32[]{:S(2)}) %collective-permute-start.10) | collective-permute-done | bytes 49184 | tf_op jit(solution)/shard_map/ppermute | solution.py:672
  57.3 9.0 %forward.3 = (bf16[528,768]{1,0:T(8,128)(2,1)S(1)}, bf16[4,384,768]{2,1,0:T(8,128)(2,1)}) custom-call(s32[34]{0:T(128)S(1)} %stack.165.at_ref.s_ref, bf16[272,256]{1,0:T(8,128)(2,1)S(1)} %copy-done.7, bf16[272,256]{1,0:T(8,128)(2,1)S(1)} %collective-permute-done.6.b1, bf16[272,256]{1,0:T(8,128)(2,1)} %collective-permute-done.7.b2, ...), custom_call_target="tpu_custom_call" | custom-call | flops 2415919104 | bytes 9437184 | tf_op jit(solution)/shard_map/forward/pallas_call | solution.py:421
  66.2 3.3 %collective-permute-start.11 = (bf16[4,384,768]{2,1,0:T(8,128)(2,1)}, bf16[4,384,768]{2,1,0:T(8,128)(2,1)S(1)}, u32[]{:S(2)}, u32[]{:S(2)}) collective-permute-start(bf16[4,384,768]{2,1,0:T(8,128)(2,1)} %get-tuple-element.48), channel_id=1, source_target_pairs={{0,16},{16,0},{1,17},{17,1},{2,18},{18,2},{3,19},{19,3},{4,20},{20... | collective-permute-start | bytes 7077896 | tf_op jit(solution)/shard_map/ppermute | solution.py:682
  69.6 5.8 %forward.2 = (bf16[528,768]{1,0:T(8,128)(2,1)S(1)}, bf16[512,768]{1,0:T(8,128)(2,1)S(1)}) custom-call(s32[34]{0:T(128)S(1)} %stack.165.at_ref.s_ref, bf16[272,256]{1,0:T(8,128)(2,1)S(1)} %copy-done.7, bf16[272,256]{1,0:T(8,128)(2,1)S(1)} %collective-permute-done.6.b1, bf16[272,256]{1,0:T(8,128)(2,1)} %collective-permute-done.7.b2, ...), custom_call_target="tpu_custom_call" | custom-call | flops 2415919104 | bytes 9437184 | tf_op jit(solution)/shard_map/forward/pallas_call | solution.py:421
  76.9 6.6 %collective-permute-start.13 = (bf16[384,768]{1,0:T(8,128)(2,1)S(1)}, bf16[384,768]{1,0:T(8,128)(2,1)S(1)}, u32[]{:S(2)}, u32[]{:S(2)}) collective-permute-start(bf16[384,768]{1,0:T(8,128)(2,1)S(1)} %get-tuple-element.51), channel_id=1, source_target_pairs={{0,64},{1,65},{2,66},{3,67},{4,68},{5,69},{6,70},{7,71},{8,72},{9,... | collective-permute-start | bytes 1769480 | tf_op jit(solution)/shard_map/ppermute | solution.py:48
  84.9 7.7 %backward.2 = (bf16[512,1536]{1,0:T(8,128)(2,1)}, f32[3,768]{1,0:T(4,128)S(1)}) custom-call(s32[34]{0:T(128)S(1)} %stack.165.at_ref.s_ref, bf16[528,768]{1,0:T(8,128)(2,1)S(1)} %get-tuple-element.54.up_ref, bf16[512,1536]{1,0:T(8,128)(2,1)S(1)} %bitcast.39, bf16[16,1536]{1,0:T(8,128)(2,1)S(1)} %collective-permute-done.9.low_ref, ...), custom_call_target="tpu_custom_call" | custom-call | flops 1207959552 | bytes 6291456 | tf_op jit(solution)/shard_map/backward/pallas_call | solution.py:498
  92.6 7.7 %backward.3 = (bf16[512,1536]{1,0:T(8,128)(2,1)}, f32[3,768]{1,0:T(4,128)S(1)}) custom-call(s32[34]{0:T(128)S(1)} %stack.165.at_ref.s_ref, bf16[528,768]{1,0:T(8,128)(2,1)S(1)} %get-tuple-element.53.up_ref, bf16[512,1536]{1,0:T(8,128)(2,1)S(1)} %bitcast.40, bf16[16,1536]{1,0:T(8,128)(2,1)S(1)} %collective-permute-done.9.low_ref, ...), custom_call_target="tpu_custom_call", output_to_operand_aliasing={{0}: (8, {})} | custom-call | flops 1207959552 | bytes 6291456 | tf_op jit(solution)/shard_map/backward/pallas_call | solution.py:498
  101.2 4.2 %collective-permute-start.16 = (bf16[112,768]{1,0:T(8,128)(2,1)S(1)}, bf16[112,768]{1,0:T(8,128)(2,1)S(1)}, u32[]{:S(2)}, u32[]{:S(2)}) collective-permute-start(bf16[112,768]{1,0:T(8,128)(2,1)S(1)} %get-tuple-element.59), channel_id=1, source_target_pairs={{0,2},{1,3},{2,0},{3,1},{4,6},{5,7},{6,4},{7,5},{8,10},{9,11},{10,... | collective-permute-start | bytes 516104 | tf_op jit(solution)/shard_map/ppermute | solution.py:48
  105.4 2.7 %collective-permute-start.18 = (bf16[112,768]{1,0:T(8,128)(2,1)S(1)}, bf16[112,768]{1,0:T(8,128)(2,1)S(1)}, u32[]{:S(2)}, u32[]{:S(2)}) collective-permute-start(bf16[112,768]{1,0:T(8,128)(2,1)S(1)} %get-tuple-element.61), channel_id=1, source_target_pairs={{0,3},{1,0},{2,1},{3,2},{4,7},{5,4},{6,5},{7,6},{8,11},{9,8},{10,9... | collective-permute-start | bytes 516104 | tf_op jit(solution)/shard_map/ppermute | solution.py:48
  108.3 2.5 %collective-permute-done.17 = bf16[112,768]{1,0:T(8,128)(2,1)S(1)} collective-permute-done((bf16[112,768]{1,0:T(8,128)(2,1)S(1)}, bf16[112,768]{1,0:T(8,128)(2,1)S(1)}, u32[]{:S(2)}, u32[]{:S(2)}) %collective-permute-start.17) | collective-permute-done | bytes 172064 | tf_op jit(solution)/shard_map/ppermute | solution.py:48
  115.3 4.2 %collective-permute-done.20 = bf16[112,768]{1,0:T(8,128)(2,1)S(1)} collective-permute-done((bf16[112,768]{1,0:T(8,128)(2,1)S(1)}, bf16[112,768]{1,0:T(8,128)(2,1)S(1)}, u32[]{:S(2)}, u32[]{:S(2)}) %collective-permute-start.20) | collective-permute-done | bytes 172064 | tf_op jit(solution)/shard_map/ppermute | solution.py:48
  119.6 2.7 %collective-permute-start.24 = (bf16[96,768]{1,0:T(8,128)(2,1)S(1)}, bf16[96,768]{1,0:T(8,128)(2,1)S(1)}, u32[]{:S(2)}, u32[]{:S(2)}) collective-permute-start(bf16[96,768]{1,0:T(8,128)(2,1)S(1)} %slice.56.refs_0_), channel_id=1, source_target_pairs={{0,3},{1,0},{2,1},{3,2},{4,7},{5,4},{6,5},{7,6},{8,11},{9,8},{10,9... | collective-permute-start | bytes 442376 | tf_op jit(solution)/shard_map/ppermute | solution.py:48
  123.5 2.5 %collective-permute-done.24.refs_3_ = bf16[96,768]{1,0:T(8,128)(2,1)S(1)} collective-permute-done((bf16[96,768]{1,0:T(8,128)(2,1)S(1)}, bf16[96,768]{1,0:T(8,128)(2,1)S(1)}, u32[]{:S(2)}, u32[]{:S(2)}) %collective-permute-start.24) | collective-permute-done | bytes 147488 | tf_op jit(solution)/shard_map/ppermute | solution.py:48
  126.0 1.9 %collective-permute-done.23.refs_2_ = bf16[96,768]{1,0:T(8,128)(2,1)S(1)} collective-permute-done((bf16[96,768]{1,0:T(8,128)(2,1)S(1)}, bf16[96,768]{1,0:T(8,128)(2,1)S(1)}, u32[]{:S(2)}, u32[]{:S(2)}) %collective-permute-start.23) | collective-permute-done | bytes 147488 | tf_op jit(solution)/shard_map/ppermute | solution.py:48
  131.3 1.7 %collective-permute-start.27 = (bf16[784,384]{1,0:T(8,128)(2,1)S(1)}, bf16[784,384]{1,0:T(8,128)(2,1)S(1)}, u32[]{:S(2)}, u32[]{:S(2)}) collective-permute-start(bf16[784,384]{1,0:T(8,128)(2,1)S(1)} %join_rows.1.own_ref), channel_id=1, source_target_pairs={{0,96},{1,97},{2,98},{3,99},{4,100},{5,101},{6,102},{7,103},{8,104... | collective-permute-start | bytes 1806344 | tf_op jit(solution)/shard_map/ppermute | solution.py:48
  133.6 3.9 %collective-permute-start.31 = (bf16[784,384]{1,0:T(8,128)(2,1)S(1)}, bf16[784,384]{1,0:T(8,128)(2,1)S(1)}, u32[]{:S(2)}, u32[]{:S(2)}) collective-permute-start(bf16[784,384]{1,0:T(8,128)(2,1)S(1)} %join_rows.1.own_ref), channel_id=1, source_target_pairs={{0,16},{16,0},{1,17},{17,1},{2,18},{18,2},{3,19},{19,3},{4,20},{20... | collective-permute-start | bytes 1806344 | tf_op jit(solution)/shard_map/ppermute | solution.py:704
  137.4 3.2 %collective-permute-done.29.own_ref = bf16[784,384]{1,0:T(8,128)(2,1)S(1)} collective-permute-done((bf16[784,384]{1,0:T(8,128)(2,1)S(1)}, bf16[784,384]{1,0:T(8,128)(2,1)S(1)}, u32[]{:S(2)}, u32[]{:S(2)}) %collective-permute-start.29) | collective-permute-done | bytes 602144 | tf_op jit(solution)/shard_map/ppermute | solution.py:48
  140.6 11.2 %collective-permute-start.30 = (bf16[784,384]{1,0:T(8,128)(2,1)S(1)}, bf16[784,384]{1,0:T(8,128)(2,1)S(1)}, u32[]{:S(2)}, u32[]{:S(2)}) collective-permute-start(bf16[784,384]{1,0:T(8,128)(2,1)S(1)} %collective-permute-done.29.own_ref), channel_id=1, source_target_pairs={{0,16},{16,0},{1,17},{17,1},{2,18},{18,2},{3,19},{19,3},{4,20},{20... | collective-permute-start | bytes 1806344 | tf_op jit(solution)/shard_map/ppermute | solution.py:704
  152.4 1.7 %lay_out.4.refs_0_ = bf16[1536,1536]{1,0:T(8,128)(2,1)} custom-call(s32[34]{0:T(128)S(1)} %stack.165.at_ref.s_ref, bf16[784,384]{1,0:T(8,128)(2,1)S(1)} %join_rows.1.own_ref, bf16[784,384]{1,0:T(8,128)(2,1)S(1)} %collective-permute-done.31.other_ref), custom_call_target="tpu_custom_call" | custom-call | tf_op jit(solution)/shard_map/lay_out/pallas_call | solution.py:613
  155.9 1.7 %lay_out.5.refs_0_ = bf16[1536,1536]{1,0:T(8,128)(2,1)} custom-call(s32[34]{0:T(128)S(1)} %stack.165.at_ref.s_ref, bf16[784,384]{1,0:T(8,128)(2,1)S(1)} %collective-permute-done.29.own_ref, bf16[784,384]{1,0:T(8,128)(2,1)S(1)} %collective-permute-done.30.other_ref, bf16[1536,1536]{1,0:T(8,128)(2,1)} %lay_out.4.refs_0_), custom_call_target="tpu_custom_call", output_to_operand_aliasing={{}: (3, {})} | custom-call | tf_op jit(solution)/shard_map/lay_out/pallas_call | solution.py:613
  (81 shorter events, 33.3 us)
Async XLA Ops:
  6.2 8.0 %collective-permute-start = (bf16[256,384]{1,0:T(8,128)(2,1)S(1)}, bf16[256,384]{1,0:T(8,128)(2,1)S(1)}, u32[]{:S(2)}, u32[]{:S(2)}) collective-permute-start(bf16[256,384]{1,0:T(8,128)(2,1)S(1)} %get-tuple-element.34), channel_id=1, source_target_pairs={{0,1},{1,2},{2,3},{3,0},{4,5},{5,6},{6,7},{7,4},{8,9},{9,10},{10,1... | collective-permute-start | bytes 589832 | tf_op jit(solution)/shard_map/ppermute | solution.py:48
  8.7 8.8 %collective-permute-start.1 = (bf16[256,384]{1,0:T(8,128)(2,1)S(1)}, bf16[256,384]{1,0:T(8,128)(2,1)S(1)}, u32[]{:S(2)}, u32[]{:S(2)}) collective-permute-start(bf16[256,384]{1,0:T(8,128)(2,1)S(1)} %get-tuple-element.35), channel_id=1, source_target_pairs={{0,2},{1,3},{2,0},{3,1},{4,6},{5,7},{6,4},{7,5},{8,10},{9,11},{10,... | collective-permute-start | bytes 589832 | tf_op jit(solution)/shard_map/ppermute | solution.py:48
  12.0 5.5 %collective-permute-start.2 = (bf16[256,384]{1,0:T(8,128)(2,1)S(1)}, bf16[256,384]{1,0:T(8,128)(2,1)S(1)}, u32[]{:S(2)}, u32[]{:S(2)}) collective-permute-start(bf16[256,384]{1,0:T(8,128)(2,1)S(1)} %get-tuple-element.36), channel_id=1, source_target_pairs={{0,3},{1,0},{2,1},{3,2},{4,7},{5,4},{6,5},{7,6},{8,11},{9,8},{10,9... | collective-permute-start | bytes 589832 | tf_op jit(solution)/shard_map/ppermute | solution.py:48
  17.5 9.7 %collective-permute-start.3 = (bf16[1040,256]{1,0:T(8,128)(2,1)S(1)}, bf16[1040,256]{1,0:T(8,128)(2,1)S(1)}, u32[]{:S(2)}, u32[]{:S(2)}) collective-permute-start(bf16[1040,256]{1,0:T(8,128)(2,1)S(1)} %stack_rows.1.refs_4_), channel_id=1, source_target_pairs={{0,4},{1,5},{2,6},{3,7},{4,8},{5,9},{6,10},{7,11},{8,12},{9,13},{1... | collective-permute-start | bytes 1597448 | tf_op jit(solution)/shard_map/ppermute | solution.py:667
  18.6 13.6 %collective-permute-start.4 = (bf16[1040,256]{1,0:T(8,128)(2,1)S(1)}, bf16[1040,256]{1,0:T(8,128)(2,1)S(1)}, u32[]{:S(2)}, u32[]{:S(2)}) collective-permute-start(bf16[1040,256]{1,0:T(8,128)(2,1)S(1)} %stack_rows.1.refs_4_), channel_id=1, source_target_pairs={{0,12},{1,13},{2,14},{3,15},{4,0},{5,1},{6,2},{7,3},{8,4},{9,5},{1... | collective-permute-start | bytes 1597448 | tf_op jit(solution)/shard_map/ppermute | solution.py:667
  20.2 14.9 %collective-permute-start.5 = (bf16[1040,256]{1,0:T(8,128)(2,1)S(1)}, bf16[1040,256]{1,0:T(8,128)(2,1)S(1)}, u32[]{:S(2)}, u32[]{:S(2)}) collective-permute-start(bf16[1040,256]{1,0:T(8,128)(2,1)S(1)} %stack_rows.1.refs_4_), channel_id=1, source_target_pairs={{0,8},{1,9},{2,10},{3,11},{4,12},{5,13},{6,14},{7,15},{8,0},{9,1},... | collective-permute-start | bytes 1597448 | tf_op jit(solution)/shard_map/ppermute | solution.py:667
  39.2 14.6 %collective-permute-start.6 = (bf16[272,256]{1,0:T(8,128)(2,1)}, bf16[272,256]{1,0:T(8,128)(2,1)S(1)}, u32[]{:S(2)}, u32[]{:S(2)}) collective-permute-start(bf16[272,256]{1,0:T(8,128)(2,1)} %get-tuple-element.41), channel_id=1, source_target_pairs={{0,3},{1,0},{2,1},{3,2},{4,7},{5,4},{6,5},{7,6},{8,11},{9,8},{10,9... | collective-permute-start | bytes 417800 | tf_op jit(solution)/shard_map/ppermute | solution.py:48
  41.3 12.5 %collective-permute-start.7 = (bf16[272,256]{1,0:T(8,128)(2,1)}, bf16[272,256]{1,0:T(8,128)(2,1)}, u32[]{:S(2)}, u32[]{:S(2)}) collective-permute-start(bf16[272,256]{1,0:T(8,128)(2,1)} %get-tuple-element.42), channel_id=1, source_target_pairs={{0,2},{1,3},{2,0},{3,1},{4,6},{5,7},{6,4},{7,5},{8,10},{9,11},{10,... | collective-permute-start | bytes 417800 | tf_op jit(solution)/shard_map/ppermute | solution.py:48
  42.1 11.7 %collective-permute-start.8 = (bf16[272,256]{1,0:T(8,128)(2,1)S(1)}, bf16[272,256]{1,0:T(8,128)(2,1)}, u32[]{:S(2)}, u32[]{:S(2)}) collective-permute-start(bf16[272,256]{1,0:T(8,128)(2,1)S(1)} %get-tuple-element.43), channel_id=1, source_target_pairs={{0,1},{1,2},{2,3},{3,0},{4,5},{5,6},{6,7},{7,4},{8,9},{9,10},{10,1... | collective-permute-start | bytes 417800 | tf_op jit(solution)/shard_map/ppermute | solution.py:48
  43.3 3.6 %collective-permute-start.9 = (bf16[16,1536]{1,0:T(8,128)(2,1)}, bf16[16,1536]{1,0:T(8,128)(2,1)S(1)}, u32[]{:S(2)}, u32[]{:S(2)}) collective-permute-start(bf16[16,1536]{1,0:T(8,128)(2,1)} %get-tuple-element.45), channel_id=1, source_target_pairs={{0,1},{1,2},{2,3},{3,4},{4,5},{5,6},{6,7},{7,8},{8,9},{9,10},{10,1... | collective-permute-start | bytes 147464 | tf_op jit(solution)/shard_map/ppermute | solution.py:671
  44.9 8.9 %collective-permute-start.10 = (bf16[16,1536]{1,0:T(8,128)(2,1)}, bf16[16,1536]{1,0:T(8,128)(2,1)S(1)}, u32[]{:S(2)}, u32[]{:S(2)}) collective-permute-start(bf16[16,1536]{1,0:T(8,128)(2,1)} %get-tuple-element.46), channel_id=1, source_target_pairs={{1,0},{2,1},{3,2},{4,3},{5,4},{6,5},{7,6},{8,7},{9,8},{10,9},{11,1... | collective-permute-start | bytes 147464 | tf_op jit(solution)/shard_map/ppermute | solution.py:672
  66.2 9.1 %collective-permute-start.11 = (bf16[4,384,768]{2,1,0:T(8,128)(2,1)}, bf16[4,384,768]{2,1,0:T(8,128)(2,1)S(1)}, u32[]{:S(2)}, u32[]{:S(2)}) collective-permute-start(bf16[4,384,768]{2,1,0:T(8,128)(2,1)} %get-tuple-element.48), channel_id=1, source_target_pairs={{0,16},{16,0},{1,17},{17,1},{2,18},{18,2},{3,19},{19,3},{4,20},{20... | collective-permute-start | bytes 7077896 | tf_op jit(solution)/shard_map/ppermute | solution.py:682
  76.7 23.6 %collective-permute-start.12 = (bf16[384,768]{1,0:T(8,128)(2,1)S(1)}, bf16[384,768]{1,0:T(8,128)(2,1)S(1)}, u32[]{:S(2)}, u32[]{:S(2)}) collective-permute-start(bf16[384,768]{1,0:T(8,128)(2,1)S(1)} %get-tuple-element.50), channel_id=1, source_target_pairs={{0,32},{1,33},{2,34},{3,35},{4,36},{5,37},{6,38},{7,39},{8,40},{9,... | collective-permute-start | bytes 1769480 | tf_op jit(solution)/shard_map/ppermute | solution.py:48
  76.9 23.4 %collective-permute-start.13 = (bf16[384,768]{1,0:T(8,128)(2,1)S(1)}, bf16[384,768]{1,0:T(8,128)(2,1)S(1)}, u32[]{:S(2)}, u32[]{:S(2)}) collective-permute-start(bf16[384,768]{1,0:T(8,128)(2,1)S(1)} %get-tuple-element.51), channel_id=1, source_target_pairs={{0,64},{1,65},{2,66},{3,67},{4,68},{5,69},{6,70},{7,71},{8,72},{9,... | collective-permute-start | bytes 1769480 | tf_op jit(solution)/shard_map/ppermute | solution.py:48
  84.8 15.5 %collective-permute-start.14 = (bf16[384,768]{1,0:T(8,128)(2,1)S(1)}, bf16[384,768]{1,0:T(8,128)(2,1)S(1)}, u32[]{:S(2)}, u32[]{:S(2)}) collective-permute-start(bf16[384,768]{1,0:T(8,128)(2,1)S(1)} %get-tuple-element.52), channel_id=1, source_target_pairs={{0,96},{1,97},{2,98},{3,99},{4,100},{5,101},{6,102},{7,103},{8,104... | collective-permute-start | bytes 1769480 | tf_op jit(solution)/shard_map/ppermute | solution.py:48
  92.6 7.7 %collective-permute-start.15 = (f32[3,768]{1,0:T(4,128)S(1)}, f32[3,768]{1,0:T(4,128)S(1)}, u32[]{:S(2)}, u32[]{:S(2)}) collective-permute-start(f32[3,768]{1,0:T(4,128)S(1)} %get-tuple-element.57), channel_id=1, source_target_pairs={{0,16},{16,0},{1,17},{17,1},{2,18},{18,2},{3,19},{19,3},{4,20},{20... | collective-permute-start | bytes 27656 | tf_op jit(solution)/shard_map/ppermute | solution.py:690
  101.2 7.1 %collective-permute-start.16 = (bf16[112,768]{1,0:T(8,128)(2,1)S(1)}, bf16[112,768]{1,0:T(8,128)(2,1)S(1)}, u32[]{:S(2)}, u32[]{:S(2)}) collective-permute-start(bf16[112,768]{1,0:T(8,128)(2,1)S(1)} %get-tuple-element.59), channel_id=1, source_target_pairs={{0,2},{1,3},{2,0},{3,1},{4,6},{5,7},{6,4},{7,5},{8,10},{9,11},{10,... | collective-permute-start | bytes 516104 | tf_op jit(solution)/shard_map/ppermute | solution.py:48
  105.4 5.5 %collective-permute-start.17 = (bf16[112,768]{1,0:T(8,128)(2,1)S(1)}, bf16[112,768]{1,0:T(8,128)(2,1)S(1)}, u32[]{:S(2)}, u32[]{:S(2)}) collective-permute-start(bf16[112,768]{1,0:T(8,128)(2,1)S(1)} %get-tuple-element.60), channel_id=1, source_target_pairs={{0,1},{1,2},{2,3},{3,0},{4,5},{5,6},{6,7},{7,4},{8,9},{9,10},{10,1... | collective-permute-start | bytes 516104 | tf_op jit(solution)/shard_map/ppermute | solution.py:48
  105.4 5.5 %collective-permute-start.18 = (bf16[112,768]{1,0:T(8,128)(2,1)S(1)}, bf16[112,768]{1,0:T(8,128)(2,1)S(1)}, u32[]{:S(2)}, u32[]{:S(2)}) collective-permute-start(bf16[112,768]{1,0:T(8,128)(2,1)S(1)} %get-tuple-element.61), channel_id=1, source_target_pairs={{0,3},{1,0},{2,1},{3,2},{4,7},{5,4},{6,5},{7,6},{8,11},{9,8},{10,9... | collective-permute-start | bytes 516104 | tf_op jit(solution)/shard_map/ppermute | solution.py:48
  110.9 4.3 %collective-permute-start.21 = (bf16[112,768]{1,0:T(8,128)(2,1)S(1)}, bf16[112,768]{1,0:T(8,128)(2,1)S(1)}, u32[]{:S(2)}, u32[]{:S(2)}) collective-permute-start(bf16[112,768]{1,0:T(8,128)(2,1)S(1)} %add_convert_fusion), channel_id=1, source_target_pairs={{0,12},{1,13},{2,14},{3,15},{4,0},{5,1},{6,2},{7,3},{8,4},{9,5},{1... | collective-permute-start | bytes 516104 | tf_op jit(solution)/shard_map/ppermute | solution.py:48
  112.1 7.3 %collective-permute-start.20 = (bf16[112,768]{1,0:T(8,128)(2,1)S(1)}, bf16[112,768]{1,0:T(8,128)(2,1)S(1)}, u32[]{:S(2)}, u32[]{:S(2)}) collective-permute-start(bf16[112,768]{1,0:T(8,128)(2,1)S(1)} %add_convert_fusion), channel_id=1, source_target_pairs={{0,4},{1,5},{2,6},{3,7},{4,8},{5,9},{6,10},{7,11},{8,12},{9,13},{1... | collective-permute-start | bytes 516104 | tf_op jit(solution)/shard_map/ppermute | solution.py:48
  112.5 7.0 %collective-permute-start.19 = (bf16[112,768]{1,0:T(8,128)(2,1)S(1)}, bf16[112,768]{1,0:T(8,128)(2,1)S(1)}, u32[]{:S(2)}, u32[]{:S(2)}) collective-permute-start(bf16[112,768]{1,0:T(8,128)(2,1)S(1)} %add_convert_fusion), channel_id=1, source_target_pairs={{0,8},{1,9},{2,10},{3,11},{4,12},{5,13},{6,14},{7,15},{8,0},{9,1},... | collective-permute-start | bytes 516104 | tf_op jit(solution)/shard_map/ppermute | solution.py:48
  119.6 6.4 %collective-permute-start.24 = (bf16[96,768]{1,0:T(8,128)(2,1)S(1)}, bf16[96,768]{1,0:T(8,128)(2,1)S(1)}, u32[]{:S(2)}, u32[]{:S(2)}) collective-permute-start(bf16[96,768]{1,0:T(8,128)(2,1)S(1)} %slice.56.refs_0_), channel_id=1, source_target_pairs={{0,3},{1,0},{2,1},{3,2},{4,7},{5,4},{6,5},{7,6},{8,11},{9,8},{10,9... | collective-permute-start | bytes 442376 | tf_op jit(solution)/shard_map/ppermute | solution.py:48
  122.3 5.6 %collective-permute-start.23 = (bf16[96,768]{1,0:T(8,128)(2,1)S(1)}, bf16[96,768]{1,0:T(8,128)(2,1)S(1)}, u32[]{:S(2)}, u32[]{:S(2)}) collective-permute-start(bf16[96,768]{1,0:T(8,128)(2,1)S(1)} %slice.56.refs_0_), channel_id=1, source_target_pairs={{0,2},{1,3},{2,0},{3,1},{4,6},{5,7},{6,4},{7,5},{8,10},{9,11},{10,... | collective-permute-start | bytes 442376 | tf_op jit(solution)/shard_map/ppermute | solution.py:48
  123.5 5.9 %collective-permute-start.22 = (bf16[96,768]{1,0:T(8,128)(2,1)S(1)}, bf16[96,768]{1,0:T(8,128)(2,1)S(1)}, u32[]{:S(2)}, u32[]{:S(2)}) collective-permute-start(bf16[96,768]{1,0:T(8,128)(2,1)S(1)} %slice.56.refs_0_), channel_id=1, source_target_pairs={{0,1},{1,2},{2,3},{3,0},{4,5},{5,6},{6,7},{7,4},{8,9},{9,10},{10,1... | collective-permute-start | bytes 442376 | tf_op jit(solution)/shard_map/ppermute | solution.py:48
  130.2 10.4 %collective-permute-start.29 = (bf16[784,384]{1,0:T(8,128)(2,1)S(1)}, bf16[784,384]{1,0:T(8,128)(2,1)S(1)}, u32[]{:S(2)}, u32[]{:S(2)}) collective-permute-start(bf16[784,384]{1,0:T(8,128)(2,1)S(1)} %join_rows.1.own_ref), channel_id=1, source_target_pairs={{0,32},{1,33},{2,34},{3,35},{4,36},{5,37},{6,38},{7,39},{8,40},{9,... | collective-permute-start | bytes 1806344 | tf_op jit(solution)/shard_map/ppermute | solution.py:48
  131.3 20.6 %collective-permute-start.27 = (bf16[784,384]{1,0:T(8,128)(2,1)S(1)}, bf16[784,384]{1,0:T(8,128)(2,1)S(1)}, u32[]{:S(2)}, u32[]{:S(2)}) collective-permute-start(bf16[784,384]{1,0:T(8,128)(2,1)S(1)} %join_rows.1.own_ref), channel_id=1, source_target_pairs={{0,96},{1,97},{2,98},{3,99},{4,100},{5,101},{6,102},{7,103},{8,104... | collective-permute-start | bytes 1806344 | tf_op jit(solution)/shard_map/ppermute | solution.py:48
  132.9 18.9 %collective-permute-start.25 = (bf16[784,384]{1,0:T(8,128)(2,1)S(1)}, bf16[784,384]{1,0:T(8,128)(2,1)S(1)}, u32[]{:S(2)}, u32[]{:S(2)}) collective-permute-start(bf16[784,384]{1,0:T(8,128)(2,1)S(1)} %join_rows.1.own_ref), channel_id=1, source_target_pairs={{0,64},{1,65},{2,66},{3,67},{4,68},{5,69},{6,70},{7,71},{8,72},{9,... | collective-permute-start | bytes 1806344 | tf_op jit(solution)/shard_map/ppermute | solution.py:48
  133.6 18.8 %collective-permute-start.31 = (bf16[784,384]{1,0:T(8,128)(2,1)S(1)}, bf16[784,384]{1,0:T(8,128)(2,1)S(1)}, u32[]{:S(2)}, u32[]{:S(2)}) collective-permute-start(bf16[784,384]{1,0:T(8,128)(2,1)S(1)} %join_rows.1.own_ref), channel_id=1, source_target_pairs={{0,16},{16,0},{1,17},{17,1},{2,18},{18,2},{3,19},{19,3},{4,20},{20... | collective-permute-start | bytes 1806344 | tf_op jit(solution)/shard_map/ppermute | solution.py:704
  140.6 13.4 %collective-permute-start.30 = (bf16[784,384]{1,0:T(8,128)(2,1)S(1)}, bf16[784,384]{1,0:T(8,128)(2,1)S(1)}, u32[]{:S(2)}, u32[]{:S(2)}) collective-permute-start(bf16[784,384]{1,0:T(8,128)(2,1)S(1)} %collective-permute-done.29.own_ref), channel_id=1, source_target_pairs={{0,16},{16,0},{1,17},{17,1},{2,18},{18,2},{3,19},{19,3},{4,20},{20... | collective-permute-start | bytes 1806344 | tf_op jit(solution)/shard_map/ppermute | solution.py:704
  151.9 2.5 %collective-permute-start.28 = (bf16[784,384]{1,0:T(8,128)(2,1)S(1)}, bf16[784,384]{1,0:T(8,128)(2,1)S(1)}, u32[]{:S(2)}, u32[]{:S(2)}) collective-permute-start(bf16[784,384]{1,0:T(8,128)(2,1)S(1)} %collective-permute-done.27.own_ref), channel_id=1, source_target_pairs={{0,16},{16,0},{1,17},{17,1},{2,18},{18,2},{3,19},{19,3},{4,20},{20... | collective-permute-start | bytes 1806344 | tf_op jit(solution)/shard_map/ppermute | solution.py:704
  151.9 3.4 %collective-permute-start.26 = (bf16[784,384]{1,0:T(8,128)(2,1)S(1)}, bf16[784,384]{1,0:T(8,128)(2,1)S(1)}, u32[]{:S(2)}, u32[]{:S(2)}) collective-permute-start(bf16[784,384]{1,0:T(8,128)(2,1)S(1)} %collective-permute-done.25.own_ref), channel_id=1, source_target_pairs={{0,16},{16,0},{1,17},{17,1},{2,18},{18,2},{3,19},{19,3},{4,20},{20... | collective-permute-start | bytes 1806344 | tf_op jit(solution)/shard_map/ppermute | solution.py:704
  (8 other events, 42.0 us)

commit v5 on v4

--- a/solution.py
+++ b/solution.py
@@ -20,8 +20,27 @@
 ANY = pl.BlockSpec(memory_space=pl.ANY)
 SUM_RINGS = (("x", "y"), ("y", "z"), ("z", "x"))
 HEAD_RING = ("y", "z")
-CORE, HEAD_AT, HAS_LOW, HAS_HIGH, FIRST_AT, THEIR_FIRST, SECOND_AT, FLAGS, BASES, VALID = 0, 1, 2, 3, 4, 5, 6, 8, 17, 33
 ROW_RING = ("z", "y")
+
+
+class Spot:
+    def __init__(self, s_ref):
+        x, core, z, y = (s_ref[n] for n in range(4))
+        first = core == 0
+        self.core, self.y, self.valid = core, y, s_ref[4]
+        self.head_at = jnp.where(first, y, z)
+        self.row_at = jnp.where(first, z, y)
+        self.first_at = jnp.where(first, x, y)
+        self.their_first = jnp.where(first, y, x)
+        self.second_at = jnp.where(first, y, z)
+        self.place = z * 4 + y
+
+    def base(self, far_by, d):
+        h, r = (self.head_at + 4 - d) % 4, (self.row_at + 4 - far_by) % 4
+        return jnp.where(self.core == 0, r * 4 + h, h * 4 + r)
+
+    def ring_place(self, d):
+        return jnp.where(self.core == 0, (self.y + 4 - d) % 4, self.y)
 
 
 def params(mib):
@@ -92,7 +111,7 @@
                 axis=1,
             ).astype(BF)
         for d in range(4):
-            outs[d][...] = held[(at_ref[HEAD_AT] + d) % 4]
+            outs[d][...] = held[(Spot(at_ref).head_at + d) % 4]
 
     return pl.pallas_call(
         kernel,
@@ -138,33 +157,37 @@
     )(*parts)
 
 
-def attend(scalars, near, q, pairs, state):
+def attend(scalars, near, q, pairs, state, behind=()):
     rows = q[0].shape[0]
     width = 4 * rows
     first = state is None
     last = len(pairs) == 4
+    strip = 32
 
     def kernel(s_ref, *refs):
+        spot = Spot(s_ref)
+        score_ref, prob_ref, peak_ref = refs[-3:]
         q_refs, refs = refs[:4], refs[4:]
         pair_refs, refs = refs[: len(pairs)], refs[len(pairs) :]
         if not first:
             old, refs = refs[0], refs[1:]
+        refs = refs[len(behind) :]
         lane = lax.broadcasted_iota(jnp.int32, (width, 256), 1)
         place = lax.broadcasted_iota(jnp.int32, (1, rows), 1)
 
         def masks(n):
+            far_by = (0, 1, 3, 2)[n]
             return jnp.concatenate(
-                [place + s_ref[BASES + 4 * n + i] < s_ref[VALID] for i in range(4)], axis=1
+                [place + spot.base(far_by, i) * rows < spot.valid for i in range(4)], axis=1
             )
 
         def values_of(ref):
             return jnp.where(lane == DV, jnp.ones((), BF), ref[:width, :])
 
-        def scores_of(query, ref, keep):
-            scores = lax.dot_general(
+        def raw_scores(query, ref):
+            return lax.dot_general(
                 query, ref[:width, 128:], (((1,), (1,)), ((), ())), preferred_element_type=F32
             )
-            return jnp.where(keep, scores, -1e30)
 
         def shares(sums):
             return sums / sums[:, DV : DV + 1]
@@ -176,14 +199,15 @@
             edge = jnp.zeros((TAIL, 128), F32)
             for d in range(4):
                 n, m = (d + 1) % 4, (d + 3) % 4
-                other = jnp.where(s_ref[FLAGS] == 0, own[4 + n : 5 + n], low[4 + d : 5 + d])
-                prev = jnp.where(s_ref[FLAGS + 1 + d] == 1, low[4 + n : 5 + n], other)
-                other = jnp.where(s_ref[FLAGS] == 0, own[m : m + 1], high[d : d + 1])
-                nxt = jnp.where(s_ref[FLAGS + 5 + d] == 1, high[m : m + 1], other)
+                at = spot.ring_place(d)
+                other = jnp.where(spot.core == 0, own[4 + n : 5 + n], low[4 + d : 5 + d])
+                prev = jnp.where(at == 0, low[4 + n : 5 + n], other)
+                other = jnp.where(spot.core == 0, own[m : m + 1], high[d : d + 1])
+                nxt = jnp.where(at == 3, high[m : m + 1], other)
                 edge = jnp.where(row == d, prev, edge)
                 edge = jnp.where(row == 4 + d, nxt, edge)
             edge = edge.astype(BF)
-            parts = [scores_of(edge, r, masks(n)) for n, r in enumerate(pair_refs)]
+            parts = [jnp.where(masks(n), raw_scores(edge, r), -1e30) for n, r in enumerate(pair_refs)]
             peak = jnp.max(parts[0], axis=1, keepdims=True)
             for s in parts[1:]:
                 peak = jnp.maximum(peak, jnp.max(s, axis=1, keepdims=True))
@@ -193,30 +217,35 @@
             edge_out = shares(edge_sums)
             row = lax.broadcasted_iota(jnp.int32, (TAIL, 256), 0)
 
-        spot = lax.broadcasted_iota(jnp.int32, (rows, 256), 1)
+        column = lax.broadcasted_iota(jnp.int32, (rows, 256), 1)
         if not last:
             refs[1][...] = jnp.zeros((8, 128), F32)
         pair_ref = pair_refs[-1]
         keep = masks(near)
         values = values_of(pair_ref)
         for i in range(4):
-            scores = scores_of(q_refs[i][:, 256:], pair_ref, keep)
-            peak = jnp.max(scores, axis=1, keepdims=True)
+            score_ref[i] = raw_scores(q_refs[i][:, 256:], pair_ref)
+        for i in range(4):
+            for k in range(0, rows, strip):
+                cut = slice(k, k + strip)
+                scores = jnp.where(keep, score_ref[i, cut, :], -1e30)
+                peak = jnp.max(scores, axis=1, keepdims=True)
+                if not first:
+                    peak = jnp.maximum(peak, old[i * rows + k : i * rows + k + strip, DV + 1 : DV + 2])
+                prob_ref[i, cut, :] = jnp.exp(scores - peak).astype(BF)
+                peak_ref[i, cut, :] = jnp.broadcast_to(peak, (strip, 128))
+            update = jnp.dot(prob_ref[i], values, preferred_element_type=F32)
+            peak = peak_ref[i, :, :1]
             if not first:
                 sums = old[i * rows : (i + 1) * rows, :]
-                before = sums[:, DV + 1 : DV + 2]
-                peak = jnp.maximum(peak, before)
-            probs = jnp.exp(scores - peak).astype(BF)
-            update = jnp.dot(probs, values, preferred_element_type=F32)
-            if not first:
-                update = update + sums * jnp.exp(before - peak)
+                update = update + sums * jnp.exp(sums[:, DV + 1 : DV + 2] - peak)
             if last:
                 refs[i][:rows, :] = shares(update).astype(BF)
                 ends = jnp.where(row == 0, edge_out[i : i + 1], jnp.zeros((TAIL, 256), F32))
                 ends = jnp.where(row == 1, edge_out[4 + i : 5 + i], ends)
                 refs[i][rows:, :] = ends.astype(BF)
             else:
-                refs[0][i * rows : (i + 1) * rows, :] = jnp.where(spot == DV + 1, peak, update)
+                refs[0][i * rows : (i + 1) * rows, :] = jnp.where(column == DV + 1, peak, update)
 
     ins = [*q, *pairs]
     if not first:
@@ -225,25 +254,22 @@
         outs = [jax.ShapeDtypeStruct((rows + TAIL, 256), BF)] * 4
     else:
         outs = [jax.ShapeDtypeStruct((4 * rows, 256), F32), jax.ShapeDtypeStruct((8, 128), F32)]
-    got = pl.pallas_call(
+    return pl.pallas_call(
         kernel,
         out_shape=outs,
-        in_specs=[SMEM] + [VMEM] * len(ins),
+        in_specs=[SMEM] + [VMEM] * len(ins) + [ANY] * len(behind),
         out_specs=[VMEM] * len(outs),
-        compiler_params=params(16),
+        scratch_shapes=[
+            pltpu.VMEM((4, rows, width), F32),
+            pltpu.VMEM((4, rows, width), BF),
+            pltpu.VMEM((4, rows, 128), F32),
+        ],
+        compiler_params=params(24),
         cost_estimate=pl.CostEstimate(
             flops=4 * 2 * rows * width * 512, bytes_accessed=4 << 20, transcendentals=4 * rows * width
         ),
         name="attend",
-    )(scalars, *ins)
-    return got
-
-
-def gelu_parts(pre):
-    slope = math.sqrt(2.0 / math.pi)
-    square = pre * pre
-    bend = jnp.tanh(slope * (pre + 0.044715 * (square * pre)))
-    return bend, square, slope
+    )(scalars, *ins, *behind)
 
 
 def edges(mark, trunk, skip, cotangent):
@@ -280,7 +306,7 @@
         in_specs=[VMEM, ANY, ANY, ANY],
         out_specs=[VMEM] * 2,
         scratch_shapes=[pltpu.VMEM((6, TAIL, columns), BF), pltpu.SemaphoreType.DMA((6,))],
-        compiler_params=params(8),
+        compiler_params=params(53),
         name="edges",
     )(mark, trunk, skip, cotangent)
 
@@ -293,6 +319,7 @@
 
 
 WIDE = 256
+STRIP = 32
 
 
 def forward(scalars, ours, back, tokens, skipped, out_heads, before, after, depth_weight, turned):
@@ -303,7 +330,7 @@
     quarter = columns // 4
 
     def side(s_ref):
-        return s_ref[CORE] if ours else 1 - s_ref[CORE]
+        return s_ref[1] if ours else 1 - s_ref[1]
 
     def kernel(s_ref, b0, b1, b2, b3, low_ref, high_ref, dw_ref, tok_hbm, skip_hbm, ow_hbm, g_hbm, *refs):
         if ours:
@@ -316,7 +343,6 @@
         j = pl.program_id(0)
 
         def copies(n):
-            put = pl.ds(n * WIDE, WIDE)
             take = pl.ds(pl.multiple_of(side(s_ref) * half + n * WIDE, 128), WIDE)
             return [
                 pltpu.make_async_copy(ow_hbm.at[:, :, take], ow.at[n], sems.at[3 * n]),
@@ -339,41 +365,42 @@
             for d in range(4):
                 att[d] = (mixed[d] * scale).astype(BF)
 
-        def chunk(n):
+        @pl.when(j < steps)
+        def _():
+            spot = Spot(s_ref)
+            n = jnp.minimum(j, steps - 1)
             for copy in copies(n):
                 copy.wait()
-            cut = pl.ds(n * WIDE, WIDE)
             low, high = low_ref[...].astype(F32), high_ref[...].astype(F32)
             grown = jnp.zeros((rows + TAIL, WIDE), F32)
             for d in range(4):
-                grown += jnp.dot(att[d], ow[n, (s_ref[HEAD_AT] + d) % 4], preferred_element_type=F32)
+                grown += jnp.dot(att[d], ow[n, (spot.head_at + d) % 4], preferred_element_type=F32)
             hidden = (tok[n].astype(F32) + grown[:rows]).astype(BF)
             low_hid = (low[:1] + grown[rows : rows + 1]).astype(BF).astype(F32)
             high_hid = (high[:1] + grown[rows + 1 : rows + 2]).astype(BF).astype(F32)
             twice = lax.broadcasted_iota(jnp.int32, (fine, rows), 0) // 2
             twice = jnp.where(twice == lax.broadcasted_iota(jnp.int32, (fine, rows), 1), 1.0, 0.0).astype(BF)
-            up = jnp.dot(twice, hidden, preferred_element_type=F32) + skp[n].astype(F32)
-            held[8 : 8 + fine, :] = up.astype(BF).astype(F32)
-            row = lax.broadcasted_iota(jnp.int32, (8, WIDE), 0)
-            edge = (low_hid + jnp.where(row == 6, low[1:2], low[2:3])).astype(BF).astype(F32)
-            held[:8, :] = jnp.where((row >= 6) & (s_ref[HAS_LOW] > 0), edge, 0.0)
+            doubled = jnp.dot(twice, hidden, preferred_element_type=F32)
+            row = lax.broadcasted_iota(jnp.int32, (TAIL, WIDE), 0)
+            edge = (low_hid + jnp.where(row == 14, low[1:2], low[2:3])).astype(BF).astype(F32)
+            edge = jnp.where((row >= 14) & (spot.place > 0), edge, 0.0)
+            held[:TAIL, :] = edge
+            up_ref[:TAIL, :] = edge.astype(BF)
             edge = (high_hid + jnp.where(row == 0, high[1:2], high[2:3])).astype(BF).astype(F32)
-            held[8 + fine :, :] = jnp.where((row < 2) & (s_ref[HAS_HIGH] > 0), edge, 0.0)
-            up_ref[...] = held[...].astype(BF)
-            pre = (
-                dw_ref[0:1, :] * held[7 : 7 + fine, :]
-                + dw_ref[1:2, :] * held[8 : 8 + fine, :]
-                + dw_ref[2:3, :] * held[9 : 9 + fine, :]
-            )
-            bend, _, _ = gelu_parts(pre)
-            value = (pre * (0.5 * (1.0 + bend))).astype(BF)
-            if ours:
-                act_ref[...] = value
-            else:
-                act_ref[:, n * WIDE : (n + 1) * WIDE] = value
-
-        for n in range(steps):
-            pl.when(j == n)(lambda n=n: chunk(n))
+            edge = jnp.where((row < 2) & (spot.place < 15), edge, 0.0)
+            held[TAIL + fine :, :] = edge
+            up_ref[TAIL + fine :, :] = edge.astype(BF)
+            for k in range(0, fine, STRIP):
+                up = (doubled[k : k + STRIP] + skp[n, k : k + STRIP, :].astype(F32)).astype(BF)
+                up_ref[TAIL + k : TAIL + k + STRIP, :] = up
+                held[TAIL + k : TAIL + k + STRIP, :] = up.astype(F32)
+            w = [dw_ref[t : t + 1, :] for t in range(3)]
+            cut = pl.ds(0 if ours else pl.multiple_of(n * WIDE, 128), WIDE)
+            for k in range(0, fine, STRIP):
+                near = held[8 + k : 24 + k + STRIP, :]
+                pre = w[0] * near[7 : 7 + STRIP] + w[1] * near[8 : 8 + STRIP] + w[2] * near[9 : 9 + STRIP]
+                bend, _, _ = gelu_parts(pre)
+                act_ref[k : k + STRIP, cut] = (pre * (0.5 + 0.5 * bend)).astype(BF)
 
         if not ours:
 
@@ -383,7 +410,7 @@
 
             @pl.when(j >= steps)
             def _():
-                at = pl.multiple_of((s_ref[THEIR_FIRST] + j - steps) % 4 * quarter, 16)
+                at = pl.multiple_of((Spot(s_ref).their_first + j - steps) % 4 * quarter, 16)
                 prod_ref[0] = jnp.dot(
                     g_ref[pl.ds(at, quarter), :], act_ref[...], preferred_element_type=F32
                 ).astype(BF)
@@ -398,8 +425,8 @@
     def flat(count, width):
         return pl.BlockSpec((count, width), lambda j, s_ref: (0, 0))
 
-    outs = [jax.ShapeDtypeStruct((fine + 16, half), BF)]
-    out_specs = [cols(fine + 16, False)]
+    outs = [jax.ShapeDtypeStruct((fine + 2 * TAIL, half), BF)]
+    out_specs = [cols(fine + 2 * TAIL, False)]
     scratch = []
     if ours:
         outs += [jax.ShapeDtypeStruct((fine, half), BF)]
@@ -412,7 +439,7 @@
         scratch += [pltpu.VMEM((fine, half), BF), pltpu.VMEM((columns, fine), BF)]
     scratch += [
         pltpu.VMEM((4, rows + TAIL, DV), BF),
-        pltpu.VMEM((fine + 16, WIDE), F32),
+        pltpu.VMEM((fine + 2 * TAIL, WIDE), F32),
         pltpu.VMEM((steps, rows, WIDE), BF),
         pltpu.VMEM((steps, fine, WIDE), BF),
         pltpu.VMEM((steps, H, DV, WIDE), BF),
@@ -430,7 +457,7 @@
             out_specs=out_specs,
             scratch_shapes=scratch,
         ),
-        compiler_params=params(48),
+        compiler_params=params(53),
         cost_estimate=pl.CostEstimate(
             flops=2 * fine * columns * columns, bytes_accessed=9 << 20, transcendentals=fine * half
         ),
@@ -444,10 +471,10 @@
     steps = half // WIDE
 
     def side(s_ref):
-        return s_ref[CORE] if ours else 1 - s_ref[CORE]
+        return s_ref[1] if ours else 1 - s_ref[1]
 
     def kernel(s_ref, up_ref, g_ref, low_ref, high_ref, pw_ref, dw_ref, *refs):
-        gs_ref, gd_ref, held, grad, ends = refs[-5:]
+        gs_ref, gd_ref, grad, upper, ends = refs[-5:]
         dims = (((1,), (1,)), ((), ()))
 
         @pl.when(pl.program_id(0) == 0)
@@ -456,35 +483,37 @@
             low, high = low_ref[...].astype(F32), high_ref[...].astype(F32)
             ends[...] = jnp.where(row == 7, low[3:4], jnp.where(row == 8, high[3:4], 0.0)).astype(BF)
 
-        upper = lax.dot_general(g_ref[...], pw_ref[...], dims, preferred_element_type=F32)
+        upper[...] = lax.dot_general(g_ref[...], pw_ref[...], dims, preferred_element_type=F32)
         outer = lax.dot_general(ends[...], pw_ref[...], dims, preferred_element_type=F32)
-        held[:8, :] = jnp.zeros((8, WIDE), F32)
-        held[8 : fine + 24, :] = up_ref[...].astype(F32)
-        held[fine + 24 :, :] = jnp.zeros((8, WIDE), F32)
-
-        def grad_of(start, count, coming):
-            pre = (
-                dw_ref[0:1, :] * held[start - 1 : start - 1 + count, :]
-                + dw_ref[1:2, :] * held[start : start + count, :]
-                + dw_ref[2:3, :] * held[start + 1 : start + 1 + count, :]
+        w = [dw_ref[t : t + 1, :] for t in range(3)]
+
+        def grad_of(near, start, count, coming):
+            taps = [near[start - 1 + t : start - 1 + t + count] for t in range(3)]
+            pre = w[0] * taps[0] + w[1] * taps[1] + w[2] * taps[2]
+            bend, square, slope = gelu_parts(pre)
+            rate = 0.5 + 0.5 * bend + (pre * (1.0 - bend * bend)) * (
+                0.5 * slope + (1.5 * slope * 0.044715) * square
             )
-            bend, square, slope = gelu_parts(pre)
-            rate = 0.5 * (1.0 + bend) + (0.5 * slope) * pre * (1.0 - bend * bend) * (
-                1.0 + (3 * 0.044715) * square
-            )
-            return (coming * rate).astype(BF).astype(F32)
-
-        grad[:8, :] = grad_of(8, 8, outer[:8])
-        mid = grad_of(16, fine, upper)
-        grad[8 : 8 + fine, :] = mid
-        grad[8 + fine :, :] = grad_of(16 + fine, 8, outer[8:])
-        gs_ref[...] = (
-            dw_ref[0:1, :] * grad[9 : 9 + fine, :]
-            + dw_ref[1:2, :] * mid
-            + dw_ref[2:3, :] * grad[7 : 7 + fine, :]
-        ).astype(BF)
+            return taps, (coming * rate).astype(BF).astype(F32)
+
+        _, grad[8:16, :] = grad_of(up_ref[:32, :].astype(F32), 8, 8, outer[:8])
+        _, grad[16 + fine : 24 + fine, :] = grad_of(up_ref[fine:, :].astype(F32), 16, 8, outer[8:])
+        sums = [jnp.zeros((8, WIDE), F32)] * 3
+        for k in range(0, fine, STRIP):
+            near = up_ref[k : k + STRIP + 2 * TAIL, :].astype(F32)
+            taps, mid = grad_of(near, TAIL, STRIP, upper[k : k + STRIP, :])
+            grad[16 + k : 16 + k + STRIP, :] = mid
+            for t in range(3):
+                term = taps[t] * mid
+                for r in range(0, STRIP, 8):
+                    sums[t] = sums[t] + term[r : r + 8]
         for t in range(3):
-            gd_ref[t : t + 1, :] = jnp.sum(held[15 + t : 15 + t + fine, :] * mid, axis=0, keepdims=True)
+            gd_ref[t : t + 1, :] = jnp.sum(sums[t], axis=0, keepdims=True)
+        for k in range(0, fine, STRIP):
+            near = grad[8 + k : 24 + k + STRIP, :]
+            gs_ref[k : k + STRIP, :] = (
+                w[0] * near[9 : 9 + STRIP] + w[1] * near[8 : 8 + STRIP] + w[2] * near[7 : 7 + STRIP]
+            ).astype(BF)
 
     def cols(count, full):
         return pl.BlockSpec((count, WIDE), lambda j, s_ref: (0, (side(s_ref) * steps if full else 0) + j))
@@ -502,7 +531,7 @@
             num_scalar_prefetch=1,
             grid=(steps,),
             in_specs=[
-                cols(fine + 16, False),
+                cols(fine + 2 * TAIL, False),
                 flat(fine),
                 flat(TAIL),
                 flat(TAIL),
@@ -512,8 +541,8 @@
             + [ANY] * (len(ins) - 6),
             out_specs=[cols(fine, True), cols(3, False)],
             scratch_shapes=[
-                pltpu.VMEM((fine + 32, WIDE), F32),
-                pltpu.VMEM((fine + 16, WIDE), F32),
+                pltpu.VMEM((fine + 2 * TAIL, WIDE), F32),
+                pltpu.VMEM((fine, WIDE), F32),
                 pltpu.VMEM((TAIL, columns), BF),
             ],
         ),
@@ -531,7 +560,7 @@
 
     def kernel(s_ref, a_ref, g_ref, arrived_ref, *outs):
         for out, d in zip(outs, steps):
-            at = pl.multiple_of((s_ref[FIRST_AT] + d) % 4 * quarter, 16)
+            at = pl.multiple_of((Spot(s_ref).first_at + d) % 4 * quarter, 16)
             block = jnp.dot(g_ref[pl.ds(at, quarter), :], a_ref[...], preferred_element_type=F32)
             out[...] = (block + arrived_ref[d].astype(F32)).astype(BF)
 
@@ -555,7 +584,7 @@
     def kernel(at_ref, *refs):
         ins, rider_ref, outs = refs[:4], refs[4], refs[5:]
         for d in range(4):
-            take = pl.ds(pl.multiple_of((at_ref[SECOND_AT] + d) % 4 * slim, 16), slim)
+            take = pl.ds(pl.multiple_of((Spot(at_ref).second_at + d) % 4 * slim, 16), slim)
             outs[d][:slim, :] = total_of([r[take, :] for r in ins]).astype(BF)
             outs[d][slim:, :] = rider_ref[...]
 
@@ -575,7 +604,7 @@
     def kernel(at_ref, *refs):
         ins, rider_ref, out, held = refs[:4], refs[4], refs[5], refs[6]
         for d in range(4):
-            put = pl.ds(pl.multiple_of((at_ref[SECOND_AT] + 4 - d) % 4 * slim, 16), slim)
+            put = pl.ds(pl.multiple_of((Spot(at_ref).second_at + 4 - d) % 4 * slim, 16), slim)
             held[put, :] = ins[d][...]
         out[:columns, :] = held[...].T
         last = rider_ref[...].astype(F32)[:8]
@@ -592,37 +621,41 @@
     )(at, *got, rider)
 
 
-def lay_out(scalars, step, own, other, whole=None):
-    half, quarter = own.shape[0] - TAIL, own.shape[1]
-
-    def kernel(s_ref, own_ref, other_ref, *refs):
-        out = refs[-1]
-        for n, ref in enumerate((own_ref, other_ref)):
-
-            @pl.when(pl.program_id(0) == n)
-            def _():
-                out[...] = ref[:half, :]
-
-    def place(n, s_ref):
-        side = jnp.where(n == 0, s_ref[CORE], 1 - s_ref[CORE])
-        at = jnp.where(n == 0, s_ref[FIRST_AT], s_ref[THEIR_FIRST])
-        return side, (at + 4 - step) % 4
-
-    block = pl.BlockSpec((half + TAIL, quarter), lambda n, s_ref: (0, 0))
+def lay_out(scalars, steps, own, other, whole=None):
+    half, quarter = own[0].shape[0] - TAIL, own[0].shape[1]
+    count = len(steps)
+
+    def kernel(s_ref, *refs):
+        out, sems = refs[-2:]
+        spot = Spot(s_ref)
+        copies = []
+        for n in range(2 * count):
+            mine = n < count
+            down = (spot.core if mine else 1 - spot.core) * half
+            over = ((spot.first_at if mine else spot.their_first) + 4 - steps[n % count]) % 4 * quarter
+            copies.append(
+                pltpu.make_async_copy(
+                    refs[n].at[pl.ds(0, half), :],
+                    out.at[pl.ds(pl.multiple_of(down, 16), half), pl.ds(pl.multiple_of(over, 128), quarter)],
+                    sems.at[n],
+                )
+            )
+        for copy in copies:
+            copy.start()
+        for copy in copies:
+            copy.wait()
+
     extra = [] if whole is None else [whole]
     return pl.pallas_call(
         kernel,
         out_shape=jax.ShapeDtypeStruct((2 * half, 4 * quarter), BF),
-        grid_spec=pltpu.PrefetchScalarGridSpec(
-            num_scalar_prefetch=1,
-            grid=(2,),
-            in_specs=[block] * 2 + [ANY] * len(extra),
-            out_specs=pl.BlockSpec((half, quarter), place),
-        ),
-        input_output_aliases={} if whole is None else {3: 0},
-        compiler_params=params(12),
+        in_specs=[SMEM] + [VMEM] * (2 * count) + [ANY] * len(extra),
+        out_specs=ANY,
+        scratch_shapes=[pltpu.SemaphoreType.DMA((2 * count,))],
+        input_output_aliases={} if whole is None else {1 + 2 * count: 0},
+        compiler_params=params(8),
         name="lay_out",
-    )(scalars, own, other, *extra)
+    )(scalars, *own, *other, *extra)
 
 
 def local(
@@ -641,26 +674,7 @@
     rows, columns = tokens.shape
     fine = skipped.shape[0]
     ix, ic, iz, iy = (lax.axis_index(a) for a in AXES)
-    index = {"x": ix, "z": iz, "y": iy}
-    place = iz * 4 + iy
-
-    def at(axes, swap=False):
-        a, b = axes[::-1] if swap else axes
-        return jnp.where(ic == 0, index[a], index[b])
-
-    def ints(*values):
-        return jnp.stack([jnp.asarray(v, jnp.int32) for v in values])
-
-    head_at, row_at = at(HEAD_RING), at(ROW_RING)
-    values = [ic, head_at, place > 0, place < 15, at(SUM_RINGS[0]), at(SUM_RINGS[0], True), at(SUM_RINGS[1]), 0, ic]
-    start_at = [jnp.where(ic == 0, (iy - d) % 4, iy) for d in range(4)]
-    values += [v == 0 for v in start_at] + [v == 3 for v in start_at]
-    for far_by in (0, 1, 3, 2):
-        for d in range(4):
-            h, r = (head_at - d) % 4, (row_at - far_by) % 4
-            values.append(jnp.where(ic == 0, r * 4 + h, h * 4 + r) * rows)
-    scalars = ints(*values, valid_bins[0])
-
+    scalars = jnp.stack([v.astype(jnp.int32) for v in (ix, ic, iz, iy, valid_bins[0])])
     blocks = project(scalars, tokens, query_weight, key_weight, value_weight)
     q = exchange(blocks, HEAD_RING)
     own = stack_rows(q)
@@ -673,7 +687,7 @@
     turned = upstream.T
 
     state, _ = attend(scalars, 1, q, [far[1]], state)
-    state, _ = attend(scalars, 2, q, [far[3]], state)
+    state, _ = attend(scalars, 2, q, [far[3]], state, (before, after))
     mixed = attend(scalars, 3, q, [own, far[1], far[3], far[2]], state)
     back = exchange(mixed, HEAD_RING, -1)
     swap = [(0, 1), (1, 0)]
@@ -702,9 +716,8 @@
     joined = join_rows(scalars, exchange([piece] * 4, SUM_RINGS[1]), rider)
     got = exchange([joined] * 4, SUM_RINGS[0])
     other = [lax.ppermute(g, "c", swap) for g in got]
-    grad_pointwise = None
-    for d in (0, 1, 3, 2):
-        grad_pointwise = lay_out(scalars, d, got[d], other[d], grad_pointwise)
+    grad_pointwise = lay_out(scalars, (0,), got[:1], other[:1])
+    grad_pointwise = lay_out(scalars, (1, 2, 3), got[1:], other[1:], grad_pointwise)
 
     def depth_of(blocks):
         rows = total_of([b[half:] for b in blocks])

time: 161 us -> 152 us (0.944)
  waiting for transfers between devices: 35.4 us -> 30.4 us
  Pallas kernels: 59.1 us -> 56.1 us
    ppermute x21, starting transfers between devices: 33.4 us -> 26.1 us  [exchange(): got[d] = lax.ppermute(pieces[d], AXES, turn(axes, sign * d))]
    ppermute x21, waiting for transfers between devices: 22.2 us -> 28.7 us  [exchange(): got[d] = lax.ppermute(pieces[d], AXES, turn(axes, sign * d))]
    ppermute x1, waiting for transfers between devices: 6.84 us -> 1.59 us  [local(): after = lax.ppermute(up, ('z', 'y'), [(i + 1, i) for i in range(15)])]
    ppermute x3, waiting for transfers between devices: 5.18 us -> 0.01 us  [local(): far = {d: lax.ppermute(own, AXES, turn(ROW_RING, d)) for d in (1, 3, 2)}]
    ppermute x1, starting transfers between devices: 0.01 us -> 3.02 us  [local(): d_arrived = lax.ppermute(d_theirs, 'c', swap)]
    unnamed x16 -> x14, local copies, waits for them, and re-layouts: 3.46 us -> 1.15 us
    pallas_call x4 -> x2, Pallas kernels: 6.62 us -> 4.87 us  [lay_out(): pl.pallas_call(kernel, out_shape=jax.ShapeDtypeStruct((2 * half, 4 * quar...]
    ppermute x4, starting transfers between devices: 15.6 us -> 17.2 us  [local(): other = [lax.ppermute(g, 'c', swap) for g in got]]
  transfers between devices with their start and end apart: 32 -> 32, of which waited for: 15 -> 16; matrix products, arithmetic and copies ran while one was open for 0% -> 1% of each run, Pallas kernels for 21% -> 22%
where the time goes in v5:
time: 152 us; the launch traced here: 151 us
  starting transfers between devices  58.5 us (38%)
  Pallas kernels  56.1 us (37%)
  waiting for transfers between devices  30.4 us (20%)
  local copies, waits for them, and re-layouts  2.84 us (2%)
  between operations  1.77 us (1%)
  other arithmetic  1.59 us (1%)
    ppermute x21, waiting for transfers between devices, exchange(): got[d] = lax.ppermute(pieces[d], AXES, turn(axes, sign * d))  28.7 us
    ppermute x21, starting transfers between devices, exchange(): got[d] = lax.ppermute(pieces[d], AXES, turn(axes, sign * d))  26.1 us
    ppermute x4, starting transfers between devices, local(): other = [lax.ppermute(g, 'c', swap) for g in got]  17.2 us
    pallas_call x2, Pallas kernels, backward(): pl.pallas_call(kernel, out_shape=[jax.ShapeDtypeStruct((fine, columns), B...  15.4 us
    pallas_call x2, Pallas kernels, forward(): pl.pallas_call(kernel, out_shape=outs, grid_spec=pltpu.PrefetchScalarGrid...  14.3 us
    pallas_call x4, Pallas kernels, attend(): pl.pallas_call(kernel, out_shape=outs, in_specs=[SMEM] + [VMEM] * len(ins...  11.7 us
    pallas_call x2, Pallas kernels, lay_out(): pl.pallas_call(kernel, out_shape=jax.ShapeDtypeStruct((2 * half, 4 * quar...  4.87 us
    pallas_call x1, Pallas kernels, project(): pl.pallas_call(kernel, out_shape=[jax.ShapeDtypeStruct((rows, 384), BF)]...  4.48 us
  transfers between devices with their start and end apart: 32, of which 16 were waited for; matrix products, arithmetic and copies ran while one was open for 1% of the time, Pallas kernels for 22%

profile of v5, /device:TPU:1, one launch (start us, length us, event | category | flops | bytes accessed | tf_op | source)
XLA Modules:
  0.0 151.2 jit_solution(17147699952325457253)
XLA Ops:
  1.4 4.5 %project.1 = (bf16[256,384]{1,0:T(8,128)(2,1)S(1)}, bf16[256,384]{1,0:T(8,128)(2,1)S(1)}, bf16[256,384]{1,0:T(8,128)(2,1)S(1)}, bf16[256,384]{1,0:T(8,128)(2,1)S(1)}) custom-call(s32[5]{0:T(128)S(1)} %stack.19.at_ref.s_ref, bf16[256,1536]{1,0:T(8,128)(2,1)} %bitcast.15, bf16[1536,256]{1,0:T(8,128)(2,1)} %wq_hbm.1, bf16[1536,256]{1,0:T(8,128)(2,1)} %wk_hbm.1, ...), custom_call_target="tpu_custom_call" | custom-call | tf_op jit(solution)/shard_map/project/pallas_call | solution.py:116
  5.9 2.5 %collective-permute-start = (bf16[256,384]{1,0:T(8,128)(2,1)S(1)}, bf16[256,384]{1,0:T(8,128)(2,1)S(1)}, u32[]{:S(2)}, u32[]{:S(2)}) collective-permute-start(bf16[256,384]{1,0:T(8,128)(2,1)S(1)} %get-tuple-element.34), channel_id=1, source_target_pairs={{0,1},{1,2},{2,3},{3,0},{4,5},{5,6},{6,7},{7,4},{8,9},{9,10},{10,1... | collective-permute-start | bytes 589832 | tf_op jit(solution)/shard_map/ppermute | solution.py:67
  8.4 3.3 %collective-permute-start.1 = (bf16[256,384]{1,0:T(8,128)(2,1)S(1)}, bf16[256,384]{1,0:T(8,128)(2,1)S(1)}, u32[]{:S(2)}, u32[]{:S(2)}) collective-permute-start(bf16[256,384]{1,0:T(8,128)(2,1)S(1)} %get-tuple-element.35), channel_id=1, source_target_pairs={{0,2},{1,3},{2,0},{3,1},{4,6},{5,7},{6,4},{7,5},{8,10},{9,11},{10,... | collective-permute-start | bytes 589832 | tf_op jit(solution)/shard_map/ppermute | solution.py:67
  13.8 3.3 %collective-permute-done.1.refs_2_ = bf16[256,384]{1,0:T(8,128)(2,1)S(1)} collective-permute-done((bf16[256,384]{1,0:T(8,128)(2,1)S(1)}, bf16[256,384]{1,0:T(8,128)(2,1)S(1)}, u32[]{:S(2)}, u32[]{:S(2)}) %collective-permute-start.1) | collective-permute-done | bytes 196640 | tf_op jit(solution)/shard_map/ppermute | solution.py:67
  21.4 2.2 %attend.4 = (f32[1024,256]{1,0:T(8,128)S(1)}, f32[8,128]{1,0:T(8,128)S(1)}) custom-call(s32[5]{0:T(128)S(1)} %stack.19.at_ref.s_ref, bf16[256,384]{1,0:T(8,128)(2,1)S(1)} %get-tuple-element.33.refs_0_, bf16[256,384]{1,0:T(8,128)(2,1)S(1)} %collective-permute-done.refs_1_, bf16[256,384]{1,0:T(8,128)(2,1)S(1)} %collective-permute-done.1.refs_2_, ...), custom_call_target="tpu_custom_call" | custom-call | flops 1073741824 | bytes 4194304 | tf_op jit(solution)/shard_map/attend/pallas_call | solution.py:257
  24.6 2.3 %collective-permute-start.6 = (bf16[16,1536]{1,0:T(8,128)(2,1)S(1)}, bf16[16,1536]{1,0:T(8,128)(2,1)S(1)}, u32[]{:S(2)}, u32[]{:S(2)}) collective-permute-start(bf16[16,1536]{1,0:T(8,128)(2,1)S(1)} %get-tuple-element.40), channel_id=1, source_target_pairs={{0,1},{1,2},{2,3},{3,4},{4,5},{5,6},{6,7},{7,8},{8,9},{9,10},{10,1... | collective-permute-start | bytes 147464 | tf_op jit(solution)/shard_map/ppermute | solution.py:685
  28.3 3.1 %attend.5 = (f32[1024,256]{1,0:T(8,128)S(1)}, f32[8,128]{1,0:T(8,128)}) custom-call(s32[5]{0:T(128)S(1)} %stack.19.at_ref.s_ref, bf16[256,384]{1,0:T(8,128)(2,1)S(1)} %get-tuple-element.33.refs_0_, bf16[256,384]{1,0:T(8,128)(2,1)S(1)} %collective-permute-done.refs_1_, bf16[256,384]{1,0:T(8,128)(2,1)S(1)} %collective-permute-done.1.refs_2_, ...), custom_call_target="tpu_custom_call" | custom-call | flops 1073741824 | bytes 4194304 | tf_op jit(solution)/shard_map/attend/pallas_call | solution.py:257
  33.0 3.1 %attend.6 = (f32[1024,256]{1,0:T(8,128)S(1)}, f32[8,128]{1,0:T(8,128)}) custom-call(s32[5]{0:T(128)S(1)} %stack.19.at_ref.s_ref, bf16[256,384]{1,0:T(8,128)(2,1)S(1)} %get-tuple-element.33.refs_0_, bf16[256,384]{1,0:T(8,128)(2,1)S(1)} %collective-permute-done.refs_1_, bf16[256,384]{1,0:T(8,128)(2,1)S(1)} %collective-permute-done.1.refs_2_, ...), custom_call_target="tpu_custom_call" | custom-call | flops 1073741824 | bytes 4194304 | tf_op jit(solution)/shard_map/attend/pallas_call | solution.py:257
  36.1 3.3 %attend.7 = (bf16[272,256]{1,0:T(8,128)(2,1)S(1)}, bf16[272,256]{1,0:T(8,128)(2,1)S(1)}, bf16[272,256]{1,0:T(8,128)(2,1)S(1)}, bf16[272,256]{1,0:T(8,128)(2,1)S(1)}) custom-call(s32[5]{0:T(128)S(1)} %stack.19.at_ref.s_ref, bf16[256,384]{1,0:T(8,128)(2,1)S(1)} %get-tuple-element.33.refs_0_, bf16[256,384]{1,0:T(8,128)(2,1)S(1)} %collective-permute-done.refs_1_, ...), custom_call_target="tpu_custom_call" | custom-call | flops 1073741824 | bytes 4194304 | tf_op jit(solution)/shard_map/attend/pallas_call | solution.py:257
  39.4 4.5 %collective-permute-start.8 = (bf16[272,256]{1,0:T(8,128)(2,1)S(1)}, bf16[272,256]{1,0:T(8,128)(2,1)S(1)}, u32[]{:S(2)}, u32[]{:S(2)}) collective-permute-start(bf16[272,256]{1,0:T(8,128)(2,1)S(1)} %get-tuple-element.44), channel_id=1, source_target_pairs={{0,3},{1,0},{2,1},{3,2},{4,7},{5,4},{6,5},{7,6},{8,11},{9,8},{10,9... | collective-permute-start | bytes 417800 | tf_op jit(solution)/shard_map/ppermute | solution.py:67
  47.4 2.0 %collective-permute-done.9.b2 = bf16[272,256]{1,0:T(8,128)(2,1)S(1)} collective-permute-done((bf16[272,256]{1,0:T(8,128)(2,1)S(1)}, bf16[272,256]{1,0:T(8,128)(2,1)S(1)}, u32[]{:S(2)}, u32[]{:S(2)}) %collective-permute-start.9) | collective-permute-done | bytes 139296 | tf_op jit(solution)/shard_map/ppermute | solution.py:67
  50.8 8.4 %forward.3 = (bf16[544,768]{1,0:T(8,128)(2,1)}, bf16[4,384,768]{2,1,0:T(8,128)(2,1)}) custom-call(s32[5]{0:T(128)S(1)} %stack.19.at_ref.s_ref, bf16[272,256]{1,0:T(8,128)(2,1)S(1)} %get-tuple-element.43.b0, bf16[272,256]{1,0:T(8,128)(2,1)S(1)} %collective-permute-done.8.b1, bf16[272,256]{1,0:T(8,128)(2,1)S(1)} %collective-permute-done.9.b2, ...), custom_call_target="tpu_custom_call" | custom-call | flops 2415919104 | bytes 9437184 | tf_op jit(solution)/shard_map/forward/pallas_call | solution.py:448
  59.2 4.4 %collective-permute-start.11 = (bf16[4,384,768]{2,1,0:T(8,128)(2,1)}, bf16[4,384,768]{2,1,0:T(8,128)(2,1)S(1)}, u32[]{:S(2)}, u32[]{:S(2)}) collective-permute-start(bf16[4,384,768]{2,1,0:T(8,128)(2,1)} %get-tuple-element.48), channel_id=1, source_target_pairs={{0,16},{16,0},{1,17},{17,1},{2,18},{18,2},{3,19},{19,3},{4,20},{20... | collective-permute-start | bytes 7077896 | tf_op jit(solution)/shard_map/ppermute | solution.py:696
  63.6 5.9 %forward.2 = (bf16[544,768]{1,0:T(8,128)(2,1)}, bf16[512,768]{1,0:T(8,128)(2,1)}) custom-call(s32[5]{0:T(128)S(1)} %stack.19.at_ref.s_ref, bf16[272,256]{1,0:T(8,128)(2,1)S(1)} %get-tuple-element.43.b0, bf16[272,256]{1,0:T(8,128)(2,1)S(1)} %collective-permute-done.8.b1, bf16[272,256]{1,0:T(8,128)(2,1)S(1)} %collective-permute-done.9.b2, ...), custom_call_target="tpu_custom_call" | custom-call | flops 2415919104 | bytes 9437184 | tf_op jit(solution)/shard_map/forward/pallas_call | solution.py:448
  72.1 1.8 %collective-permute-start.13 = (bf16[384,768]{1,0:T(8,128)(2,1)S(1)}, bf16[384,768]{1,0:T(8,128)(2,1)S(1)}, u32[]{:S(2)}, u32[]{:S(2)}) collective-permute-start(bf16[384,768]{1,0:T(8,128)(2,1)S(1)} %get-tuple-element.51), channel_id=1, source_target_pairs={{0,64},{1,65},{2,66},{3,67},{4,68},{5,69},{6,70},{7,71},{8,72},{9,... | collective-permute-start | bytes 1769480 | tf_op jit(solution)/shard_map/ppermute | solution.py:67
  76.1 7.7 %backward.2 = (bf16[512,1536]{1,0:T(8,128)(2,1)}, f32[3,768]{1,0:T(4,128)S(1)}) custom-call(s32[5]{0:T(128)S(1)} %stack.19.at_ref.s_ref, bf16[544,768]{1,0:T(8,128)(2,1)S(1)} %copy-done.4, bf16[512,1536]{1,0:T(8,128)(2,1)S(1)} %bitcast.13, bf16[16,1536]{1,0:T(8,128)(2,1)S(1)} %collective-permute-done.6.refs_6_.low_ref, ...), custom_call_target="tpu_custom_call" | custom-call | flops 1207959552 | bytes 6291456 | tf_op jit(solution)/shard_map/backward/pallas_call | solution.py:527
  83.8 3.0 %collective-permute-start.15 = (f32[3,768]{1,0:T(4,128)S(1)}, f32[3,768]{1,0:T(4,128)S(1)}, u32[]{:S(2)}, u32[]{:S(2)}) collective-permute-start(f32[3,768]{1,0:T(4,128)S(1)} %get-tuple-element.57), channel_id=1, source_target_pairs={{0,16},{16,0},{1,17},{17,1},{2,18},{18,2},{3,19},{19,3},{4,20},{20... | collective-permute-start | bytes 27656 | tf_op jit(solution)/shard_map/ppermute | solution.py:704
  86.9 7.7 %backward.3 = (bf16[512,1536]{1,0:T(8,128)(2,1)}, f32[3,768]{1,0:T(4,128)S(1)}) custom-call(s32[5]{0:T(128)S(1)} %stack.19.at_ref.s_ref, bf16[544,768]{1,0:T(8,128)(2,1)S(1)} %copy-done.5, bf16[512,1536]{1,0:T(8,128)(2,1)S(1)} %bitcast.14, bf16[16,1536]{1,0:T(8,128)(2,1)S(1)} %collective-permute-done.6.refs_6_.low_ref, ...), custom_call_target="tpu_custom_call", output_to_operand_aliasing={{0}: (8, {})} | custom-call | flops 1207959552 | bytes 6291456 | tf_op jit(solution)/shard_map/backward/pallas_call | solution.py:527
  97.1 2.7 %collective-permute-start.18 = (bf16[112,768]{1,0:T(8,128)(2,1)S(1)}, bf16[112,768]{1,0:T(8,128)(2,1)S(1)}, u32[]{:S(2)}, u32[]{:S(2)}) collective-permute-start(bf16[112,768]{1,0:T(8,128)(2,1)S(1)} %get-tuple-element.61), channel_id=1, source_target_pairs={{0,3},{1,0},{2,1},{3,2},{4,7},{5,4},{6,5},{7,6},{8,11},{9,8},{10,9... | collective-permute-start | bytes 516104 | tf_op jit(solution)/shard_map/ppermute | solution.py:67
  99.7 1.8 %collective-permute-done.16 = bf16[112,768]{1,0:T(8,128)(2,1)S(1)} collective-permute-done((bf16[112,768]{1,0:T(8,128)(2,1)S(1)}, bf16[112,768]{1,0:T(8,128)(2,1)S(1)}, u32[]{:S(2)}, u32[]{:S(2)}) %collective-permute-start.16) | collective-permute-done | bytes 172064 | tf_op jit(solution)/shard_map/ppermute | solution.py:67
  101.6 1.8 %collective-permute-done.17 = bf16[112,768]{1,0:T(8,128)(2,1)S(1)} collective-permute-done((bf16[112,768]{1,0:T(8,128)(2,1)S(1)}, bf16[112,768]{1,0:T(8,128)(2,1)S(1)}, u32[]{:S(2)}, u32[]{:S(2)}) %collective-permute-start.17) | collective-permute-done | bytes 172064 | tf_op jit(solution)/shard_map/ppermute | solution.py:67
  105.7 2.5 %collective-permute-done.21 = bf16[112,768]{1,0:T(8,128)(2,1)S(1)} collective-permute-done((bf16[112,768]{1,0:T(8,128)(2,1)S(1)}, bf16[112,768]{1,0:T(8,128)(2,1)S(1)}, u32[]{:S(2)}, u32[]{:S(2)}) %collective-permute-start.21) | collective-permute-done | bytes 172064 | tf_op jit(solution)/shard_map/ppermute | solution.py:67
  108.1 3.4 %collective-permute-done.20 = bf16[112,768]{1,0:T(8,128)(2,1)S(1)} collective-permute-done((bf16[112,768]{1,0:T(8,128)(2,1)S(1)}, bf16[112,768]{1,0:T(8,128)(2,1)S(1)}, u32[]{:S(2)}, u32[]{:S(2)}) %collective-permute-start.20) | collective-permute-done | bytes 172064 | tf_op jit(solution)/shard_map/ppermute | solution.py:67
  111.6 1.9 %collective-permute-start.24 = (bf16[96,768]{1,0:T(8,128)(2,1)S(1)}, bf16[96,768]{1,0:T(8,128)(2,1)S(1)}, u32[]{:S(2)}, u32[]{:S(2)}) collective-permute-start(bf16[96,768]{1,0:T(8,128)(2,1)S(1)} %slice.56.refs_0_), channel_id=1, source_target_pairs={{0,3},{1,0},{2,1},{3,2},{4,7},{5,4},{6,5},{7,6},{8,11},{9,8},{10,9... | collective-permute-start | bytes 442376 | tf_op jit(solution)/shard_map/ppermute | solution.py:67
  114.2 3.0 %collective-permute-done.24.refs_3_ = bf16[96,768]{1,0:T(8,128)(2,1)S(1)} collective-permute-done((bf16[96,768]{1,0:T(8,128)(2,1)S(1)}, bf16[96,768]{1,0:T(8,128)(2,1)S(1)}, u32[]{:S(2)}, u32[]{:S(2)}) %collective-permute-start.24) | collective-permute-done | bytes 147488 | tf_op jit(solution)/shard_map/ppermute | solution.py:67
  117.1 1.9 %collective-permute-done.23.refs_2_ = bf16[96,768]{1,0:T(8,128)(2,1)S(1)} collective-permute-done((bf16[96,768]{1,0:T(8,128)(2,1)S(1)}, bf16[96,768]{1,0:T(8,128)(2,1)S(1)}, u32[]{:S(2)}, u32[]{:S(2)}) %collective-permute-start.23) | collective-permute-done | bytes 147488 | tf_op jit(solution)/shard_map/ppermute | solution.py:67
  123.8 4.5 %collective-permute-start.31 = (bf16[784,384]{1,0:T(8,128)(2,1)S(1)}, bf16[784,384]{1,0:T(8,128)(2,1)S(1)}, u32[]{:S(2)}, u32[]{:S(2)}) collective-permute-start(bf16[784,384]{1,0:T(8,128)(2,1)S(1)} %join_rows.1.refs_0_), channel_id=1, source_target_pairs={{0,16},{16,0},{1,17},{17,1},{2,18},{18,2},{3,19},{19,3},{4,20},{20... | collective-permute-start | bytes 1806344 | tf_op jit(solution)/shard_map/ppermute | solution.py:718
  128.2 2.6 %collective-permute-done.27.refs_2_ = bf16[784,384]{1,0:T(8,128)(2,1)S(1)} collective-permute-done((bf16[784,384]{1,0:T(8,128)(2,1)S(1)}, bf16[784,384]{1,0:T(8,128)(2,1)S(1)}, u32[]{:S(2)}, u32[]{:S(2)}) %collective-permute-start.27) | collective-permute-done | bytes 602144 | tf_op jit(solution)/shard_map/ppermute | solution.py:67
  130.8 4.0 %collective-permute-start.30 = (bf16[784,384]{1,0:T(8,128)(2,1)S(1)}, bf16[784,384]{1,0:T(8,128)(2,1)}, u32[]{:S(2)}, u32[]{:S(2)}) collective-permute-start(bf16[784,384]{1,0:T(8,128)(2,1)S(1)} %collective-permute-done.27.refs_2_), channel_id=1, source_target_pairs={{0,16},{16,0},{1,17},{17,1},{2,18},{18,2},{3,19},{19,3},{4,20},{20... | collective-permute-start | bytes 1806344 | tf_op jit(solution)/shard_map/ppermute | solution.py:718
  134.9 3.3 %collective-permute-start.29 = (bf16[784,384]{1,0:T(8,128)(2,1)S(1)}, bf16[784,384]{1,0:T(8,128)(2,1)}, u32[]{:S(2)}, u32[]{:S(2)}) collective-permute-start(bf16[784,384]{1,0:T(8,128)(2,1)S(1)} %collective-permute-done.26.refs_1_), channel_id=1, source_target_pairs={{0,16},{16,0},{1,17},{17,1},{2,18},{18,2},{3,19},{19,3},{4,20},{20... | collective-permute-start | bytes 1806344 | tf_op jit(solution)/shard_map/ppermute | solution.py:718
  139.1 5.4 %collective-permute-start.28 = (bf16[784,384]{1,0:T(8,128)(2,1)S(1)}, bf16[784,384]{1,0:T(8,128)(2,1)}, u32[]{:S(2)}, u32[]{:S(2)}) collective-permute-start(bf16[784,384]{1,0:T(8,128)(2,1)S(1)} %collective-permute-done.25.refs_0_), channel_id=1, source_target_pairs={{0,16},{16,0},{1,17},{17,1},{2,18},{18,2},{3,19},{19,3},{4,20},{20... | collective-permute-start | bytes 1806344 | tf_op jit(solution)/shard_map/ppermute | solution.py:718
  147.7 3.3 %lay_out.3 = bf16[1536,1536]{1,0:T(8,128)(2,1)} custom-call(s32[5]{0:T(128)S(1)} %stack.19.at_ref.s_ref, bf16[784,384]{1,0:T(8,128)(2,1)S(1)} %collective-permute-done.25.refs_0_, bf16[784,384]{1,0:T(8,128)(2,1)S(1)} %collective-permute-done.26.refs_1_, bf16[784,384]{1,0:T(8,128)(2,1)S(1)} %collective-permute-done.27.refs_2_, ...), custom_call_target="tpu_custom_call", output_to_operand_aliasing={{}: (7, {})} | custom-call | tf_op jit(solution)/shard_map/lay_out/pallas_call | solution.py:649
  (77 shorter events, 34.4 us)
Async XLA Ops:
  5.9 8.0 %collective-permute-start = (bf16[256,384]{1,0:T(8,128)(2,1)S(1)}, bf16[256,384]{1,0:T(8,128)(2,1)S(1)}, u32[]{:S(2)}, u32[]{:S(2)}) collective-permute-start(bf16[256,384]{1,0:T(8,128)(2,1)S(1)} %get-tuple-element.34), channel_id=1, source_target_pairs={{0,1},{1,2},{2,3},{3,0},{4,5},{5,6},{6,7},{7,4},{8,9},{9,10},{10,1... | collective-permute-start | bytes 589832 | tf_op jit(solution)/shard_map/ppermute | solution.py:67
  8.4 8.8 %collective-permute-start.1 = (bf16[256,384]{1,0:T(8,128)(2,1)S(1)}, bf16[256,384]{1,0:T(8,128)(2,1)S(1)}, u32[]{:S(2)}, u32[]{:S(2)}) collective-permute-start(bf16[256,384]{1,0:T(8,128)(2,1)S(1)} %get-tuple-element.35), channel_id=1, source_target_pairs={{0,2},{1,3},{2,0},{3,1},{4,6},{5,7},{6,4},{7,5},{8,10},{9,11},{10,... | collective-permute-start | bytes 589832 | tf_op jit(solution)/shard_map/ppermute | solution.py:67
  11.7 5.5 %collective-permute-start.2 = (bf16[256,384]{1,0:T(8,128)(2,1)S(1)}, bf16[256,384]{1,0:T(8,128)(2,1)S(1)}, u32[]{:S(2)}, u32[]{:S(2)}) collective-permute-start(bf16[256,384]{1,0:T(8,128)(2,1)S(1)} %get-tuple-element.36), channel_id=1, source_target_pairs={{0,3},{1,0},{2,1},{3,2},{4,7},{5,4},{6,5},{7,6},{8,11},{9,8},{10,9... | collective-permute-start | bytes 589832 | tf_op jit(solution)/shard_map/ppermute | solution.py:67
  17.2 11.1 %collective-permute-start.3 = (bf16[1040,256]{1,0:T(8,128)(2,1)S(1)}, bf16[1040,256]{1,0:T(8,128)(2,1)S(1)}, u32[]{:S(2)}, u32[]{:S(2)}) collective-permute-start(bf16[1040,256]{1,0:T(8,128)(2,1)S(1)} %stack_rows.1.refs_4_), channel_id=1, source_target_pairs={{0,4},{1,5},{2,6},{3,7},{4,8},{5,9},{6,10},{7,11},{8,12},{9,13},{1... | collective-permute-start | bytes 1597448 | tf_op jit(solution)/shard_map/ppermute | solution.py:681
  18.3 14.7 %collective-permute-start.4 = (bf16[1040,256]{1,0:T(8,128)(2,1)S(1)}, bf16[1040,256]{1,0:T(8,128)(2,1)S(1)}, u32[]{:S(2)}, u32[]{:S(2)}) collective-permute-start(bf16[1040,256]{1,0:T(8,128)(2,1)S(1)} %stack_rows.1.refs_4_), channel_id=1, source_target_pairs={{0,12},{1,13},{2,14},{3,15},{4,0},{5,1},{6,2},{7,3},{8,4},{9,5},{1... | collective-permute-start | bytes 1597448 | tf_op jit(solution)/shard_map/ppermute | solution.py:681
  20.0 16.1 %collective-permute-start.5 = (bf16[1040,256]{1,0:T(8,128)(2,1)S(1)}, bf16[1040,256]{1,0:T(8,128)(2,1)S(1)}, u32[]{:S(2)}, u32[]{:S(2)}) collective-permute-start(bf16[1040,256]{1,0:T(8,128)(2,1)S(1)} %stack_rows.1.refs_4_), channel_id=1, source_target_pairs={{0,8},{1,9},{2,10},{3,11},{4,12},{5,13},{6,14},{7,15},{8,0},{9,1},... | collective-permute-start | bytes 1597448 | tf_op jit(solution)/shard_map/ppermute | solution.py:681
  24.6 6.7 %collective-permute-start.6 = (bf16[16,1536]{1,0:T(8,128)(2,1)S(1)}, bf16[16,1536]{1,0:T(8,128)(2,1)S(1)}, u32[]{:S(2)}, u32[]{:S(2)}) collective-permute-start(bf16[16,1536]{1,0:T(8,128)(2,1)S(1)} %get-tuple-element.40), channel_id=1, source_target_pairs={{0,1},{1,2},{2,3},{3,4},{4,5},{5,6},{6,7},{7,8},{8,9},{9,10},{10,1... | collective-permute-start | bytes 147464 | tf_op jit(solution)/shard_map/ppermute | solution.py:685
  27.0 6.0 %collective-permute-start.7 = (bf16[16,1536]{1,0:T(8,128)(2,1)S(1)}, bf16[16,1536]{1,0:T(8,128)(2,1)S(1)}, u32[]{:S(2)}, u32[]{:S(2)}) collective-permute-start(bf16[16,1536]{1,0:T(8,128)(2,1)S(1)} %get-tuple-element.41), channel_id=1, source_target_pairs={{1,0},{2,1},{3,2},{4,3},{5,4},{6,5},{7,6},{8,7},{9,8},{10,9},{11,1... | collective-permute-start | bytes 147464 | tf_op jit(solution)/shard_map/ppermute | solution.py:686
  39.4 8.0 %collective-permute-start.8 = (bf16[272,256]{1,0:T(8,128)(2,1)S(1)}, bf16[272,256]{1,0:T(8,128)(2,1)S(1)}, u32[]{:S(2)}, u32[]{:S(2)}) collective-permute-start(bf16[272,256]{1,0:T(8,128)(2,1)S(1)} %get-tuple-element.44), channel_id=1, source_target_pairs={{0,3},{1,0},{2,1},{3,2},{4,7},{5,4},{6,5},{7,6},{8,11},{9,8},{10,9... | collective-permute-start | bytes 417800 | tf_op jit(solution)/shard_map/ppermute | solution.py:67
  43.9 5.5 %collective-permute-start.9 = (bf16[272,256]{1,0:T(8,128)(2,1)S(1)}, bf16[272,256]{1,0:T(8,128)(2,1)S(1)}, u32[]{:S(2)}, u32[]{:S(2)}) collective-permute-start(bf16[272,256]{1,0:T(8,128)(2,1)S(1)} %get-tuple-element.45), channel_id=1, source_target_pairs={{0,2},{1,3},{2,0},{3,1},{4,6},{5,7},{6,4},{7,5},{8,10},{9,11},{10,... | collective-permute-start | bytes 417800 | tf_op jit(solution)/shard_map/ppermute | solution.py:67
  44.9 5.9 %collective-permute-start.10 = (bf16[272,256]{1,0:T(8,128)(2,1)S(1)}, bf16[272,256]{1,0:T(8,128)(2,1)S(1)}, u32[]{:S(2)}, u32[]{:S(2)}) collective-permute-start(bf16[272,256]{1,0:T(8,128)(2,1)S(1)} %get-tuple-element.46), channel_id=1, source_target_pairs={{0,1},{1,2},{2,3},{3,0},{4,5},{5,6},{6,7},{7,4},{8,9},{9,10},{10,1... | collective-permute-start | bytes 417800 | tf_op jit(solution)/shard_map/ppermute | solution.py:67
  59.2 10.3 %collective-permute-start.11 = (bf16[4,384,768]{2,1,0:T(8,128)(2,1)}, bf16[4,384,768]{2,1,0:T(8,128)(2,1)S(1)}, u32[]{:S(2)}, u32[]{:S(2)}) collective-permute-start(bf16[4,384,768]{2,1,0:T(8,128)(2,1)} %get-tuple-element.48), channel_id=1, source_target_pairs={{0,16},{16,0},{1,17},{17,1},{2,18},{18,2},{3,19},{19,3},{4,20},{20... | collective-permute-start | bytes 7077896 | tf_op jit(solution)/shard_map/ppermute | solution.py:696
  72.0 22.6 %collective-permute-start.12 = (bf16[384,768]{1,0:T(8,128)(2,1)S(1)}, bf16[384,768]{1,0:T(8,128)(2,1)S(1)}, u32[]{:S(2)}, u32[]{:S(2)}) collective-permute-start(bf16[384,768]{1,0:T(8,128)(2,1)S(1)} %get-tuple-element.50), channel_id=1, source_target_pairs={{0,32},{1,33},{2,34},{3,35},{4,36},{5,37},{6,38},{7,39},{8,40},{9,... | collective-permute-start | bytes 1769480 | tf_op jit(solution)/shard_map/ppermute | solution.py:67
  72.1 22.5 %collective-permute-start.13 = (bf16[384,768]{1,0:T(8,128)(2,1)S(1)}, bf16[384,768]{1,0:T(8,128)(2,1)S(1)}, u32[]{:S(2)}, u32[]{:S(2)}) collective-permute-start(bf16[384,768]{1,0:T(8,128)(2,1)S(1)} %get-tuple-element.51), channel_id=1, source_target_pairs={{0,64},{1,65},{2,66},{3,67},{4,68},{5,69},{6,70},{7,71},{8,72},{9,... | collective-permute-start | bytes 1769480 | tf_op jit(solution)/shard_map/ppermute | solution.py:67
  75.2 19.4 %collective-permute-start.14 = (bf16[384,768]{1,0:T(8,128)(2,1)S(1)}, bf16[384,768]{1,0:T(8,128)(2,1)S(1)}, u32[]{:S(2)}, u32[]{:S(2)}) collective-permute-start(bf16[384,768]{1,0:T(8,128)(2,1)S(1)} %get-tuple-element.52), channel_id=1, source_target_pairs={{0,96},{1,97},{2,98},{3,99},{4,100},{5,101},{6,102},{7,103},{8,104... | collective-permute-start | bytes 1769480 | tf_op jit(solution)/shard_map/ppermute | solution.py:67
  83.8 10.7 %collective-permute-start.15 = (f32[3,768]{1,0:T(4,128)S(1)}, f32[3,768]{1,0:T(4,128)S(1)}, u32[]{:S(2)}, u32[]{:S(2)}) collective-permute-start(f32[3,768]{1,0:T(4,128)S(1)} %get-tuple-element.57), channel_id=1, source_target_pairs={{0,16},{16,0},{1,17},{17,1},{2,18},{18,2},{3,19},{19,3},{4,20},{20... | collective-permute-start | bytes 27656 | tf_op jit(solution)/shard_map/ppermute | solution.py:704
  95.4 6.1 %collective-permute-start.16 = (bf16[112,768]{1,0:T(8,128)(2,1)S(1)}, bf16[112,768]{1,0:T(8,128)(2,1)S(1)}, u32[]{:S(2)}, u32[]{:S(2)}) collective-permute-start(bf16[112,768]{1,0:T(8,128)(2,1)S(1)} %get-tuple-element.59), channel_id=1, source_target_pairs={{0,2},{1,3},{2,0},{3,1},{4,6},{5,7},{6,4},{7,5},{8,10},{9,11},{10,... | collective-permute-start | bytes 516104 | tf_op jit(solution)/shard_map/ppermute | solution.py:67
  97.1 6.3 %collective-permute-start.17 = (bf16[112,768]{1,0:T(8,128)(2,1)S(1)}, bf16[112,768]{1,0:T(8,128)(2,1)S(1)}, u32[]{:S(2)}, u32[]{:S(2)}) collective-permute-start(bf16[112,768]{1,0:T(8,128)(2,1)S(1)} %get-tuple-element.60), channel_id=1, source_target_pairs={{0,1},{1,2},{2,3},{3,0},{4,5},{5,6},{6,7},{7,4},{8,9},{9,10},{10,1... | collective-permute-start | bytes 516104 | tf_op jit(solution)/shard_map/ppermute | solution.py:67
  97.1 6.3 %collective-permute-start.18 = (bf16[112,768]{1,0:T(8,128)(2,1)S(1)}, bf16[112,768]{1,0:T(8,128)(2,1)S(1)}, u32[]{:S(2)}, u32[]{:S(2)}) collective-permute-start(bf16[112,768]{1,0:T(8,128)(2,1)S(1)} %get-tuple-element.61), channel_id=1, source_target_pairs={{0,3},{1,0},{2,1},{3,2},{4,7},{5,4},{6,5},{7,6},{8,11},{9,8},{10,9... | collective-permute-start | bytes 516104 | tf_op jit(solution)/shard_map/ppermute | solution.py:67
  103.5 4.6 %collective-permute-start.21 = (bf16[112,768]{1,0:T(8,128)(2,1)S(1)}, bf16[112,768]{1,0:T(8,128)(2,1)S(1)}, u32[]{:S(2)}, u32[]{:S(2)}) collective-permute-start(bf16[112,768]{1,0:T(8,128)(2,1)S(1)} %add_convert_fusion), channel_id=1, source_target_pairs={{0,12},{1,13},{2,14},{3,15},{4,0},{5,1},{6,2},{7,3},{8,4},{9,5},{1... | collective-permute-start | bytes 516104 | tf_op jit(solution)/shard_map/ppermute | solution.py:67
  103.6 7.9 %collective-permute-start.20 = (bf16[112,768]{1,0:T(8,128)(2,1)S(1)}, bf16[112,768]{1,0:T(8,128)(2,1)S(1)}, u32[]{:S(2)}, u32[]{:S(2)}) collective-permute-start(bf16[112,768]{1,0:T(8,128)(2,1)S(1)} %add_convert_fusion), channel_id=1, source_target_pairs={{0,4},{1,5},{2,6},{3,7},{4,8},{5,9},{6,10},{7,11},{8,12},{9,13},{1... | collective-permute-start | bytes 516104 | tf_op jit(solution)/shard_map/ppermute | solution.py:67
  105.0 6.4 %collective-permute-start.19 = (bf16[112,768]{1,0:T(8,128)(2,1)S(1)}, bf16[112,768]{1,0:T(8,128)(2,1)S(1)}, u32[]{:S(2)}, u32[]{:S(2)}) collective-permute-start(bf16[112,768]{1,0:T(8,128)(2,1)S(1)} %add_convert_fusion), channel_id=1, source_target_pairs={{0,8},{1,9},{2,10},{3,11},{4,12},{5,13},{6,14},{7,15},{8,0},{9,1},... | collective-permute-start | bytes 516104 | tf_op jit(solution)/shard_map/ppermute | solution.py:67
  111.6 5.5 %collective-permute-start.24 = (bf16[96,768]{1,0:T(8,128)(2,1)S(1)}, bf16[96,768]{1,0:T(8,128)(2,1)S(1)}, u32[]{:S(2)}, u32[]{:S(2)}) collective-permute-start(bf16[96,768]{1,0:T(8,128)(2,1)S(1)} %slice.56.refs_0_), channel_id=1, source_target_pairs={{0,3},{1,0},{2,1},{3,2},{4,7},{5,4},{6,5},{7,6},{8,11},{9,8},{10,9... | collective-permute-start | bytes 442376 | tf_op jit(solution)/shard_map/ppermute | solution.py:67
  113.5 5.6 %collective-permute-start.23 = (bf16[96,768]{1,0:T(8,128)(2,1)S(1)}, bf16[96,768]{1,0:T(8,128)(2,1)S(1)}, u32[]{:S(2)}, u32[]{:S(2)}) collective-permute-start(bf16[96,768]{1,0:T(8,128)(2,1)S(1)} %slice.56.refs_0_), channel_id=1, source_target_pairs={{0,2},{1,3},{2,0},{3,1},{4,6},{5,7},{6,4},{7,5},{8,10},{9,11},{10,... | collective-permute-start | bytes 442376 | tf_op jit(solution)/shard_map/ppermute | solution.py:67
  113.7 7.1 %collective-permute-start.22 = (bf16[96,768]{1,0:T(8,128)(2,1)S(1)}, bf16[96,768]{1,0:T(8,128)(2,1)S(1)}, u32[]{:S(2)}, u32[]{:S(2)}) collective-permute-start(bf16[96,768]{1,0:T(8,128)(2,1)S(1)} %slice.56.refs_0_), channel_id=1, source_target_pairs={{0,1},{1,2},{2,3},{3,0},{4,5},{5,6},{6,7},{7,4},{8,9},{9,10},{10,1... | collective-permute-start | bytes 442376 | tf_op jit(solution)/shard_map/ppermute | solution.py:67
  121.6 9.2 %collective-permute-start.27 = (bf16[784,384]{1,0:T(8,128)(2,1)S(1)}, bf16[784,384]{1,0:T(8,128)(2,1)S(1)}, u32[]{:S(2)}, u32[]{:S(2)}) collective-permute-start(bf16[784,384]{1,0:T(8,128)(2,1)S(1)} %join_rows.1.refs_0_), channel_id=1, source_target_pairs={{0,96},{1,97},{2,98},{3,99},{4,100},{5,101},{6,102},{7,103},{8,104... | collective-permute-start | bytes 1806344 | tf_op jit(solution)/shard_map/ppermute | solution.py:67
  122.0 12.9 %collective-permute-start.26 = (bf16[784,384]{1,0:T(8,128)(2,1)S(1)}, bf16[784,384]{1,0:T(8,128)(2,1)S(1)}, u32[]{:S(2)}, u32[]{:S(2)}) collective-permute-start(bf16[784,384]{1,0:T(8,128)(2,1)S(1)} %join_rows.1.refs_0_), channel_id=1, source_target_pairs={{0,64},{1,65},{2,66},{3,67},{4,68},{5,69},{6,70},{7,71},{8,72},{9,... | collective-permute-start | bytes 1806344 | tf_op jit(solution)/shard_map/ppermute | solution.py:67
  123.1 16.0 %collective-permute-start.25 = (bf16[784,384]{1,0:T(8,128)(2,1)S(1)}, bf16[784,384]{1,0:T(8,128)(2,1)S(1)}, u32[]{:S(2)}, u32[]{:S(2)}) collective-permute-start(bf16[784,384]{1,0:T(8,128)(2,1)S(1)} %join_rows.1.refs_0_), channel_id=1, source_target_pairs={{0,32},{1,33},{2,34},{3,35},{4,36},{5,37},{6,38},{7,39},{8,40},{9,... | collective-permute-start | bytes 1806344 | tf_op jit(solution)/shard_map/ppermute | solution.py:67
  123.8 20.8 %collective-permute-start.31 = (bf16[784,384]{1,0:T(8,128)(2,1)S(1)}, bf16[784,384]{1,0:T(8,128)(2,1)S(1)}, u32[]{:S(2)}, u32[]{:S(2)}) collective-permute-start(bf16[784,384]{1,0:T(8,128)(2,1)S(1)} %join_rows.1.refs_0_), channel_id=1, source_target_pairs={{0,16},{16,0},{1,17},{17,1},{2,18},{18,2},{3,19},{19,3},{4,20},{20... | collective-permute-start | bytes 1806344 | tf_op jit(solution)/shard_map/ppermute | solution.py:718
  130.8 15.3 %collective-permute-start.30 = (bf16[784,384]{1,0:T(8,128)(2,1)S(1)}, bf16[784,384]{1,0:T(8,128)(2,1)}, u32[]{:S(2)}, u32[]{:S(2)}) collective-permute-start(bf16[784,384]{1,0:T(8,128)(2,1)S(1)} %collective-permute-done.27.refs_2_), channel_id=1, source_target_pairs={{0,16},{16,0},{1,17},{17,1},{2,18},{18,2},{3,19},{19,3},{4,20},{20... | collective-permute-start | bytes 1806344 | tf_op jit(solution)/shard_map/ppermute | solution.py:718
  134.9 11.3 %collective-permute-start.29 = (bf16[784,384]{1,0:T(8,128)(2,1)S(1)}, bf16[784,384]{1,0:T(8,128)(2,1)}, u32[]{:S(2)}, u32[]{:S(2)}) collective-permute-start(bf16[784,384]{1,0:T(8,128)(2,1)S(1)} %collective-permute-done.26.refs_1_), channel_id=1, source_target_pairs={{0,16},{16,0},{1,17},{17,1},{2,18},{18,2},{3,19},{19,3},{4,20},{20... | collective-permute-start | bytes 1806344 | tf_op jit(solution)/shard_map/ppermute | solution.py:718
  139.1 7.2 %collective-permute-start.28 = (bf16[784,384]{1,0:T(8,128)(2,1)S(1)}, bf16[784,384]{1,0:T(8,128)(2,1)}, u32[]{:S(2)}, u32[]{:S(2)}) collective-permute-start(bf16[784,384]{1,0:T(8,128)(2,1)S(1)} %collective-permute-done.25.refs_0_), channel_id=1, source_target_pairs={{0,16},{16,0},{1,17},{17,1},{2,18},{18,2},{3,19},{19,3},{4,20},{20... | collective-permute-start | bytes 1806344 | tf_op jit(solution)/shard_map/ppermute | solution.py:718
  (7 other events, 52.9 us)

commit v6 on v5

--- a/solution.py
+++ b/solution.py
@@ -131,11 +131,11 @@
     )(at, tokens, query_weight, key_weight, value_weight)
 
 
-def stack_rows(parts):
+def stack_rows(parts, behind):
     rows = parts[0].shape[0]
 
     def kernel(*refs):
-        ins, out = refs[:4], refs[4]
+        ins, out = refs[:4], refs[5]
         row = lax.broadcasted_iota(jnp.int32, (TAIL, 128), 0)
         tail = jnp.zeros((TAIL, 128), F32)
         for d in range(4):
@@ -150,11 +150,11 @@
     return pl.pallas_call(
         kernel,
         out_shape=jax.ShapeDtypeStruct((4 * rows + TAIL, 256), BF),
-        in_specs=[VMEM] * 4,
+        in_specs=[VMEM] * 4 + [ANY],
         out_specs=VMEM,
         compiler_params=params(8),
         name="stack_rows",
-    )(*parts)
+    )(*parts, behind)
 
 
 def attend(scalars, near, q, pairs, state, behind=()):
@@ -170,7 +170,7 @@
         q_refs, refs = refs[:4], refs[4:]
         pair_refs, refs = refs[: len(pairs)], refs[len(pairs) :]
         if not first:
-            old, refs = refs[0], refs[1:]
+            old, old_peak, refs = refs[0], refs[1], refs[2:]
         refs = refs[len(behind) :]
         lane = lax.broadcasted_iota(jnp.int32, (width, 256), 1)
         place = lax.broadcasted_iota(jnp.int32, (1, rows), 1)
@@ -217,9 +217,6 @@
             edge_out = shares(edge_sums)
             row = lax.broadcasted_iota(jnp.int32, (TAIL, 256), 0)
 
-        column = lax.broadcasted_iota(jnp.int32, (rows, 256), 1)
-        if not last:
-            refs[1][...] = jnp.zeros((8, 128), F32)
         pair_ref = pair_refs[-1]
         keep = masks(near)
         values = values_of(pair_ref)
@@ -229,31 +226,32 @@
             for k in range(0, rows, strip):
                 cut = slice(k, k + strip)
                 scores = jnp.where(keep, score_ref[i, cut, :], -1e30)
-                peak = jnp.max(scores, axis=1, keepdims=True)
+                peak = jnp.broadcast_to(jnp.max(scores, axis=1, keepdims=True), (strip, 128))
                 if not first:
-                    peak = jnp.maximum(peak, old[i * rows + k : i * rows + k + strip, DV + 1 : DV + 2])
-                prob_ref[i, cut, :] = jnp.exp(scores - peak).astype(BF)
-                peak_ref[i, cut, :] = jnp.broadcast_to(peak, (strip, 128))
+                    peak = jnp.maximum(peak, old_peak[i * rows + k : i * rows + k + strip, :])
+                across = jnp.concatenate([peak] * (width // 128), axis=1)
+                prob_ref[i, cut, :] = jnp.exp(scores - across).astype(BF)
+                peak_ref[i, cut, :] = peak
             update = jnp.dot(prob_ref[i], values, preferred_element_type=F32)
-            peak = peak_ref[i, :, :1]
             if not first:
-                sums = old[i * rows : (i + 1) * rows, :]
-                update = update + sums * jnp.exp(sums[:, DV + 1 : DV + 2] - peak)
+                shrink = jnp.exp(old_peak[i * rows : (i + 1) * rows, :] - peak_ref[i])
+                update = update + old[i * rows : (i + 1) * rows, :] * jnp.concatenate([shrink] * 2, axis=1)
             if last:
                 refs[i][:rows, :] = shares(update).astype(BF)
                 ends = jnp.where(row == 0, edge_out[i : i + 1], jnp.zeros((TAIL, 256), F32))
                 ends = jnp.where(row == 1, edge_out[4 + i : 5 + i], ends)
                 refs[i][rows:, :] = ends.astype(BF)
             else:
-                refs[0][i * rows : (i + 1) * rows, :] = jnp.where(column == DV + 1, peak, update)
+                refs[0][i * rows : (i + 1) * rows, :] = update
+                refs[1][i * rows : (i + 1) * rows, :] = peak_ref[i]
 
     ins = [*q, *pairs]
     if not first:
-        ins += [state]
+        ins += [*state]
     if last:
         outs = [jax.ShapeDtypeStruct((rows + TAIL, 256), BF)] * 4
     else:
-        outs = [jax.ShapeDtypeStruct((4 * rows, 256), F32), jax.ShapeDtypeStruct((8, 128), F32)]
+        outs = [jax.ShapeDtypeStruct((4 * rows, n), F32) for n in (256, 128)]
     return pl.pallas_call(
         kernel,
         out_shape=outs,
@@ -303,7 +301,7 @@
     return pl.pallas_call(
         kernel,
         out_shape=[jax.ShapeDtypeStruct((TAIL, columns), BF)] * 2,
-        in_specs=[VMEM, ANY, ANY, ANY],
+        in_specs=[ANY] * 4,
         out_specs=[VMEM] * 2,
         scratch_shapes=[pltpu.VMEM((6, TAIL, columns), BF), pltpu.SemaphoreType.DMA((6,))],
         compiler_params=params(53),
@@ -465,16 +463,23 @@
     )(scalars, *back, before, after, depth_weight, tokens, skipped, out_heads, turned)
 
 
-def backward(scalars, ours, up, upstream, before, after, point_weight, depth_weight, behind, whole=None):
+def backward(scalars, theirs, ours, upstream, before, after, point_weight, depth_weight, behind):
     fine, columns = upstream.shape
     half = columns // 2
     steps = half // WIDE
 
-    def side(s_ref):
-        return s_ref[1] if ours else 1 - s_ref[1]
-
-    def kernel(s_ref, up_ref, g_ref, low_ref, high_ref, pw_ref, dw_ref, *refs):
-        gs_ref, gd_ref, grad, upper, ends = refs[-5:]
+    def kernel(s_ref, theirs_ref, ours_ref, g_ref, low_ref, high_ref, pw_ref, dw_ref, behind_ref, *refs):
+        gs_ref, gd_theirs, gd_ours, grad, upper, ends, up_ref = refs
+        j = pl.program_id(0)
+
+        @pl.when(j < steps)
+        def _():
+            up_ref[...] = theirs_ref[...]
+
+        @pl.when(j >= steps)
+        def _():
+            up_ref[...] = ours_ref[...]
+
         dims = (((1,), (1,)), ((), ()))
 
         @pl.when(pl.program_id(0) == 0)
@@ -507,52 +512,69 @@
                 term = taps[t] * mid
                 for r in range(0, STRIP, 8):
                     sums[t] = sums[t] + term[r : r + 8]
-        for t in range(3):
-            gd_ref[t : t + 1, :] = jnp.sum(sums[t], axis=0, keepdims=True)
+        depth = [jnp.sum(total, axis=0, keepdims=True) for total in sums]
+        for ref, mine in ((gd_theirs, j < steps), (gd_ours, j >= steps)):
+
+            @pl.when(mine)
+            def _():
+                for t in range(3):
+                    ref[t : t + 1, :] = depth[t]
+
         for k in range(0, fine, STRIP):
             near = grad[8 + k : 24 + k + STRIP, :]
             gs_ref[k : k + STRIP, :] = (
                 w[0] * near[9 : 9 + STRIP] + w[1] * near[8 : 8 + STRIP] + w[2] * near[7 : 7 + STRIP]
             ).astype(BF)
 
-    def cols(count, full):
-        return pl.BlockSpec((count, WIDE), lambda j, s_ref: (0, (side(s_ref) * steps if full else 0) + j))
+    def block(j, s_ref):
+        return jnp.where(j < steps, (1 - s_ref[1]) * steps + j, s_ref[1] * steps + j - steps)
+
+    def cols(count):
+        return pl.BlockSpec((count, WIDE), lambda j, s_ref: (0, block(j, s_ref)))
+
+    def early(count):
+        return pl.BlockSpec((count, WIDE), lambda j, s_ref: (0, jnp.minimum(j, steps - 1)))
+
+    def late(count):
+        return pl.BlockSpec((count, WIDE), lambda j, s_ref: (0, jnp.maximum(j - steps, 0)))
 
     def flat(count):
         return pl.BlockSpec((count, columns), lambda j, s_ref: (0, 0))
 
-    ins = [up, upstream, before, after, point_weight, depth_weight, behind]
-    if whole is not None:
-        ins.append(whole)
-    return pl.pallas_call(
-        kernel,
-        out_shape=[jax.ShapeDtypeStruct((fine, columns), BF), jax.ShapeDtypeStruct((3, half), F32)],
+    return pl.pallas_call(
+        kernel,
+        out_shape=[
+            jax.ShapeDtypeStruct((fine, columns), BF),
+            jax.ShapeDtypeStruct((3, half), F32),
+            jax.ShapeDtypeStruct((3, half), F32),
+        ],
         grid_spec=pltpu.PrefetchScalarGridSpec(
             num_scalar_prefetch=1,
-            grid=(steps,),
+            grid=(2 * steps,),
             in_specs=[
-                cols(fine + 2 * TAIL, False),
+                early(fine + 2 * TAIL),
+                late(fine + 2 * TAIL),
                 flat(fine),
                 flat(TAIL),
                 flat(TAIL),
-                pl.BlockSpec((WIDE, columns), lambda j, s_ref: (side(s_ref) * steps + j, 0)),
-                cols(3, True),
-            ]
-            + [ANY] * (len(ins) - 6),
-            out_specs=[cols(fine, True), cols(3, False)],
+                pl.BlockSpec((WIDE, columns), lambda j, s_ref: (block(j, s_ref), 0)),
+                cols(3),
+                ANY,
+            ],
+            out_specs=[cols(fine), early(3), late(3)],
             scratch_shapes=[
                 pltpu.VMEM((fine + 2 * TAIL, WIDE), F32),
                 pltpu.VMEM((fine, WIDE), F32),
                 pltpu.VMEM((TAIL, columns), BF),
+                pltpu.VMEM((fine + 2 * TAIL, WIDE), BF),
             ],
         ),
-        input_output_aliases={} if whole is None else {8: 0},
         compiler_params=params(48),
         cost_estimate=pl.CostEstimate(
-            flops=fine * columns * columns, bytes_accessed=6 << 20, transcendentals=fine * half
+            flops=2 * fine * columns * columns, bytes_accessed=11 << 20, transcendentals=fine * columns
         ),
         name="backward",
-    )(scalars, *ins)
+    )(scalars, theirs, ours, upstream, before, after, point_weight, depth_weight, behind)
 
 
 def product(scalars, act, turned, steps, arrived):
@@ -577,66 +599,68 @@
     )(scalars, act, turned, arrived)
 
 
-def split_rows(at, got, rider):
+def split_rows(at, got):
     rows, columns = got[0].shape
     slim = rows // 4
 
     def kernel(at_ref, *refs):
-        ins, rider_ref, outs = refs[:4], refs[4], refs[5:]
+        ins, outs = refs[:4], refs[4:]
         for d in range(4):
             take = pl.ds(pl.multiple_of((Spot(at_ref).second_at + d) % 4 * slim, 16), slim)
-            outs[d][:slim, :] = total_of([r[take, :] for r in ins]).astype(BF)
-            outs[d][slim:, :] = rider_ref[...]
-
-    return pl.pallas_call(
-        kernel,
-        out_shape=[jax.ShapeDtypeStruct((slim + TAIL, columns), BF)] * 4,
-        in_specs=[SMEM] + [VMEM] * 5,
+            outs[d][...] = total_of([r[take, :] for r in ins]).astype(BF)
+
+    return pl.pallas_call(
+        kernel,
+        out_shape=[jax.ShapeDtypeStruct((slim, columns), BF)] * 4,
+        in_specs=[SMEM] + [VMEM] * 4,
         out_specs=[VMEM] * 4,
         compiler_params=params(10),
         name="split_rows",
-    )(at, *got, rider)
-
-
-def join_rows(at, got, rider):
-    slim, columns = got[0].shape
+    )(at, *got)
+
+
+def join_rows(at, got):
+    slim, columns = got[0].shape[0] - TAIL, got[0].shape[1]
+    quarter = 4 * slim
 
     def kernel(at_ref, *refs):
-        ins, rider_ref, out, held = refs[:4], refs[4], refs[5], refs[6]
+        ins, upper, lower, held = refs[:4], refs[4], refs[5], refs[6]
         for d in range(4):
             put = pl.ds(pl.multiple_of((Spot(at_ref).second_at + 4 - d) % 4 * slim, 16), slim)
-            held[put, :] = ins[d][...]
-        out[:columns, :] = held[...].T
-        last = rider_ref[...].astype(F32)[:8]
-        out[columns:, :] = jnp.concatenate([last[:, : 4 * slim], last[:, 4 * slim :]], axis=0).astype(BF)
-
-    return pl.pallas_call(
-        kernel,
-        out_shape=jax.ShapeDtypeStruct((columns + TAIL, 4 * slim), BF),
-        in_specs=[SMEM] + [VMEM] * 5,
-        out_specs=VMEM,
-        scratch_shapes=[pltpu.VMEM((4 * slim, columns), BF)],
+            held[put, :] = ins[d][:slim, :]
+        turned = held[...].T
+        upper[...] = turned[: columns // 2]
+        lower[: columns // 2, :] = turned[columns // 2 :]
+        last = total_of([r[slim:, :] for r in ins])[:8]
+        lower[columns // 2 :, :] = jnp.concatenate([last[:, :quarter], last[:, quarter:]], axis=0).astype(BF)
+
+    return pl.pallas_call(
+        kernel,
+        out_shape=[jax.ShapeDtypeStruct((columns // 2 + n, quarter), BF) for n in (0, TAIL)],
+        in_specs=[SMEM] + [VMEM] * 4,
+        out_specs=[VMEM] * 2,
+        scratch_shapes=[pltpu.VMEM((quarter, columns), BF)],
         compiler_params=params(10),
         name="join_rows",
-    )(at, *got, rider)
-
-
-def lay_out(scalars, steps, own, other, whole=None):
-    half, quarter = own[0].shape[0] - TAIL, own[0].shape[1]
-    count = len(steps)
+    )(at, *got)
+
+
+def lay_out(scalars, own, other):
+    part, quarter = own[0][0].shape
+    half = 2 * part
 
     def kernel(s_ref, *refs):
         out, sems = refs[-2:]
         spot = Spot(s_ref)
         copies = []
-        for n in range(2 * count):
-            mine = n < count
-            down = (spot.core if mine else 1 - spot.core) * half
-            over = ((spot.first_at if mine else spot.their_first) + 4 - steps[n % count]) % 4 * quarter
+        for n in range(16):
+            mine, d, low = n < 8, n // 2 % 4, n % 2
+            down = (spot.core if mine else 1 - spot.core) * half + low * part
+            over = ((spot.first_at if mine else spot.their_first) + 4 - d) % 4 * quarter
             copies.append(
                 pltpu.make_async_copy(
-                    refs[n].at[pl.ds(0, half), :],
-                    out.at[pl.ds(pl.multiple_of(down, 16), half), pl.ds(pl.multiple_of(over, 128), quarter)],
+                    refs[n].at[pl.ds(0, part), :],
+                    out.at[pl.ds(pl.multiple_of(down, 16), part), pl.ds(pl.multiple_of(over, 128), quarter)],
                     sems.at[n],
                 )
             )
@@ -645,17 +669,15 @@
         for copy in copies:
             copy.wait()
 
-    extra = [] if whole is None else [whole]
     return pl.pallas_call(
         kernel,
         out_shape=jax.ShapeDtypeStruct((2 * half, 4 * quarter), BF),
-        in_specs=[SMEM] + [VMEM] * (2 * count) + [ANY] * len(extra),
+        in_specs=[SMEM] + [VMEM] * 16,
         out_specs=ANY,
-        scratch_shapes=[pltpu.SemaphoreType.DMA((2 * count,))],
-        input_output_aliases={} if whole is None else {1 + 2 * count: 0},
+        scratch_shapes=[pltpu.SemaphoreType.DMA((16,))],
         compiler_params=params(8),
         name="lay_out",
-    )(scalars, *own, *other, *extra)
+    )(scalars, *[p for pieces in (own, other) for pair in pieces for p in pair])
 
 
 def local(
@@ -676,18 +698,18 @@
     ix, ic, iz, iy = (lax.axis_index(a) for a in AXES)
     scalars = jnp.stack([v.astype(jnp.int32) for v in (ix, ic, iz, iy, valid_bins[0])])
     blocks = project(scalars, tokens, query_weight, key_weight, value_weight)
-    q = exchange(blocks, HEAD_RING)
-    own = stack_rows(q)
-    far = {d: lax.ppermute(own, AXES, turn(ROW_RING, d)) for d in (1, 3, 2)}
-    state, mark = attend(scalars, 0, q, [own], None)
-
-    down, up = edges(mark, tokens, skipped, upstream)
+    down, up = edges(blocks[0], tokens, skipped, upstream)
     before = lax.ppermute(down, ("z", "y"), [(i, i + 1) for i in range(15)])
     after = lax.ppermute(up, ("z", "y"), [(i + 1, i) for i in range(15)])
+    q = exchange(blocks, HEAD_RING)
+    own = stack_rows(q, down)
+    far = {d: lax.ppermute(own, AXES, turn(ROW_RING, d)) for d in (1, 3, 2)}
+    state = attend(scalars, 0, q, [own], None, (before, after))
+
     turned = upstream.T
 
-    state, _ = attend(scalars, 1, q, [far[1]], state)
-    state, _ = attend(scalars, 2, q, [far[3]], state, (before, after))
+    state = attend(scalars, 1, q, [far[1]], state)
+    state = attend(scalars, 2, q, [far[3]], state)
     mixed = attend(scalars, 3, q, [own, far[1], far[3], far[2]], state)
     back = exchange(mixed, HEAD_RING, -1)
     swap = [(0, 1), (1, 0)]
@@ -699,31 +721,36 @@
     piece_3, piece_0 = product(scalars, act, turned, (3, 0), arrived)
     got = exchange([piece_0, piece_1, piece_2, piece_3], SUM_RINGS[0])
 
-    given = (upstream, before, after, point_weight, depth_weight, piece_0)
-    grad_skip, d_theirs = backward(scalars, False, up_theirs, *given)
-    d_arrived = lax.ppermute(d_theirs, "c", swap)
-    grad_skip, d_mine = backward(scalars, True, up_ours, *given, grad_skip)
-    d_sum = d_mine + d_arrived
-    half = columns // 2
+    grad_skip, d_theirs, d_mine = backward(
+        scalars, up_theirs, up_ours, upstream, before, after, point_weight, depth_weight, piece_0
+    )
+    d_sum = d_mine + lax.ppermute(d_theirs, "c", swap)
     rider = jnp.pad(d_sum.astype(BF), ((0, TAIL - 3), (0, 0)))
 
-    slim = columns // 16
-    got = exchange(split_rows(scalars, got, rider), SUM_RINGS[1])
-    got = exchange([total_of(got).astype(BF)] * 4, SUM_RINGS[2])
+    got = exchange(split_rows(scalars, got), SUM_RINGS[1])
+    mixed = jnp.concatenate([total_of(got).astype(BF), rider], axis=0)
+    got = exchange([mixed] * 4, SUM_RINGS[2])
     norm_scale = 1.0 / math.sqrt(128 * fine)
     summed = (total_of(got) * norm_scale).astype(BF)
-    piece, rider = summed[:slim], summed[slim:]
-    joined = join_rows(scalars, exchange([piece] * 4, SUM_RINGS[1]), rider)
-    got = exchange([joined] * 4, SUM_RINGS[0])
-    other = [lax.ppermute(g, "c", swap) for g in got]
-    grad_pointwise = lay_out(scalars, (0,), got[:1], other[:1])
-    grad_pointwise = lay_out(scalars, (1, 2, 3), got[1:], other[1:], grad_pointwise)
-
-    def depth_of(blocks):
-        rows = total_of([b[half:] for b in blocks])
+    upper, lower = join_rows(scalars, exchange([summed] * 4, SUM_RINGS[1]))
+
+    def go(block, step):
+        return lax.ppermute(block, AXES, turn(SUM_RINGS[0], step))
+
+    upper_1, lower_3 = go(upper, 1), go(lower, 3)
+    lower_1, upper_3 = go(lower, 1), go(upper, 3)
+    upper_2, lower_2 = go(upper_1, 1), go(lower_3, 3)
+    own = [(upper, lower), (upper_1, lower_1), (upper_2, lower_2), (upper_3, lower_3)]
+    other = [tuple(lax.ppermute(p, "c", swap) for p in pair) for pair in own]
+    grad_pointwise = lay_out(scalars, own, other)
+
+    half = columns // 2
+
+    def depth_of(pairs):
+        rows = total_of([low[half // 2 :] for _, low in pairs])
         return jnp.concatenate([rows[:3], rows[8:11]], axis=1)
 
-    d_own, d_other = depth_of(got), depth_of(other)
+    d_own, d_other = depth_of(own), depth_of(other)
     grad_depth = jnp.concatenate(
         [jnp.where(ic == 0, d_own, d_other), jnp.where(ic == 0, d_other, d_own)], axis=1
     )

time: 152 us -> 153 us (level)
  waiting for transfers between devices: 30.4 us -> 38.6 us
  Pallas kernels: 56.1 us -> 50 us
    ppermute x5 -> x15, waiting for transfers between devices: 0.15 us -> 6.48 us  [the longest x6 5.61 us: go(): return lax.ppermute(block, AXES, turn(SUM_RINGS[0], step))]
    ppermute x1, waiting for transfers between devices: 0.01 us -> 6.34 us  [local(): before = lax.ppermute(down, ('z', 'y'), [(i, i + 1) for i in range(15)])]
    ppermute x5 -> x15, starting transfers between devices: 20.2 us -> 26.5 us  [the longest x8 14.8 us: local(): other = [tuple((lax.ppermute(p, 'c', swap) for p in pair)) for pair in own]]
    ppermute x21 -> x18, waiting for transfers between devices: 28.7 us -> 23.6 us  [exchange(): got[d] = lax.ppermute(pieces[d], AXES, turn(axes, sign * d))]
    ppermute x21 -> x18, starting transfers between devices: 26.1 us -> 22.5 us  [exchange(): got[d] = lax.ppermute(pieces[d], AXES, turn(axes, sign * d))]
    ppermute x1, starting transfers between devices: 4.4 us -> 2.13 us  [local(): arrived = lax.ppermute(sent, 'c', swap)]
    pallas_call x2 -> x1, Pallas kernels: 15.4 us -> 13.2 us  [backward(): pl.pallas_call(kernel, out_shape=[jax.ShapeDtypeStruct((fine, columns), B...]
    pallas_call x2 -> x1, Pallas kernels: 4.87 us -> 2.86 us  [lay_out(): pl.pallas_call(kernel, out_shape=jax.ShapeDtypeStruct((2 * half, 4 * quar...]
  transfers between devices with their start and end apart: 32 -> 39, of which waited for: 16 -> 18; matrix products, arithmetic and copies ran while one was open for 1% -> 1% of each run, Pallas kernels for 22% -> 19%
where the time goes in v6:
time: 153 us
  starting transfers between devices  58.9 us (38%)
  Pallas kernels  50 us (33%)
  waiting for transfers between devices  38.6 us (25%)
  local copies, waits for them, and re-layouts  2.82 us (2%)
  between operations  1.77 us (1%)
    ppermute x18, waiting for transfers between devices, exchange(): got[d] = lax.ppermute(pieces[d], AXES, turn(axes, sign * d))  23.6 us
    ppermute x18, starting transfers between devices, exchange(): got[d] = lax.ppermute(pieces[d], AXES, turn(axes, sign * d))  22.5 us
    ppermute x8, starting transfers between devices, local(): other = [tuple((lax.ppermute(p, 'c', swap) for p in pair)) for pair in own]  14.8 us
    pallas_call x2, Pallas kernels, forward(): pl.pallas_call(kernel, out_shape=outs, grid_spec=pltpu.PrefetchScalarGrid...  14.3 us
    pallas_call x1, Pallas kernels, backward(): pl.pallas_call(kernel, out_shape=[jax.ShapeDtypeStruct((fine, columns), B...  13.2 us
    pallas_call x4, Pallas kernels, attend(): pl.pallas_call(kernel, out_shape=outs, in_specs=[SMEM] + [VMEM] * len(ins...  9.85 us
    ppermute x6, starting transfers between devices, go(): return lax.ppermute(block, AXES, turn(SUM_RINGS[0], step))  8.71 us
    ppermute x1, waiting for transfers between devices, local(): before = lax.ppermute(down, ('z', 'y'), [(i, i + 1) for i in range(15)])  6.34 us
  transfers between devices with their start and end apart: 39, of which 18 were waited for; matrix products, arithmetic and copies ran while one was open for 1% of the time, Pallas kernels for 19%

profile of v6, /device:TPU:1, one launch (start us, length us, event | category | flops | bytes accessed | tf_op | source)
XLA Modules:
  0.0 153.0 jit_solution(13402351307968360083)
XLA Ops:
  1.4 4.5 %project.1 = (bf16[256,384]{1,0:T(8,128)(2,1)S(1)}, bf16[256,384]{1,0:T(8,128)(2,1)S(1)}, bf16[256,384]{1,0:T(8,128)(2,1)S(1)}, bf16[256,384]{1,0:T(8,128)(2,1)S(1)}) custom-call(s32[5]{0:T(128)S(1)} %stack.19.at_ref.s_ref, bf16[256,1536]{1,0:T(8,128)(2,1)} %bitcast.14, bf16[1536,256]{1,0:T(8,128)(2,1)} %wq_hbm.1, bf16[1536,256]{1,0:T(8,128)(2,1)} %wk_hbm.1, ...), custom_call_target="tpu_custom_call" | custom-call | tf_op jit(solution)/shard_map/project/pallas_call | solution.py:116
  5.9 2.5 %collective-permute-start = (bf16[256,384]{1,0:T(8,128)(2,1)S(1)}, bf16[256,384]{1,0:T(8,128)(2,1)S(1)}, u32[]{:S(2)}, u32[]{:S(2)}) collective-permute-start(bf16[256,384]{1,0:T(8,128)(2,1)S(1)} %get-tuple-element.37), channel_id=1, source_target_pairs={{0,1},{1,2},{2,3},{3,0},{4,5},{5,6},{6,7},{7,4},{8,9},{9,10},{10,1... | collective-permute-start | bytes 589832 | tf_op jit(solution)/shard_map/ppermute | solution.py:67
  8.4 3.3 %collective-permute-start.1 = (bf16[256,384]{1,0:T(8,128)(2,1)S(1)}, bf16[256,384]{1,0:T(8,128)(2,1)S(1)}, u32[]{:S(2)}, u32[]{:S(2)}) collective-permute-start(bf16[256,384]{1,0:T(8,128)(2,1)S(1)} %get-tuple-element.38), channel_id=1, source_target_pairs={{0,2},{1,3},{2,0},{3,1},{4,6},{5,7},{6,4},{7,5},{8,10},{9,11},{10,... | collective-permute-start | bytes 589832 | tf_op jit(solution)/shard_map/ppermute | solution.py:67
  13.8 3.3 %collective-permute-done.1.refs_2_ = bf16[256,384]{1,0:T(8,128)(2,1)S(1)} collective-permute-done((bf16[256,384]{1,0:T(8,128)(2,1)S(1)}, bf16[256,384]{1,0:T(8,128)(2,1)S(1)}, u32[]{:S(2)}, u32[]{:S(2)}) %collective-permute-start.1) | collective-permute-done | bytes 196640 | tf_op jit(solution)/shard_map/ppermute | solution.py:67
  21.4 2.3 %collective-permute-start.6 = (bf16[16,1536]{1,0:T(8,128)(2,1)S(1)}, bf16[16,1536]{1,0:T(8,128)(2,1)S(1)}, u32[]{:S(2)}, u32[]{:S(2)}) collective-permute-start(bf16[16,1536]{1,0:T(8,128)(2,1)S(1)} %get-tuple-element.40.refs_4_), channel_id=1, source_target_pairs={{0,1},{1,2},{2,3},{3,4},{4,5},{5,6},{6,7},{7,8},{8,9},{9,10},{10,1... | collective-permute-start | bytes 147464 | tf_op jit(solution)/shard_map/ppermute | solution.py:702
  25.0 6.3 %collective-permute-done.6.refs_5_.low_ref = bf16[16,1536]{1,0:T(8,128)(2,1)S(1)} collective-permute-done((bf16[16,1536]{1,0:T(8,128)(2,1)S(1)}, bf16[16,1536]{1,0:T(8,128)(2,1)S(1)}, u32[]{:S(2)}, u32[]{:S(2)}) %collective-permute-start.6) | collective-permute-done | bytes 49184 | tf_op jit(solution)/shard_map/ppermute | solution.py:702
  31.3 2.2 %collective-permute-done.7.refs_6_.high_ref = bf16[16,1536]{1,0:T(8,128)(2,1)S(1)} collective-permute-done((bf16[16,1536]{1,0:T(8,128)(2,1)S(1)}, bf16[16,1536]{1,0:T(8,128)(2,1)S(1)}, u32[]{:S(2)}, u32[]{:S(2)}) %collective-permute-start.7) | collective-permute-done | bytes 49184 | tf_op jit(solution)/shard_map/ppermute | solution.py:703
  33.5 2.2 %attend.4 = (f32[1024,256]{1,0:T(8,128)S(1)}, f32[1024,128]{1,0:T(8,128)S(1)}) custom-call(s32[5]{0:T(128)S(1)} %stack.19.at_ref.s_ref, bf16[256,384]{1,0:T(8,128)(2,1)S(1)} %get-tuple-element.36.mark_ref.refs_0_, bf16[256,384]{1,0:T(8,128)(2,1)S(1)} %collective-permute-done.refs_1_, bf16[256,384]{1,0:T(8,128)(2,1)S(1)} %collective-permute-done.1.refs_2_, ...), custom_call_target="tpu_custom_call" | custom-call | flops 1073741824 | bytes 4194304 | tf_op jit(solution)/shard_map/attend/pallas_call | solution.py:255
  35.7 2.2 %attend.5 = (f32[1024,256]{1,0:T(8,128)S(1)}, f32[1024,128]{1,0:T(8,128)S(1)}) custom-call(s32[5]{0:T(128)S(1)} %stack.19.at_ref.s_ref, bf16[256,384]{1,0:T(8,128)(2,1)S(1)} %get-tuple-element.36.mark_ref.refs_0_, bf16[256,384]{1,0:T(8,128)(2,1)S(1)} %collective-permute-done.refs_1_, bf16[256,384]{1,0:T(8,128)(2,1)S(1)} %collective-permute-done.1.refs_2_, ...), custom_call_target="tpu_custom_call" | custom-call | flops 1073741824 | bytes 4194304 | tf_op jit(solution)/shard_map/attend/pallas_call | solution.py:255
  38.0 2.2 %attend.6 = (f32[1024,256]{1,0:T(8,128)S(1)}, f32[1024,128]{1,0:T(8,128)S(1)}) custom-call(s32[5]{0:T(128)S(1)} %stack.19.at_ref.s_ref, bf16[256,384]{1,0:T(8,128)(2,1)S(1)} %get-tuple-element.36.mark_ref.refs_0_, bf16[256,384]{1,0:T(8,128)(2,1)S(1)} %collective-permute-done.refs_1_, bf16[256,384]{1,0:T(8,128)(2,1)S(1)} %collective-permute-done.1.refs_2_, ...), custom_call_target="tpu_custom_call" | custom-call | flops 1073741824 | bytes 4194304 | tf_op jit(solution)/shard_map/attend/pallas_call | solution.py:255
  40.3 3.2 %attend.7 = (bf16[272,256]{1,0:T(8,128)(2,1)S(1)}, bf16[272,256]{1,0:T(8,128)(2,1)S(1)}, bf16[272,256]{1,0:T(8,128)(2,1)S(1)}, bf16[272,256]{1,0:T(8,128)(2,1)S(1)}) custom-call(s32[5]{0:T(128)S(1)} %stack.19.at_ref.s_ref, bf16[256,384]{1,0:T(8,128)(2,1)S(1)} %get-tuple-element.36.mark_ref.refs_0_, bf16[256,384]{1,0:T(8,128)(2,1)S(1)} %collective-permute-done.refs_1_, ...), custom_call_target="tpu_custom_call" | custom-call | flops 1073741824 | bytes 4194304 | tf_op jit(solution)/shard_map/attend/pallas_call | solution.py:255
  43.4 3.3 %collective-permute-start.8 = (bf16[272,256]{1,0:T(8,128)(2,1)S(1)}, bf16[272,256]{1,0:T(8,128)(2,1)S(1)}, u32[]{:S(2)}, u32[]{:S(2)}) collective-permute-start(bf16[272,256]{1,0:T(8,128)(2,1)S(1)} %get-tuple-element.49), channel_id=1, source_target_pairs={{0,3},{1,0},{2,1},{3,2},{4,7},{5,4},{6,5},{7,6},{8,11},{9,8},{10,9... | collective-permute-start | bytes 417800 | tf_op jit(solution)/shard_map/ppermute | solution.py:67
  50.2 2.0 %collective-permute-done.9.b2 = bf16[272,256]{1,0:T(8,128)(2,1)S(1)} collective-permute-done((bf16[272,256]{1,0:T(8,128)(2,1)S(1)}, bf16[272,256]{1,0:T(8,128)(2,1)S(1)}, u32[]{:S(2)}, u32[]{:S(2)}) %collective-permute-start.9) | collective-permute-done | bytes 139296 | tf_op jit(solution)/shard_map/ppermute | solution.py:67
  53.9 8.4 %forward.3 = (bf16[544,768]{1,0:T(8,128)(2,1)}, bf16[4,384,768]{2,1,0:T(8,128)(2,1)}) custom-call(s32[5]{0:T(128)S(1)} %stack.19.at_ref.s_ref, bf16[272,256]{1,0:T(8,128)(2,1)S(1)} %get-tuple-element.48.b0, bf16[272,256]{1,0:T(8,128)(2,1)S(1)} %collective-permute-done.8.b1, bf16[272,256]{1,0:T(8,128)(2,1)S(1)} %collective-permute-done.9.b2, ...), custom_call_target="tpu_custom_call" | custom-call | flops 2415919104 | bytes 9437184 | tf_op jit(solution)/shard_map/forward/pallas_call | solution.py:446
  62.3 2.1 %collective-permute-start.11 = (bf16[4,384,768]{2,1,0:T(8,128)(2,1)}, bf16[4,384,768]{2,1,0:T(8,128)(2,1)S(1)}, u32[]{:S(2)}, u32[]{:S(2)}) collective-permute-start(bf16[4,384,768]{2,1,0:T(8,128)(2,1)} %get-tuple-element.53), channel_id=1, source_target_pairs={{0,16},{16,0},{1,17},{17,1},{2,18},{18,2},{3,19},{19,3},{4,20},{20... | collective-permute-start | bytes 7077896 | tf_op jit(solution)/shard_map/ppermute | solution.py:718
  64.5 5.9 %forward.2 = (bf16[544,768]{1,0:T(8,128)(2,1)}, bf16[512,768]{1,0:T(8,128)(2,1)}) custom-call(s32[5]{0:T(128)S(1)} %stack.19.at_ref.s_ref, bf16[272,256]{1,0:T(8,128)(2,1)S(1)} %get-tuple-element.48.b0, bf16[272,256]{1,0:T(8,128)(2,1)S(1)} %collective-permute-done.8.b1, bf16[272,256]{1,0:T(8,128)(2,1)S(1)} %collective-permute-done.9.b2, ...), custom_call_target="tpu_custom_call" | custom-call | flops 2415919104 | bytes 9437184 | tf_op jit(solution)/shard_map/forward/pallas_call | solution.py:446
  77.0 13.2 %backward.1 = (bf16[512,1536]{1,0:T(8,128)(2,1)}, f32[3,768]{1,0:T(4,128)S(1)}, f32[3,768]{1,0:T(4,128)S(1)}) custom-call(s32[5]{0:T(128)S(1)} %stack.19.at_ref.s_ref, bf16[544,768]{1,0:T(8,128)(2,1)S(1)} %copy-done.4, bf16[544,768]{1,0:T(8,128)(2,1)S(1)} %copy-done.5, bf16[512,1536]{1,0:T(8,128)(2,1)S(1)} %bitcast.13, ...), custom_call_target="tpu_custom_call" | custom-call | flops 2415919104 | bytes 11534336 | tf_op jit(solution)/shard_map/backward/pallas_call | solution.py:544
  90.2 3.0 %collective-permute-start.18 = (f32[3,768]{1,0:T(4,128)S(1)}, f32[3,768]{1,0:T(4,128)S(1)}, u32[]{:S(2)}, u32[]{:S(2)}) collective-permute-start(f32[3,768]{1,0:T(4,128)S(1)} %get-tuple-element.65), channel_id=1, source_target_pairs={{0,16},{16,0},{1,17},{17,1},{2,18},{18,2},{3,19},{19,3},{4,20},{20... | collective-permute-start | bytes 27656 | tf_op jit(solution)/shard_map/ppermute | solution.py:727
  95.6 2.1 %collective-permute-start.15 = (bf16[96,768]{1,0:T(8,128)(2,1)S(1)}, bf16[96,768]{1,0:T(8,128)(2,1)S(1)}, u32[]{:S(2)}, u32[]{:S(2)}) collective-permute-start(bf16[96,768]{1,0:T(8,128)(2,1)S(1)} %get-tuple-element.59), channel_id=1, source_target_pairs={{0,2},{1,3},{2,0},{3,1},{4,6},{5,7},{6,4},{7,5},{8,10},{9,11},{10,... | collective-permute-start | bytes 442376 | tf_op jit(solution)/shard_map/ppermute | solution.py:67
  98.4 1.9 %collective-permute-done.16 = bf16[96,768]{1,0:T(8,128)(2,1)S(1)} collective-permute-done((bf16[96,768]{1,0:T(8,128)(2,1)S(1)}, bf16[96,768]{1,0:T(8,128)(2,1)S(1)}, u32[]{:S(2)}, u32[]{:S(2)}) %collective-permute-start.16) | collective-permute-done | bytes 147488 | tf_op jit(solution)/shard_map/ppermute | solution.py:67
  100.3 1.8 %collective-permute-done.15 = bf16[96,768]{1,0:T(8,128)(2,1)S(1)} collective-permute-done((bf16[96,768]{1,0:T(8,128)(2,1)S(1)}, bf16[96,768]{1,0:T(8,128)(2,1)S(1)}, u32[]{:S(2)}, u32[]{:S(2)}) %collective-permute-start.15) | collective-permute-done | bytes 147488 | tf_op jit(solution)/shard_map/ppermute | solution.py:67
  104.4 2.5 %collective-permute-done.21 = bf16[112,768]{1,0:T(8,128)(2,1)S(1)} collective-permute-done((bf16[112,768]{1,0:T(8,128)(2,1)S(1)}, bf16[112,768]{1,0:T(8,128)(2,1)S(1)}, u32[]{:S(2)}, u32[]{:S(2)}) %collective-permute-start.21) | collective-permute-done | bytes 172064 | tf_op jit(solution)/shard_map/ppermute | solution.py:67
  106.9 3.1 %collective-permute-done.20 = bf16[112,768]{1,0:T(8,128)(2,1)S(1)} collective-permute-done((bf16[112,768]{1,0:T(8,128)(2,1)S(1)}, bf16[112,768]{1,0:T(8,128)(2,1)S(1)}, u32[]{:S(2)}, u32[]{:S(2)}) %collective-permute-start.20) | collective-permute-done | bytes 172064 | tf_op jit(solution)/shard_map/ppermute | solution.py:67
  113.3 4.4 %collective-permute-done.22.refs_1_ = bf16[112,768]{1,0:T(8,128)(2,1)S(1)} collective-permute-done((bf16[112,768]{1,0:T(8,128)(2,1)S(1)}, bf16[112,768]{1,0:T(8,128)(2,1)S(1)}, u32[]{:S(2)}, u32[]{:S(2)}) %collective-permute-start.22) | collective-permute-done | bytes 172064 | tf_op jit(solution)/shard_map/ppermute | solution.py:67
  120.7 4.2 %collective-permute-done.28.refs_7_ = bf16[400,384]{1,0:T(8,128)(2,1)S(1)} collective-permute-done((bf16[400,384]{1,0:T(8,128)(2,1)S(1)}, bf16[400,384]{1,0:T(8,128)(2,1)S(1)}, u32[]{:S(2)}, u32[]{:S(2)}) %collective-permute-start.28) | collective-permute-done | bytes 307232 | tf_op jit(solution)/shard_map/ppermute | solution.py:738
  125.0 2.2 %collective-permute-start.29 = (bf16[400,384]{1,0:T(8,128)(2,1)S(1)}, bf16[400,384]{1,0:T(8,128)(2,1)S(1)}, u32[]{:S(2)}, u32[]{:S(2)}) collective-permute-start(bf16[400,384]{1,0:T(8,128)(2,1)S(1)} %collective-permute-done.28.refs_7_), channel_id=1, source_target_pairs={{0,96},{1,97},{2,98},{3,99},{4,100},{5,101},{6,102},{7,103},{8,104... | collective-permute-start | bytes 921608 | tf_op jit(solution)/shard_map/ppermute | solution.py:738
  127.2 2.7 %collective-permute-start.30 = (bf16[384,384]{1,0:T(8,128)(2,1)S(1)}, bf16[384,384]{1,0:T(8,128)(2,1)S(1)}, u32[]{:S(2)}, u32[]{:S(2)}) collective-permute-start(bf16[384,384]{1,0:T(8,128)(2,1)S(1)} %get-tuple-element.66.refs_0_), channel_id=1, source_target_pairs={{0,96},{1,97},{2,98},{3,99},{4,100},{5,101},{6,102},{7,103},{8,104... | collective-permute-start | bytes 884744 | tf_op jit(solution)/shard_map/ppermute | solution.py:738
  129.8 5.4 %collective-permute-start.32 = (bf16[400,384]{1,0:T(8,128)(2,1)S(1)}, bf16[400,384]{1,0:T(8,128)(2,1)S(1)}, u32[]{:S(2)}, u32[]{:S(2)}) collective-permute-start(bf16[400,384]{1,0:T(8,128)(2,1)S(1)} %get-tuple-element.67.refs_1_), channel_id=1, source_target_pairs={{0,16},{16,0},{1,17},{17,1},{2,18},{18,2},{3,19},{19,3},{4,20},{20... | collective-permute-start | bytes 921608 | tf_op jit(solution)/shard_map/ppermute | solution.py:744
  135.2 2.3 %collective-permute-start.27 = (bf16[384,384]{1,0:T(8,128)(2,1)S(1)}, bf16[384,384]{1,0:T(8,128)(2,1)S(1)}, u32[]{:S(2)}, u32[]{:S(2)}) collective-permute-start(bf16[384,384]{1,0:T(8,128)(2,1)S(1)} %collective-permute-done.25.refs_2_), channel_id=1, source_target_pairs={{0,32},{1,33},{2,34},{3,35},{4,36},{5,37},{6,38},{7,39},{8,40},{9,... | collective-permute-start | bytes 884744 | tf_op jit(solution)/shard_map/ppermute | solution.py:738
  137.5 2.4 %collective-permute-start.38 = (bf16[400,384]{1,0:T(8,128)(2,1)S(1)}, bf16[400,384]{1,0:T(8,128)(2,1)S(1)}, u32[]{:S(2)}, u32[]{:S(2)}) collective-permute-start(bf16[400,384]{1,0:T(8,128)(2,1)S(1)} %collective-permute-done.28.refs_7_), channel_id=1, source_target_pairs={{0,16},{16,0},{1,17},{17,1},{2,18},{18,2},{3,19},{19,3},{4,20},{20... | collective-permute-start | bytes 921608 | tf_op jit(solution)/shard_map/ppermute | solution.py:744
  142.0 5.8 %collective-permute-start.33 = (bf16[384,384]{1,0:T(8,128)(2,1)S(1)}, bf16[384,384]{1,0:T(8,128)(2,1)S(1)}, u32[]{:S(2)}, u32[]{:S(2)}) collective-permute-start(bf16[384,384]{1,0:T(8,128)(2,1)S(1)} %collective-permute-done.25.refs_2_), channel_id=1, source_target_pairs={{0,16},{16,0},{1,17},{17,1},{2,18},{18,2},{3,19},{19,3},{4,20},{20... | collective-permute-start | bytes 884744 | tf_op jit(solution)/shard_map/ppermute | solution.py:744
  149.9 2.9 %lay_out.1 = bf16[1536,1536]{1,0:T(8,128)(2,1)} custom-call(s32[5]{0:T(128)S(1)} %stack.19.at_ref.s_ref, bf16[384,384]{1,0:T(8,128)(2,1)S(1)} %get-tuple-element.66.refs_0_, bf16[400,384]{1,0:T(8,128)(2,1)S(1)} %get-tuple-element.67.refs_1_, bf16[384,384]{1,0:T(8,128)(2,1)S(1)} %collective-permute-done.25.refs_2_, ...), custom_call_target="tpu_custom_call" | custom-call | tf_op jit(solution)/shard_map/lay_out/pallas_call | solution.py:672
  (85 shorter events, 35.1 us)
Async XLA Ops:
  5.9 8.0 %collective-permute-start = (bf16[256,384]{1,0:T(8,128)(2,1)S(1)}, bf16[256,384]{1,0:T(8,128)(2,1)S(1)}, u32[]{:S(2)}, u32[]{:S(2)}) collective-permute-start(bf16[256,384]{1,0:T(8,128)(2,1)S(1)} %get-tuple-element.37), channel_id=1, source_target_pairs={{0,1},{1,2},{2,3},{3,0},{4,5},{5,6},{6,7},{7,4},{8,9},{9,10},{10,1... | collective-permute-start | bytes 589832 | tf_op jit(solution)/shard_map/ppermute | solution.py:67
  8.4 8.8 %collective-permute-start.1 = (bf16[256,384]{1,0:T(8,128)(2,1)S(1)}, bf16[256,384]{1,0:T(8,128)(2,1)S(1)}, u32[]{:S(2)}, u32[]{:S(2)}) collective-permute-start(bf16[256,384]{1,0:T(8,128)(2,1)S(1)} %get-tuple-element.38), channel_id=1, source_target_pairs={{0,2},{1,3},{2,0},{3,1},{4,6},{5,7},{6,4},{7,5},{8,10},{9,11},{10,... | collective-permute-start | bytes 589832 | tf_op jit(solution)/shard_map/ppermute | solution.py:67
  17.2 18.5 %collective-permute-start.3 = (bf16[1040,256]{1,0:T(8,128)(2,1)S(1)}, bf16[1040,256]{1,0:T(8,128)(2,1)S(1)}, u32[]{:S(2)}, u32[]{:S(2)}) collective-permute-start(bf16[1040,256]{1,0:T(8,128)(2,1)S(1)} %stack_rows.1.refs_4_), channel_id=1, source_target_pairs={{0,4},{1,5},{2,6},{3,7},{4,8},{5,9},{6,10},{7,11},{8,12},{9,13},{1... | collective-permute-start | bytes 1597448 | tf_op jit(solution)/shard_map/ppermute | solution.py:706
  18.3 19.7 %collective-permute-start.4 = (bf16[1040,256]{1,0:T(8,128)(2,1)S(1)}, bf16[1040,256]{1,0:T(8,128)(2,1)S(1)}, u32[]{:S(2)}, u32[]{:S(2)}) collective-permute-start(bf16[1040,256]{1,0:T(8,128)(2,1)S(1)} %stack_rows.1.refs_4_), channel_id=1, source_target_pairs={{0,12},{1,13},{2,14},{3,15},{4,0},{5,1},{6,2},{7,3},{8,4},{9,5},{1... | collective-permute-start | bytes 1597448 | tf_op jit(solution)/shard_map/ppermute | solution.py:706
  19.9 20.3 %collective-permute-start.5 = (bf16[1040,256]{1,0:T(8,128)(2,1)S(1)}, bf16[1040,256]{1,0:T(8,128)(2,1)S(1)}, u32[]{:S(2)}, u32[]{:S(2)}) collective-permute-start(bf16[1040,256]{1,0:T(8,128)(2,1)S(1)} %stack_rows.1.refs_4_), channel_id=1, source_target_pairs={{0,8},{1,9},{2,10},{3,11},{4,12},{5,13},{6,14},{7,15},{8,0},{9,1},... | collective-permute-start | bytes 1597448 | tf_op jit(solution)/shard_map/ppermute | solution.py:706
  21.4 9.9 %collective-permute-start.6 = (bf16[16,1536]{1,0:T(8,128)(2,1)S(1)}, bf16[16,1536]{1,0:T(8,128)(2,1)S(1)}, u32[]{:S(2)}, u32[]{:S(2)}) collective-permute-start(bf16[16,1536]{1,0:T(8,128)(2,1)S(1)} %get-tuple-element.40.refs_4_), channel_id=1, source_target_pairs={{0,1},{1,2},{2,3},{3,4},{4,5},{5,6},{6,7},{7,8},{8,9},{9,10},{10,1... | collective-permute-start | bytes 147464 | tf_op jit(solution)/shard_map/ppermute | solution.py:702
  23.7 9.8 %collective-permute-start.7 = (bf16[16,1536]{1,0:T(8,128)(2,1)S(1)}, bf16[16,1536]{1,0:T(8,128)(2,1)S(1)}, u32[]{:S(2)}, u32[]{:S(2)}) collective-permute-start(bf16[16,1536]{1,0:T(8,128)(2,1)S(1)} %get-tuple-element.41), channel_id=1, source_target_pairs={{1,0},{2,1},{3,2},{4,3},{5,4},{6,5},{7,6},{8,7},{9,8},{10,9},{11,1... | collective-permute-start | bytes 147464 | tf_op jit(solution)/shard_map/ppermute | solution.py:703
  43.4 6.8 %collective-permute-start.8 = (bf16[272,256]{1,0:T(8,128)(2,1)S(1)}, bf16[272,256]{1,0:T(8,128)(2,1)S(1)}, u32[]{:S(2)}, u32[]{:S(2)}) collective-permute-start(bf16[272,256]{1,0:T(8,128)(2,1)S(1)} %get-tuple-element.49), channel_id=1, source_target_pairs={{0,3},{1,0},{2,1},{3,2},{4,7},{5,4},{6,5},{7,6},{8,11},{9,8},{10,9... | collective-permute-start | bytes 417800 | tf_op jit(solution)/shard_map/ppermute | solution.py:67
  47.5 6.4 %collective-permute-start.10 = (bf16[272,256]{1,0:T(8,128)(2,1)S(1)}, bf16[272,256]{1,0:T(8,128)(2,1)S(1)}, u32[]{:S(2)}, u32[]{:S(2)}) collective-permute-start(bf16[272,256]{1,0:T(8,128)(2,1)S(1)} %get-tuple-element.51), channel_id=1, source_target_pairs={{0,1},{1,2},{2,3},{3,0},{4,5},{5,6},{6,7},{7,4},{8,9},{9,10},{10,1... | collective-permute-start | bytes 417800 | tf_op jit(solution)/shard_map/ppermute | solution.py:67
  62.3 8.0 %collective-permute-start.11 = (bf16[4,384,768]{2,1,0:T(8,128)(2,1)}, bf16[4,384,768]{2,1,0:T(8,128)(2,1)S(1)}, u32[]{:S(2)}, u32[]{:S(2)}) collective-permute-start(bf16[4,384,768]{2,1,0:T(8,128)(2,1)} %get-tuple-element.53), channel_id=1, source_target_pairs={{0,16},{16,0},{1,17},{17,1},{2,18},{18,2},{3,19},{19,3},{4,20},{20... | collective-permute-start | bytes 7077896 | tf_op jit(solution)/shard_map/ppermute | solution.py:718
  72.8 20.4 %collective-permute-start.12 = (bf16[384,768]{1,0:T(8,128)(2,1)S(1)}, bf16[384,768]{1,0:T(8,128)(2,1)S(1)}, u32[]{:S(2)}, u32[]{:S(2)}) collective-permute-start(bf16[384,768]{1,0:T(8,128)(2,1)S(1)} %get-tuple-element.55), channel_id=1, source_target_pairs={{0,32},{1,33},{2,34},{3,35},{4,36},{5,37},{6,38},{7,39},{8,40},{9,... | collective-permute-start | bytes 1769480 | tf_op jit(solution)/shard_map/ppermute | solution.py:67
  72.9 20.3 %collective-permute-start.13 = (bf16[384,768]{1,0:T(8,128)(2,1)S(1)}, bf16[384,768]{1,0:T(8,128)(2,1)S(1)}, u32[]{:S(2)}, u32[]{:S(2)}) collective-permute-start(bf16[384,768]{1,0:T(8,128)(2,1)S(1)} %get-tuple-element.56), channel_id=1, source_target_pairs={{0,64},{1,65},{2,66},{3,67},{4,68},{5,69},{6,70},{7,71},{8,72},{9,... | collective-permute-start | bytes 1769480 | tf_op jit(solution)/shard_map/ppermute | solution.py:67
  75.7 17.5 %collective-permute-start.14 = (bf16[384,768]{1,0:T(8,128)(2,1)S(1)}, bf16[384,768]{1,0:T(8,128)(2,1)S(1)}, u32[]{:S(2)}, u32[]{:S(2)}) collective-permute-start(bf16[384,768]{1,0:T(8,128)(2,1)S(1)} %get-tuple-element.57), channel_id=1, source_target_pairs={{0,96},{1,97},{2,98},{3,99},{4,100},{5,101},{6,102},{7,103},{8,104... | collective-permute-start | bytes 1769480 | tf_op jit(solution)/shard_map/ppermute | solution.py:67
  90.2 7.5 %collective-permute-start.18 = (f32[3,768]{1,0:T(4,128)S(1)}, f32[3,768]{1,0:T(4,128)S(1)}, u32[]{:S(2)}, u32[]{:S(2)}) collective-permute-start(f32[3,768]{1,0:T(4,128)S(1)} %get-tuple-element.65), channel_id=1, source_target_pairs={{0,16},{16,0},{1,17},{17,1},{2,18},{18,2},{3,19},{19,3},{4,20},{20... | collective-permute-start | bytes 27656 | tf_op jit(solution)/shard_map/ppermute | solution.py:727
  95.6 6.5 %collective-permute-start.15 = (bf16[96,768]{1,0:T(8,128)(2,1)S(1)}, bf16[96,768]{1,0:T(8,128)(2,1)S(1)}, u32[]{:S(2)}, u32[]{:S(2)}) collective-permute-start(bf16[96,768]{1,0:T(8,128)(2,1)S(1)} %get-tuple-element.59), channel_id=1, source_target_pairs={{0,2},{1,3},{2,0},{3,1},{4,6},{5,7},{6,4},{7,5},{8,10},{9,11},{10,... | collective-permute-start | bytes 442376 | tf_op jit(solution)/shard_map/ppermute | solution.py:67
  102.3 7.7 %collective-permute-start.20 = (bf16[112,768]{1,0:T(8,128)(2,1)S(1)}, bf16[112,768]{1,0:T(8,128)(2,1)S(1)}, u32[]{:S(2)}, u32[]{:S(2)}) collective-permute-start(bf16[112,768]{1,0:T(8,128)(2,1)S(1)} %fusion.1), channel_id=1, source_target_pairs={{0,4},{1,5},{2,6},{3,7},{4,8},{5,9},{6,10},{7,11},{8,12},{9,13},{1... | collective-permute-start | bytes 516104 | tf_op jit(solution)/shard_map/ppermute | solution.py:67
  103.8 6.2 %collective-permute-start.19 = (bf16[112,768]{1,0:T(8,128)(2,1)S(1)}, bf16[112,768]{1,0:T(8,128)(2,1)S(1)}, u32[]{:S(2)}, u32[]{:S(2)}) collective-permute-start(bf16[112,768]{1,0:T(8,128)(2,1)S(1)} %fusion.1), channel_id=1, source_target_pairs={{0,8},{1,9},{2,10},{3,11},{4,12},{5,13},{6,14},{7,15},{8,0},{9,1},... | collective-permute-start | bytes 516104 | tf_op jit(solution)/shard_map/ppermute | solution.py:67
  110.1 7.7 %collective-permute-start.22 = (bf16[112,768]{1,0:T(8,128)(2,1)S(1)}, bf16[112,768]{1,0:T(8,128)(2,1)S(1)}, u32[]{:S(2)}, u32[]{:S(2)}) collective-permute-start(bf16[112,768]{1,0:T(8,128)(2,1)S(1)} %multiply_convert_fusion.refs_0_), channel_id=1, source_target_pairs={{0,1},{1,2},{2,3},{3,0},{4,5},{5,6},{6,7},{7,4},{8,9},{9,10},{10,1... | collective-permute-start | bytes 516104 | tf_op jit(solution)/shard_map/ppermute | solution.py:67
  110.4 7.4 %collective-permute-start.23 = (bf16[112,768]{1,0:T(8,128)(2,1)S(1)}, bf16[112,768]{1,0:T(8,128)(2,1)S(1)}, u32[]{:S(2)}, u32[]{:S(2)}) collective-permute-start(bf16[112,768]{1,0:T(8,128)(2,1)S(1)} %multiply_convert_fusion.refs_0_), channel_id=1, source_target_pairs={{0,2},{1,3},{2,0},{3,1},{4,6},{5,7},{6,4},{7,5},{8,10},{9,11},{10,... | collective-permute-start | bytes 516104 | tf_op jit(solution)/shard_map/ppermute | solution.py:67
  112.1 6.3 %collective-permute-start.24 = (bf16[112,768]{1,0:T(8,128)(2,1)S(1)}, bf16[112,768]{1,0:T(8,128)(2,1)S(1)}, u32[]{:S(2)}, u32[]{:S(2)}) collective-permute-start(bf16[112,768]{1,0:T(8,128)(2,1)S(1)} %multiply_convert_fusion.refs_0_), channel_id=1, source_target_pairs={{0,3},{1,0},{2,1},{3,2},{4,7},{5,4},{6,5},{7,6},{8,11},{9,8},{10,9... | collective-permute-start | bytes 516104 | tf_op jit(solution)/shard_map/ppermute | solution.py:67
  119.2 5.8 %collective-permute-start.28 = (bf16[400,384]{1,0:T(8,128)(2,1)S(1)}, bf16[400,384]{1,0:T(8,128)(2,1)S(1)}, u32[]{:S(2)}, u32[]{:S(2)}) collective-permute-start(bf16[400,384]{1,0:T(8,128)(2,1)S(1)} %get-tuple-element.67.refs_1_), channel_id=1, source_target_pairs={{0,96},{1,97},{2,98},{3,99},{4,100},{5,101},{6,102},{7,103},{8,104... | collective-permute-start | bytes 921608 | tf_op jit(solution)/shard_map/ppermute | solution.py:738
  120.2 19.7 %collective-permute-start.26 = (bf16[400,384]{1,0:T(8,128)(2,1)S(1)}, bf16[400,384]{1,0:T(8,128)(2,1)S(1)}, u32[]{:S(2)}, u32[]{:S(2)}) collective-permute-start(bf16[400,384]{1,0:T(8,128)(2,1)S(1)} %get-tuple-element.67.refs_1_), channel_id=1, source_target_pairs={{0,32},{1,33},{2,34},{3,35},{4,36},{5,37},{6,38},{7,39},{8,40},{9,... | collective-permute-start | bytes 921608 | tf_op jit(solution)/shard_map/ppermute | solution.py:738
  125.0 15.1 %collective-permute-start.29 = (bf16[400,384]{1,0:T(8,128)(2,1)S(1)}, bf16[400,384]{1,0:T(8,128)(2,1)S(1)}, u32[]{:S(2)}, u32[]{:S(2)}) collective-permute-start(bf16[400,384]{1,0:T(8,128)(2,1)S(1)} %collective-permute-done.28.refs_7_), channel_id=1, source_target_pairs={{0,96},{1,97},{2,98},{3,99},{4,100},{5,101},{6,102},{7,103},{8,104... | collective-permute-start | bytes 921608 | tf_op jit(solution)/shard_map/ppermute | solution.py:738
  127.2 8.1 %collective-permute-start.25 = (bf16[384,384]{1,0:T(8,128)(2,1)S(1)}, bf16[384,384]{1,0:T(8,128)(2,1)S(1)}, u32[]{:S(2)}, u32[]{:S(2)}) collective-permute-start(bf16[384,384]{1,0:T(8,128)(2,1)S(1)} %get-tuple-element.66.refs_0_), channel_id=1, source_target_pairs={{0,32},{1,33},{2,34},{3,35},{4,36},{5,37},{6,38},{7,39},{8,40},{9,... | collective-permute-start | bytes 884744 | tf_op jit(solution)/shard_map/ppermute | solution.py:738
  127.2 10.4 %collective-permute-start.30 = (bf16[384,384]{1,0:T(8,128)(2,1)S(1)}, bf16[384,384]{1,0:T(8,128)(2,1)S(1)}, u32[]{:S(2)}, u32[]{:S(2)}) collective-permute-start(bf16[384,384]{1,0:T(8,128)(2,1)S(1)} %get-tuple-element.66.refs_0_), channel_id=1, source_target_pairs={{0,96},{1,97},{2,98},{3,99},{4,100},{5,101},{6,102},{7,103},{8,104... | collective-permute-start | bytes 884744 | tf_op jit(solution)/shard_map/ppermute | solution.py:738
  129.8 10.6 %collective-permute-start.32 = (bf16[400,384]{1,0:T(8,128)(2,1)S(1)}, bf16[400,384]{1,0:T(8,128)(2,1)S(1)}, u32[]{:S(2)}, u32[]{:S(2)}) collective-permute-start(bf16[400,384]{1,0:T(8,128)(2,1)S(1)} %get-tuple-element.67.refs_1_), channel_id=1, source_target_pairs={{0,16},{16,0},{1,17},{17,1},{2,18},{18,2},{3,19},{19,3},{4,20},{20... | collective-permute-start | bytes 921608 | tf_op jit(solution)/shard_map/ppermute | solution.py:744
  135.2 6.8 %collective-permute-start.27 = (bf16[384,384]{1,0:T(8,128)(2,1)S(1)}, bf16[384,384]{1,0:T(8,128)(2,1)S(1)}, u32[]{:S(2)}, u32[]{:S(2)}) collective-permute-start(bf16[384,384]{1,0:T(8,128)(2,1)S(1)} %collective-permute-done.25.refs_2_), channel_id=1, source_target_pairs={{0,32},{1,33},{2,34},{3,35},{4,36},{5,37},{6,38},{7,39},{8,40},{9,... | collective-permute-start | bytes 884744 | tf_op jit(solution)/shard_map/ppermute | solution.py:738
  137.5 10.4 %collective-permute-start.38 = (bf16[400,384]{1,0:T(8,128)(2,1)S(1)}, bf16[400,384]{1,0:T(8,128)(2,1)S(1)}, u32[]{:S(2)}, u32[]{:S(2)}) collective-permute-start(bf16[400,384]{1,0:T(8,128)(2,1)S(1)} %collective-permute-done.28.refs_7_), channel_id=1, source_target_pairs={{0,16},{16,0},{1,17},{17,1},{2,18},{18,2},{3,19},{19,3},{4,20},{20... | collective-permute-start | bytes 921608 | tf_op jit(solution)/shard_map/ppermute | solution.py:744
  139.9 7.9 %collective-permute-start.34 = (bf16[400,384]{1,0:T(8,128)(2,1)S(1)}, bf16[400,384]{1,0:T(8,128)(2,1)S(1)}, u32[]{:S(2)}, u32[]{:S(2)}) collective-permute-start(bf16[400,384]{1,0:T(8,128)(2,1)S(1)} %collective-permute-done.26.refs_3_), channel_id=1, source_target_pairs={{0,16},{16,0},{1,17},{17,1},{2,18},{18,2},{3,19},{19,3},{4,20},{20... | collective-permute-start | bytes 921608 | tf_op jit(solution)/shard_map/ppermute | solution.py:744
  140.0 8.3 %collective-permute-start.36 = (bf16[400,384]{1,0:T(8,128)(2,1)S(1)}, bf16[400,384]{1,0:T(8,128)(2,1)S(1)}, u32[]{:S(2)}, u32[]{:S(2)}) collective-permute-start(bf16[400,384]{1,0:T(8,128)(2,1)S(1)} %collective-permute-done.29.refs_5_), channel_id=1, source_target_pairs={{0,16},{16,0},{1,17},{17,1},{2,18},{18,2},{3,19},{19,3},{4,20},{20... | collective-permute-start | bytes 921608 | tf_op jit(solution)/shard_map/ppermute | solution.py:744
  140.5 8.6 %collective-permute-start.31 = (bf16[384,384]{1,0:T(8,128)(2,1)S(1)}, bf16[384,384]{1,0:T(8,128)(2,1)S(1)}, u32[]{:S(2)}, u32[]{:S(2)}) collective-permute-start(bf16[384,384]{1,0:T(8,128)(2,1)S(1)} %get-tuple-element.66.refs_0_), channel_id=1, source_target_pairs={{0,16},{16,0},{1,17},{17,1},{2,18},{18,2},{3,19},{19,3},{4,20},{20... | collective-permute-start | bytes 884744 | tf_op jit(solution)/shard_map/ppermute | solution.py:744
  142.0 7.1 %collective-permute-start.33 = (bf16[384,384]{1,0:T(8,128)(2,1)S(1)}, bf16[384,384]{1,0:T(8,128)(2,1)S(1)}, u32[]{:S(2)}, u32[]{:S(2)}) collective-permute-start(bf16[384,384]{1,0:T(8,128)(2,1)S(1)} %collective-permute-done.25.refs_2_), channel_id=1, source_target_pairs={{0,16},{16,0},{1,17},{17,1},{2,18},{18,2},{3,19},{19,3},{4,20},{20... | collective-permute-start | bytes 884744 | tf_op jit(solution)/shard_map/ppermute | solution.py:744
  (13 other events, 64.2 us)

commit v7 on v6

--- a/solution.py
+++ b/solution.py
@@ -316,7 +316,7 @@
     return bend, square, slope
 
 
-WIDE = 256
+WIDE = 384
 STRIP = 32
 
 
@@ -408,10 +408,11 @@
 
             @pl.when(j >= steps)
             def _():
-                at = pl.multiple_of((Spot(s_ref).their_first + j - steps) % 4 * quarter, 16)
-                prod_ref[0] = jnp.dot(
-                    g_ref[pl.ds(at, quarter), :], act_ref[...], preferred_element_type=F32
-                ).astype(BF)
+                for n in range(2):
+                    at = pl.multiple_of((Spot(s_ref).their_first + 2 * (j - steps) + n) % 4 * quarter, 16)
+                    prod_ref[n] = jnp.dot(
+                        g_ref[pl.ds(at, quarter), :], act_ref[...], preferred_element_type=F32
+                    ).astype(BF)
 
     def cols(count, full):
         def place(j, s_ref):
@@ -432,7 +433,7 @@
     else:
         outs += [jax.ShapeDtypeStruct((4, quarter, half), BF)]
         out_specs += [
-            pl.BlockSpec((1, quarter, half), lambda j, s_ref: (jnp.maximum(j - steps, 0), 0, 0))
+            pl.BlockSpec((2, quarter, half), lambda j, s_ref: (jnp.maximum(j - steps, 0), 0, 0))
         ]
         scratch += [pltpu.VMEM((fine, half), BF), pltpu.VMEM((columns, fine), BF)]
     scratch += [
@@ -448,7 +449,7 @@
         out_shape=outs,
         grid_spec=pltpu.PrefetchScalarGridSpec(
             num_scalar_prefetch=1,
-            grid=(steps if ours else steps + 4,),
+            grid=(steps if ours else steps + 2,),
             in_specs=[flat(rows + TAIL, 256)] * 4
             + [cols(TAIL, True), cols(TAIL, True), cols(3, True)]
             + [ANY] * 4,
@@ -624,21 +625,19 @@
     quarter = 4 * slim
 
     def kernel(at_ref, *refs):
-        ins, upper, lower, held = refs[:4], refs[4], refs[5], refs[6]
+        ins, out, held = refs[:4], refs[4], refs[5]
         for d in range(4):
             put = pl.ds(pl.multiple_of((Spot(at_ref).second_at + 4 - d) % 4 * slim, 16), slim)
             held[put, :] = ins[d][:slim, :]
-        turned = held[...].T
-        upper[...] = turned[: columns // 2]
-        lower[: columns // 2, :] = turned[columns // 2 :]
+        out[:columns, :] = held[...].T
         last = total_of([r[slim:, :] for r in ins])[:8]
-        lower[columns // 2 :, :] = jnp.concatenate([last[:, :quarter], last[:, quarter:]], axis=0).astype(BF)
-
-    return pl.pallas_call(
-        kernel,
-        out_shape=[jax.ShapeDtypeStruct((columns // 2 + n, quarter), BF) for n in (0, TAIL)],
+        out[columns:, :] = jnp.concatenate([last[:, :quarter], last[:, quarter:]], axis=0).astype(BF)
+
+    return pl.pallas_call(
+        kernel,
+        out_shape=jax.ShapeDtypeStruct((columns + TAIL, quarter), BF),
         in_specs=[SMEM] + [VMEM] * 4,
-        out_specs=[VMEM] * 2,
+        out_specs=VMEM,
         scratch_shapes=[pltpu.VMEM((quarter, columns), BF)],
         compiler_params=params(10),
         name="join_rows",
@@ -646,21 +645,22 @@
 
 
 def lay_out(scalars, own, other):
-    part, quarter = own[0][0].shape
+    part, quarter = own[3].shape
     half = 2 * part
 
     def kernel(s_ref, *refs):
         out, sems = refs[-2:]
         spot = Spot(s_ref)
         copies = []
-        for n in range(16):
-            mine, d, low = n < 8, n // 2 % 4, n % 2
-            down = (spot.core if mine else 1 - spot.core) * half + low * part
+        for n in range(10):
+            mine = n < 5
+            d, start, count = ((0, 0, half), (1, 0, half), (3, 0, half), (2, 0, part), (2, part, part))[n % 5]
+            down = (spot.core if mine else 1 - spot.core) * half + start
             over = ((spot.first_at if mine else spot.their_first) + 4 - d) % 4 * quarter
             copies.append(
                 pltpu.make_async_copy(
-                    refs[n].at[pl.ds(0, part), :],
-                    out.at[pl.ds(pl.multiple_of(down, 16), part), pl.ds(pl.multiple_of(over, 128), quarter)],
+                    refs[n].at[pl.ds(0, count), :],
+                    out.at[pl.ds(pl.multiple_of(down, 16), count), pl.ds(pl.multiple_of(over, 128), quarter)],
                     sems.at[n],
                 )
             )
@@ -672,12 +672,12 @@
     return pl.pallas_call(
         kernel,
         out_shape=jax.ShapeDtypeStruct((2 * half, 4 * quarter), BF),
-        in_specs=[SMEM] + [VMEM] * 16,
+        in_specs=[SMEM] + [VMEM] * 10,
         out_specs=ANY,
-        scratch_shapes=[pltpu.SemaphoreType.DMA((16,))],
+        scratch_shapes=[pltpu.SemaphoreType.DMA((10,))],
         compiler_params=params(8),
         name="lay_out",
-    )(scalars, *[p for pieces in (own, other) for pair in pieces for p in pair])
+    )(scalars, *own, *other)
 
 
 def local(
@@ -704,13 +704,13 @@
     q = exchange(blocks, HEAD_RING)
     own = stack_rows(q, down)
     far = {d: lax.ppermute(own, AXES, turn(ROW_RING, d)) for d in (1, 3, 2)}
-    state = attend(scalars, 0, q, [own], None, (before, after))
+    state = attend(scalars, 0, q, [own], None)
 
     turned = upstream.T
 
     state = attend(scalars, 1, q, [far[1]], state)
     state = attend(scalars, 2, q, [far[3]], state)
-    mixed = attend(scalars, 3, q, [own, far[1], far[3], far[2]], state)
+    mixed = attend(scalars, 3, q, [own, far[1], far[3], far[2]], state, (before, after))
     back = exchange(mixed, HEAD_RING, -1)
     swap = [(0, 1), (1, 0)]
     given = (back, tokens, skipped, out_weight.reshape(H, DV, -1), before, after, depth_weight, turned)
@@ -732,22 +732,19 @@
     got = exchange([mixed] * 4, SUM_RINGS[2])
     norm_scale = 1.0 / math.sqrt(128 * fine)
     summed = (total_of(got) * norm_scale).astype(BF)
-    upper, lower = join_rows(scalars, exchange([summed] * 4, SUM_RINGS[1]))
+    joined = join_rows(scalars, exchange([summed] * 4, SUM_RINGS[1]))
 
     def go(block, step):
         return lax.ppermute(block, AXES, turn(SUM_RINGS[0], step))
 
-    upper_1, lower_3 = go(upper, 1), go(lower, 3)
-    lower_1, upper_3 = go(lower, 1), go(upper, 3)
-    upper_2, lower_2 = go(upper_1, 1), go(lower_3, 3)
-    own = [(upper, lower), (upper_1, lower_1), (upper_2, lower_2), (upper_3, lower_3)]
-    other = [tuple(lax.ppermute(p, "c", swap) for p in pair) for pair in own]
+    half, part = columns // 2, columns // 4
+    one, three = go(joined, 1), go(joined, 3)
+    own = [joined, one, three, go(one[:part], 1), go(three[part:], 3)]
+    other = [lax.ppermute(p, "c", swap) for p in own]
     grad_pointwise = lay_out(scalars, own, other)
 
-    half = columns // 2
-
-    def depth_of(pairs):
-        rows = total_of([low[half // 2 :] for _, low in pairs])
+    def depth_of(blocks):
+        rows = total_of([blocks[0][half:], blocks[1][half:], blocks[4][part:], blocks[2][half:]])
         return jnp.concatenate([rows[:3], rows[8:11]], axis=1)
 
     d_own, d_other = depth_of(own), depth_of(other)

time: 153 us -> 148 us (0.967)
  starting transfers between devices: 58.9 us -> 53.5 us
  waiting for transfers between devices: 38.6 us -> 36.4 us
    ppermute x1, waiting for transfers between devices: 6.34 us -> 0.01 us  [local(): before = lax.ppermute(down, ('z', 'y'), [(i, i + 1) for i in range(15)])]
    ppermute x6 -> x4, starting transfers between devices: 8.71 us -> 3.64 us  [go(): return lax.ppermute(block, AXES, turn(SUM_RINGS[0], step))]
    ppermute x6 -> x4, waiting for transfers between devices: 5.61 us -> 9.42 us  [go(): return lax.ppermute(block, AXES, turn(SUM_RINGS[0], step))]
    ppermute x18, starting transfers between devices: 22.5 us -> 26.2 us  [exchange(): got[d] = lax.ppermute(pieces[d], AXES, turn(axes, sign * d))]
    ppermute x8 -> x5, starting transfers between devices: 14.8 us -> 11.4 us  [local(): other = [lax.ppermute(p, 'c', swap) for p in own]]
    ppermute x3, waiting for transfers between devices: 0.01 us -> 2.44 us  [local(): far = {d: lax.ppermute(own, AXES, turn(ROW_RING, d)) for d in (1, 3, 2)}]
    ppermute x1, waiting for transfers between devices: 2.2 us -> 0.01 us  [local(): after = lax.ppermute(up, ('z', 'y'), [(i + 1, i) for i in range(15)])]
  transfers between devices with their start and end apart: 39 -> 34, of which waited for: 18 -> 15; matrix products, arithmetic and copies ran while one was open for 1% -> 3% of each run, Pallas kernels for 19% -> 19%
where the time goes in v7:
time: 148 us; the launch traced here: 147 us
  starting transfers between devices  53.5 us (36%)
  Pallas kernels  49.6 us (34%)
  waiting for transfers between devices  36.4 us (25%)
  local copies, waits for them, and re-layouts  4.31 us (3%)
  between operations  1.79 us (1%)
  other arithmetic  1.55 us (1%)
    ppermute x18, starting transfers between devices, exchange(): got[d] = lax.ppermute(pieces[d], AXES, turn(axes, sign * d))  26.2 us
    ppermute x18, waiting for transfers between devices, exchange(): got[d] = lax.ppermute(pieces[d], AXES, turn(axes, sign * d))  23 us
    pallas_call x2, Pallas kernels, forward(): pl.pallas_call(kernel, out_shape=outs, grid_spec=pltpu.PrefetchScalarGrid...  13.6 us
    pallas_call x1, Pallas kernels, backward(): pl.pallas_call(kernel, out_shape=[jax.ShapeDtypeStruct((fine, columns), B...  12.9 us
    ppermute x5, starting transfers between devices, local(): other = [lax.ppermute(p, 'c', swap) for p in own]  11.4 us
    pallas_call x4, Pallas kernels, attend(): pl.pallas_call(kernel, out_shape=outs, in_specs=[SMEM] + [VMEM] * len(ins...  9.85 us
    ppermute x4, waiting for transfers between devices, go(): return lax.ppermute(block, AXES, turn(SUM_RINGS[0], step))  9.42 us
    pallas_call x1, Pallas kernels, project(): pl.pallas_call(kernel, out_shape=[jax.ShapeDtypeStruct((rows, 384), BF)]...  4.48 us
  transfers between devices with their start and end apart: 34, of which 15 were waited for; matrix products, arithmetic and copies ran while one was open for 3% of the time, Pallas kernels for 19%

profile of v7, /device:TPU:1, one launch (start us, length us, event | category | flops | bytes accessed | tf_op | source)
XLA Modules:
  0.0 147.2 jit_solution(14575540559052951089)
XLA Ops:
  1.4 4.5 %project.1 = (bf16[256,384]{1,0:T(8,128)(2,1)S(1)}, bf16[256,384]{1,0:T(8,128)(2,1)S(1)}, bf16[256,384]{1,0:T(8,128)(2,1)S(1)}, bf16[256,384]{1,0:T(8,128)(2,1)S(1)}) custom-call(s32[5]{0:T(128)S(1)} %stack.19.at_ref.s_ref, bf16[256,1536]{1,0:T(8,128)(2,1)} %bitcast.14, bf16[1536,256]{1,0:T(8,128)(2,1)} %wq_hbm.1, bf16[1536,256]{1,0:T(8,128)(2,1)} %wk_hbm.1, ...), custom_call_target="tpu_custom_call" | custom-call | tf_op jit(solution)/shard_map/project/pallas_call | solution.py:116
  5.9 2.5 %collective-permute-start = (bf16[256,384]{1,0:T(8,128)(2,1)S(1)}, bf16[256,384]{1,0:T(8,128)(2,1)S(1)}, u32[]{:S(2)}, u32[]{:S(2)}) collective-permute-start(bf16[256,384]{1,0:T(8,128)(2,1)S(1)} %get-tuple-element.35), channel_id=1, source_target_pairs={{0,1},{1,2},{2,3},{3,0},{4,5},{5,6},{6,7},{7,4},{8,9},{9,10},{10,1... | collective-permute-start | bytes 589832 | tf_op jit(solution)/shard_map/ppermute | solution.py:67
  8.4 3.3 %collective-permute-start.1 = (bf16[256,384]{1,0:T(8,128)(2,1)S(1)}, bf16[256,384]{1,0:T(8,128)(2,1)S(1)}, u32[]{:S(2)}, u32[]{:S(2)}) collective-permute-start(bf16[256,384]{1,0:T(8,128)(2,1)S(1)} %get-tuple-element.36), channel_id=1, source_target_pairs={{0,2},{1,3},{2,0},{3,1},{4,6},{5,7},{6,4},{7,5},{8,10},{9,11},{10,... | collective-permute-start | bytes 589832 | tf_op jit(solution)/shard_map/ppermute | solution.py:67
  13.8 3.3 %collective-permute-done.1.refs_2_ = bf16[256,384]{1,0:T(8,128)(2,1)S(1)} collective-permute-done((bf16[256,384]{1,0:T(8,128)(2,1)S(1)}, bf16[256,384]{1,0:T(8,128)(2,1)S(1)}, u32[]{:S(2)}, u32[]{:S(2)}) %collective-permute-start.1) | collective-permute-done | bytes 196640 | tf_op jit(solution)/shard_map/ppermute | solution.py:67
  21.4 2.3 %collective-permute-start.6 = (bf16[16,1536]{1,0:T(8,128)(2,1)S(1)}, bf16[16,1536]{1,0:T(8,128)(2,1)S(1)}, u32[]{:S(2)}, u32[]{:S(2)}) collective-permute-start(bf16[16,1536]{1,0:T(8,128)(2,1)S(1)} %get-tuple-element.38.refs_4_), channel_id=1, source_target_pairs={{0,1},{1,2},{2,3},{3,4},{4,5},{5,6},{6,7},{7,8},{8,9},{9,10},{10,1... | collective-permute-start | bytes 147464 | tf_op jit(solution)/shard_map/ppermute | solution.py:702
  25.0 2.2 %attend.4 = (f32[1024,256]{1,0:T(8,128)S(1)}, f32[1024,128]{1,0:T(8,128)S(1)}) custom-call(s32[5]{0:T(128)S(1)} %stack.19.at_ref.s_ref, bf16[256,384]{1,0:T(8,128)(2,1)S(1)} %get-tuple-element.34.mark_ref.refs_0_, bf16[256,384]{1,0:T(8,128)(2,1)S(1)} %collective-permute-done.refs_1_, bf16[256,384]{1,0:T(8,128)(2,1)S(1)} %collective-permute-done.1.refs_2_, ...), custom_call_target="tpu_custom_call" | custom-call | flops 1073741824 | bytes 4194304 | tf_op jit(solution)/shard_map/attend/pallas_call | solution.py:255
  27.2 2.2 %attend.5 = (f32[1024,256]{1,0:T(8,128)S(1)}, f32[1024,128]{1,0:T(8,128)S(1)}) custom-call(s32[5]{0:T(128)S(1)} %stack.19.at_ref.s_ref, bf16[256,384]{1,0:T(8,128)(2,1)S(1)} %get-tuple-element.34.mark_ref.refs_0_, bf16[256,384]{1,0:T(8,128)(2,1)S(1)} %collective-permute-done.refs_1_, bf16[256,384]{1,0:T(8,128)(2,1)S(1)} %collective-permute-done.1.refs_2_, ...), custom_call_target="tpu_custom_call" | custom-call | flops 1073741824 | bytes 4194304 | tf_op jit(solution)/shard_map/attend/pallas_call | solution.py:255
  29.4 2.4 %collective-permute-done.4.refs_4_.refs_6_ = bf16[1040,256]{1,0:T(8,128)(2,1)S(1)} collective-permute-done((bf16[1040,256]{1,0:T(8,128)(2,1)S(1)}, bf16[1040,256]{1,0:T(8,128)(2,1)S(1)}, u32[]{:S(2)}, u32[]{:S(2)}) %collective-permute-start.4) | collective-permute-done | bytes 532512 | tf_op jit(solution)/shard_map/ppermute | solution.py:706
  31.9 2.2 %attend.6 = (f32[1024,256]{1,0:T(8,128)S(1)}, f32[1024,128]{1,0:T(8,128)S(1)}) custom-call(s32[5]{0:T(128)S(1)} %stack.19.at_ref.s_ref, bf16[256,384]{1,0:T(8,128)(2,1)S(1)} %get-tuple-element.34.mark_ref.refs_0_, bf16[256,384]{1,0:T(8,128)(2,1)S(1)} %collective-permute-done.refs_1_, bf16[256,384]{1,0:T(8,128)(2,1)S(1)} %collective-permute-done.1.refs_2_, ...), custom_call_target="tpu_custom_call" | custom-call | flops 1073741824 | bytes 4194304 | tf_op jit(solution)/shard_map/attend/pallas_call | solution.py:255
  34.2 3.2 %attend.7 = (bf16[272,256]{1,0:T(8,128)(2,1)S(1)}, bf16[272,256]{1,0:T(8,128)(2,1)S(1)}, bf16[272,256]{1,0:T(8,128)(2,1)S(1)}, bf16[272,256]{1,0:T(8,128)(2,1)S(1)}) custom-call(s32[5]{0:T(128)S(1)} %stack.19.at_ref.s_ref, bf16[256,384]{1,0:T(8,128)(2,1)S(1)} %get-tuple-element.34.mark_ref.refs_0_, bf16[256,384]{1,0:T(8,128)(2,1)S(1)} %collective-permute-done.refs_1_, ...), custom_call_target="tpu_custom_call" | custom-call | flops 1073741824 | bytes 4194304 | tf_op jit(solution)/shard_map/attend/pallas_call | solution.py:255
  37.3 3.5 %collective-permute-start.8 = (bf16[272,256]{1,0:T(8,128)(2,1)S(1)}, bf16[272,256]{1,0:T(8,128)(2,1)S(1)}, u32[]{:S(2)}, u32[]{:S(2)}) collective-permute-start(bf16[272,256]{1,0:T(8,128)(2,1)S(1)} %get-tuple-element.47), channel_id=1, source_target_pairs={{0,3},{1,0},{2,1},{3,2},{4,7},{5,4},{6,5},{7,6},{8,11},{9,8},{10,9... | collective-permute-start | bytes 417800 | tf_op jit(solution)/shard_map/ppermute | solution.py:67
  44.3 2.0 %collective-permute-done.9.b2 = bf16[272,256]{1,0:T(8,128)(2,1)S(1)} collective-permute-done((bf16[272,256]{1,0:T(8,128)(2,1)S(1)}, bf16[272,256]{1,0:T(8,128)(2,1)S(1)}, u32[]{:S(2)}, u32[]{:S(2)}) %collective-permute-start.9) | collective-permute-done | bytes 139296 | tf_op jit(solution)/shard_map/ppermute | solution.py:67
  46.3 1.7 %collective-permute-done.10.b3 = bf16[272,256]{1,0:T(8,128)(2,1)S(1)} collective-permute-done((bf16[272,256]{1,0:T(8,128)(2,1)S(1)}, bf16[272,256]{1,0:T(8,128)(2,1)S(1)}, u32[]{:S(2)}, u32[]{:S(2)}) %collective-permute-start.10) | collective-permute-done | bytes 139296 | tf_op jit(solution)/shard_map/ppermute | solution.py:67
  48.0 7.8 %forward.3 = (bf16[544,768]{1,0:T(8,128)(2,1)}, bf16[4,384,768]{2,1,0:T(8,128)(2,1)}) custom-call(s32[5]{0:T(128)S(1)} %stack.19.at_ref.s_ref, bf16[272,256]{1,0:T(8,128)(2,1)S(1)} %get-tuple-element.46.b0, bf16[272,256]{1,0:T(8,128)(2,1)S(1)} %collective-permute-done.8.b1, bf16[272,256]{1,0:T(8,128)(2,1)S(1)} %collective-permute-done.9.b2, ...), custom_call_target="tpu_custom_call" | custom-call | flops 2415919104 | bytes 9437184 | tf_op jit(solution)/shard_map/forward/pallas_call | solution.py:447
  55.8 2.2 %collective-permute-start.11 = (bf16[4,384,768]{2,1,0:T(8,128)(2,1)}, bf16[4,384,768]{2,1,0:T(8,128)(2,1)S(1)}, u32[]{:S(2)}, u32[]{:S(2)}) collective-permute-start(bf16[4,384,768]{2,1,0:T(8,128)(2,1)} %get-tuple-element.51), channel_id=1, source_target_pairs={{0,16},{16,0},{1,17},{17,1},{2,18},{18,2},{3,19},{19,3},{4,20},{20... | collective-permute-start | bytes 7077896 | tf_op jit(solution)/shard_map/ppermute | solution.py:718
  58.0 5.8 %forward.2 = (bf16[544,768]{1,0:T(8,128)(2,1)}, bf16[512,768]{1,0:T(8,128)(2,1)}) custom-call(s32[5]{0:T(128)S(1)} %stack.19.at_ref.s_ref, bf16[272,256]{1,0:T(8,128)(2,1)S(1)} %get-tuple-element.46.b0, bf16[272,256]{1,0:T(8,128)(2,1)S(1)} %collective-permute-done.8.b1, bf16[272,256]{1,0:T(8,128)(2,1)S(1)} %collective-permute-done.9.b2, ...), custom_call_target="tpu_custom_call" | custom-call | flops 2415919104 | bytes 9437184 | tf_op jit(solution)/shard_map/forward/pallas_call | solution.py:447
  69.2 1.9 %collective-permute-start.14 = (bf16[384,768]{1,0:T(8,128)(2,1)S(1)}, bf16[384,768]{1,0:T(8,128)(2,1)S(1)}, u32[]{:S(2)}, u32[]{:S(2)}) collective-permute-start(bf16[384,768]{1,0:T(8,128)(2,1)S(1)} %get-tuple-element.55), channel_id=1, source_target_pairs={{0,96},{1,97},{2,98},{3,99},{4,100},{5,101},{6,102},{7,103},{8,104... | collective-permute-start | bytes 1769480 | tf_op jit(solution)/shard_map/ppermute | solution.py:67
  71.2 12.9 %backward.1 = (bf16[512,1536]{1,0:T(8,128)(2,1)}, f32[3,768]{1,0:T(4,128)S(1)}, f32[3,768]{1,0:T(4,128)S(1)}) custom-call(s32[5]{0:T(128)S(1)} %stack.19.at_ref.s_ref, bf16[544,768]{1,0:T(8,128)(2,1)S(1)} %copy-done.4, bf16[544,768]{1,0:T(8,128)(2,1)S(1)} %copy-done.5, bf16[512,1536]{1,0:T(8,128)(2,1)S(1)} %bitcast.13, ...), custom_call_target="tpu_custom_call" | custom-call | flops 2415919104 | bytes 11534336 | tf_op jit(solution)/shard_map/backward/pallas_call | solution.py:545
  84.1 2.3 %collective-permute-start.18 = (f32[3,768]{1,0:T(4,128)S(1)}, f32[3,768]{1,0:T(4,128)S(1)}, u32[]{:S(2)}, u32[]{:S(2)}) collective-permute-start(f32[3,768]{1,0:T(4,128)S(1)} %get-tuple-element.63), channel_id=1, source_target_pairs={{0,16},{16,0},{1,17},{17,1},{2,18},{18,2},{3,19},{19,3},{4,20},{20... | collective-permute-start | bytes 27656 | tf_op jit(solution)/shard_map/ppermute | solution.py:727
  87.3 3.5 %collective-permute-start.17 = (bf16[96,768]{1,0:T(8,128)(2,1)S(1)}, bf16[96,768]{1,0:T(8,128)(2,1)S(1)}, u32[]{:S(2)}, u32[]{:S(2)}) collective-permute-start(bf16[96,768]{1,0:T(8,128)(2,1)S(1)} %get-tuple-element.59), channel_id=1, source_target_pairs={{0,3},{1,0},{2,1},{3,2},{4,7},{5,4},{6,5},{7,6},{8,11},{9,8},{10,9... | collective-permute-start | bytes 442376 | tf_op jit(solution)/shard_map/ppermute | solution.py:67
  90.7 2.6 %collective-permute-start.15 = (bf16[96,768]{1,0:T(8,128)(2,1)S(1)}, bf16[96,768]{1,0:T(8,128)(2,1)S(1)}, u32[]{:S(2)}, u32[]{:S(2)}) collective-permute-start(bf16[96,768]{1,0:T(8,128)(2,1)S(1)} %get-tuple-element.57), channel_id=1, source_target_pairs={{0,2},{1,3},{2,0},{3,1},{4,6},{5,7},{6,4},{7,5},{8,10},{9,11},{10,... | collective-permute-start | bytes 442376 | tf_op jit(solution)/shard_map/ppermute | solution.py:67
  93.4 2.6 %collective-permute-done.16 = bf16[96,768]{1,0:T(8,128)(2,1)S(1)} collective-permute-done((bf16[96,768]{1,0:T(8,128)(2,1)S(1)}, bf16[96,768]{1,0:T(8,128)(2,1)S(1)}, u32[]{:S(2)}, u32[]{:S(2)}) %collective-permute-start.16) | collective-permute-done | bytes 147488 | tf_op jit(solution)/shard_map/ppermute | solution.py:67
  99.8 2.2 %collective-permute-done.21 = bf16[112,768]{1,0:T(8,128)(2,1)S(1)} collective-permute-done((bf16[112,768]{1,0:T(8,128)(2,1)S(1)}, bf16[112,768]{1,0:T(8,128)(2,1)S(1)}, u32[]{:S(2)}, u32[]{:S(2)}) %collective-permute-start.21) | collective-permute-done | bytes 172064 | tf_op jit(solution)/shard_map/ppermute | solution.py:67
  102.0 3.5 %collective-permute-done.20 = bf16[112,768]{1,0:T(8,128)(2,1)S(1)} collective-permute-done((bf16[112,768]{1,0:T(8,128)(2,1)S(1)}, bf16[112,768]{1,0:T(8,128)(2,1)S(1)}, u32[]{:S(2)}, u32[]{:S(2)}) %collective-permute-start.20) | collective-permute-done | bytes 172064 | tf_op jit(solution)/shard_map/ppermute | solution.py:67
  105.7 2.6 %collective-permute-start.23 = (bf16[112,768]{1,0:T(8,128)(2,1)S(1)}, bf16[112,768]{1,0:T(8,128)(2,1)S(1)}, u32[]{:S(2)}, u32[]{:S(2)}) collective-permute-start(bf16[112,768]{1,0:T(8,128)(2,1)S(1)} %multiply_convert_fusion.refs_0_), channel_id=1, source_target_pairs={{0,2},{1,3},{2,0},{3,1},{4,6},{5,7},{6,4},{7,5},{8,10},{9,11},{10,... | collective-permute-start | bytes 516104 | tf_op jit(solution)/shard_map/ppermute | solution.py:67
  109.0 4.3 %collective-permute-done.22.refs_1_ = bf16[112,768]{1,0:T(8,128)(2,1)S(1)} collective-permute-done((bf16[112,768]{1,0:T(8,128)(2,1)S(1)}, bf16[112,768]{1,0:T(8,128)(2,1)S(1)}, u32[]{:S(2)}, u32[]{:S(2)}) %collective-permute-start.22) | collective-permute-done | bytes 172064 | tf_op jit(solution)/shard_map/ppermute | solution.py:67
  116.2 7.7 %collective-permute-done.26.refs_2_ = bf16[784,384]{1,0:T(8,128)(2,1)S(1)} collective-permute-done((bf16[784,384]{1,0:T(8,128)(2,1)S(1)}, bf16[784,384]{1,0:T(8,128)(2,1)S(1)}, u32[]{:S(2)}, u32[]{:S(2)}) %collective-permute-start.26) | collective-permute-done | bytes 602144 | tf_op jit(solution)/shard_map/ppermute | solution.py:738
  124.6 2.1 %collective-permute-start.28 = (bf16[400,384]{1,0:T(8,128)(2,1)}, bf16[400,384]{1,0:T(8,128)(2,1)S(1)}, u32[]{:S(2)}, u32[]{:S(2)}) collective-permute-start(bf16[400,384]{1,0:T(8,128)(2,1)} %slice.57), channel_id=1, source_target_pairs={{0,96},{1,97},{2,98},{3,99},{4,100},{5,101},{6,102},{7,103},{8,104... | collective-permute-start | bytes 921608 | tf_op jit(solution)/shard_map/ppermute | solution.py:738
  127.5 4.9 %collective-permute-start.29 = (bf16[784,384]{1,0:T(8,128)(2,1)S(1)}, bf16[784,384]{1,0:T(8,128)(2,1)S(1)}, u32[]{:S(2)}, u32[]{:S(2)}) collective-permute-start(bf16[784,384]{1,0:T(8,128)(2,1)S(1)} %join_rows.1.refs_0_), channel_id=1, source_target_pairs={{0,16},{16,0},{1,17},{17,1},{2,18},{18,2},{3,19},{19,3},{4,20},{20... | collective-permute-start | bytes 1806344 | tf_op jit(solution)/shard_map/ppermute | solution.py:743
  132.9 1.7 %collective-permute-done.27.refs_3_ = bf16[384,384]{1,0:T(8,128)(2,1)} collective-permute-done((bf16[384,384]{1,0:T(8,128)(2,1)}, bf16[384,384]{1,0:T(8,128)(2,1)}, u32[]{:S(2)}, u32[]{:S(2)}) %collective-permute-start.27) | collective-permute-done | bytes 294944 | tf_op jit(solution)/shard_map/ppermute | solution.py:738
  134.6 6.0 %collective-permute-start.32 = (bf16[384,384]{1,0:T(8,128)(2,1)}, bf16[384,384]{1,0:T(8,128)(2,1)S(1)}, u32[]{:S(2)}, u32[]{:S(2)}) collective-permute-start(bf16[384,384]{1,0:T(8,128)(2,1)} %collective-permute-done.27.refs_3_), channel_id=1, source_target_pairs={{0,16},{16,0},{1,17},{17,1},{2,18},{18,2},{3,19},{19,3},{4,20},{20... | collective-permute-start | bytes 884744 | tf_op jit(solution)/shard_map/ppermute | solution.py:743
  143.6 3.4 %lay_out.1 = bf16[1536,1536]{1,0:T(8,128)(2,1)} custom-call(s32[5]{0:T(128)S(1)} %stack.19.at_ref.s_ref, bf16[784,384]{1,0:T(8,128)(2,1)S(1)} %join_rows.1.refs_0_, bf16[784,384]{1,0:T(8,128)(2,1)S(1)} %collective-permute-done.25.refs_1_, bf16[784,384]{1,0:T(8,128)(2,1)S(1)} %collective-permute-done.26.refs_2_, ...), custom_call_target="tpu_custom_call" | custom-call | tf_op jit(solution)/shard_map/lay_out/pallas_call | solution.py:672
  (77 shorter events, 30.0 us)
Async XLA Ops:
  5.9 8.0 %collective-permute-start = (bf16[256,384]{1,0:T(8,128)(2,1)S(1)}, bf16[256,384]{1,0:T(8,128)(2,1)S(1)}, u32[]{:S(2)}, u32[]{:S(2)}) collective-permute-start(bf16[256,384]{1,0:T(8,128)(2,1)S(1)} %get-tuple-element.35), channel_id=1, source_target_pairs={{0,1},{1,2},{2,3},{3,0},{4,5},{5,6},{6,7},{7,4},{8,9},{9,10},{10,1... | collective-permute-start | bytes 589832 | tf_op jit(solution)/shard_map/ppermute | solution.py:67
  8.4 8.8 %collective-permute-start.1 = (bf16[256,384]{1,0:T(8,128)(2,1)S(1)}, bf16[256,384]{1,0:T(8,128)(2,1)S(1)}, u32[]{:S(2)}, u32[]{:S(2)}) collective-permute-start(bf16[256,384]{1,0:T(8,128)(2,1)S(1)} %get-tuple-element.36), channel_id=1, source_target_pairs={{0,2},{1,3},{2,0},{3,1},{4,6},{5,7},{6,4},{7,5},{8,10},{9,11},{10,... | collective-permute-start | bytes 589832 | tf_op jit(solution)/shard_map/ppermute | solution.py:67
  11.7 5.5 %collective-permute-start.2 = (bf16[256,384]{1,0:T(8,128)(2,1)S(1)}, bf16[256,384]{1,0:T(8,128)(2,1)S(1)}, u32[]{:S(2)}, u32[]{:S(2)}) collective-permute-start(bf16[256,384]{1,0:T(8,128)(2,1)S(1)} %get-tuple-element.37), channel_id=1, source_target_pairs={{0,3},{1,0},{2,1},{3,2},{4,7},{5,4},{6,5},{7,6},{8,11},{9,8},{10,9... | collective-permute-start | bytes 589832 | tf_op jit(solution)/shard_map/ppermute | solution.py:67
  17.2 10.0 %collective-permute-start.3 = (bf16[1040,256]{1,0:T(8,128)(2,1)S(1)}, bf16[1040,256]{1,0:T(8,128)(2,1)S(1)}, u32[]{:S(2)}, u32[]{:S(2)}) collective-permute-start(bf16[1040,256]{1,0:T(8,128)(2,1)S(1)} %stack_rows.1.refs_4_), channel_id=1, source_target_pairs={{0,4},{1,5},{2,6},{3,7},{4,8},{5,9},{6,10},{7,11},{8,12},{9,13},{1... | collective-permute-start | bytes 1597448 | tf_op jit(solution)/shard_map/ppermute | solution.py:706
  18.3 13.6 %collective-permute-start.4 = (bf16[1040,256]{1,0:T(8,128)(2,1)S(1)}, bf16[1040,256]{1,0:T(8,128)(2,1)S(1)}, u32[]{:S(2)}, u32[]{:S(2)}) collective-permute-start(bf16[1040,256]{1,0:T(8,128)(2,1)S(1)} %stack_rows.1.refs_4_), channel_id=1, source_target_pairs={{0,12},{1,13},{2,14},{3,15},{4,0},{5,1},{6,2},{7,3},{8,4},{9,5},{1... | collective-permute-start | bytes 1597448 | tf_op jit(solution)/shard_map/ppermute | solution.py:706
  19.9 14.2 %collective-permute-start.5 = (bf16[1040,256]{1,0:T(8,128)(2,1)S(1)}, bf16[1040,256]{1,0:T(8,128)(2,1)S(1)}, u32[]{:S(2)}, u32[]{:S(2)}) collective-permute-start(bf16[1040,256]{1,0:T(8,128)(2,1)S(1)} %stack_rows.1.refs_4_), channel_id=1, source_target_pairs={{0,8},{1,9},{2,10},{3,11},{4,12},{5,13},{6,14},{7,15},{8,0},{9,1},... | collective-permute-start | bytes 1597448 | tf_op jit(solution)/shard_map/ppermute | solution.py:706
  21.4 12.8 %collective-permute-start.6 = (bf16[16,1536]{1,0:T(8,128)(2,1)S(1)}, bf16[16,1536]{1,0:T(8,128)(2,1)S(1)}, u32[]{:S(2)}, u32[]{:S(2)}) collective-permute-start(bf16[16,1536]{1,0:T(8,128)(2,1)S(1)} %get-tuple-element.38.refs_4_), channel_id=1, source_target_pairs={{0,1},{1,2},{2,3},{3,4},{4,5},{5,6},{6,7},{7,8},{8,9},{9,10},{10,1... | collective-permute-start | bytes 147464 | tf_op jit(solution)/shard_map/ppermute | solution.py:702
  23.7 10.5 %collective-permute-start.7 = (bf16[16,1536]{1,0:T(8,128)(2,1)S(1)}, bf16[16,1536]{1,0:T(8,128)(2,1)S(1)}, u32[]{:S(2)}, u32[]{:S(2)}) collective-permute-start(bf16[16,1536]{1,0:T(8,128)(2,1)S(1)} %get-tuple-element.45), channel_id=1, source_target_pairs={{1,0},{2,1},{3,2},{4,3},{5,4},{6,5},{7,6},{8,7},{9,8},{10,9},{11,1... | collective-permute-start | bytes 147464 | tf_op jit(solution)/shard_map/ppermute | solution.py:703
  37.3 7.0 %collective-permute-start.8 = (bf16[272,256]{1,0:T(8,128)(2,1)S(1)}, bf16[272,256]{1,0:T(8,128)(2,1)S(1)}, u32[]{:S(2)}, u32[]{:S(2)}) collective-permute-start(bf16[272,256]{1,0:T(8,128)(2,1)S(1)} %get-tuple-element.47), channel_id=1, source_target_pairs={{0,3},{1,0},{2,1},{3,2},{4,7},{5,4},{6,5},{7,6},{8,11},{9,8},{10,9... | collective-permute-start | bytes 417800 | tf_op jit(solution)/shard_map/ppermute | solution.py:67
  40.8 5.5 %collective-permute-start.9 = (bf16[272,256]{1,0:T(8,128)(2,1)S(1)}, bf16[272,256]{1,0:T(8,128)(2,1)S(1)}, u32[]{:S(2)}, u32[]{:S(2)}) collective-permute-start(bf16[272,256]{1,0:T(8,128)(2,1)S(1)} %get-tuple-element.48), channel_id=1, source_target_pairs={{0,2},{1,3},{2,0},{3,1},{4,6},{5,7},{6,4},{7,5},{8,10},{9,11},{10,... | collective-permute-start | bytes 417800 | tf_op jit(solution)/shard_map/ppermute | solution.py:67
  41.8 6.2 %collective-permute-start.10 = (bf16[272,256]{1,0:T(8,128)(2,1)S(1)}, bf16[272,256]{1,0:T(8,128)(2,1)S(1)}, u32[]{:S(2)}, u32[]{:S(2)}) collective-permute-start(bf16[272,256]{1,0:T(8,128)(2,1)S(1)} %get-tuple-element.49), channel_id=1, source_target_pairs={{0,1},{1,2},{2,3},{3,0},{4,5},{5,6},{6,7},{7,4},{8,9},{9,10},{10,1... | collective-permute-start | bytes 417800 | tf_op jit(solution)/shard_map/ppermute | solution.py:67
  55.8 8.1 %collective-permute-start.11 = (bf16[4,384,768]{2,1,0:T(8,128)(2,1)}, bf16[4,384,768]{2,1,0:T(8,128)(2,1)S(1)}, u32[]{:S(2)}, u32[]{:S(2)}) collective-permute-start(bf16[4,384,768]{2,1,0:T(8,128)(2,1)} %get-tuple-element.51), channel_id=1, source_target_pairs={{0,16},{16,0},{1,17},{17,1},{2,18},{18,2},{3,19},{19,3},{4,20},{20... | collective-permute-start | bytes 7077896 | tf_op jit(solution)/shard_map/ppermute | solution.py:718
  66.3 20.1 %collective-permute-start.12 = (bf16[384,768]{1,0:T(8,128)(2,1)S(1)}, bf16[384,768]{1,0:T(8,128)(2,1)S(1)}, u32[]{:S(2)}, u32[]{:S(2)}) collective-permute-start(bf16[384,768]{1,0:T(8,128)(2,1)S(1)} %get-tuple-element.53), channel_id=1, source_target_pairs={{0,32},{1,33},{2,34},{3,35},{4,36},{5,37},{6,38},{7,39},{8,40},{9,... | collective-permute-start | bytes 1769480 | tf_op jit(solution)/shard_map/ppermute | solution.py:67
  66.4 20.0 %collective-permute-start.13 = (bf16[384,768]{1,0:T(8,128)(2,1)S(1)}, bf16[384,768]{1,0:T(8,128)(2,1)S(1)}, u32[]{:S(2)}, u32[]{:S(2)}) collective-permute-start(bf16[384,768]{1,0:T(8,128)(2,1)S(1)} %get-tuple-element.54), channel_id=1, source_target_pairs={{0,64},{1,65},{2,66},{3,67},{4,68},{5,69},{6,70},{7,71},{8,72},{9,... | collective-permute-start | bytes 1769480 | tf_op jit(solution)/shard_map/ppermute | solution.py:67
  69.2 17.2 %collective-permute-start.14 = (bf16[384,768]{1,0:T(8,128)(2,1)S(1)}, bf16[384,768]{1,0:T(8,128)(2,1)S(1)}, u32[]{:S(2)}, u32[]{:S(2)}) collective-permute-start(bf16[384,768]{1,0:T(8,128)(2,1)S(1)} %get-tuple-element.55), channel_id=1, source_target_pairs={{0,96},{1,97},{2,98},{3,99},{4,100},{5,101},{6,102},{7,103},{8,104... | collective-permute-start | bytes 1769480 | tf_op jit(solution)/shard_map/ppermute | solution.py:67
  84.1 9.3 %collective-permute-start.18 = (f32[3,768]{1,0:T(4,128)S(1)}, f32[3,768]{1,0:T(4,128)S(1)}, u32[]{:S(2)}, u32[]{:S(2)}) collective-permute-start(f32[3,768]{1,0:T(4,128)S(1)} %get-tuple-element.63), channel_id=1, source_target_pairs={{0,16},{16,0},{1,17},{17,1},{2,18},{18,2},{3,19},{19,3},{4,20},{20... | collective-permute-start | bytes 27656 | tf_op jit(solution)/shard_map/ppermute | solution.py:727
  87.3 6.1 %collective-permute-start.17 = (bf16[96,768]{1,0:T(8,128)(2,1)S(1)}, bf16[96,768]{1,0:T(8,128)(2,1)S(1)}, u32[]{:S(2)}, u32[]{:S(2)}) collective-permute-start(bf16[96,768]{1,0:T(8,128)(2,1)S(1)} %get-tuple-element.59), channel_id=1, source_target_pairs={{0,3},{1,0},{2,1},{3,2},{4,7},{5,4},{6,5},{7,6},{8,11},{9,8},{10,9... | collective-permute-start | bytes 442376 | tf_op jit(solution)/shard_map/ppermute | solution.py:67
  90.7 5.2 %collective-permute-start.16 = (bf16[96,768]{1,0:T(8,128)(2,1)S(1)}, bf16[96,768]{1,0:T(8,128)(2,1)S(1)}, u32[]{:S(2)}, u32[]{:S(2)}) collective-permute-start(bf16[96,768]{1,0:T(8,128)(2,1)S(1)} %get-tuple-element.58), channel_id=1, source_target_pairs={{0,1},{1,2},{2,3},{3,0},{4,5},{5,6},{6,7},{7,4},{8,9},{9,10},{10,1... | collective-permute-start | bytes 442376 | tf_op jit(solution)/shard_map/ppermute | solution.py:67
  90.7 6.8 %collective-permute-start.15 = (bf16[96,768]{1,0:T(8,128)(2,1)S(1)}, bf16[96,768]{1,0:T(8,128)(2,1)S(1)}, u32[]{:S(2)}, u32[]{:S(2)}) collective-permute-start(bf16[96,768]{1,0:T(8,128)(2,1)S(1)} %get-tuple-element.57), channel_id=1, source_target_pairs={{0,2},{1,3},{2,0},{3,1},{4,6},{5,7},{6,4},{7,5},{8,10},{9,11},{10,... | collective-permute-start | bytes 442376 | tf_op jit(solution)/shard_map/ppermute | solution.py:67
  97.9 7.6 %collective-permute-start.20 = (bf16[112,768]{1,0:T(8,128)(2,1)S(1)}, bf16[112,768]{1,0:T(8,128)(2,1)S(1)}, u32[]{:S(2)}, u32[]{:S(2)}) collective-permute-start(bf16[112,768]{1,0:T(8,128)(2,1)S(1)} %fusion.1), channel_id=1, source_target_pairs={{0,4},{1,5},{2,6},{3,7},{4,8},{5,9},{6,10},{7,11},{8,12},{9,13},{1... | collective-permute-start | bytes 516104 | tf_op jit(solution)/shard_map/ppermute | solution.py:67
  99.2 6.3 %collective-permute-start.19 = (bf16[112,768]{1,0:T(8,128)(2,1)S(1)}, bf16[112,768]{1,0:T(8,128)(2,1)S(1)}, u32[]{:S(2)}, u32[]{:S(2)}) collective-permute-start(bf16[112,768]{1,0:T(8,128)(2,1)S(1)} %fusion.1), channel_id=1, source_target_pairs={{0,8},{1,9},{2,10},{3,11},{4,12},{5,13},{6,14},{7,15},{8,0},{9,1},... | collective-permute-start | bytes 516104 | tf_op jit(solution)/shard_map/ppermute | solution.py:67
  105.6 7.7 %collective-permute-start.22 = (bf16[112,768]{1,0:T(8,128)(2,1)S(1)}, bf16[112,768]{1,0:T(8,128)(2,1)S(1)}, u32[]{:S(2)}, u32[]{:S(2)}) collective-permute-start(bf16[112,768]{1,0:T(8,128)(2,1)S(1)} %multiply_convert_fusion.refs_0_), channel_id=1, source_target_pairs={{0,1},{1,2},{2,3},{3,0},{4,5},{5,6},{6,7},{7,4},{8,9},{9,10},{10,1... | collective-permute-start | bytes 516104 | tf_op jit(solution)/shard_map/ppermute | solution.py:67
  105.7 7.6 %collective-permute-start.23 = (bf16[112,768]{1,0:T(8,128)(2,1)S(1)}, bf16[112,768]{1,0:T(8,128)(2,1)S(1)}, u32[]{:S(2)}, u32[]{:S(2)}) collective-permute-start(bf16[112,768]{1,0:T(8,128)(2,1)S(1)} %multiply_convert_fusion.refs_0_), channel_id=1, source_target_pairs={{0,2},{1,3},{2,0},{3,1},{4,6},{5,7},{6,4},{7,5},{8,10},{9,11},{10,... | collective-permute-start | bytes 516104 | tf_op jit(solution)/shard_map/ppermute | solution.py:67
  108.2 5.6 %collective-permute-start.24 = (bf16[112,768]{1,0:T(8,128)(2,1)S(1)}, bf16[112,768]{1,0:T(8,128)(2,1)S(1)}, u32[]{:S(2)}, u32[]{:S(2)}) collective-permute-start(bf16[112,768]{1,0:T(8,128)(2,1)S(1)} %multiply_convert_fusion.refs_0_), channel_id=1, source_target_pairs={{0,3},{1,0},{2,1},{3,2},{4,7},{5,4},{6,5},{7,6},{8,11},{9,8},{10,9... | collective-permute-start | bytes 516104 | tf_op jit(solution)/shard_map/ppermute | solution.py:67
  114.6 9.2 %collective-permute-start.26 = (bf16[784,384]{1,0:T(8,128)(2,1)S(1)}, bf16[784,384]{1,0:T(8,128)(2,1)S(1)}, u32[]{:S(2)}, u32[]{:S(2)}) collective-permute-start(bf16[784,384]{1,0:T(8,128)(2,1)S(1)} %join_rows.1.refs_0_), channel_id=1, source_target_pairs={{0,96},{1,97},{2,98},{3,99},{4,100},{5,101},{6,102},{7,103},{8,104... | collective-permute-start | bytes 1806344 | tf_op jit(solution)/shard_map/ppermute | solution.py:738
  115.9 10.8 %collective-permute-start.25 = (bf16[784,384]{1,0:T(8,128)(2,1)S(1)}, bf16[784,384]{1,0:T(8,128)(2,1)S(1)}, u32[]{:S(2)}, u32[]{:S(2)}) collective-permute-start(bf16[784,384]{1,0:T(8,128)(2,1)S(1)} %join_rows.1.refs_0_), channel_id=1, source_target_pairs={{0,32},{1,33},{2,34},{3,35},{4,36},{5,37},{6,38},{7,39},{8,40},{9,... | collective-permute-start | bytes 1806344 | tf_op jit(solution)/shard_map/ppermute | solution.py:738
  124.6 16.0 %collective-permute-start.28 = (bf16[400,384]{1,0:T(8,128)(2,1)}, bf16[400,384]{1,0:T(8,128)(2,1)S(1)}, u32[]{:S(2)}, u32[]{:S(2)}) collective-permute-start(bf16[400,384]{1,0:T(8,128)(2,1)} %slice.57), channel_id=1, source_target_pairs={{0,96},{1,97},{2,98},{3,99},{4,100},{5,101},{6,102},{7,103},{8,104... | collective-permute-start | bytes 921608 | tf_op jit(solution)/shard_map/ppermute | solution.py:738
  127.5 7.1 %collective-permute-start.27 = (bf16[384,384]{1,0:T(8,128)(2,1)}, bf16[384,384]{1,0:T(8,128)(2,1)}, u32[]{:S(2)}, u32[]{:S(2)}) collective-permute-start(bf16[384,384]{1,0:T(8,128)(2,1)} %slice.56), channel_id=1, source_target_pairs={{0,32},{1,33},{2,34},{3,35},{4,36},{5,37},{6,38},{7,39},{8,40},{9,... | collective-permute-start | bytes 884744 | tf_op jit(solution)/shard_map/ppermute | solution.py:738
  127.5 13.2 %collective-permute-start.29 = (bf16[784,384]{1,0:T(8,128)(2,1)S(1)}, bf16[784,384]{1,0:T(8,128)(2,1)S(1)}, u32[]{:S(2)}, u32[]{:S(2)}) collective-permute-start(bf16[784,384]{1,0:T(8,128)(2,1)S(1)} %join_rows.1.refs_0_), channel_id=1, source_target_pairs={{0,16},{16,0},{1,17},{17,1},{2,18},{18,2},{3,19},{19,3},{4,20},{20... | collective-permute-start | bytes 1806344 | tf_op jit(solution)/shard_map/ppermute | solution.py:743
  132.4 8.3 %collective-permute-start.30 = (bf16[784,384]{1,0:T(8,128)(2,1)S(1)}, bf16[784,384]{1,0:T(8,128)(2,1)S(1)}, u32[]{:S(2)}, u32[]{:S(2)}) collective-permute-start(bf16[784,384]{1,0:T(8,128)(2,1)S(1)} %collective-permute-done.25.refs_1_), channel_id=1, source_target_pairs={{0,16},{16,0},{1,17},{17,1},{2,18},{18,2},{3,19},{19,3},{4,20},{20... | collective-permute-start | bytes 1806344 | tf_op jit(solution)/shard_map/ppermute | solution.py:743
  132.4 8.3 %collective-permute-start.31 = (bf16[784,384]{1,0:T(8,128)(2,1)S(1)}, bf16[784,384]{1,0:T(8,128)(2,1)}, u32[]{:S(2)}, u32[]{:S(2)}) collective-permute-start(bf16[784,384]{1,0:T(8,128)(2,1)S(1)} %collective-permute-done.26.refs_2_), channel_id=1, source_target_pairs={{0,16},{16,0},{1,17},{17,1},{2,18},{18,2},{3,19},{19,3},{4,20},{20... | collective-permute-start | bytes 1806344 | tf_op jit(solution)/shard_map/ppermute | solution.py:743
  134.6 9.0 %collective-permute-start.32 = (bf16[384,384]{1,0:T(8,128)(2,1)}, bf16[384,384]{1,0:T(8,128)(2,1)S(1)}, u32[]{:S(2)}, u32[]{:S(2)}) collective-permute-start(bf16[384,384]{1,0:T(8,128)(2,1)} %collective-permute-done.27.refs_3_), channel_id=1, source_target_pairs={{0,16},{16,0},{1,17},{17,1},{2,18},{18,2},{3,19},{19,3},{4,20},{20... | collective-permute-start | bytes 884744 | tf_op jit(solution)/shard_map/ppermute | solution.py:743
  (8 other events, 43.1 us)

commit v8 on v7

--- a/solution.py
+++ b/solution.py
@@ -27,7 +27,7 @@
     def __init__(self, s_ref):
         x, core, z, y = (s_ref[n] for n in range(4))
         first = core == 0
-        self.core, self.y, self.valid = core, y, s_ref[4]
+        self.core, self.y = core, y
         self.head_at = jnp.where(first, y, z)
         self.row_at = jnp.where(first, z, y)
         self.first_at = jnp.where(first, x, y)
@@ -178,7 +178,7 @@
         def masks(n):
             far_by = (0, 1, 3, 2)[n]
             return jnp.concatenate(
-                [place + spot.base(far_by, i) * rows < spot.valid for i in range(4)], axis=1
+                [place + spot.base(far_by, i) * rows < s_ref[4] for i in range(4)], axis=1
             )
 
         def values_of(ref):
@@ -330,33 +330,18 @@
     def side(s_ref):
         return s_ref[1] if ours else 1 - s_ref[1]
 
-    def kernel(s_ref, b0, b1, b2, b3, low_ref, high_ref, dw_ref, tok_hbm, skip_hbm, ow_hbm, g_hbm, *refs):
+    def kernel(s_ref, b0, b1, b2, b3, low_ref, high_ref, dw_ref, tok_ref, skip_ref, ow_ref, g_ref, *refs):
         if ours:
             up_ref, act_ref = refs[:2]
             refs = refs[2:]
         else:
-            up_ref, prod_ref, act_ref, g_ref = refs[:4]
-            refs = refs[4:]
-        att, held, tok, skp, ow, sems = refs
+            up_ref, prod_ref, act_ref = refs[:3]
+            refs = refs[3:]
+        att, held = refs
         j = pl.program_id(0)
-
-        def copies(n):
-            take = pl.ds(pl.multiple_of(side(s_ref) * half + n * WIDE, 128), WIDE)
-            return [
-                pltpu.make_async_copy(ow_hbm.at[:, :, take], ow.at[n], sems.at[3 * n]),
-                pltpu.make_async_copy(tok_hbm.at[:, take], tok.at[n], sems.at[3 * n + 1]),
-                pltpu.make_async_copy(skip_hbm.at[:, take], skp.at[n], sems.at[3 * n + 2]),
-            ]
-
-        turned_copy = None if ours else pltpu.make_async_copy(g_hbm, g_ref, sems.at[3 * steps])
 
         @pl.when(j == 0)
         def _():
-            for n in range(steps):
-                for copy in copies(n):
-                    copy.start()
-            if not ours:
-                turned_copy.start()
             mixed = [b[:, :DV].astype(F32) for b in (b0, b1, b2, b3)]
             squares = sum(jnp.sum(m * m, axis=1, keepdims=True) for m in mixed)
             scale = lax.rsqrt(squares * (1.0 / (H * DV)) + 1e-05)
@@ -367,13 +352,12 @@
         def _():
             spot = Spot(s_ref)
             n = jnp.minimum(j, steps - 1)
-            for copy in copies(n):
-                copy.wait()
+            take = pl.ds(pl.multiple_of((side(s_ref) * steps + n) * WIDE, 128), WIDE)
             low, high = low_ref[...].astype(F32), high_ref[...].astype(F32)
             grown = jnp.zeros((rows + TAIL, WIDE), F32)
             for d in range(4):
-                grown += jnp.dot(att[d], ow[n, (spot.head_at + d) % 4], preferred_element_type=F32)
-            hidden = (tok[n].astype(F32) + grown[:rows]).astype(BF)
+                grown += jnp.dot(att[d], ow_ref[(spot.head_at + d) % 4, :, take], preferred_element_type=F32)
+            hidden = (tok_ref[:, take].astype(F32) + grown[:rows]).astype(BF)
             low_hid = (low[:1] + grown[rows : rows + 1]).astype(BF).astype(F32)
             high_hid = (high[:1] + grown[rows + 1 : rows + 2]).astype(BF).astype(F32)
             twice = lax.broadcasted_iota(jnp.int32, (fine, rows), 0) // 2
@@ -389,7 +373,7 @@
             held[TAIL + fine :, :] = edge
             up_ref[TAIL + fine :, :] = edge.astype(BF)
             for k in range(0, fine, STRIP):
-                up = (doubled[k : k + STRIP] + skp[n, k : k + STRIP, :].astype(F32)).astype(BF)
+                up = (doubled[k : k + STRIP] + skip_ref[k : k + STRIP, take].astype(F32)).astype(BF)
                 up_ref[TAIL + k : TAIL + k + STRIP, :] = up
                 held[TAIL + k : TAIL + k + STRIP, :] = up.astype(F32)
             w = [dw_ref[t : t + 1, :] for t in range(3)]
@@ -401,10 +385,6 @@
                 act_ref[k : k + STRIP, cut] = (pre * (0.5 + 0.5 * bend)).astype(BF)
 
         if not ours:
-
-            @pl.when(j == steps)
-            def _():
-                turned_copy.wait()
 
             @pl.when(j >= steps)
             def _():
@@ -435,14 +415,10 @@
         out_specs += [
             pl.BlockSpec((2, quarter, half), lambda j, s_ref: (jnp.maximum(j - steps, 0), 0, 0))
         ]
-        scratch += [pltpu.VMEM((fine, half), BF), pltpu.VMEM((columns, fine), BF)]
+        scratch += [pltpu.VMEM((fine, half), BF)]
     scratch += [
         pltpu.VMEM((4, rows + TAIL, DV), BF),
         pltpu.VMEM((fine + 2 * TAIL, WIDE), F32),
-        pltpu.VMEM((steps, rows, WIDE), BF),
-        pltpu.VMEM((steps, fine, WIDE), BF),
-        pltpu.VMEM((steps, H, DV, WIDE), BF),
-        pltpu.SemaphoreType.DMA((3 * steps + 1,)),
     ]
     return pl.pallas_call(
         kernel,
@@ -452,16 +428,38 @@
             grid=(steps if ours else steps + 2,),
             in_specs=[flat(rows + TAIL, 256)] * 4
             + [cols(TAIL, True), cols(TAIL, True), cols(3, True)]
-            + [ANY] * 4,
+            + [VMEM] * 4,
             out_specs=out_specs,
             scratch_shapes=scratch,
         ),
-        compiler_params=params(53),
+        compiler_params=params(24),
         cost_estimate=pl.CostEstimate(
             flops=2 * fine * columns * columns, bytes_accessed=9 << 20, transcendentals=fine * half
         ),
         name="forward",
     )(scalars, *back, before, after, depth_weight, tokens, skipped, out_heads, turned)
+
+
+def load(behind, *arrays):
+    count = len(arrays)
+
+    def kernel(behind_ref, *refs):
+        sems = refs[-1]
+        copies = [pltpu.make_async_copy(refs[n], refs[count + n], sems.at[n]) for n in range(count)]
+        for copy in copies:
+            copy.start()
+        for copy in copies:
+            copy.wait()
+
+    return pl.pallas_call(
+        kernel,
+        out_shape=[jax.ShapeDtypeStruct(a.shape, a.dtype) for a in arrays],
+        in_specs=[ANY] * (1 + count),
+        out_specs=[VMEM] * count,
+        scratch_shapes=[pltpu.SemaphoreType.DMA((count,))],
+        compiler_params=params(45),
+        name="load",
+    )(behind, *arrays)
 
 
 def backward(scalars, theirs, ours, upstream, before, after, point_weight, depth_weight, behind):
@@ -645,37 +643,46 @@
 
 
 def lay_out(scalars, own, other):
-    part, quarter = own[3].shape
-    half = 2 * part
+    half, quarter = own[0].shape[0] - TAIL, own[0].shape[1]
+    parts = 4
+    part = half // parts
 
     def kernel(s_ref, *refs):
-        out, sems = refs[-2:]
+        out, depth, sems = refs[-3:]
         spot = Spot(s_ref)
         copies = []
-        for n in range(10):
-            mine = n < 5
-            d, start, count = ((0, 0, half), (1, 0, half), (3, 0, half), (2, 0, part), (2, part, part))[n % 5]
-            down = (spot.core if mine else 1 - spot.core) * half + start
-            over = ((spot.first_at if mine else spot.their_first) + 4 - d) % 4 * quarter
-            copies.append(
-                pltpu.make_async_copy(
-                    refs[n].at[pl.ds(0, count), :],
-                    out.at[pl.ds(pl.multiple_of(down, 16), count), pl.ds(pl.multiple_of(over, 128), quarter)],
-                    sems.at[n],
+        for n in range(8):
+            mine = n < 4
+            down = (spot.core if mine else 1 - spot.core) * half
+            over = ((spot.first_at if mine else spot.their_first) + 4 - n % 4) % 4 * quarter
+            for k in range(parts):
+                start = pl.multiple_of(down + k * part, 16)
+                copies.append(
+                    pltpu.make_async_copy(
+                        refs[n].at[pl.ds(k * part, part), :],
+                        out.at[pl.ds(start, part), pl.ds(pl.multiple_of(over, 128), quarter)],
+                        sems.at[parts * n + k],
+                    )
                 )
-            )
         for copy in copies:
             copy.start()
+        for n, side in ((0, spot.core), (4, 1 - spot.core)):
+            rows = total_of([refs[n + d][half:, :] for d in range(4)])
+            rows = jnp.concatenate([rows[:3], rows[8:11]], axis=1)
+            depth[:, pl.ds(pl.multiple_of(side * half, 128), half)] = rows
         for copy in copies:
             copy.wait()
 
     return pl.pallas_call(
         kernel,
-        out_shape=jax.ShapeDtypeStruct((2 * half, 4 * quarter), BF),
-        in_specs=[SMEM] + [VMEM] * 10,
-        out_specs=ANY,
-        scratch_shapes=[pltpu.SemaphoreType.DMA((10,))],
-        compiler_params=params(8),
+        out_shape=[
+            jax.ShapeDtypeStruct((2 * half, 4 * quarter), BF),
+            jax.ShapeDtypeStruct((3, 2 * half), F32),
+        ],
+        in_specs=[SMEM] + [VMEM] * 8,
+        out_specs=[ANY, VMEM],
+        scratch_shapes=[pltpu.SemaphoreType.DMA((8 * parts,))],
+        compiler_params=params(12),
         name="lay_out",
     )(scalars, *own, *other)
 
@@ -696,8 +703,9 @@
     rows, columns = tokens.shape
     fine = skipped.shape[0]
     ix, ic, iz, iy = (lax.axis_index(a) for a in AXES)
-    scalars = jnp.stack([v.astype(jnp.int32) for v in (ix, ic, iz, iy, valid_bins[0])])
-    blocks = project(scalars, tokens, query_weight, key_weight, value_weight)
+    spot = jnp.stack([v.astype(jnp.int32) for v in (ix, ic, iz, iy)])
+    scalars = jnp.concatenate([spot, valid_bins.astype(jnp.int32)])
+    blocks = project(spot, tokens, query_weight, key_weight, value_weight)
     down, up = edges(blocks[0], tokens, skipped, upstream)
     before = lax.ppermute(down, ("z", "y"), [(i, i + 1) for i in range(15)])
     after = lax.ppermute(up, ("z", "y"), [(i + 1, i) for i in range(15)])
@@ -712,8 +720,9 @@
     state = attend(scalars, 2, q, [far[3]], state)
     mixed = attend(scalars, 3, q, [own, far[1], far[3], far[2]], state, (before, after))
     back = exchange(mixed, HEAD_RING, -1)
+    tokens_v, skipped_v, out_v = load(mixed[0], tokens, skipped, out_weight.reshape(H, DV, -1))
     swap = [(0, 1), (1, 0)]
-    given = (back, tokens, skipped, out_weight.reshape(H, DV, -1), before, after, depth_weight, turned)
+    given = (back, tokens_v, skipped_v, out_v, before, after, depth_weight, turned)
     up_theirs, sent = forward(scalars, False, *given)
     arrived = lax.ppermute(sent, "c", swap)
     up_ours, act = forward(scalars, True, *given)
@@ -734,23 +743,9 @@
     summed = (total_of(got) * norm_scale).astype(BF)
     joined = join_rows(scalars, exchange([summed] * 4, SUM_RINGS[1]))
 
-    def go(block, step):
-        return lax.ppermute(block, AXES, turn(SUM_RINGS[0], step))
-
-    half, part = columns // 2, columns // 4
-    one, three = go(joined, 1), go(joined, 3)
-    own = [joined, one, three, go(one[:part], 1), go(three[part:], 3)]
-    other = [lax.ppermute(p, "c", swap) for p in own]
-    grad_pointwise = lay_out(scalars, own, other)
-
-    def depth_of(blocks):
-        rows = total_of([blocks[0][half:], blocks[1][half:], blocks[4][part:], blocks[2][half:]])
-        return jnp.concatenate([rows[:3], rows[8:11]], axis=1)
-
-    d_own, d_other = depth_of(own), depth_of(other)
-    grad_depth = jnp.concatenate(
-        [jnp.where(ic == 0, d_own, d_other), jnp.where(ic == 0, d_other, d_own)], axis=1
-    )
+    own = exchange([joined] * 4, SUM_RINGS[0])
+    other = [lax.ppermute(block, "c", swap) for block in own]
+    grad_pointwise, grad_depth = lay_out(scalars, own, other)
     return (grad_pointwise, grad_depth, grad_skip[None])
 
 

time: 148 us -> 139 us (0.939)
  waiting for transfers between devices: 36.4 us -> 31.5 us
  Pallas kernels: 49.6 us -> 48 us
    ppermute x9 -> x4, waiting for transfers between devices: 11 us -> 1.64 us  [local(): other = [lax.ppermute(block, 'c', swap) for block in own]]
    ppermute x18 -> x21, waiting for transfers between devices: 23 us -> 27.8 us  [exchange(): got[d] = lax.ppermute(pieces[d], AXES, turn(axes, sign * d))]
    pallas_call x2, Pallas kernels: 13.6 us -> 9.4 us  [forward(): pl.pallas_call(kernel, out_shape=outs, grid_spec=pltpu.PrefetchScalarGrid...]
    ppermute x9 -> x4, starting transfers between devices: 15.1 us -> 10.9 us  [local(): other = [lax.ppermute(block, 'c', swap) for block in own]]
    ppermute x18 -> x21, starting transfers between devices: 26.2 us -> 29.7 us  [exchange(): got[d] = lax.ppermute(pieces[d], AXES, turn(axes, sign * d))]
    pallas_call x1 -> x2, Pallas kernels: 3.44 us -> 5.45 us  [the longest x1 3.6 us: lay_out(): pl.pallas_call(kernel, out_shape=[jax.ShapeDtypeStruct((2 * half, 4 * qua...]
    slice x4 -> x0, local copies, waits for them, and re-layouts: 1.5 us -> none  [the longest x2 1.49 us: local(): own = [joined, one, three, go(one[:part], 1), go(three[part:], 3)]]
  transfers between devices with their start and end apart: 34 -> 32, of which waited for: 15 -> 14; matrix products, arithmetic and copies ran while one was open for 3% -> 1% of each run, Pallas kernels for 19% -> 21%
where the time goes in v8:
time: 139 us; the launch traced here: 138 us
  starting transfers between devices  53.6 us (39%)
  Pallas kernels  48 us (35%)
  waiting for transfers between devices  31.5 us (23%)
  local copies, waits for them, and re-layouts  3.22 us (2%)
  between operations  1.71 us (1%)
    ppermute x21, starting transfers between devices, exchange(): got[d] = lax.ppermute(pieces[d], AXES, turn(axes, sign * d))  29.7 us
    ppermute x21, waiting for transfers between devices, exchange(): got[d] = lax.ppermute(pieces[d], AXES, turn(axes, sign * d))  27.8 us
    pallas_call x1, Pallas kernels, backward(): pl.pallas_call(kernel, out_shape=[jax.ShapeDtypeStruct((fine, columns), B...  12.9 us
    ppermute x4, starting transfers between devices, local(): other = [lax.ppermute(block, 'c', swap) for block in own]  10.9 us
    pallas_call x4, Pallas kernels, attend(): pl.pallas_call(kernel, out_shape=outs, in_specs=[SMEM] + [VMEM] * len(ins...  10.3 us
    pallas_call x2, Pallas kernels, forward(): pl.pallas_call(kernel, out_shape=outs, grid_spec=pltpu.PrefetchScalarGrid...  9.4 us
    pallas_call x1, Pallas kernels, project(): pl.pallas_call(kernel, out_shape=[jax.ShapeDtypeStruct((rows, 384), BF)]...  4.48 us
    ppermute x3, starting transfers between devices, local(): far = {d: lax.ppermute(own, AXES, turn(ROW_RING, d)) for d in (1, 3, 2)}  4.15 us
  transfers between devices with their start and end apart: 32, of which 14 were waited for; matrix products, arithmetic and copies ran while one was open for 1% of the time, Pallas kernels for 21%

profile of v8, /device:TPU:1, one launch (start us, length us, event | category | flops | bytes accessed | tf_op | source)
XLA Modules:
  0.0 138.3 jit_solution(17386930512708672909)
XLA Ops:
  0.7 4.5 %project.1 = (bf16[256,384]{1,0:T(8,128)(2,1)S(1)}, bf16[256,384]{1,0:T(8,128)(2,1)S(1)}, bf16[256,384]{1,0:T(8,128)(2,1)S(1)}, bf16[256,384]{1,0:T(8,128)(2,1)S(1)}) custom-call(s32[4]{0:T(128)S(1)} %pad_add_fusion.at_ref, bf16[256,1536]{1,0:T(8,128)(2,1)} %bitcast.11, bf16[1536,256]{1,0:T(8,128)(2,1)} %wq_hbm.1, bf16[1536,256]{1,0:T(8,128)(2,1)} %wk_hbm.1, ...), custom_call_target="tpu_custom_call" | custom-call | tf_op jit(solution)/shard_map/project/pallas_call | solution.py:116
  5.2 2.5 %collective-permute-start = (bf16[256,384]{1,0:T(8,128)(2,1)S(1)}, bf16[256,384]{1,0:T(8,128)(2,1)S(1)}, u32[]{:S(2)}, u32[]{:S(2)}) collective-permute-start(bf16[256,384]{1,0:T(8,128)(2,1)S(1)} %get-tuple-element.40), channel_id=1, source_target_pairs={{0,1},{1,2},{2,3},{3,0},{4,5},{5,6},{6,7},{7,4},{8,9},{9,10},{10,1... | collective-permute-start | bytes 589832 | tf_op jit(solution)/shard_map/ppermute | solution.py:67
  7.7 3.3 %collective-permute-start.1 = (bf16[256,384]{1,0:T(8,128)(2,1)S(1)}, bf16[256,384]{1,0:T(8,128)(2,1)S(1)}, u32[]{:S(2)}, u32[]{:S(2)}) collective-permute-start(bf16[256,384]{1,0:T(8,128)(2,1)S(1)} %get-tuple-element.41), channel_id=1, source_target_pairs={{0,2},{1,3},{2,0},{3,1},{4,6},{5,7},{6,4},{7,5},{8,10},{9,11},{10,... | collective-permute-start | bytes 589832 | tf_op jit(solution)/shard_map/ppermute | solution.py:67
  13.2 3.3 %collective-permute-done.1.refs_2_ = bf16[256,384]{1,0:T(8,128)(2,1)S(1)} collective-permute-done((bf16[256,384]{1,0:T(8,128)(2,1)S(1)}, bf16[256,384]{1,0:T(8,128)(2,1)S(1)}, u32[]{:S(2)}, u32[]{:S(2)}) %collective-permute-start.1) | collective-permute-done | bytes 196640 | tf_op jit(solution)/shard_map/ppermute | solution.py:67
  20.7 2.3 %collective-permute-start.6 = (bf16[16,1536]{1,0:T(8,128)(2,1)S(1)}, bf16[16,1536]{1,0:T(8,128)(2,1)S(1)}, u32[]{:S(2)}, u32[]{:S(2)}) collective-permute-start(bf16[16,1536]{1,0:T(8,128)(2,1)S(1)} %get-tuple-element.43.refs_4_), channel_id=1, source_target_pairs={{0,1},{1,2},{2,3},{3,4},{4,5},{5,6},{6,7},{7,8},{8,9},{9,10},{10,1... | collective-permute-start | bytes 147464 | tf_op jit(solution)/shard_map/ppermute | solution.py:710
  25.0 2.1 %attend.4 = (f32[1024,256]{1,0:T(8,128)S(1)}, f32[1024,128]{1,0:T(8,128)S(1)}) custom-call(s32[5]{0:T(128)S(1)} %concatenate.7.s_ref.at_ref, bf16[256,384]{1,0:T(8,128)(2,1)S(1)} %get-tuple-element.39.mark_ref.refs_0_, bf16[256,384]{1,0:T(8,128)(2,1)S(1)} %collective-permute-done.refs_1_, bf16[256,384]{1,0:T(8,128)(2,1)S(1)} %collective-permute-done.1.refs_2_, ...), custom_call_target="tpu_custom_call" | custom-call | flops 1073741824 | bytes 4194304 | tf_op jit(solution)/shard_map/attend/pallas_call | solution.py:255
  27.2 2.2 %attend.5 = (f32[1024,256]{1,0:T(8,128)S(1)}, f32[1024,128]{1,0:T(8,128)S(1)}) custom-call(s32[5]{0:T(128)S(1)} %concatenate.7.s_ref.at_ref, bf16[256,384]{1,0:T(8,128)(2,1)S(1)} %get-tuple-element.39.mark_ref.refs_0_, bf16[256,384]{1,0:T(8,128)(2,1)S(1)} %collective-permute-done.refs_1_, bf16[256,384]{1,0:T(8,128)(2,1)S(1)} %collective-permute-done.1.refs_2_, ...), custom_call_target="tpu_custom_call" | custom-call | flops 1073741824 | bytes 4194304 | tf_op jit(solution)/shard_map/attend/pallas_call | solution.py:255
  29.4 1.8 %collective-permute-done.4.refs_4_.refs_6_ = bf16[1040,256]{1,0:T(8,128)(2,1)S(1)} collective-permute-done((bf16[1040,256]{1,0:T(8,128)(2,1)S(1)}, bf16[1040,256]{1,0:T(8,128)(2,1)S(1)}, u32[]{:S(2)}, u32[]{:S(2)}) %collective-permute-start.4) | collective-permute-done | bytes 532512 | tf_op jit(solution)/shard_map/ppermute | solution.py:714
  31.2 2.2 %attend.6 = (f32[1024,256]{1,0:T(8,128)S(1)}, f32[1024,128]{1,0:T(8,128)S(1)}) custom-call(s32[5]{0:T(128)S(1)} %concatenate.7.s_ref.at_ref, bf16[256,384]{1,0:T(8,128)(2,1)S(1)} %get-tuple-element.39.mark_ref.refs_0_, bf16[256,384]{1,0:T(8,128)(2,1)S(1)} %collective-permute-done.refs_1_, bf16[256,384]{1,0:T(8,128)(2,1)S(1)} %collective-permute-done.1.refs_2_, ...), custom_call_target="tpu_custom_call" | custom-call | flops 1073741824 | bytes 4194304 | tf_op jit(solution)/shard_map/attend/pallas_call | solution.py:255
  33.5 3.8 %attend.7 = (bf16[272,256]{1,0:T(8,128)(2,1)S(1)}, bf16[272,256]{1,0:T(8,128)(2,1)}, bf16[272,256]{1,0:T(8,128)(2,1)S(1)}, bf16[272,256]{1,0:T(8,128)(2,1)S(1)}) custom-call(s32[5]{0:T(128)S(1)} %concatenate.7.s_ref.at_ref, bf16[256,384]{1,0:T(8,128)(2,1)S(1)} %get-tuple-element.39.mark_ref.refs_0_, bf16[256,384]{1,0:T(8,128)(2,1)S(1)} %collective-permute-done.refs_1_, ...), custom_call_target="tpu_custom_call" | custom-call | flops 1073741824 | bytes 4194304 | tf_op jit(solution)/shard_map/attend/pallas_call | solution.py:255
  37.3 4.0 %collective-permute-start.8 = (bf16[272,256]{1,0:T(8,128)(2,1)}, bf16[272,256]{1,0:T(8,128)(2,1)S(1)}, u32[]{:S(2)}, u32[]{:S(2)}) collective-permute-start(bf16[272,256]{1,0:T(8,128)(2,1)} %get-tuple-element.52), channel_id=1, source_target_pairs={{0,3},{1,0},{2,1},{3,2},{4,7},{5,4},{6,5},{7,6},{8,11},{9,8},{10,9... | collective-permute-start | bytes 417800 | tf_op jit(solution)/shard_map/ppermute | solution.py:67
  45.5 1.8 %load.1 = (bf16[256,1536]{1,0:T(8,128)(2,1)S(1)}, bf16[512,1536]{1,0:T(8,128)(2,1)S(1)}, bf16[4,192,1536]{2,1,0:T(8,128)(2,1)S(1)}) custom-call(bf16[272,256]{1,0:T(8,128)(2,1)S(1)} %get-tuple-element.51.behind_ref.b0, bf16[256,1536]{1,0:T(8,128)(2,1)S(1)} %bitcast.13, bf16[512,1536]{1,0:T(8,128)(2,1)S(1)} %bitcast.18, bf16[4,192,1536]{2,1,0:T(8,128)(2,1)} %bitcast.19), custom_call_target="tpu_custom_call" | custom-call | tf_op jit(solution)/shard_map/load/pallas_call | solution.py:454
  48.5 5.5 %forward.3 = (bf16[544,768]{1,0:T(8,128)(2,1)S(1)}, bf16[4,384,768]{2,1,0:T(8,128)(2,1)S(1)}) custom-call(s32[5]{0:T(128)S(1)} %concatenate.7.s_ref.at_ref, bf16[272,256]{1,0:T(8,128)(2,1)S(1)} %get-tuple-element.51.behind_ref.b0, bf16[272,256]{1,0:T(8,128)(2,1)S(1)} %collective-permute-done.8.b1, bf16[272,256]{1,0:T(8,128)(2,1)S(1)} %collective-permute-done.9.b2, ...), custom_call_target="tpu_custom_call" | custom-call | flops 2415919104 | bytes 9437184 | tf_op jit(solution)/shard_map/forward/pallas_call | solution.py:423
  54.0 2.2 %collective-permute-start.11 = (bf16[4,384,768]{2,1,0:T(8,128)(2,1)S(1)}, bf16[4,384,768]{2,1,0:T(8,128)(2,1)S(1)}, u32[]{:S(2)}, u32[]{:S(2)}) collective-permute-start(bf16[4,384,768]{2,1,0:T(8,128)(2,1)S(1)} %get-tuple-element.59), channel_id=1, source_target_pairs={{0,16},{16,0},{1,17},{17,1},{2,18},{18,2},{3,19},{19,3},{4,20},{20... | collective-permute-start | bytes 7077896 | tf_op jit(solution)/shard_map/ppermute | solution.py:727
  56.2 3.9 %forward.2 = (bf16[544,768]{1,0:T(8,128)(2,1)S(1)}, bf16[512,768]{1,0:T(8,128)(2,1)S(1)}) custom-call(s32[5]{0:T(128)S(1)} %concatenate.7.s_ref.at_ref, bf16[272,256]{1,0:T(8,128)(2,1)S(1)} %get-tuple-element.51.behind_ref.b0, bf16[272,256]{1,0:T(8,128)(2,1)S(1)} %collective-permute-done.8.b1, bf16[272,256]{1,0:T(8,128)(2,1)S(1)} %collective-permute-done.9.b2, ...), custom_call_target="tpu_custom_call" | custom-call | flops 2415919104 | bytes 9437184 | tf_op jit(solution)/shard_map/forward/pallas_call | solution.py:423
  61.9 2.2 %collective-permute-start.13 = (bf16[384,768]{1,0:T(8,128)(2,1)S(1)}, bf16[384,768]{1,0:T(8,128)(2,1)S(1)}, u32[]{:S(2)}, u32[]{:S(2)}) collective-permute-start(bf16[384,768]{1,0:T(8,128)(2,1)S(1)} %get-tuple-element.62), channel_id=1, source_target_pairs={{0,64},{1,65},{2,66},{3,67},{4,68},{5,69},{6,70},{7,71},{8,72},{9,... | collective-permute-start | bytes 1769480 | tf_op jit(solution)/shard_map/ppermute | solution.py:67
  66.1 12.9 %backward.1 = (bf16[512,1536]{1,0:T(8,128)(2,1)}, f32[3,768]{1,0:T(4,128)S(1)}, f32[3,768]{1,0:T(4,128)S(1)}) custom-call(s32[5]{0:T(128)S(1)} %concatenate.7.s_ref.at_ref, bf16[544,768]{1,0:T(8,128)(2,1)S(1)} %get-tuple-element.68.theirs_ref, bf16[544,768]{1,0:T(8,128)(2,1)S(1)} %get-tuple-element.69.ours_ref, bf16[512,1536]{1,0:T(8,128)(2,1)S(1)} %bitcast.16, ...), custom_call_target="tpu_custom_call" | custom-call | flops 2415919104 | bytes 11534336 | tf_op jit(solution)/shard_map/backward/pallas_call | solution.py:543
  79.1 3.0 %collective-permute-start.18 = (f32[3,768]{1,0:T(4,128)S(1)}, f32[3,768]{1,0:T(4,128)S(1)}, u32[]{:S(2)}, u32[]{:S(2)}) collective-permute-start(f32[3,768]{1,0:T(4,128)S(1)} %get-tuple-element.71), channel_id=1, source_target_pairs={{0,16},{16,0},{1,17},{17,1},{2,18},{18,2},{3,19},{19,3},{4,20},{20... | collective-permute-start | bytes 27656 | tf_op jit(solution)/shard_map/ppermute | solution.py:736
  83.0 4.0 %collective-permute-start.15 = (bf16[96,768]{1,0:T(8,128)(2,1)S(1)}, bf16[96,768]{1,0:T(8,128)(2,1)S(1)}, u32[]{:S(2)}, u32[]{:S(2)}) collective-permute-start(bf16[96,768]{1,0:T(8,128)(2,1)S(1)} %get-tuple-element.65), channel_id=1, source_target_pairs={{0,2},{1,3},{2,0},{3,1},{4,6},{5,7},{6,4},{7,5},{8,10},{9,11},{10,... | collective-permute-start | bytes 442376 | tf_op jit(solution)/shard_map/ppermute | solution.py:67
  87.0 2.7 %collective-permute-start.17 = (bf16[96,768]{1,0:T(8,128)(2,1)S(1)}, bf16[96,768]{1,0:T(8,128)(2,1)S(1)}, u32[]{:S(2)}, u32[]{:S(2)}) collective-permute-start(bf16[96,768]{1,0:T(8,128)(2,1)S(1)} %get-tuple-element.67), channel_id=1, source_target_pairs={{0,3},{1,0},{2,1},{3,2},{4,7},{5,4},{6,5},{7,6},{8,11},{9,8},{10,9... | collective-permute-start | bytes 442376 | tf_op jit(solution)/shard_map/ppermute | solution.py:67
  89.7 2.5 %collective-permute-done.16 = bf16[96,768]{1,0:T(8,128)(2,1)S(1)} collective-permute-done((bf16[96,768]{1,0:T(8,128)(2,1)S(1)}, bf16[96,768]{1,0:T(8,128)(2,1)S(1)}, u32[]{:S(2)}, u32[]{:S(2)}) %collective-permute-start.16) | collective-permute-done | bytes 147488 | tf_op jit(solution)/shard_map/ppermute | solution.py:67
  95.2 4.8 %collective-permute-done.20 = bf16[112,768]{1,0:T(8,128)(2,1)S(1)} collective-permute-done((bf16[112,768]{1,0:T(8,128)(2,1)S(1)}, bf16[112,768]{1,0:T(8,128)(2,1)S(1)}, u32[]{:S(2)}, u32[]{:S(2)}) %collective-permute-start.20) | collective-permute-done | bytes 172064 | tf_op jit(solution)/shard_map/ppermute | solution.py:67
  100.7 2.7 %collective-permute-start.24 = (bf16[112,768]{1,0:T(8,128)(2,1)S(1)}, bf16[112,768]{1,0:T(8,128)(2,1)S(1)}, u32[]{:S(2)}, u32[]{:S(2)}) collective-permute-start(bf16[112,768]{1,0:T(8,128)(2,1)S(1)} %multiply_convert_fusion.refs_0_), channel_id=1, source_target_pairs={{0,3},{1,0},{2,1},{3,2},{4,7},{5,4},{6,5},{7,6},{8,11},{9,8},{10,9... | collective-permute-start | bytes 516104 | tf_op jit(solution)/shard_map/ppermute | solution.py:67
  104.1 3.5 %collective-permute-done.24.refs_3_ = bf16[112,768]{1,0:T(8,128)(2,1)S(1)} collective-permute-done((bf16[112,768]{1,0:T(8,128)(2,1)S(1)}, bf16[112,768]{1,0:T(8,128)(2,1)S(1)}, u32[]{:S(2)}, u32[]{:S(2)}) %collective-permute-start.24) | collective-permute-done | bytes 172064 | tf_op jit(solution)/shard_map/ppermute | solution.py:67
  107.6 1.9 %collective-permute-done.23.refs_2_ = bf16[112,768]{1,0:T(8,128)(2,1)S(1)} collective-permute-done((bf16[112,768]{1,0:T(8,128)(2,1)S(1)}, bf16[112,768]{1,0:T(8,128)(2,1)S(1)}, u32[]{:S(2)}, u32[]{:S(2)}) %collective-permute-start.23) | collective-permute-done | bytes 172064 | tf_op jit(solution)/shard_map/ppermute | solution.py:67
  113.8 2.9 %collective-permute-start.28 = (bf16[784,384]{1,0:T(8,128)(2,1)S(1)}, bf16[784,384]{1,0:T(8,128)(2,1)S(1)}, u32[]{:S(2)}, u32[]{:S(2)}) collective-permute-start(bf16[784,384]{1,0:T(8,128)(2,1)S(1)} %join_rows.1.refs_0_), channel_id=1, source_target_pairs={{0,16},{16,0},{1,17},{17,1},{2,18},{18,2},{3,19},{19,3},{4,20},{20... | collective-permute-start | bytes 1806344 | tf_op jit(solution)/shard_map/ppermute | solution.py:747
  116.6 4.4 %collective-permute-done.27.refs_3_ = bf16[784,384]{1,0:T(8,128)(2,1)S(1)} collective-permute-done((bf16[784,384]{1,0:T(8,128)(2,1)S(1)}, bf16[784,384]{1,0:T(8,128)(2,1)S(1)}, u32[]{:S(2)}, u32[]{:S(2)}) %collective-permute-start.27) | collective-permute-done | bytes 602144 | tf_op jit(solution)/shard_map/ppermute | solution.py:67
  121.1 2.8 %collective-permute-start.31 = (bf16[784,384]{1,0:T(8,128)(2,1)S(1)}, bf16[784,384]{1,0:T(8,128)(2,1)S(1)}, u32[]{:S(2)}, u32[]{:S(2)}) collective-permute-start(bf16[784,384]{1,0:T(8,128)(2,1)S(1)} %collective-permute-done.27.refs_3_), channel_id=1, source_target_pairs={{0,16},{16,0},{1,17},{17,1},{2,18},{18,2},{3,19},{19,3},{4,20},{20... | collective-permute-start | bytes 1806344 | tf_op jit(solution)/shard_map/ppermute | solution.py:747
  123.9 2.6 %collective-permute-start.30 = (bf16[784,384]{1,0:T(8,128)(2,1)S(1)}, bf16[784,384]{1,0:T(8,128)(2,1)S(1)}, u32[]{:S(2)}, u32[]{:S(2)}) collective-permute-start(bf16[784,384]{1,0:T(8,128)(2,1)S(1)} %collective-permute-done.26.refs_2_), channel_id=1, source_target_pairs={{0,16},{16,0},{1,17},{17,1},{2,18},{18,2},{3,19},{19,3},{4,20},{20... | collective-permute-start | bytes 1806344 | tf_op jit(solution)/shard_map/ppermute | solution.py:747
  126.5 3.7 %collective-permute-done.25.refs_1_ = bf16[784,384]{1,0:T(8,128)(2,1)S(1)} collective-permute-done((bf16[784,384]{1,0:T(8,128)(2,1)S(1)}, bf16[784,384]{1,0:T(8,128)(2,1)S(1)}, u32[]{:S(2)}, u32[]{:S(2)}) %collective-permute-start.25) | collective-permute-done | bytes 602144 | tf_op jit(solution)/shard_map/ppermute | solution.py:67
  130.2 2.6 %collective-permute-start.29 = (bf16[784,384]{1,0:T(8,128)(2,1)S(1)}, bf16[784,384]{1,0:T(8,128)(2,1)S(1)}, u32[]{:S(2)}, u32[]{:S(2)}) collective-permute-start(bf16[784,384]{1,0:T(8,128)(2,1)S(1)} %collective-permute-done.25.refs_1_), channel_id=1, source_target_pairs={{0,16},{16,0},{1,17},{17,1},{2,18},{18,2},{3,19},{19,3},{4,20},{20... | collective-permute-start | bytes 1806344 | tf_op jit(solution)/shard_map/ppermute | solution.py:747
  134.5 3.6 %lay_out.1 = (bf16[1536,1536]{1,0:T(8,128)(2,1)}, f32[3,1536]{1,0:T(4,128)}) custom-call(s32[5]{0:T(128)S(1)} %concatenate.7.s_ref.at_ref, bf16[784,384]{1,0:T(8,128)(2,1)S(1)} %join_rows.1.refs_0_, bf16[784,384]{1,0:T(8,128)(2,1)S(1)} %collective-permute-done.25.refs_1_, bf16[784,384]{1,0:T(8,128)(2,1)S(1)} %collective-permute-done.26.refs_2_, ...), custom_call_target="tpu_custom_call" | custom-call | tf_op jit(solution)/shard_map/lay_out/pallas_call | solution.py:676
  (63 shorter events, 28.1 us)
Async XLA Ops:
  5.2 8.0 %collective-permute-start = (bf16[256,384]{1,0:T(8,128)(2,1)S(1)}, bf16[256,384]{1,0:T(8,128)(2,1)S(1)}, u32[]{:S(2)}, u32[]{:S(2)}) collective-permute-start(bf16[256,384]{1,0:T(8,128)(2,1)S(1)} %get-tuple-element.40), channel_id=1, source_target_pairs={{0,1},{1,2},{2,3},{3,0},{4,5},{5,6},{6,7},{7,4},{8,9},{9,10},{10,1... | collective-permute-start | bytes 589832 | tf_op jit(solution)/shard_map/ppermute | solution.py:67
  7.7 8.8 %collective-permute-start.1 = (bf16[256,384]{1,0:T(8,128)(2,1)S(1)}, bf16[256,384]{1,0:T(8,128)(2,1)S(1)}, u32[]{:S(2)}, u32[]{:S(2)}) collective-permute-start(bf16[256,384]{1,0:T(8,128)(2,1)S(1)} %get-tuple-element.41), channel_id=1, source_target_pairs={{0,2},{1,3},{2,0},{3,1},{4,6},{5,7},{6,4},{7,5},{8,10},{9,11},{10,... | collective-permute-start | bytes 589832 | tf_op jit(solution)/shard_map/ppermute | solution.py:67
  11.0 5.5 %collective-permute-start.2 = (bf16[256,384]{1,0:T(8,128)(2,1)S(1)}, bf16[256,384]{1,0:T(8,128)(2,1)S(1)}, u32[]{:S(2)}, u32[]{:S(2)}) collective-permute-start(bf16[256,384]{1,0:T(8,128)(2,1)S(1)} %get-tuple-element.42), channel_id=1, source_target_pairs={{0,3},{1,0},{2,1},{3,2},{4,7},{5,4},{6,5},{7,6},{8,11},{9,8},{10,9... | collective-permute-start | bytes 589832 | tf_op jit(solution)/shard_map/ppermute | solution.py:67
  16.6 10.6 %collective-permute-start.3 = (bf16[1040,256]{1,0:T(8,128)(2,1)S(1)}, bf16[1040,256]{1,0:T(8,128)(2,1)S(1)}, u32[]{:S(2)}, u32[]{:S(2)}) collective-permute-start(bf16[1040,256]{1,0:T(8,128)(2,1)S(1)} %stack_rows.1.refs_4_), channel_id=1, source_target_pairs={{0,4},{1,5},{2,6},{3,7},{4,8},{5,9},{6,10},{7,11},{8,12},{9,13},{1... | collective-permute-start | bytes 1597448 | tf_op jit(solution)/shard_map/ppermute | solution.py:714
  17.6 13.6 %collective-permute-start.4 = (bf16[1040,256]{1,0:T(8,128)(2,1)S(1)}, bf16[1040,256]{1,0:T(8,128)(2,1)S(1)}, u32[]{:S(2)}, u32[]{:S(2)}) collective-permute-start(bf16[1040,256]{1,0:T(8,128)(2,1)S(1)} %stack_rows.1.refs_4_), channel_id=1, source_target_pairs={{0,12},{1,13},{2,14},{3,15},{4,0},{5,1},{6,2},{7,3},{8,4},{9,5},{1... | collective-permute-start | bytes 1597448 | tf_op jit(solution)/shard_map/ppermute | solution.py:714
  19.3 14.2 %collective-permute-start.5 = (bf16[1040,256]{1,0:T(8,128)(2,1)S(1)}, bf16[1040,256]{1,0:T(8,128)(2,1)S(1)}, u32[]{:S(2)}, u32[]{:S(2)}) collective-permute-start(bf16[1040,256]{1,0:T(8,128)(2,1)S(1)} %stack_rows.1.refs_4_), channel_id=1, source_target_pairs={{0,8},{1,9},{2,10},{3,11},{4,12},{5,13},{6,14},{7,15},{8,0},{9,1},... | collective-permute-start | bytes 1597448 | tf_op jit(solution)/shard_map/ppermute | solution.py:714
  20.7 12.8 %collective-permute-start.6 = (bf16[16,1536]{1,0:T(8,128)(2,1)S(1)}, bf16[16,1536]{1,0:T(8,128)(2,1)S(1)}, u32[]{:S(2)}, u32[]{:S(2)}) collective-permute-start(bf16[16,1536]{1,0:T(8,128)(2,1)S(1)} %get-tuple-element.43.refs_4_), channel_id=1, source_target_pairs={{0,1},{1,2},{2,3},{3,4},{4,5},{5,6},{6,7},{7,8},{8,9},{9,10},{10,1... | collective-permute-start | bytes 147464 | tf_op jit(solution)/shard_map/ppermute | solution.py:710
  23.0 10.5 %collective-permute-start.7 = (bf16[16,1536]{1,0:T(8,128)(2,1)S(1)}, bf16[16,1536]{1,0:T(8,128)(2,1)S(1)}, u32[]{:S(2)}, u32[]{:S(2)}) collective-permute-start(bf16[16,1536]{1,0:T(8,128)(2,1)S(1)} %get-tuple-element.50), channel_id=1, source_target_pairs={{1,0},{2,1},{3,2},{4,3},{5,4},{6,5},{7,6},{8,7},{9,8},{10,9},{11,1... | collective-permute-start | bytes 147464 | tf_op jit(solution)/shard_map/ppermute | solution.py:711
  37.3 10.1 %collective-permute-start.8 = (bf16[272,256]{1,0:T(8,128)(2,1)}, bf16[272,256]{1,0:T(8,128)(2,1)S(1)}, u32[]{:S(2)}, u32[]{:S(2)}) collective-permute-start(bf16[272,256]{1,0:T(8,128)(2,1)} %get-tuple-element.52), channel_id=1, source_target_pairs={{0,3},{1,0},{2,1},{3,2},{4,7},{5,4},{6,5},{7,6},{8,11},{9,8},{10,9... | collective-permute-start | bytes 417800 | tf_op jit(solution)/shard_map/ppermute | solution.py:67
  41.3 6.1 %collective-permute-start.9 = (bf16[272,256]{1,0:T(8,128)(2,1)S(1)}, bf16[272,256]{1,0:T(8,128)(2,1)S(1)}, u32[]{:S(2)}, u32[]{:S(2)}) collective-permute-start(bf16[272,256]{1,0:T(8,128)(2,1)S(1)} %get-tuple-element.53), channel_id=1, source_target_pairs={{0,2},{1,3},{2,0},{3,1},{4,6},{5,7},{6,4},{7,5},{8,10},{9,11},{10,... | collective-permute-start | bytes 417800 | tf_op jit(solution)/shard_map/ppermute | solution.py:67
  42.3 6.2 %collective-permute-start.10 = (bf16[272,256]{1,0:T(8,128)(2,1)S(1)}, bf16[272,256]{1,0:T(8,128)(2,1)S(1)}, u32[]{:S(2)}, u32[]{:S(2)}) collective-permute-start(bf16[272,256]{1,0:T(8,128)(2,1)S(1)} %get-tuple-element.54), channel_id=1, source_target_pairs={{0,1},{1,2},{2,3},{3,0},{4,5},{5,6},{6,7},{7,4},{8,9},{9,10},{10,1... | collective-permute-start | bytes 417800 | tf_op jit(solution)/shard_map/ppermute | solution.py:67
  54.0 6.3 %collective-permute-start.11 = (bf16[4,384,768]{2,1,0:T(8,128)(2,1)S(1)}, bf16[4,384,768]{2,1,0:T(8,128)(2,1)S(1)}, u32[]{:S(2)}, u32[]{:S(2)}) collective-permute-start(bf16[4,384,768]{2,1,0:T(8,128)(2,1)S(1)} %get-tuple-element.59), channel_id=1, source_target_pairs={{0,16},{16,0},{1,17},{17,1},{2,18},{18,2},{3,19},{19,3},{4,20},{20... | collective-permute-start | bytes 7077896 | tf_op jit(solution)/shard_map/ppermute | solution.py:727
  61.6 20.4 %collective-permute-start.12 = (bf16[384,768]{1,0:T(8,128)(2,1)S(1)}, bf16[384,768]{1,0:T(8,128)(2,1)S(1)}, u32[]{:S(2)}, u32[]{:S(2)}) collective-permute-start(bf16[384,768]{1,0:T(8,128)(2,1)S(1)} %get-tuple-element.61), channel_id=1, source_target_pairs={{0,32},{1,33},{2,34},{3,35},{4,36},{5,37},{6,38},{7,39},{8,40},{9,... | collective-permute-start | bytes 1769480 | tf_op jit(solution)/shard_map/ppermute | solution.py:67
  61.9 20.1 %collective-permute-start.13 = (bf16[384,768]{1,0:T(8,128)(2,1)S(1)}, bf16[384,768]{1,0:T(8,128)(2,1)S(1)}, u32[]{:S(2)}, u32[]{:S(2)}) collective-permute-start(bf16[384,768]{1,0:T(8,128)(2,1)S(1)} %get-tuple-element.62), channel_id=1, source_target_pairs={{0,64},{1,65},{2,66},{3,67},{4,68},{5,69},{6,70},{7,71},{8,72},{9,... | collective-permute-start | bytes 1769480 | tf_op jit(solution)/shard_map/ppermute | solution.py:67
  65.4 16.7 %collective-permute-start.14 = (bf16[384,768]{1,0:T(8,128)(2,1)S(1)}, bf16[384,768]{1,0:T(8,128)(2,1)S(1)}, u32[]{:S(2)}, u32[]{:S(2)}) collective-permute-start(bf16[384,768]{1,0:T(8,128)(2,1)S(1)} %get-tuple-element.63), channel_id=1, source_target_pairs={{0,96},{1,97},{2,98},{3,99},{4,100},{5,101},{6,102},{7,103},{8,104... | collective-permute-start | bytes 1769480 | tf_op jit(solution)/shard_map/ppermute | solution.py:67
  79.1 10.6 %collective-permute-start.18 = (f32[3,768]{1,0:T(4,128)S(1)}, f32[3,768]{1,0:T(4,128)S(1)}, u32[]{:S(2)}, u32[]{:S(2)}) collective-permute-start(f32[3,768]{1,0:T(4,128)S(1)} %get-tuple-element.71), channel_id=1, source_target_pairs={{0,16},{16,0},{1,17},{17,1},{2,18},{18,2},{3,19},{19,3},{4,20},{20... | collective-permute-start | bytes 27656 | tf_op jit(solution)/shard_map/ppermute | solution.py:736
  83.0 6.7 %collective-permute-start.15 = (bf16[96,768]{1,0:T(8,128)(2,1)S(1)}, bf16[96,768]{1,0:T(8,128)(2,1)S(1)}, u32[]{:S(2)}, u32[]{:S(2)}) collective-permute-start(bf16[96,768]{1,0:T(8,128)(2,1)S(1)} %get-tuple-element.65), channel_id=1, source_target_pairs={{0,2},{1,3},{2,0},{3,1},{4,6},{5,7},{6,4},{7,5},{8,10},{9,11},{10,... | collective-permute-start | bytes 442376 | tf_op jit(solution)/shard_map/ppermute | solution.py:67
  87.0 5.2 %collective-permute-start.16 = (bf16[96,768]{1,0:T(8,128)(2,1)S(1)}, bf16[96,768]{1,0:T(8,128)(2,1)S(1)}, u32[]{:S(2)}, u32[]{:S(2)}) collective-permute-start(bf16[96,768]{1,0:T(8,128)(2,1)S(1)} %get-tuple-element.66), channel_id=1, source_target_pairs={{0,1},{1,2},{2,3},{3,0},{4,5},{5,6},{6,7},{7,4},{8,9},{9,10},{10,1... | collective-permute-start | bytes 442376 | tf_op jit(solution)/shard_map/ppermute | solution.py:67
  87.0 5.2 %collective-permute-start.17 = (bf16[96,768]{1,0:T(8,128)(2,1)S(1)}, bf16[96,768]{1,0:T(8,128)(2,1)S(1)}, u32[]{:S(2)}, u32[]{:S(2)}) collective-permute-start(bf16[96,768]{1,0:T(8,128)(2,1)S(1)} %get-tuple-element.67), channel_id=1, source_target_pairs={{0,3},{1,0},{2,1},{3,2},{4,7},{5,4},{6,5},{7,6},{8,11},{9,8},{10,9... | collective-permute-start | bytes 442376 | tf_op jit(solution)/shard_map/ppermute | solution.py:67
  92.3 7.7 %collective-permute-start.20 = (bf16[112,768]{1,0:T(8,128)(2,1)S(1)}, bf16[112,768]{1,0:T(8,128)(2,1)S(1)}, u32[]{:S(2)}, u32[]{:S(2)}) collective-permute-start(bf16[112,768]{1,0:T(8,128)(2,1)S(1)} %fusion.1), channel_id=1, source_target_pairs={{0,4},{1,5},{2,6},{3,7},{4,8},{5,9},{6,10},{7,11},{8,12},{9,13},{1... | collective-permute-start | bytes 516104 | tf_op jit(solution)/shard_map/ppermute | solution.py:67
  92.7 7.3 %collective-permute-start.19 = (bf16[112,768]{1,0:T(8,128)(2,1)S(1)}, bf16[112,768]{1,0:T(8,128)(2,1)S(1)}, u32[]{:S(2)}, u32[]{:S(2)}) collective-permute-start(bf16[112,768]{1,0:T(8,128)(2,1)S(1)} %fusion.1), channel_id=1, source_target_pairs={{0,8},{1,9},{2,10},{3,11},{4,12},{5,13},{6,14},{7,15},{8,0},{9,1},... | collective-permute-start | bytes 516104 | tf_op jit(solution)/shard_map/ppermute | solution.py:67
  93.3 7.2 %collective-permute-start.21 = (bf16[112,768]{1,0:T(8,128)(2,1)S(1)}, bf16[112,768]{1,0:T(8,128)(2,1)S(1)}, u32[]{:S(2)}, u32[]{:S(2)}) collective-permute-start(bf16[112,768]{1,0:T(8,128)(2,1)S(1)} %fusion.1), channel_id=1, source_target_pairs={{0,12},{1,13},{2,14},{3,15},{4,0},{5,1},{6,2},{7,3},{8,4},{9,5},{1... | collective-permute-start | bytes 516104 | tf_op jit(solution)/shard_map/ppermute | solution.py:67
  100.7 6.9 %collective-permute-start.24 = (bf16[112,768]{1,0:T(8,128)(2,1)S(1)}, bf16[112,768]{1,0:T(8,128)(2,1)S(1)}, u32[]{:S(2)}, u32[]{:S(2)}) collective-permute-start(bf16[112,768]{1,0:T(8,128)(2,1)S(1)} %multiply_convert_fusion.refs_0_), channel_id=1, source_target_pairs={{0,3},{1,0},{2,1},{3,2},{4,7},{5,4},{6,5},{7,6},{8,11},{9,8},{10,9... | collective-permute-start | bytes 516104 | tf_op jit(solution)/shard_map/ppermute | solution.py:67
  103.4 6.1 %collective-permute-start.23 = (bf16[112,768]{1,0:T(8,128)(2,1)S(1)}, bf16[112,768]{1,0:T(8,128)(2,1)S(1)}, u32[]{:S(2)}, u32[]{:S(2)}) collective-permute-start(bf16[112,768]{1,0:T(8,128)(2,1)S(1)} %multiply_convert_fusion.refs_0_), channel_id=1, source_target_pairs={{0,2},{1,3},{2,0},{3,1},{4,6},{5,7},{6,4},{7,5},{8,10},{9,11},{10,... | collective-permute-start | bytes 516104 | tf_op jit(solution)/shard_map/ppermute | solution.py:67
  103.4 7.6 %collective-permute-start.22 = (bf16[112,768]{1,0:T(8,128)(2,1)S(1)}, bf16[112,768]{1,0:T(8,128)(2,1)S(1)}, u32[]{:S(2)}, u32[]{:S(2)}) collective-permute-start(bf16[112,768]{1,0:T(8,128)(2,1)S(1)} %multiply_convert_fusion.refs_0_), channel_id=1, source_target_pairs={{0,1},{1,2},{2,3},{3,0},{4,5},{5,6},{6,7},{7,4},{8,9},{9,10},{10,1... | collective-permute-start | bytes 516104 | tf_op jit(solution)/shard_map/ppermute | solution.py:67
  111.8 9.2 %collective-permute-start.27 = (bf16[784,384]{1,0:T(8,128)(2,1)S(1)}, bf16[784,384]{1,0:T(8,128)(2,1)S(1)}, u32[]{:S(2)}, u32[]{:S(2)}) collective-permute-start(bf16[784,384]{1,0:T(8,128)(2,1)S(1)} %join_rows.1.refs_0_), channel_id=1, source_target_pairs={{0,96},{1,97},{2,98},{3,99},{4,100},{5,101},{6,102},{7,103},{8,104... | collective-permute-start | bytes 1806344 | tf_op jit(solution)/shard_map/ppermute | solution.py:67
  113.1 10.8 %collective-permute-start.26 = (bf16[784,384]{1,0:T(8,128)(2,1)S(1)}, bf16[784,384]{1,0:T(8,128)(2,1)S(1)}, u32[]{:S(2)}, u32[]{:S(2)}) collective-permute-start(bf16[784,384]{1,0:T(8,128)(2,1)S(1)} %join_rows.1.refs_0_), channel_id=1, source_target_pairs={{0,64},{1,65},{2,66},{3,67},{4,68},{5,69},{6,70},{7,71},{8,72},{9,... | collective-permute-start | bytes 1806344 | tf_op jit(solution)/shard_map/ppermute | solution.py:67
  113.6 16.6 %collective-permute-start.25 = (bf16[784,384]{1,0:T(8,128)(2,1)S(1)}, bf16[784,384]{1,0:T(8,128)(2,1)S(1)}, u32[]{:S(2)}, u32[]{:S(2)}) collective-permute-start(bf16[784,384]{1,0:T(8,128)(2,1)S(1)} %join_rows.1.refs_0_), channel_id=1, source_target_pairs={{0,32},{1,33},{2,34},{3,35},{4,36},{5,37},{6,38},{7,39},{8,40},{9,... | collective-permute-start | bytes 1806344 | tf_op jit(solution)/shard_map/ppermute | solution.py:67
  113.8 19.1 %collective-permute-start.28 = (bf16[784,384]{1,0:T(8,128)(2,1)S(1)}, bf16[784,384]{1,0:T(8,128)(2,1)S(1)}, u32[]{:S(2)}, u32[]{:S(2)}) collective-permute-start(bf16[784,384]{1,0:T(8,128)(2,1)S(1)} %join_rows.1.refs_0_), channel_id=1, source_target_pairs={{0,16},{16,0},{1,17},{17,1},{2,18},{18,2},{3,19},{19,3},{4,20},{20... | collective-permute-start | bytes 1806344 | tf_op jit(solution)/shard_map/ppermute | solution.py:747
  121.1 11.8 %collective-permute-start.31 = (bf16[784,384]{1,0:T(8,128)(2,1)S(1)}, bf16[784,384]{1,0:T(8,128)(2,1)S(1)}, u32[]{:S(2)}, u32[]{:S(2)}) collective-permute-start(bf16[784,384]{1,0:T(8,128)(2,1)S(1)} %collective-permute-done.27.refs_3_), channel_id=1, source_target_pairs={{0,16},{16,0},{1,17},{17,1},{2,18},{18,2},{3,19},{19,3},{4,20},{20... | collective-permute-start | bytes 1806344 | tf_op jit(solution)/shard_map/ppermute | solution.py:747
  123.9 8.9 %collective-permute-start.30 = (bf16[784,384]{1,0:T(8,128)(2,1)S(1)}, bf16[784,384]{1,0:T(8,128)(2,1)S(1)}, u32[]{:S(2)}, u32[]{:S(2)}) collective-permute-start(bf16[784,384]{1,0:T(8,128)(2,1)S(1)} %collective-permute-done.26.refs_2_), channel_id=1, source_target_pairs={{0,16},{16,0},{1,17},{17,1},{2,18},{18,2},{3,19},{19,3},{4,20},{20... | collective-permute-start | bytes 1806344 | tf_op jit(solution)/shard_map/ppermute | solution.py:747
  130.2 4.3 %collective-permute-start.29 = (bf16[784,384]{1,0:T(8,128)(2,1)S(1)}, bf16[784,384]{1,0:T(8,128)(2,1)S(1)}, u32[]{:S(2)}, u32[]{:S(2)}) collective-permute-start(bf16[784,384]{1,0:T(8,128)(2,1)S(1)} %collective-permute-done.25.refs_1_), channel_id=1, source_target_pairs={{0,16},{16,0},{1,17},{17,1},{2,18},{18,2},{3,19},{19,3},{4,20},{20... | collective-permute-start | bytes 1806344 | tf_op jit(solution)/shard_map/ppermute | solution.py:747
  (4 other events, 15.4 us)

commit v9 on v8

--- a/solution.py
+++ b/solution.py
@@ -61,9 +61,9 @@
     return pairs
 
 
-def exchange(pieces, axes, sign=1):
+def exchange(pieces, axes, sign=1, order=(2, 1, 3)):
     got = [pieces[0], None, None, None]
-    for d in (2, 1, 3):
+    for d in order:
         got[d] = lax.ppermute(pieces[d], AXES, turn(axes, sign * d))
     return got
 
@@ -79,37 +79,42 @@
 
     def kernel(at_ref, tok_hbm, wq_hbm, wk_hbm, wv_hbm, *refs):
         outs, (tok_ref, wq_ref, wk_ref, wv_ref, held, sems) = refs[:4], refs[4:]
-        low, high = pl.ds(0, cut), pl.ds(cut, depth - cut)
-        copies = [
-            pltpu.make_async_copy(tok_hbm, tok_ref, sems.at[0]),
-            pltpu.make_async_copy(wv_hbm.at[low, :], wv_ref.at[low, :], sems.at[1]),
-            pltpu.make_async_copy(wv_hbm.at[high, :], wv_ref.at[high, :], sems.at[2]),
-            pltpu.make_async_copy(wk_hbm, wk_ref, sems.at[3]),
-            pltpu.make_async_copy(wq_hbm, wq_ref, sems.at[4]),
-        ]
+        wide = 2 * DV
+        cuts = [pl.ds(n * cut, cut) for n in range(2)]
+        copies = [pltpu.make_async_copy(tok_hbm, tok_ref, sems.at[0])]
+        for w_hbm, w_ref in ((wk_hbm, wk_ref), (wq_hbm, wq_ref)):
+            copies += [pltpu.make_async_copy(w_hbm.at[c, :], w_ref.at[c, :], sems.at[len(copies) + n]) for n, c in enumerate(cuts)]
+        for n in range(2):
+            across = pl.ds(n * wide, wide)
+            copies += [
+                pltpu.make_async_copy(wv_hbm.at[c, across], wv_ref.at[c, across], sems.at[len(copies) + m])
+                for m, c in enumerate(cuts)
+            ]
         for copy in copies:
             copy.start()
-        copies[0].wait()
+        for copy in copies[:3]:
+            copy.wait()
         tok = tok_ref[...]
-        copies[1].wait()
-        v = jnp.dot(tok[:, :cut], wv_ref[:cut, :], preferred_element_type=F32)
-        copies[2].wait()
-        v += jnp.dot(tok[:, cut:], wv_ref[cut:, :], preferred_element_type=F32)
-        copies[3].wait()
         k = jnp.dot(tok, wk_ref[...], preferred_element_type=F32)
-        copies[4].wait()
+        for copy in copies[3:5]:
+            copy.wait()
         q = jnp.dot(tok, wq_ref[...], preferred_element_type=F32) * (1.0 / math.sqrt(DH))
         zero = jnp.zeros((rows, DH), F32)
-        for h in range(H):
-            held[h] = jnp.concatenate(
-                [
-                    v[:, h * DV : (h + 1) * DV],
-                    k[:, h * DH : (h + 1) * DH],
-                    zero,
-                    q[:, h * DH : (h + 1) * DH],
-                ],
-                axis=1,
-            ).astype(BF)
+        for n in range(2):
+            for copy in copies[5 + 2 * n : 7 + 2 * n]:
+                copy.wait()
+            v = jnp.dot(tok, wv_ref[:, n * wide : (n + 1) * wide], preferred_element_type=F32)
+            for m in range(2):
+                h = 2 * n + m
+                held[h] = jnp.concatenate(
+                    [
+                        v[:, m * DV : (m + 1) * DV],
+                        k[:, h * DH : (h + 1) * DH],
+                        zero,
+                        q[:, h * DH : (h + 1) * DH],
+                    ],
+                    axis=1,
+                ).astype(BF)
         for d in range(4):
             outs[d][...] = held[(Spot(at_ref).head_at + d) % 4]
 
@@ -124,7 +129,7 @@
             pltpu.VMEM((depth, H * DH), BF),
             pltpu.VMEM((depth, H * DV), BF),
             pltpu.VMEM((4, rows, 384), BF),
-            pltpu.SemaphoreType.DMA((5,)),
+            pltpu.SemaphoreType.DMA((9,)),
         ],
         compiler_params=params(53),
         name="project",
@@ -176,7 +181,7 @@
         place = lax.broadcasted_iota(jnp.int32, (1, rows), 1)
 
         def masks(n):
-            far_by = (0, 1, 3, 2)[n]
+            far_by = (0, 2, 3, 1)[n]
             return jnp.concatenate(
                 [place + spot.base(far_by, i) * rows < s_ref[4] for i in range(4)], axis=1
             )
@@ -194,7 +199,7 @@
 
         if last:
             tails = [r[width:, 128:].astype(F32) for r in pair_refs]
-            own, low, high = tails[0], tails[1], tails[2]
+            own, high, low = tails[0], tails[2], tails[3]
             row = lax.broadcasted_iota(jnp.int32, (TAIL, 128), 0)
             edge = jnp.zeros((TAIL, 128), F32)
             for d in range(4):
@@ -457,7 +462,7 @@
         in_specs=[ANY] * (1 + count),
         out_specs=[VMEM] * count,
         scratch_shapes=[pltpu.SemaphoreType.DMA((count,))],
-        compiler_params=params(45),
+        compiler_params=params(47),
         name="load",
     )(behind, *arrays)
 
@@ -711,14 +716,14 @@
     after = lax.ppermute(up, ("z", "y"), [(i + 1, i) for i in range(15)])
     q = exchange(blocks, HEAD_RING)
     own = stack_rows(q, down)
-    far = {d: lax.ppermute(own, AXES, turn(ROW_RING, d)) for d in (1, 3, 2)}
+    far = {d: lax.ppermute(own, AXES, turn(ROW_RING, d)) for d in (2, 3, 1)}
     state = attend(scalars, 0, q, [own], None)
 
     turned = upstream.T
 
-    state = attend(scalars, 1, q, [far[1]], state)
+    state = attend(scalars, 1, q, [far[2]], state)
     state = attend(scalars, 2, q, [far[3]], state)
-    mixed = attend(scalars, 3, q, [own, far[1], far[3], far[2]], state, (before, after))
+    mixed = attend(scalars, 3, q, [own, far[2], far[3], far[1]], state, (before, after))
     back = exchange(mixed, HEAD_RING, -1)
     tokens_v, skipped_v, out_v = load(mixed[0], tokens, skipped, out_weight.reshape(H, DV, -1))
     swap = [(0, 1), (1, 0)]
@@ -726,7 +731,8 @@
     up_theirs, sent = forward(scalars, False, *given)
     arrived = lax.ppermute(sent, "c", swap)
     up_ours, act = forward(scalars, True, *given)
-    piece_2, piece_1 = product(scalars, act, turned, (2, 1), arrived)
+    (piece_2,) = product(scalars, act, turned, (2,), arrived)
+    (piece_1,) = product(scalars, act, turned, (1,), arrived)
     piece_3, piece_0 = product(scalars, act, turned, (3, 0), arrived)
     got = exchange([piece_0, piece_1, piece_2, piece_3], SUM_RINGS[0])
 
@@ -743,7 +749,7 @@
     summed = (total_of(got) * norm_scale).astype(BF)
     joined = join_rows(scalars, exchange([summed] * 4, SUM_RINGS[1]))
 
-    own = exchange([joined] * 4, SUM_RINGS[0])
+    own = exchange([joined] * 4, SUM_RINGS[0], order=(1, 3, 2))
     other = [lax.ppermute(block, "c", swap) for block in own]
     grad_pointwise, grad_depth = lay_out(scalars, own, other)
     return (grad_pointwise, grad_depth, grad_skip[None])

time: 139 us -> 141 us (1.014)
  starting transfers between devices: 53.6 us -> 59 us
  waiting for transfers between devices: 31.5 us -> 27.2 us
    ppermute x4, starting transfers between devices: 10.9 us -> 20 us  [local(): other = [lax.ppermute(block, 'c', swap) for block in own]]
    ppermute x21, starting transfers between devices: 29.7 us -> 23.5 us  [exchange(): got[d] = lax.ppermute(pieces[d], AXES, turn(axes, sign * d))]
    ppermute x21, waiting for transfers between devices: 27.8 us -> 21.8 us  [exchange(): got[d] = lax.ppermute(pieces[d], AXES, turn(axes, sign * d))]
    ppermute x1, starting transfers between devices: 2.17 us -> 4.44 us  [local(): arrived = lax.ppermute(sent, 'c', swap)]
    ppermute x3, waiting for transfers between devices: 1.83 us -> 3.47 us  [local(): far = {d: lax.ppermute(own, AXES, turn(ROW_RING, d)) for d in (2, 3, 1)}]
    pallas_call x2 -> x3, Pallas kernels: 2.63 us -> 3.34 us  [product(): pl.pallas_call(kernel, out_shape=[jax.ShapeDtypeStruct((quarter, half), B...]
  transfers between devices with their start and end apart: 32 -> 32, of which waited for: 14 -> 16; matrix products, arithmetic and copies ran while one was open for 1% -> 1% of each run, Pallas kernels for 21% -> 21%
where the time goes in v9:
time: 141 us; the launch traced here: 140 us
  starting transfers between devices  59 us (42%)
  Pallas kernels  48.6 us (34%)
  waiting for transfers between devices  27.2 us (19%)
  local copies, waits for them, and re-layouts  3.22 us (2%)
  between operations  1.72 us (1%)
    ppermute x21, starting transfers between devices, exchange(): got[d] = lax.ppermute(pieces[d], AXES, turn(axes, sign * d))  23.5 us
    ppermute x21, waiting for transfers between devices, exchange(): got[d] = lax.ppermute(pieces[d], AXES, turn(axes, sign * d))  21.8 us
    ppermute x4, starting transfers between devices, local(): other = [lax.ppermute(block, 'c', swap) for block in own]  20 us
    pallas_call x1, Pallas kernels, backward(): pl.pallas_call(kernel, out_shape=[jax.ShapeDtypeStruct((fine, columns), B...  12.9 us
    pallas_call x4, Pallas kernels, attend(): pl.pallas_call(kernel, out_shape=outs, in_specs=[SMEM] + [VMEM] * len(ins...  10.4 us
    pallas_call x2, Pallas kernels, forward(): pl.pallas_call(kernel, out_shape=outs, grid_spec=pltpu.PrefetchScalarGrid...  9.41 us
    pallas_call x1, Pallas kernels, project(): pl.pallas_call(kernel, out_shape=[jax.ShapeDtypeStruct((rows, 384), BF)]...  4.45 us
    ppermute x1, starting transfers between devices, local(): arrived = lax.ppermute(sent, 'c', swap)  4.44 us
  transfers between devices with their start and end apart: 32, of which 16 were waited for; matrix products, arithmetic and copies ran while one was open for 1% of the time, Pallas kernels for 21%

profile of v9, /device:TPU:1, one launch (start us, length us, event | category | flops | bytes accessed | tf_op | source)
XLA Modules:
  0.0 140.1 jit_solution(8196049529163166659)
XLA Ops:
  0.7 4.5 %project.1 = (bf16[256,384]{1,0:T(8,128)(2,1)S(1)}, bf16[256,384]{1,0:T(8,128)(2,1)S(1)}, bf16[256,384]{1,0:T(8,128)(2,1)S(1)}, bf16[256,384]{1,0:T(8,128)(2,1)S(1)}) custom-call(s32[4]{0:T(128)S(1)} %pad_add_fusion.at_ref, bf16[256,1536]{1,0:T(8,128)(2,1)} %bitcast.11, bf16[1536,256]{1,0:T(8,128)(2,1)} %wq_hbm.1, bf16[1536,256]{1,0:T(8,128)(2,1)} %wk_hbm.1, ...), custom_call_target="tpu_custom_call" | custom-call | tf_op jit(solution)/shard_map/project/pallas_call | solution.py:121
  5.2 2.5 %collective-permute-start = (bf16[256,384]{1,0:T(8,128)(2,1)S(1)}, bf16[256,384]{1,0:T(8,128)(2,1)S(1)}, u32[]{:S(2)}, u32[]{:S(2)}) collective-permute-start(bf16[256,384]{1,0:T(8,128)(2,1)S(1)} %get-tuple-element.38), channel_id=1, source_target_pairs={{0,1},{1,2},{2,3},{3,0},{4,5},{5,6},{6,7},{7,4},{8,9},{9,10},{10,1... | collective-permute-start | bytes 589832 | tf_op jit(solution)/shard_map/ppermute | solution.py:67
  7.7 3.3 %collective-permute-start.1 = (bf16[256,384]{1,0:T(8,128)(2,1)S(1)}, bf16[256,384]{1,0:T(8,128)(2,1)S(1)}, u32[]{:S(2)}, u32[]{:S(2)}) collective-permute-start(bf16[256,384]{1,0:T(8,128)(2,1)S(1)} %get-tuple-element.39), channel_id=1, source_target_pairs={{0,2},{1,3},{2,0},{3,1},{4,6},{5,7},{6,4},{7,5},{8,10},{9,11},{10,... | collective-permute-start | bytes 589832 | tf_op jit(solution)/shard_map/ppermute | solution.py:67
  13.1 3.3 %collective-permute-done.1.refs_2_ = bf16[256,384]{1,0:T(8,128)(2,1)S(1)} collective-permute-done((bf16[256,384]{1,0:T(8,128)(2,1)S(1)}, bf16[256,384]{1,0:T(8,128)(2,1)S(1)}, u32[]{:S(2)}, u32[]{:S(2)}) %collective-permute-start.1) | collective-permute-done | bytes 196640 | tf_op jit(solution)/shard_map/ppermute | solution.py:67
  16.5 2.7 %collective-permute-start.3 = (bf16[1040,256]{1,0:T(8,128)(2,1)S(1)}, bf16[1040,256]{1,0:T(8,128)(2,1)S(1)}, u32[]{:S(2)}, u32[]{:S(2)}) collective-permute-start(bf16[1040,256]{1,0:T(8,128)(2,1)S(1)} %stack_rows.1.refs_4_), channel_id=1, source_target_pairs={{0,8},{1,9},{2,10},{3,11},{4,12},{5,13},{6,14},{7,15},{8,0},{9,1},... | collective-permute-start | bytes 1597448 | tf_op jit(solution)/shard_map/ppermute | solution.py:719
  20.7 2.3 %collective-permute-start.6 = (bf16[16,1536]{1,0:T(8,128)(2,1)S(1)}, bf16[16,1536]{1,0:T(8,128)(2,1)S(1)}, u32[]{:S(2)}, u32[]{:S(2)}) collective-permute-start(bf16[16,1536]{1,0:T(8,128)(2,1)S(1)} %get-tuple-element.41.refs_4_), channel_id=1, source_target_pairs={{0,1},{1,2},{2,3},{3,4},{4,5},{5,6},{6,7},{7,8},{8,9},{9,10},{10,1... | collective-permute-start | bytes 147464 | tf_op jit(solution)/shard_map/ppermute | solution.py:715
  25.0 2.1 %attend.4 = (f32[1024,256]{1,0:T(8,128)S(1)}, f32[1024,128]{1,0:T(8,128)S(1)}) custom-call(s32[5]{0:T(128)S(1)} %concatenate.7.s_ref.at_ref, bf16[256,384]{1,0:T(8,128)(2,1)S(1)} %get-tuple-element.37.mark_ref.refs_0_, bf16[256,384]{1,0:T(8,128)(2,1)S(1)} %collective-permute-done.refs_1_, bf16[256,384]{1,0:T(8,128)(2,1)S(1)} %collective-permute-done.1.refs_2_, ...), custom_call_target="tpu_custom_call" | custom-call | flops 1073741824 | bytes 4194304 | tf_op jit(solution)/shard_map/attend/pallas_call | solution.py:260
  27.2 2.2 %attend.5 = (f32[1024,256]{1,0:T(8,128)S(1)}, f32[1024,128]{1,0:T(8,128)S(1)}) custom-call(s32[5]{0:T(128)S(1)} %concatenate.7.s_ref.at_ref, bf16[256,384]{1,0:T(8,128)(2,1)S(1)} %get-tuple-element.37.mark_ref.refs_0_, bf16[256,384]{1,0:T(8,128)(2,1)S(1)} %collective-permute-done.refs_1_, bf16[256,384]{1,0:T(8,128)(2,1)S(1)} %collective-permute-done.1.refs_2_, ...), custom_call_target="tpu_custom_call" | custom-call | flops 1073741824 | bytes 4194304 | tf_op jit(solution)/shard_map/attend/pallas_call | solution.py:260
  29.4 3.5 %collective-permute-done.4.refs_4_.refs_6_ = bf16[1040,256]{1,0:T(8,128)(2,1)S(1)} collective-permute-done((bf16[1040,256]{1,0:T(8,128)(2,1)S(1)}, bf16[1040,256]{1,0:T(8,128)(2,1)S(1)}, u32[]{:S(2)}, u32[]{:S(2)}) %collective-permute-start.4) | collective-permute-done | bytes 532512 | tf_op jit(solution)/shard_map/ppermute | solution.py:719
  32.8 2.2 %attend.6 = (f32[1024,256]{1,0:T(8,128)S(1)}, f32[1024,128]{1,0:T(8,128)S(1)}) custom-call(s32[5]{0:T(128)S(1)} %concatenate.7.s_ref.at_ref, bf16[256,384]{1,0:T(8,128)(2,1)S(1)} %get-tuple-element.37.mark_ref.refs_0_, bf16[256,384]{1,0:T(8,128)(2,1)S(1)} %collective-permute-done.refs_1_, bf16[256,384]{1,0:T(8,128)(2,1)S(1)} %collective-permute-done.1.refs_2_, ...), custom_call_target="tpu_custom_call" | custom-call | flops 1073741824 | bytes 4194304 | tf_op jit(solution)/shard_map/attend/pallas_call | solution.py:260
  35.1 3.8 %attend.7 = (bf16[272,256]{1,0:T(8,128)(2,1)S(1)}, bf16[272,256]{1,0:T(8,128)(2,1)}, bf16[272,256]{1,0:T(8,128)(2,1)S(1)}, bf16[272,256]{1,0:T(8,128)(2,1)S(1)}) custom-call(s32[5]{0:T(128)S(1)} %concatenate.7.s_ref.at_ref, bf16[256,384]{1,0:T(8,128)(2,1)S(1)} %get-tuple-element.37.mark_ref.refs_0_, bf16[256,384]{1,0:T(8,128)(2,1)S(1)} %collective-permute-done.refs_1_, ...), custom_call_target="tpu_custom_call" | custom-call | flops 1073741824 | bytes 4194304 | tf_op jit(solution)/shard_map/attend/pallas_call | solution.py:260
  38.9 2.4 %collective-permute-start.8 = (bf16[272,256]{1,0:T(8,128)(2,1)}, bf16[272,256]{1,0:T(8,128)(2,1)S(1)}, u32[]{:S(2)}, u32[]{:S(2)}) collective-permute-start(bf16[272,256]{1,0:T(8,128)(2,1)} %get-tuple-element.50), channel_id=1, source_target_pairs={{0,3},{1,0},{2,1},{3,2},{4,7},{5,4},{6,5},{7,6},{8,11},{9,8},{10,9... | collective-permute-start | bytes 417800 | tf_op jit(solution)/shard_map/ppermute | solution.py:67
  42.4 1.7 %copy.13.g_ref = bf16[1536,512]{1,0:T(8,128)(2,1)S(1)} copy(bf16[1536,512]{0,1:T(8,128)(2,1)} %bitcast.15) | data formatting | bytes 3145728 | tf_op jit(solution)/shard_map/transpose | solution.py:722
  45.5 1.8 %load.1 = (bf16[256,1536]{1,0:T(8,128)(2,1)S(1)}, bf16[512,1536]{1,0:T(8,128)(2,1)S(1)}, bf16[4,192,1536]{2,1,0:T(8,128)(2,1)S(1)}) custom-call(bf16[272,256]{1,0:T(8,128)(2,1)S(1)} %get-tuple-element.49.behind_ref.b0, bf16[256,1536]{1,0:T(8,128)(2,1)S(1)} %bitcast.13, bf16[512,1536]{1,0:T(8,128)(2,1)S(1)} %bitcast.18, bf16[4,192,1536]{2,1,0:T(8,128)(2,1)} %bitcast.19), custom_call_target="tpu_custom_call" | custom-call | tf_op jit(solution)/shard_map/load/pallas_call | solution.py:459
  48.2 5.5 %forward.3 = (bf16[544,768]{1,0:T(8,128)(2,1)S(1)}, bf16[4,384,768]{2,1,0:T(8,128)(2,1)S(1)}) custom-call(s32[5]{0:T(128)S(1)} %concatenate.7.s_ref.at_ref, bf16[272,256]{1,0:T(8,128)(2,1)S(1)} %get-tuple-element.49.behind_ref.b0, bf16[272,256]{1,0:T(8,128)(2,1)S(1)} %collective-permute-done.8.b1, bf16[272,256]{1,0:T(8,128)(2,1)S(1)} %collective-permute-done.9.b2, ...), custom_call_target="tpu_custom_call" | custom-call | flops 2415919104 | bytes 9437184 | tf_op jit(solution)/shard_map/forward/pallas_call | solution.py:428
  53.7 4.4 %collective-permute-start.11 = (bf16[4,384,768]{2,1,0:T(8,128)(2,1)S(1)}, bf16[4,384,768]{2,1,0:T(8,128)(2,1)S(1)}, u32[]{:S(2)}, u32[]{:S(2)}) collective-permute-start(bf16[4,384,768]{2,1,0:T(8,128)(2,1)S(1)} %get-tuple-element.57), channel_id=1, source_target_pairs={{0,16},{16,0},{1,17},{17,1},{2,18},{18,2},{3,19},{19,3},{4,20},{20... | collective-permute-start | bytes 7077896 | tf_op jit(solution)/shard_map/ppermute | solution.py:732
  58.1 3.9 %forward.2 = (bf16[544,768]{1,0:T(8,128)(2,1)S(1)}, bf16[512,768]{1,0:T(8,128)(2,1)S(1)}) custom-call(s32[5]{0:T(128)S(1)} %concatenate.7.s_ref.at_ref, bf16[272,256]{1,0:T(8,128)(2,1)S(1)} %get-tuple-element.49.behind_ref.b0, bf16[272,256]{1,0:T(8,128)(2,1)S(1)} %collective-permute-done.8.b1, bf16[272,256]{1,0:T(8,128)(2,1)S(1)} %collective-permute-done.9.b2, ...), custom_call_target="tpu_custom_call" | custom-call | flops 2415919104 | bytes 9437184 | tf_op jit(solution)/shard_map/forward/pallas_call | solution.py:428
  68.0 12.9 %backward.1 = (bf16[512,1536]{1,0:T(8,128)(2,1)}, f32[3,768]{1,0:T(4,128)S(1)}, f32[3,768]{1,0:T(4,128)S(1)}) custom-call(s32[5]{0:T(128)S(1)} %concatenate.7.s_ref.at_ref, bf16[544,768]{1,0:T(8,128)(2,1)S(1)} %get-tuple-element.64.theirs_ref, bf16[544,768]{1,0:T(8,128)(2,1)S(1)} %get-tuple-element.65.ours_ref, bf16[512,1536]{1,0:T(8,128)(2,1)S(1)} %bitcast.16, ...), custom_call_target="tpu_custom_call" | custom-call | flops 2415919104 | bytes 11534336 | tf_op jit(solution)/shard_map/backward/pallas_call | solution.py:548
  80.9 3.3 %collective-permute-start.18 = (f32[3,768]{1,0:T(4,128)S(1)}, f32[3,768]{1,0:T(4,128)S(1)}, u32[]{:S(2)}, u32[]{:S(2)}) collective-permute-start(f32[3,768]{1,0:T(4,128)S(1)} %get-tuple-element.67), channel_id=1, source_target_pairs={{0,16},{16,0},{1,17},{17,1},{2,18},{18,2},{3,19},{19,3},{4,20},{20... | collective-permute-start | bytes 27656 | tf_op jit(solution)/shard_map/ppermute | solution.py:742
  85.2 2.0 %collective-permute-start.16 = (bf16[96,768]{1,0:T(8,128)(2,1)S(1)}, bf16[96,768]{1,0:T(8,128)(2,1)S(1)}, u32[]{:S(2)}, u32[]{:S(2)}) collective-permute-start(bf16[96,768]{1,0:T(8,128)(2,1)S(1)} %get-tuple-element.62), channel_id=1, source_target_pairs={{0,1},{1,2},{2,3},{3,0},{4,5},{5,6},{6,7},{7,4},{8,9},{9,10},{10,1... | collective-permute-start | bytes 442376 | tf_op jit(solution)/shard_map/ppermute | solution.py:67
  88.0 3.1 %collective-permute-done.15 = bf16[96,768]{1,0:T(8,128)(2,1)S(1)} collective-permute-done((bf16[96,768]{1,0:T(8,128)(2,1)S(1)}, bf16[96,768]{1,0:T(8,128)(2,1)S(1)}, u32[]{:S(2)}, u32[]{:S(2)}) %collective-permute-start.15) | collective-permute-done | bytes 147488 | tf_op jit(solution)/shard_map/ppermute | solution.py:67
  94.6 2.0 %collective-permute-start.21 = (bf16[112,768]{1,0:T(8,128)(2,1)S(1)}, bf16[112,768]{1,0:T(8,128)(2,1)S(1)}, u32[]{:S(2)}, u32[]{:S(2)}) collective-permute-start(bf16[112,768]{1,0:T(8,128)(2,1)S(1)} %fusion.1), channel_id=1, source_target_pairs={{0,12},{1,13},{2,14},{3,15},{4,0},{5,1},{6,2},{7,3},{8,4},{9,5},{1... | collective-permute-start | bytes 516104 | tf_op jit(solution)/shard_map/ppermute | solution.py:67
  98.0 1.8 %collective-permute-done.19 = bf16[112,768]{1,0:T(8,128)(2,1)S(1)} collective-permute-done((bf16[112,768]{1,0:T(8,128)(2,1)S(1)}, bf16[112,768]{1,0:T(8,128)(2,1)S(1)}, u32[]{:S(2)}, u32[]{:S(2)}) %collective-permute-start.19) | collective-permute-done | bytes 172064 | tf_op jit(solution)/shard_map/ppermute | solution.py:67
  100.8 1.7 %collective-permute-start.24 = (bf16[112,768]{1,0:T(8,128)(2,1)S(1)}, bf16[112,768]{1,0:T(8,128)(2,1)S(1)}, u32[]{:S(2)}, u32[]{:S(2)}) collective-permute-start(bf16[112,768]{1,0:T(8,128)(2,1)S(1)} %multiply_convert_fusion.refs_0_), channel_id=1, source_target_pairs={{0,3},{1,0},{2,1},{3,2},{4,7},{5,4},{6,5},{7,6},{8,11},{9,8},{10,9... | collective-permute-start | bytes 516104 | tf_op jit(solution)/shard_map/ppermute | solution.py:67
  103.2 3.5 %collective-permute-done.24.refs_3_ = bf16[112,768]{1,0:T(8,128)(2,1)S(1)} collective-permute-done((bf16[112,768]{1,0:T(8,128)(2,1)S(1)}, bf16[112,768]{1,0:T(8,128)(2,1)S(1)}, u32[]{:S(2)}, u32[]{:S(2)}) %collective-permute-start.24) | collective-permute-done | bytes 172064 | tf_op jit(solution)/shard_map/ppermute | solution.py:67
  106.7 1.7 %collective-permute-done.23.refs_2_ = bf16[112,768]{1,0:T(8,128)(2,1)S(1)} collective-permute-done((bf16[112,768]{1,0:T(8,128)(2,1)S(1)}, bf16[112,768]{1,0:T(8,128)(2,1)S(1)}, u32[]{:S(2)}, u32[]{:S(2)}) %collective-permute-start.23) | collective-permute-done | bytes 172064 | tf_op jit(solution)/shard_map/ppermute | solution.py:67
  108.4 1.7 %collective-permute-done.22.refs_1_ = bf16[112,768]{1,0:T(8,128)(2,1)S(1)} collective-permute-done((bf16[112,768]{1,0:T(8,128)(2,1)S(1)}, bf16[112,768]{1,0:T(8,128)(2,1)S(1)}, u32[]{:S(2)}, u32[]{:S(2)}) %collective-permute-start.22) | collective-permute-done | bytes 172064 | tf_op jit(solution)/shard_map/ppermute | solution.py:67
  112.8 6.2 %collective-permute-start.28 = (bf16[784,384]{1,0:T(8,128)(2,1)S(1)}, bf16[784,384]{1,0:T(8,128)(2,1)S(1)}, u32[]{:S(2)}, u32[]{:S(2)}) collective-permute-start(bf16[784,384]{1,0:T(8,128)(2,1)S(1)} %join_rows.1.refs_0_), channel_id=1, source_target_pairs={{0,16},{16,0},{1,17},{17,1},{2,18},{18,2},{3,19},{19,3},{4,20},{20... | collective-permute-start | bytes 1806344 | tf_op jit(solution)/shard_map/ppermute | solution.py:753
  120.2 6.4 %collective-permute-start.31 = (bf16[784,384]{1,0:T(8,128)(2,1)S(1)}, bf16[784,384]{1,0:T(8,128)(2,1)S(1)}, u32[]{:S(2)}, u32[]{:S(2)}) collective-permute-start(bf16[784,384]{1,0:T(8,128)(2,1)S(1)} %collective-permute-done.27.refs_3_), channel_id=1, source_target_pairs={{0,16},{16,0},{1,17},{17,1},{2,18},{18,2},{3,19},{19,3},{4,20},{20... | collective-permute-start | bytes 1806344 | tf_op jit(solution)/shard_map/ppermute | solution.py:753
  126.6 1.7 %collective-permute-start.30 = (bf16[784,384]{1,0:T(8,128)(2,1)S(1)}, bf16[784,384]{1,0:T(8,128)(2,1)S(1)}, u32[]{:S(2)}, u32[]{:S(2)}) collective-permute-start(bf16[784,384]{1,0:T(8,128)(2,1)S(1)} %collective-permute-done.26.refs_2_), channel_id=1, source_target_pairs={{0,16},{16,0},{1,17},{17,1},{2,18},{18,2},{3,19},{19,3},{4,20},{20... | collective-permute-start | bytes 1806344 | tf_op jit(solution)/shard_map/ppermute | solution.py:753
  128.9 5.7 %collective-permute-start.29 = (bf16[784,384]{1,0:T(8,128)(2,1)S(1)}, bf16[784,384]{1,0:T(8,128)(2,1)S(1)}, u32[]{:S(2)}, u32[]{:S(2)}) collective-permute-start(bf16[784,384]{1,0:T(8,128)(2,1)S(1)} %collective-permute-done.25.refs_1_), channel_id=1, source_target_pairs={{0,16},{16,0},{1,17},{17,1},{2,18},{18,2},{3,19},{19,3},{4,20},{20... | collective-permute-start | bytes 1806344 | tf_op jit(solution)/shard_map/ppermute | solution.py:753
  136.3 3.6 %lay_out.1 = (bf16[1536,1536]{1,0:T(8,128)(2,1)}, f32[3,1536]{1,0:T(4,128)}) custom-call(s32[5]{0:T(128)S(1)} %concatenate.7.s_ref.at_ref, bf16[784,384]{1,0:T(8,128)(2,1)S(1)} %join_rows.1.refs_0_, bf16[784,384]{1,0:T(8,128)(2,1)S(1)} %collective-permute-done.25.refs_1_, bf16[784,384]{1,0:T(8,128)(2,1)S(1)} %collective-permute-done.26.refs_2_, ...), custom_call_target="tpu_custom_call" | custom-call | tf_op jit(solution)/shard_map/lay_out/pallas_call | solution.py:681
  (64 shorter events, 28.8 us)
Async XLA Ops:
  5.2 8.0 %collective-permute-start = (bf16[256,384]{1,0:T(8,128)(2,1)S(1)}, bf16[256,384]{1,0:T(8,128)(2,1)S(1)}, u32[]{:S(2)}, u32[]{:S(2)}) collective-permute-start(bf16[256,384]{1,0:T(8,128)(2,1)S(1)} %get-tuple-element.38), channel_id=1, source_target_pairs={{0,1},{1,2},{2,3},{3,0},{4,5},{5,6},{6,7},{7,4},{8,9},{9,10},{10,1... | collective-permute-start | bytes 589832 | tf_op jit(solution)/shard_map/ppermute | solution.py:67
  7.7 8.8 %collective-permute-start.1 = (bf16[256,384]{1,0:T(8,128)(2,1)S(1)}, bf16[256,384]{1,0:T(8,128)(2,1)S(1)}, u32[]{:S(2)}, u32[]{:S(2)}) collective-permute-start(bf16[256,384]{1,0:T(8,128)(2,1)S(1)} %get-tuple-element.39), channel_id=1, source_target_pairs={{0,2},{1,3},{2,0},{3,1},{4,6},{5,7},{6,4},{7,5},{8,10},{9,11},{10,... | collective-permute-start | bytes 589832 | tf_op jit(solution)/shard_map/ppermute | solution.py:67
  11.0 5.5 %collective-permute-start.2 = (bf16[256,384]{1,0:T(8,128)(2,1)S(1)}, bf16[256,384]{1,0:T(8,128)(2,1)S(1)}, u32[]{:S(2)}, u32[]{:S(2)}) collective-permute-start(bf16[256,384]{1,0:T(8,128)(2,1)S(1)} %get-tuple-element.40), channel_id=1, source_target_pairs={{0,3},{1,0},{2,1},{3,2},{4,7},{5,4},{6,5},{7,6},{8,11},{9,8},{10,9... | collective-permute-start | bytes 589832 | tf_op jit(solution)/shard_map/ppermute | solution.py:67
  16.5 10.6 %collective-permute-start.3 = (bf16[1040,256]{1,0:T(8,128)(2,1)S(1)}, bf16[1040,256]{1,0:T(8,128)(2,1)S(1)}, u32[]{:S(2)}, u32[]{:S(2)}) collective-permute-start(bf16[1040,256]{1,0:T(8,128)(2,1)S(1)} %stack_rows.1.refs_4_), channel_id=1, source_target_pairs={{0,8},{1,9},{2,10},{3,11},{4,12},{5,13},{6,14},{7,15},{8,0},{9,1},... | collective-permute-start | bytes 1597448 | tf_op jit(solution)/shard_map/ppermute | solution.py:719
  19.2 13.6 %collective-permute-start.4 = (bf16[1040,256]{1,0:T(8,128)(2,1)S(1)}, bf16[1040,256]{1,0:T(8,128)(2,1)S(1)}, u32[]{:S(2)}, u32[]{:S(2)}) collective-permute-start(bf16[1040,256]{1,0:T(8,128)(2,1)S(1)} %stack_rows.1.refs_4_), channel_id=1, source_target_pairs={{0,12},{1,13},{2,14},{3,15},{4,0},{5,1},{6,2},{7,3},{8,4},{9,5},{1... | collective-permute-start | bytes 1597448 | tf_op jit(solution)/shard_map/ppermute | solution.py:719
  20.0 15.1 %collective-permute-start.5 = (bf16[1040,256]{1,0:T(8,128)(2,1)S(1)}, bf16[1040,256]{1,0:T(8,128)(2,1)S(1)}, u32[]{:S(2)}, u32[]{:S(2)}) collective-permute-start(bf16[1040,256]{1,0:T(8,128)(2,1)S(1)} %stack_rows.1.refs_4_), channel_id=1, source_target_pairs={{0,4},{1,5},{2,6},{3,7},{4,8},{5,9},{6,10},{7,11},{8,12},{9,13},{1... | collective-permute-start | bytes 1597448 | tf_op jit(solution)/shard_map/ppermute | solution.py:719
  20.7 14.4 %collective-permute-start.6 = (bf16[16,1536]{1,0:T(8,128)(2,1)S(1)}, bf16[16,1536]{1,0:T(8,128)(2,1)S(1)}, u32[]{:S(2)}, u32[]{:S(2)}) collective-permute-start(bf16[16,1536]{1,0:T(8,128)(2,1)S(1)} %get-tuple-element.41.refs_4_), channel_id=1, source_target_pairs={{0,1},{1,2},{2,3},{3,4},{4,5},{5,6},{6,7},{7,8},{8,9},{9,10},{10,1... | collective-permute-start | bytes 147464 | tf_op jit(solution)/shard_map/ppermute | solution.py:715
  23.0 12.1 %collective-permute-start.7 = (bf16[16,1536]{1,0:T(8,128)(2,1)S(1)}, bf16[16,1536]{1,0:T(8,128)(2,1)S(1)}, u32[]{:S(2)}, u32[]{:S(2)}) collective-permute-start(bf16[16,1536]{1,0:T(8,128)(2,1)S(1)} %get-tuple-element.48), channel_id=1, source_target_pairs={{1,0},{2,1},{3,2},{4,3},{5,4},{6,5},{7,6},{8,7},{9,8},{10,9},{11,1... | collective-permute-start | bytes 147464 | tf_op jit(solution)/shard_map/ppermute | solution.py:716
  38.9 8.5 %collective-permute-start.8 = (bf16[272,256]{1,0:T(8,128)(2,1)}, bf16[272,256]{1,0:T(8,128)(2,1)S(1)}, u32[]{:S(2)}, u32[]{:S(2)}) collective-permute-start(bf16[272,256]{1,0:T(8,128)(2,1)} %get-tuple-element.50), channel_id=1, source_target_pairs={{0,3},{1,0},{2,1},{3,2},{4,7},{5,4},{6,5},{7,6},{8,11},{9,8},{10,9... | collective-permute-start | bytes 417800 | tf_op jit(solution)/shard_map/ppermute | solution.py:67
  41.3 6.1 %collective-permute-start.9 = (bf16[272,256]{1,0:T(8,128)(2,1)S(1)}, bf16[272,256]{1,0:T(8,128)(2,1)S(1)}, u32[]{:S(2)}, u32[]{:S(2)}) collective-permute-start(bf16[272,256]{1,0:T(8,128)(2,1)S(1)} %get-tuple-element.51), channel_id=1, source_target_pairs={{0,2},{1,3},{2,0},{3,1},{4,6},{5,7},{6,4},{7,5},{8,10},{9,11},{10,... | collective-permute-start | bytes 417800 | tf_op jit(solution)/shard_map/ppermute | solution.py:67
  42.3 5.9 %collective-permute-start.10 = (bf16[272,256]{1,0:T(8,128)(2,1)S(1)}, bf16[272,256]{1,0:T(8,128)(2,1)S(1)}, u32[]{:S(2)}, u32[]{:S(2)}) collective-permute-start(bf16[272,256]{1,0:T(8,128)(2,1)S(1)} %get-tuple-element.52), channel_id=1, source_target_pairs={{0,1},{1,2},{2,3},{3,0},{4,5},{5,6},{6,7},{7,4},{8,9},{9,10},{10,1... | collective-permute-start | bytes 417800 | tf_op jit(solution)/shard_map/ppermute | solution.py:67
  53.7 8.6 %collective-permute-start.11 = (bf16[4,384,768]{2,1,0:T(8,128)(2,1)S(1)}, bf16[4,384,768]{2,1,0:T(8,128)(2,1)S(1)}, u32[]{:S(2)}, u32[]{:S(2)}) collective-permute-start(bf16[4,384,768]{2,1,0:T(8,128)(2,1)S(1)} %get-tuple-element.57), channel_id=1, source_target_pairs={{0,16},{16,0},{1,17},{17,1},{2,18},{18,2},{3,19},{19,3},{4,20},{20... | collective-permute-start | bytes 7077896 | tf_op jit(solution)/shard_map/ppermute | solution.py:732
  63.6 20.6 %collective-permute-start.14 = (bf16[384,768]{1,0:T(8,128)(2,1)S(1)}, bf16[384,768]{1,0:T(8,128)(2,1)S(1)}, u32[]{:S(2)}, u32[]{:S(2)}) collective-permute-start(bf16[384,768]{1,0:T(8,128)(2,1)S(1)} %get-tuple-element.59), channel_id=1, source_target_pairs={{0,96},{1,97},{2,98},{3,99},{4,100},{5,101},{6,102},{7,103},{8,104... | collective-permute-start | bytes 1769480 | tf_op jit(solution)/shard_map/ppermute | solution.py:67
  65.1 19.1 %collective-permute-start.12 = (bf16[384,768]{1,0:T(8,128)(2,1)S(1)}, bf16[384,768]{1,0:T(8,128)(2,1)S(1)}, u32[]{:S(2)}, u32[]{:S(2)}) collective-permute-start(bf16[384,768]{1,0:T(8,128)(2,1)S(1)} %product.4), channel_id=1, source_target_pairs={{0,32},{1,33},{2,34},{3,35},{4,36},{5,37},{6,38},{7,39},{8,40},{9,... | collective-permute-start | bytes 1769480 | tf_op jit(solution)/shard_map/ppermute | solution.py:67
  67.3 17.0 %collective-permute-start.13 = (bf16[384,768]{1,0:T(8,128)(2,1)S(1)}, bf16[384,768]{1,0:T(8,128)(2,1)S(1)}, u32[]{:S(2)}, u32[]{:S(2)}) collective-permute-start(bf16[384,768]{1,0:T(8,128)(2,1)S(1)} %product.5), channel_id=1, source_target_pairs={{0,64},{1,65},{2,66},{3,67},{4,68},{5,69},{6,70},{7,71},{8,72},{9,... | collective-permute-start | bytes 1769480 | tf_op jit(solution)/shard_map/ppermute | solution.py:67
  80.9 7.0 %collective-permute-start.18 = (f32[3,768]{1,0:T(4,128)S(1)}, f32[3,768]{1,0:T(4,128)S(1)}, u32[]{:S(2)}, u32[]{:S(2)}) collective-permute-start(f32[3,768]{1,0:T(4,128)S(1)} %get-tuple-element.67), channel_id=1, source_target_pairs={{0,16},{16,0},{1,17},{17,1},{2,18},{18,2},{3,19},{19,3},{4,20},{20... | collective-permute-start | bytes 27656 | tf_op jit(solution)/shard_map/ppermute | solution.py:742
  85.1 5.9 %collective-permute-start.15 = (bf16[96,768]{1,0:T(8,128)(2,1)S(1)}, bf16[96,768]{1,0:T(8,128)(2,1)S(1)}, u32[]{:S(2)}, u32[]{:S(2)}) collective-permute-start(bf16[96,768]{1,0:T(8,128)(2,1)S(1)} %get-tuple-element.61), channel_id=1, source_target_pairs={{0,2},{1,3},{2,0},{3,1},{4,6},{5,7},{6,4},{7,5},{8,10},{9,11},{10,... | collective-permute-start | bytes 442376 | tf_op jit(solution)/shard_map/ppermute | solution.py:67
  85.2 7.1 %collective-permute-start.16 = (bf16[96,768]{1,0:T(8,128)(2,1)S(1)}, bf16[96,768]{1,0:T(8,128)(2,1)S(1)}, u32[]{:S(2)}, u32[]{:S(2)}) collective-permute-start(bf16[96,768]{1,0:T(8,128)(2,1)S(1)} %get-tuple-element.62), channel_id=1, source_target_pairs={{0,1},{1,2},{2,3},{3,0},{4,5},{5,6},{6,7},{7,4},{8,9},{9,10},{10,1... | collective-permute-start | bytes 442376 | tf_op jit(solution)/shard_map/ppermute | solution.py:67
  87.2 5.2 %collective-permute-start.17 = (bf16[96,768]{1,0:T(8,128)(2,1)S(1)}, bf16[96,768]{1,0:T(8,128)(2,1)S(1)}, u32[]{:S(2)}, u32[]{:S(2)}) collective-permute-start(bf16[96,768]{1,0:T(8,128)(2,1)S(1)} %get-tuple-element.63), channel_id=1, source_target_pairs={{0,3},{1,0},{2,1},{3,2},{4,7},{5,4},{6,5},{7,6},{8,11},{9,8},{10,9... | collective-permute-start | bytes 442376 | tf_op jit(solution)/shard_map/ppermute | solution.py:67
  92.5 5.5 %collective-permute-start.20 = (bf16[112,768]{1,0:T(8,128)(2,1)S(1)}, bf16[112,768]{1,0:T(8,128)(2,1)S(1)}, u32[]{:S(2)}, u32[]{:S(2)}) collective-permute-start(bf16[112,768]{1,0:T(8,128)(2,1)S(1)} %fusion.1), channel_id=1, source_target_pairs={{0,4},{1,5},{2,6},{3,7},{4,8},{5,9},{6,10},{7,11},{8,12},{9,13},{1... | collective-permute-start | bytes 516104 | tf_op jit(solution)/shard_map/ppermute | solution.py:67
  94.1 5.8 %collective-permute-start.19 = (bf16[112,768]{1,0:T(8,128)(2,1)S(1)}, bf16[112,768]{1,0:T(8,128)(2,1)S(1)}, u32[]{:S(2)}, u32[]{:S(2)}) collective-permute-start(bf16[112,768]{1,0:T(8,128)(2,1)S(1)} %fusion.1), channel_id=1, source_target_pairs={{0,8},{1,9},{2,10},{3,11},{4,12},{5,13},{6,14},{7,15},{8,0},{9,1},... | collective-permute-start | bytes 516104 | tf_op jit(solution)/shard_map/ppermute | solution.py:67
  94.6 6.1 %collective-permute-start.21 = (bf16[112,768]{1,0:T(8,128)(2,1)S(1)}, bf16[112,768]{1,0:T(8,128)(2,1)S(1)}, u32[]{:S(2)}, u32[]{:S(2)}) collective-permute-start(bf16[112,768]{1,0:T(8,128)(2,1)S(1)} %fusion.1), channel_id=1, source_target_pairs={{0,12},{1,13},{2,14},{3,15},{4,0},{5,1},{6,2},{7,3},{8,4},{9,5},{1... | collective-permute-start | bytes 516104 | tf_op jit(solution)/shard_map/ppermute | solution.py:67
  100.8 5.9 %collective-permute-start.24 = (bf16[112,768]{1,0:T(8,128)(2,1)S(1)}, bf16[112,768]{1,0:T(8,128)(2,1)S(1)}, u32[]{:S(2)}, u32[]{:S(2)}) collective-permute-start(bf16[112,768]{1,0:T(8,128)(2,1)S(1)} %multiply_convert_fusion.refs_0_), channel_id=1, source_target_pairs={{0,3},{1,0},{2,1},{3,2},{4,7},{5,4},{6,5},{7,6},{8,11},{9,8},{10,9... | collective-permute-start | bytes 516104 | tf_op jit(solution)/shard_map/ppermute | solution.py:67
  102.5 5.9 %collective-permute-start.23 = (bf16[112,768]{1,0:T(8,128)(2,1)S(1)}, bf16[112,768]{1,0:T(8,128)(2,1)S(1)}, u32[]{:S(2)}, u32[]{:S(2)}) collective-permute-start(bf16[112,768]{1,0:T(8,128)(2,1)S(1)} %multiply_convert_fusion.refs_0_), channel_id=1, source_target_pairs={{0,2},{1,3},{2,0},{3,1},{4,6},{5,7},{6,4},{7,5},{8,10},{9,11},{10,... | collective-permute-start | bytes 516104 | tf_op jit(solution)/shard_map/ppermute | solution.py:67
  103.1 7.0 %collective-permute-start.22 = (bf16[112,768]{1,0:T(8,128)(2,1)S(1)}, bf16[112,768]{1,0:T(8,128)(2,1)S(1)}, u32[]{:S(2)}, u32[]{:S(2)}) collective-permute-start(bf16[112,768]{1,0:T(8,128)(2,1)S(1)} %multiply_convert_fusion.refs_0_), channel_id=1, source_target_pairs={{0,1},{1,2},{2,3},{3,0},{4,5},{5,6},{6,7},{7,4},{8,9},{9,10},{10,1... | collective-permute-start | bytes 516104 | tf_op jit(solution)/shard_map/ppermute | solution.py:67
  110.9 9.2 %collective-permute-start.27 = (bf16[784,384]{1,0:T(8,128)(2,1)S(1)}, bf16[784,384]{1,0:T(8,128)(2,1)S(1)}, u32[]{:S(2)}, u32[]{:S(2)}) collective-permute-start(bf16[784,384]{1,0:T(8,128)(2,1)S(1)} %join_rows.1.refs_0_), channel_id=1, source_target_pairs={{0,96},{1,97},{2,98},{3,99},{4,100},{5,101},{6,102},{7,103},{8,104... | collective-permute-start | bytes 1806344 | tf_op jit(solution)/shard_map/ppermute | solution.py:67
  111.8 14.8 %collective-permute-start.26 = (bf16[784,384]{1,0:T(8,128)(2,1)S(1)}, bf16[784,384]{1,0:T(8,128)(2,1)S(1)}, u32[]{:S(2)}, u32[]{:S(2)}) collective-permute-start(bf16[784,384]{1,0:T(8,128)(2,1)S(1)} %join_rows.1.refs_0_), channel_id=1, source_target_pairs={{0,64},{1,65},{2,66},{3,67},{4,68},{5,69},{6,70},{7,71},{8,72},{9,... | collective-permute-start | bytes 1806344 | tf_op jit(solution)/shard_map/ppermute | solution.py:67
  112.8 16.1 %collective-permute-start.25 = (bf16[784,384]{1,0:T(8,128)(2,1)S(1)}, bf16[784,384]{1,0:T(8,128)(2,1)S(1)}, u32[]{:S(2)}, u32[]{:S(2)}) collective-permute-start(bf16[784,384]{1,0:T(8,128)(2,1)S(1)} %join_rows.1.refs_0_), channel_id=1, source_target_pairs={{0,32},{1,33},{2,34},{3,35},{4,36},{5,37},{6,38},{7,39},{8,40},{9,... | collective-permute-start | bytes 1806344 | tf_op jit(solution)/shard_map/ppermute | solution.py:67
  112.8 21.8 %collective-permute-start.28 = (bf16[784,384]{1,0:T(8,128)(2,1)S(1)}, bf16[784,384]{1,0:T(8,128)(2,1)S(1)}, u32[]{:S(2)}, u32[]{:S(2)}) collective-permute-start(bf16[784,384]{1,0:T(8,128)(2,1)S(1)} %join_rows.1.refs_0_), channel_id=1, source_target_pairs={{0,16},{16,0},{1,17},{17,1},{2,18},{18,2},{3,19},{19,3},{4,20},{20... | collective-permute-start | bytes 1806344 | tf_op jit(solution)/shard_map/ppermute | solution.py:753
  120.2 14.5 %collective-permute-start.31 = (bf16[784,384]{1,0:T(8,128)(2,1)S(1)}, bf16[784,384]{1,0:T(8,128)(2,1)S(1)}, u32[]{:S(2)}, u32[]{:S(2)}) collective-permute-start(bf16[784,384]{1,0:T(8,128)(2,1)S(1)} %collective-permute-done.27.refs_3_), channel_id=1, source_target_pairs={{0,16},{16,0},{1,17},{17,1},{2,18},{18,2},{3,19},{19,3},{4,20},{20... | collective-permute-start | bytes 1806344 | tf_op jit(solution)/shard_map/ppermute | solution.py:753
  126.6 8.1 %collective-permute-start.30 = (bf16[784,384]{1,0:T(8,128)(2,1)S(1)}, bf16[784,384]{1,0:T(8,128)(2,1)S(1)}, u32[]{:S(2)}, u32[]{:S(2)}) collective-permute-start(bf16[784,384]{1,0:T(8,128)(2,1)S(1)} %collective-permute-done.26.refs_2_), channel_id=1, source_target_pairs={{0,16},{16,0},{1,17},{17,1},{2,18},{18,2},{3,19},{19,3},{4,20},{20... | collective-permute-start | bytes 1806344 | tf_op jit(solution)/shard_map/ppermute | solution.py:753
  128.9 7.4 %collective-permute-start.29 = (bf16[784,384]{1,0:T(8,128)(2,1)S(1)}, bf16[784,384]{1,0:T(8,128)(2,1)S(1)}, u32[]{:S(2)}, u32[]{:S(2)}) collective-permute-start(bf16[784,384]{1,0:T(8,128)(2,1)S(1)} %collective-permute-done.25.refs_1_), channel_id=1, source_target_pairs={{0,16},{16,0},{1,17},{17,1},{2,18},{18,2},{3,19},{19,3},{4,20},{20... | collective-permute-start | bytes 1806344 | tf_op jit(solution)/shard_map/ppermute | solution.py:753
  (4 other events, 12.1 us)

commit v10 on v8

--- a/solution.py
+++ b/solution.py
@@ -73,11 +73,12 @@
     return (a + c) + (b + d)
 
 
-def project(at, tokens, query_weight, key_weight, value_weight):
+def project(tokens, query_weight, key_weight, value_weight):
     rows, depth = tokens.shape
     cut = depth // 2
 
-    def kernel(at_ref, tok_hbm, wq_hbm, wk_hbm, wv_hbm, *refs):
+    def kernel(tok_hbm, wq_hbm, wk_hbm, wv_hbm, *refs):
+        head_at = jnp.where(lax.axis_index("c") == 0, lax.axis_index("y"), lax.axis_index("z"))
         outs, (tok_ref, wq_ref, wk_ref, wv_ref, held, sems) = refs[:4], refs[4:]
         low, high = pl.ds(0, cut), pl.ds(cut, depth - cut)
         copies = [
@@ -99,49 +100,46 @@
         k = jnp.dot(tok, wk_ref[...], preferred_element_type=F32)
         copies[4].wait()
         q = jnp.dot(tok, wq_ref[...], preferred_element_type=F32) * (1.0 / math.sqrt(DH))
-        zero = jnp.zeros((rows, DH), F32)
         for h in range(H):
-            held[h] = jnp.concatenate(
-                [
-                    v[:, h * DV : (h + 1) * DV],
-                    k[:, h * DH : (h + 1) * DH],
-                    zero,
-                    q[:, h * DH : (h + 1) * DH],
-                ],
-                axis=1,
+            part = slice(h * DH, (h + 1) * DH)
+            held[h, :rows, :] = jnp.concatenate([v[:, h * DV : (h + 1) * DV], k[:, part]], axis=1).astype(BF)
+            held[h, rows:, :] = jnp.concatenate(
+                [q[n * rows // 4 : (n + 1) * rows // 4, part] for n in range(4)], axis=1
             ).astype(BF)
         for d in range(4):
-            outs[d][...] = held[(Spot(at_ref).head_at + d) % 4]
-
-    return pl.pallas_call(
-        kernel,
-        out_shape=[jax.ShapeDtypeStruct((rows, 384), BF)] * 4,
-        in_specs=[SMEM] + [ANY] * 4,
+            outs[d][...] = held[(head_at + d) % 4]
+
+    return pl.pallas_call(
+        kernel,
+        out_shape=[jax.ShapeDtypeStruct((rows + rows // 4, 256), BF)] * 4,
+        in_specs=[ANY] * 4,
         out_specs=[VMEM] * 4,
         scratch_shapes=[
             pltpu.VMEM((rows, depth), BF),
             pltpu.VMEM((depth, H * DH), BF),
             pltpu.VMEM((depth, H * DH), BF),
             pltpu.VMEM((depth, H * DV), BF),
-            pltpu.VMEM((4, rows, 384), BF),
+            pltpu.VMEM((4, rows + rows // 4, 256), BF),
             pltpu.SemaphoreType.DMA((5,)),
         ],
         compiler_params=params(53),
         name="project",
-    )(at, tokens, query_weight, key_weight, value_weight)
+    )(tokens, query_weight, key_weight, value_weight)
 
 
 def stack_rows(parts, behind):
-    rows = parts[0].shape[0]
+    rows = parts[0].shape[0] * 4 // 5
 
     def kernel(*refs):
         ins, out = refs[:4], refs[5]
+        zero = jnp.zeros((1, DH), F32)
         row = lax.broadcasted_iota(jnp.int32, (TAIL, 128), 0)
         tail = jnp.zeros((TAIL, 128), F32)
         for d in range(4):
-            out[d * rows : (d + 1) * rows, :] = ins[d][:, :256]
-            first = ins[d][:TAIL, 256:].astype(F32)[:1]
-            final = ins[d][rows - TAIL :, 256:].astype(F32)[TAIL - 1 :]
+            out[d * rows : (d + 1) * rows, :] = ins[d][:rows, :]
+            first = ins[d][rows : rows + TAIL, :].astype(F32)[:1, :DH]
+            final = ins[d][rows + rows // 4 - TAIL :, :].astype(F32)[TAIL - 1 :, 3 * DH :]
+            first, final = (jnp.concatenate([zero, r], axis=1) for r in (first, final))
             tail = jnp.where(row == d, first, tail)
             tail = jnp.where(row == 4 + d, final, tail)
         out[4 * rows :, :128] = jnp.zeros((TAIL, 128), BF)
@@ -155,6 +153,29 @@
         compiler_params=params(8),
         name="stack_rows",
     )(*parts, behind)
+
+
+def spread(parts):
+    rows = parts[0].shape[0] * 4 // 5
+    quarter = rows // 4
+
+    def kernel(*refs):
+        zero = jnp.zeros((quarter, DH), F32)
+        for d in range(4):
+            packed = refs[d][rows:, :].astype(F32)
+            for n in range(4):
+                refs[4 + d][n * quarter : (n + 1) * quarter, :] = jnp.concatenate(
+                    [zero, packed[:, n * DH : (n + 1) * DH]], axis=1
+                ).astype(BF)
+
+    return pl.pallas_call(
+        kernel,
+        out_shape=[jax.ShapeDtypeStruct((rows, 128), BF)] * 4,
+        in_specs=[VMEM] * 4,
+        out_specs=[VMEM] * 4,
+        compiler_params=params(8),
+        name="spread",
+    )(*parts)
 
 
 def attend(scalars, near, q, pairs, state, behind=()):
@@ -215,13 +236,12 @@
             for s, r in zip(parts, pair_refs):
                 edge_sums += jnp.dot(jnp.exp(s - peak).astype(BF), values_of(r), preferred_element_type=F32)
             edge_out = shares(edge_sums)
-            row = lax.broadcasted_iota(jnp.int32, (TAIL, 256), 0)
 
         pair_ref = pair_refs[-1]
         keep = masks(near)
         values = values_of(pair_ref)
         for i in range(4):
-            score_ref[i] = raw_scores(q_refs[i][:, 256:], pair_ref)
+            score_ref[i] = raw_scores(q_refs[i][...], pair_ref)
         for i in range(4):
             for k in range(0, rows, strip):
                 cut = slice(k, k + strip)
@@ -237,10 +257,18 @@
                 shrink = jnp.exp(old_peak[i * rows : (i + 1) * rows, :] - peak_ref[i])
                 update = update + old[i * rows : (i + 1) * rows, :] * jnp.concatenate([shrink] * 2, axis=1)
             if last:
-                refs[i][:rows, :] = shares(update).astype(BF)
-                ends = jnp.where(row == 0, edge_out[i : i + 1], jnp.zeros((TAIL, 256), F32))
-                ends = jnp.where(row == 1, edge_out[4 + i : 5 + i], ends)
-                refs[i][rows:, :] = ends.astype(BF)
+                share = shares(update)
+                high = share[:, 128:DV]
+                refs[i][:rows, :] = share[:, :128].astype(BF)
+                refs[i][rows : rows + rows // 2, :] = jnp.concatenate(
+                    [high[: rows // 2], high[rows // 2 :]], axis=1
+                ).astype(BF)
+                ends = jnp.zeros((TAIL, 128), F32)
+                for n in range(4):
+                    at = i + 4 * (n % 2)
+                    part = edge_out[at : at + 1, :128] if n < 2 else edge_out[at : at + 1, 128:]
+                    ends = jnp.where(row == n, part, ends)
+                refs[i][rows + rows // 2 :, :] = ends.astype(BF)
             else:
                 refs[0][i * rows : (i + 1) * rows, :] = update
                 refs[1][i * rows : (i + 1) * rows, :] = peak_ref[i]
@@ -249,7 +277,7 @@
     if not first:
         ins += [*state]
     if last:
-        outs = [jax.ShapeDtypeStruct((rows + TAIL, 256), BF)] * 4
+        outs = [jax.ShapeDtypeStruct((rows + rows // 2 + TAIL, 128), BF)] * 4
     else:
         outs = [jax.ShapeDtypeStruct((4 * rows, n), F32) for n in (256, 128)]
     return pl.pallas_call(
@@ -342,7 +370,15 @@
 
         @pl.when(j == 0)
         def _():
-            mixed = [b[:, :DV].astype(F32) for b in (b0, b1, b2, b3)]
+            mixed = []
+            for b in (b0, b1, b2, b3):
+                pair = b[rows : rows + rows // 2, :].astype(F32)
+                last = b[rows + rows // 2 :, :].astype(F32)
+                high = jnp.concatenate(
+                    [pair[:, :64], pair[:, 64:], last[2:4, :64], jnp.zeros((TAIL - 2, 64), F32)], axis=0
+                )
+                left = jnp.concatenate([b[:rows, :].astype(F32), last], axis=0)
+                mixed.append(jnp.concatenate([left, high], axis=1))
             squares = sum(jnp.sum(m * m, axis=1, keepdims=True) for m in mixed)
             scale = lax.rsqrt(squares * (1.0 / (H * DV)) + 1e-05)
             for d in range(4):
@@ -426,7 +462,7 @@
         grid_spec=pltpu.PrefetchScalarGridSpec(
             num_scalar_prefetch=1,
             grid=(steps if ours else steps + 2,),
-            in_specs=[flat(rows + TAIL, 256)] * 4
+            in_specs=[flat(rows + rows // 2 + TAIL, 128)] * 4
             + [cols(TAIL, True), cols(TAIL, True), cols(3, True)]
             + [VMEM] * 4,
             out_specs=out_specs,
@@ -705,12 +741,13 @@
     ix, ic, iz, iy = (lax.axis_index(a) for a in AXES)
     spot = jnp.stack([v.astype(jnp.int32) for v in (ix, ic, iz, iy)])
     scalars = jnp.concatenate([spot, valid_bins.astype(jnp.int32)])
-    blocks = project(spot, tokens, query_weight, key_weight, value_weight)
+    blocks = project(tokens, query_weight, key_weight, value_weight)
     down, up = edges(blocks[0], tokens, skipped, upstream)
     before = lax.ppermute(down, ("z", "y"), [(i, i + 1) for i in range(15)])
     after = lax.ppermute(up, ("z", "y"), [(i + 1, i) for i in range(15)])
-    q = exchange(blocks, HEAD_RING)
-    own = stack_rows(q, down)
+    blocks = exchange(blocks, HEAD_RING)
+    own = stack_rows(blocks, down)
+    q = spread(blocks)
     far = {d: lax.ppermute(own, AXES, turn(ROW_RING, d)) for d in (1, 3, 2)}
     state = attend(scalars, 0, q, [own], None)
 

time: 139 us -> 137 us (0.986)
  waiting for transfers between devices: 31.5 us -> 28.4 us
  starting transfers between devices: 53.6 us -> 56 us
    ppermute x21, waiting for transfers between devices: 27.8 us -> 25 us  [exchange(): got[d] = lax.ppermute(pieces[d], AXES, turn(axes, sign * d))]
    ppermute x21, starting transfers between devices: 29.7 us -> 31.5 us  [exchange(): got[d] = lax.ppermute(pieces[d], AXES, turn(axes, sign * d))]
    pallas_call x1 -> x2, Pallas kernels: 4.48 us -> 4.02 us  [the longest x1 3.92 us: project(): pl.pallas_call(kernel, out_shape=[jax.ShapeDtypeStruct((rows + rows // 4,...]
  transfers between devices with their start and end apart: 32 -> 32, of which waited for: 14 -> 13; matrix products, arithmetic and copies ran while one was open for 1% -> 1% of each run, Pallas kernels for 21% -> 21%
where the time goes in v10:
time: 137 us
  starting transfers between devices  56 us (41%)
  Pallas kernels  47.3 us (35%)
  waiting for transfers between devices  28.4 us (21%)
  local copies, waits for them, and re-layouts  3.21 us (2%)
  between operations  1.72 us (1%)
    ppermute x21, starting transfers between devices, exchange(): got[d] = lax.ppermute(pieces[d], AXES, turn(axes, sign * d))  31.5 us
    ppermute x21, waiting for transfers between devices, exchange(): got[d] = lax.ppermute(pieces[d], AXES, turn(axes, sign * d))  25 us
    pallas_call x1, Pallas kernels, backward(): pl.pallas_call(kernel, out_shape=[jax.ShapeDtypeStruct((fine, columns), B...  12.9 us
    ppermute x4, starting transfers between devices, local(): other = [lax.ppermute(block, 'c', swap) for block in own]  11.8 us
    pallas_call x4, Pallas kernels, attend(): pl.pallas_call(kernel, out_shape=outs, in_specs=[SMEM] + [VMEM] * len(ins...  9.97 us
    pallas_call x2, Pallas kernels, forward(): pl.pallas_call(kernel, out_shape=outs, grid_spec=pltpu.PrefetchScalarGrid...  9.51 us
    ppermute x3, starting transfers between devices, local(): far = {d: lax.ppermute(own, AXES, turn(ROW_RING, d)) for d in (1, 3, 2)}  4.13 us
    pallas_call x1, Pallas kernels, project(): pl.pallas_call(kernel, out_shape=[jax.ShapeDtypeStruct((rows + rows // 4,...  3.92 us
  transfers between devices with their start and end apart: 32, of which 13 were waited for; matrix products, arithmetic and copies ran while one was open for 1% of the time, Pallas kernels for 21%

profile of v10, /device:TPU:1, one launch (start us, length us, event | category | flops | bytes accessed | tf_op | source)
XLA Modules:
  0.0 136.8 jit_solution(14593951522278298787)
XLA Ops:
  0.6 3.9 %project.1 = (bf16[320,256]{1,0:T(8,128)(2,1)S(1)}, bf16[320,256]{1,0:T(8,128)(2,1)S(1)}, bf16[320,256]{1,0:T(8,128)(2,1)S(1)}, bf16[320,256]{1,0:T(8,128)(2,1)S(1)}) custom-call(bf16[256,1536]{1,0:T(8,128)(2,1)} %bitcast.11, bf16[1536,256]{1,0:T(8,128)(2,1)} %wq_hbm.1, bf16[1536,256]{1,0:T(8,128)(2,1)} %wk_hbm.1, bf16[1536,768]{1,0:T(8,128)(2,1)} %wv_hbm.1), custom_call_target="tpu_custom_call" | custom-call | tf_op jit(solution)/shard_map/project/pallas_call | solution.py:112
  4.6 2.5 %collective-permute-start = (bf16[320,256]{1,0:T(8,128)(2,1)S(1)}, bf16[320,256]{1,0:T(8,128)(2,1)S(1)}, u32[]{:S(2)}, u32[]{:S(2)}) collective-permute-start(bf16[320,256]{1,0:T(8,128)(2,1)S(1)} %get-tuple-element.44), channel_id=1, source_target_pairs={{0,1},{1,2},{2,3},{3,0},{4,5},{5,6},{6,7},{7,4},{8,9},{9,10},{10,1... | collective-permute-start | bytes 491528 | tf_op jit(solution)/shard_map/ppermute | solution.py:67
  7.1 3.3 %collective-permute-start.1 = (bf16[320,256]{1,0:T(8,128)(2,1)S(1)}, bf16[320,256]{1,0:T(8,128)(2,1)S(1)}, u32[]{:S(2)}, u32[]{:S(2)}) collective-permute-start(bf16[320,256]{1,0:T(8,128)(2,1)S(1)} %get-tuple-element.45), channel_id=1, source_target_pairs={{0,2},{1,3},{2,0},{3,1},{4,6},{5,7},{6,4},{7,5},{8,10},{9,11},{10,... | collective-permute-start | bytes 491528 | tf_op jit(solution)/shard_map/ppermute | solution.py:67
  12.2 3.0 %collective-permute-done.1.refs_2_ = bf16[320,256]{1,0:T(8,128)(2,1)S(1)} collective-permute-done((bf16[320,256]{1,0:T(8,128)(2,1)S(1)}, bf16[320,256]{1,0:T(8,128)(2,1)S(1)}, u32[]{:S(2)}, u32[]{:S(2)}) %collective-permute-start.1) | collective-permute-done | bytes 163872 | tf_op jit(solution)/shard_map/ppermute | solution.py:67
  19.4 2.3 %collective-permute-start.6 = (bf16[16,1536]{1,0:T(8,128)(2,1)S(1)}, bf16[16,1536]{1,0:T(8,128)(2,1)S(1)}, u32[]{:S(2)}, u32[]{:S(2)}) collective-permute-start(bf16[16,1536]{1,0:T(8,128)(2,1)S(1)} %get-tuple-element.51.refs_4_), channel_id=1, source_target_pairs={{0,1},{1,2},{2,3},{3,4},{4,5},{5,6},{6,7},{7,8},{8,9},{9,10},{10,1... | collective-permute-start | bytes 147464 | tf_op jit(solution)/shard_map/ppermute | solution.py:746
  23.8 2.2 %attend.4 = (f32[1024,256]{1,0:T(8,128)S(1)}, f32[1024,128]{1,0:T(8,128)S(1)}) custom-call(s32[5]{0:T(128)S(1)} %concatenate.6.s_ref.at_ref, bf16[256,128]{1,0:T(8,128)(2,1)S(1)} %get-tuple-element.47.refs_0_, bf16[256,128]{1,0:T(8,128)(2,1)S(1)} %get-tuple-element.48.refs_1_, bf16[256,128]{1,0:T(8,128)(2,1)S(1)} %get-tuple-element.49.refs_2_, ...), custom_call_target="tpu_custom_call" | custom-call | flops 1073741824 | bytes 4194304 | tf_op jit(solution)/shard_map/attend/pallas_call | solution.py:283
  26.1 2.3 %attend.5 = (f32[1024,256]{1,0:T(8,128)S(1)}, f32[1024,128]{1,0:T(8,128)S(1)}) custom-call(s32[5]{0:T(128)S(1)} %concatenate.6.s_ref.at_ref, bf16[256,128]{1,0:T(8,128)(2,1)S(1)} %get-tuple-element.47.refs_0_, bf16[256,128]{1,0:T(8,128)(2,1)S(1)} %get-tuple-element.48.refs_1_, bf16[256,128]{1,0:T(8,128)(2,1)S(1)} %get-tuple-element.49.refs_2_, ...), custom_call_target="tpu_custom_call" | custom-call | flops 1073741824 | bytes 4194304 | tf_op jit(solution)/shard_map/attend/pallas_call | solution.py:283
  29.9 2.2 %attend.6 = (f32[1024,256]{1,0:T(8,128)S(1)}, f32[1024,128]{1,0:T(8,128)S(1)}) custom-call(s32[5]{0:T(128)S(1)} %concatenate.6.s_ref.at_ref, bf16[256,128]{1,0:T(8,128)(2,1)S(1)} %get-tuple-element.47.refs_0_, bf16[256,128]{1,0:T(8,128)(2,1)S(1)} %get-tuple-element.48.refs_1_, bf16[256,128]{1,0:T(8,128)(2,1)S(1)} %get-tuple-element.49.refs_2_, ...), custom_call_target="tpu_custom_call" | custom-call | flops 1073741824 | bytes 4194304 | tf_op jit(solution)/shard_map/attend/pallas_call | solution.py:283
  32.2 3.3 %attend.7 = (bf16[400,128]{1,0:T(8,128)(2,1)S(1)}, bf16[400,128]{1,0:T(8,128)(2,1)S(1)}, bf16[400,128]{1,0:T(8,128)(2,1)S(1)}, bf16[400,128]{1,0:T(8,128)(2,1)S(1)}) custom-call(s32[5]{0:T(128)S(1)} %concatenate.6.s_ref.at_ref, bf16[256,128]{1,0:T(8,128)(2,1)S(1)} %get-tuple-element.47.refs_0_, bf16[256,128]{1,0:T(8,128)(2,1)S(1)} %get-tuple-element.48.refs_1_, ...), custom_call_target="tpu_custom_call" | custom-call | flops 1073741824 | bytes 4194304 | tf_op jit(solution)/shard_map/attend/pallas_call | solution.py:283
  35.5 4.3 %collective-permute-start.8 = (bf16[400,128]{1,0:T(8,128)(2,1)S(1)}, bf16[400,128]{1,0:T(8,128)(2,1)S(1)}, u32[]{:S(2)}, u32[]{:S(2)}) collective-permute-start(bf16[400,128]{1,0:T(8,128)(2,1)S(1)} %get-tuple-element.60), channel_id=1, source_target_pairs={{0,3},{1,0},{2,1},{3,2},{4,7},{5,4},{6,5},{7,6},{8,11},{9,8},{10,9... | collective-permute-start | bytes 307208 | tf_op jit(solution)/shard_map/ppermute | solution.py:67
  40.9 1.7 %copy.13.g_ref = bf16[1536,512]{1,0:T(8,128)(2,1)S(1)} copy(bf16[1536,512]{0,1:T(8,128)(2,1)} %bitcast.15) | data formatting | bytes 3145728 | tf_op jit(solution)/shard_map/transpose | solution.py:754
  44.0 1.8 %load.1 = (bf16[256,1536]{1,0:T(8,128)(2,1)S(1)}, bf16[512,1536]{1,0:T(8,128)(2,1)S(1)}, bf16[4,192,1536]{2,1,0:T(8,128)(2,1)S(1)}) custom-call(bf16[400,128]{1,0:T(8,128)(2,1)S(1)} %get-tuple-element.59.behind_ref.b0, bf16[256,1536]{1,0:T(8,128)(2,1)S(1)} %bitcast.13, bf16[512,1536]{1,0:T(8,128)(2,1)S(1)} %bitcast.18, bf16[4,192,1536]{2,1,0:T(8,128)(2,1)} %bitcast.19), custom_call_target="tpu_custom_call" | custom-call | tf_op jit(solution)/shard_map/load/pallas_call | solution.py:490
  46.2 5.5 %forward.3 = (bf16[544,768]{1,0:T(8,128)(2,1)S(1)}, bf16[4,384,768]{2,1,0:T(8,128)(2,1)S(1)}) custom-call(s32[5]{0:T(128)S(1)} %concatenate.6.s_ref.at_ref, bf16[400,128]{1,0:T(8,128)(2,1)S(1)} %get-tuple-element.59.behind_ref.b0, bf16[400,128]{1,0:T(8,128)(2,1)S(1)} %collective-permute-done.8.b1, bf16[400,128]{1,0:T(8,128)(2,1)S(1)} %collective-permute-done.9.b2, ...), custom_call_target="tpu_custom_call" | custom-call | flops 2415919104 | bytes 9437184 | tf_op jit(solution)/shard_map/forward/pallas_call | solution.py:459
  51.8 2.5 %collective-permute-start.11 = (bf16[4,384,768]{2,1,0:T(8,128)(2,1)S(1)}, bf16[4,384,768]{2,1,0:T(8,128)(2,1)S(1)}, u32[]{:S(2)}, u32[]{:S(2)}) collective-permute-start(bf16[4,384,768]{2,1,0:T(8,128)(2,1)S(1)} %get-tuple-element.67), channel_id=1, source_target_pairs={{0,16},{16,0},{1,17},{17,1},{2,18},{18,2},{3,19},{19,3},{4,20},{20... | collective-permute-start | bytes 7077896 | tf_op jit(solution)/shard_map/ppermute | solution.py:764
  54.3 4.0 %forward.2 = (bf16[544,768]{1,0:T(8,128)(2,1)S(1)}, bf16[512,768]{1,0:T(8,128)(2,1)S(1)}) custom-call(s32[5]{0:T(128)S(1)} %concatenate.6.s_ref.at_ref, bf16[400,128]{1,0:T(8,128)(2,1)S(1)} %get-tuple-element.59.behind_ref.b0, bf16[400,128]{1,0:T(8,128)(2,1)S(1)} %collective-permute-done.8.b1, bf16[400,128]{1,0:T(8,128)(2,1)S(1)} %collective-permute-done.9.b2, ...), custom_call_target="tpu_custom_call" | custom-call | flops 2415919104 | bytes 9437184 | tf_op jit(solution)/shard_map/forward/pallas_call | solution.py:459
  60.8 1.8 %collective-permute-start.13 = (bf16[384,768]{1,0:T(8,128)(2,1)S(1)}, bf16[384,768]{1,0:T(8,128)(2,1)S(1)}, u32[]{:S(2)}, u32[]{:S(2)}) collective-permute-start(bf16[384,768]{1,0:T(8,128)(2,1)S(1)} %get-tuple-element.70), channel_id=1, source_target_pairs={{0,64},{1,65},{2,66},{3,67},{4,68},{5,69},{6,70},{7,71},{8,72},{9,... | collective-permute-start | bytes 1769480 | tf_op jit(solution)/shard_map/ppermute | solution.py:67
  64.7 12.9 %backward.1 = (bf16[512,1536]{1,0:T(8,128)(2,1)}, f32[3,768]{1,0:T(4,128)S(1)}, f32[3,768]{1,0:T(4,128)S(1)}) custom-call(s32[5]{0:T(128)S(1)} %concatenate.6.s_ref.at_ref, bf16[544,768]{1,0:T(8,128)(2,1)S(1)} %get-tuple-element.76.theirs_ref, bf16[544,768]{1,0:T(8,128)(2,1)S(1)} %get-tuple-element.77.ours_ref, bf16[512,1536]{1,0:T(8,128)(2,1)S(1)} %bitcast.16, ...), custom_call_target="tpu_custom_call" | custom-call | flops 2415919104 | bytes 11534336 | tf_op jit(solution)/shard_map/backward/pallas_call | solution.py:579
  77.7 2.5 %collective-permute-start.18 = (f32[3,768]{1,0:T(4,128)S(1)}, f32[3,768]{1,0:T(4,128)S(1)}, u32[]{:S(2)}, u32[]{:S(2)}) collective-permute-start(f32[3,768]{1,0:T(4,128)S(1)} %get-tuple-element.79), channel_id=1, source_target_pairs={{0,16},{16,0},{1,17},{17,1},{2,18},{18,2},{3,19},{19,3},{4,20},{20... | collective-permute-start | bytes 27656 | tf_op jit(solution)/shard_map/ppermute | solution.py:773
  81.1 3.8 %collective-permute-start.15 = (bf16[96,768]{1,0:T(8,128)(2,1)S(1)}, bf16[96,768]{1,0:T(8,128)(2,1)S(1)}, u32[]{:S(2)}, u32[]{:S(2)}) collective-permute-start(bf16[96,768]{1,0:T(8,128)(2,1)S(1)} %get-tuple-element.73), channel_id=1, source_target_pairs={{0,2},{1,3},{2,0},{3,1},{4,6},{5,7},{6,4},{7,5},{8,10},{9,11},{10,... | collective-permute-start | bytes 442376 | tf_op jit(solution)/shard_map/ppermute | solution.py:67
  84.9 2.7 %collective-permute-start.17 = (bf16[96,768]{1,0:T(8,128)(2,1)S(1)}, bf16[96,768]{1,0:T(8,128)(2,1)S(1)}, u32[]{:S(2)}, u32[]{:S(2)}) collective-permute-start(bf16[96,768]{1,0:T(8,128)(2,1)S(1)} %get-tuple-element.75), channel_id=1, source_target_pairs={{0,3},{1,0},{2,1},{3,2},{4,7},{5,4},{6,5},{7,6},{8,11},{9,8},{10,9... | collective-permute-start | bytes 442376 | tf_op jit(solution)/shard_map/ppermute | solution.py:67
  87.6 2.5 %collective-permute-done.16 = bf16[96,768]{1,0:T(8,128)(2,1)S(1)} collective-permute-done((bf16[96,768]{1,0:T(8,128)(2,1)S(1)}, bf16[96,768]{1,0:T(8,128)(2,1)S(1)}, u32[]{:S(2)}, u32[]{:S(2)}) %collective-permute-start.16) | collective-permute-done | bytes 147488 | tf_op jit(solution)/shard_map/ppermute | solution.py:67
  93.3 4.6 %collective-permute-done.20 = bf16[112,768]{1,0:T(8,128)(2,1)S(1)} collective-permute-done((bf16[112,768]{1,0:T(8,128)(2,1)S(1)}, bf16[112,768]{1,0:T(8,128)(2,1)S(1)}, u32[]{:S(2)}, u32[]{:S(2)}) %collective-permute-start.20) | collective-permute-done | bytes 172064 | tf_op jit(solution)/shard_map/ppermute | solution.py:67
  98.6 2.7 %collective-permute-start.24 = (bf16[112,768]{1,0:T(8,128)(2,1)S(1)}, bf16[112,768]{1,0:T(8,128)(2,1)S(1)}, u32[]{:S(2)}, u32[]{:S(2)}) collective-permute-start(bf16[112,768]{1,0:T(8,128)(2,1)S(1)} %multiply_convert_fusion.refs_0_), channel_id=1, source_target_pairs={{0,3},{1,0},{2,1},{3,2},{4,7},{5,4},{6,5},{7,6},{8,11},{9,8},{10,9... | collective-permute-start | bytes 516104 | tf_op jit(solution)/shard_map/ppermute | solution.py:67
  102.0 3.5 %collective-permute-done.24.refs_3_ = bf16[112,768]{1,0:T(8,128)(2,1)S(1)} collective-permute-done((bf16[112,768]{1,0:T(8,128)(2,1)S(1)}, bf16[112,768]{1,0:T(8,128)(2,1)S(1)}, u32[]{:S(2)}, u32[]{:S(2)}) %collective-permute-start.24) | collective-permute-done | bytes 172064 | tf_op jit(solution)/shard_map/ppermute | solution.py:67
  107.2 1.7 %collective-permute-done.22.refs_1_ = bf16[112,768]{1,0:T(8,128)(2,1)S(1)} collective-permute-done((bf16[112,768]{1,0:T(8,128)(2,1)S(1)}, bf16[112,768]{1,0:T(8,128)(2,1)S(1)}, u32[]{:S(2)}, u32[]{:S(2)}) %collective-permute-start.22) | collective-permute-done | bytes 172064 | tf_op jit(solution)/shard_map/ppermute | solution.py:67
  112.6 2.6 %collective-permute-start.28 = (bf16[784,384]{1,0:T(8,128)(2,1)S(1)}, bf16[784,384]{1,0:T(8,128)(2,1)S(1)}, u32[]{:S(2)}, u32[]{:S(2)}) collective-permute-start(bf16[784,384]{1,0:T(8,128)(2,1)S(1)} %join_rows.1.refs_0_), channel_id=1, source_target_pairs={{0,16},{16,0},{1,17},{17,1},{2,18},{18,2},{3,19},{19,3},{4,20},{20... | collective-permute-start | bytes 1806344 | tf_op jit(solution)/shard_map/ppermute | solution.py:784
  115.2 3.8 %collective-permute-done.27.refs_3_ = bf16[784,384]{1,0:T(8,128)(2,1)S(1)} collective-permute-done((bf16[784,384]{1,0:T(8,128)(2,1)S(1)}, bf16[784,384]{1,0:T(8,128)(2,1)S(1)}, u32[]{:S(2)}, u32[]{:S(2)}) %collective-permute-start.27) | collective-permute-done | bytes 602144 | tf_op jit(solution)/shard_map/ppermute | solution.py:67
  119.0 3.5 %collective-permute-start.31 = (bf16[784,384]{1,0:T(8,128)(2,1)S(1)}, bf16[784,384]{1,0:T(8,128)(2,1)S(1)}, u32[]{:S(2)}, u32[]{:S(2)}) collective-permute-start(bf16[784,384]{1,0:T(8,128)(2,1)S(1)} %collective-permute-done.27.refs_3_), channel_id=1, source_target_pairs={{0,16},{16,0},{1,17},{17,1},{2,18},{18,2},{3,19},{19,3},{4,20},{20... | collective-permute-start | bytes 1806344 | tf_op jit(solution)/shard_map/ppermute | solution.py:784
  122.5 2.5 %collective-permute-start.30 = (bf16[784,384]{1,0:T(8,128)(2,1)S(1)}, bf16[784,384]{1,0:T(8,128)(2,1)S(1)}, u32[]{:S(2)}, u32[]{:S(2)}) collective-permute-start(bf16[784,384]{1,0:T(8,128)(2,1)S(1)} %collective-permute-done.26.refs_2_), channel_id=1, source_target_pairs={{0,16},{16,0},{1,17},{17,1},{2,18},{18,2},{3,19},{19,3},{4,20},{20... | collective-permute-start | bytes 1806344 | tf_op jit(solution)/shard_map/ppermute | solution.py:784
  125.0 3.3 %collective-permute-done.25.refs_1_ = bf16[784,384]{1,0:T(8,128)(2,1)S(1)} collective-permute-done((bf16[784,384]{1,0:T(8,128)(2,1)S(1)}, bf16[784,384]{1,0:T(8,128)(2,1)S(1)}, u32[]{:S(2)}, u32[]{:S(2)}) %collective-permute-start.25) | collective-permute-done | bytes 602144 | tf_op jit(solution)/shard_map/ppermute | solution.py:67
  128.3 3.1 %collective-permute-start.29 = (bf16[784,384]{1,0:T(8,128)(2,1)S(1)}, bf16[784,384]{1,0:T(8,128)(2,1)S(1)}, u32[]{:S(2)}, u32[]{:S(2)}) collective-permute-start(bf16[784,384]{1,0:T(8,128)(2,1)S(1)} %collective-permute-done.25.refs_1_), channel_id=1, source_target_pairs={{0,16},{16,0},{1,17},{17,1},{2,18},{18,2},{3,19},{19,3},{4,20},{20... | collective-permute-start | bytes 1806344 | tf_op jit(solution)/shard_map/ppermute | solution.py:784
  133.0 3.6 %lay_out.1 = (bf16[1536,1536]{1,0:T(8,128)(2,1)}, f32[3,1536]{1,0:T(4,128)}) custom-call(s32[5]{0:T(128)S(1)} %concatenate.6.s_ref.at_ref, bf16[784,384]{1,0:T(8,128)(2,1)S(1)} %join_rows.1.refs_0_, bf16[784,384]{1,0:T(8,128)(2,1)S(1)} %collective-permute-done.25.refs_1_, bf16[784,384]{1,0:T(8,128)(2,1)S(1)} %collective-permute-done.26.refs_2_, ...), custom_call_target="tpu_custom_call" | custom-call | tf_op jit(solution)/shard_map/lay_out/pallas_call | solution.py:712
  (63 shorter events, 28.9 us)
Async XLA Ops:
  4.6 7.6 %collective-permute-start = (bf16[320,256]{1,0:T(8,128)(2,1)S(1)}, bf16[320,256]{1,0:T(8,128)(2,1)S(1)}, u32[]{:S(2)}, u32[]{:S(2)}) collective-permute-start(bf16[320,256]{1,0:T(8,128)(2,1)S(1)} %get-tuple-element.44), channel_id=1, source_target_pairs={{0,1},{1,2},{2,3},{3,0},{4,5},{5,6},{6,7},{7,4},{8,9},{9,10},{10,1... | collective-permute-start | bytes 491528 | tf_op jit(solution)/shard_map/ppermute | solution.py:67
  7.1 8.1 %collective-permute-start.1 = (bf16[320,256]{1,0:T(8,128)(2,1)S(1)}, bf16[320,256]{1,0:T(8,128)(2,1)S(1)}, u32[]{:S(2)}, u32[]{:S(2)}) collective-permute-start(bf16[320,256]{1,0:T(8,128)(2,1)S(1)} %get-tuple-element.45), channel_id=1, source_target_pairs={{0,2},{1,3},{2,0},{3,1},{4,6},{5,7},{6,4},{7,5},{8,10},{9,11},{10,... | collective-permute-start | bytes 491528 | tf_op jit(solution)/shard_map/ppermute | solution.py:67
  10.4 4.8 %collective-permute-start.2 = (bf16[320,256]{1,0:T(8,128)(2,1)S(1)}, bf16[320,256]{1,0:T(8,128)(2,1)S(1)}, u32[]{:S(2)}, u32[]{:S(2)}) collective-permute-start(bf16[320,256]{1,0:T(8,128)(2,1)S(1)} %get-tuple-element.46), channel_id=1, source_target_pairs={{0,3},{1,0},{2,1},{3,2},{4,7},{5,4},{6,5},{7,6},{8,11},{9,8},{10,9... | collective-permute-start | bytes 491528 | tf_op jit(solution)/shard_map/ppermute | solution.py:67
  15.3 10.8 %collective-permute-start.3 = (bf16[1040,256]{1,0:T(8,128)(2,1)S(1)}, bf16[1040,256]{1,0:T(8,128)(2,1)S(1)}, u32[]{:S(2)}, u32[]{:S(2)}) collective-permute-start(bf16[1040,256]{1,0:T(8,128)(2,1)S(1)} %stack_rows.1.refs_4_), channel_id=1, source_target_pairs={{0,4},{1,5},{2,6},{3,7},{4,8},{5,9},{6,10},{7,11},{8,12},{9,13},{1... | collective-permute-start | bytes 1597448 | tf_op jit(solution)/shard_map/ppermute | solution.py:751
  16.3 13.6 %collective-permute-start.4 = (bf16[1040,256]{1,0:T(8,128)(2,1)S(1)}, bf16[1040,256]{1,0:T(8,128)(2,1)S(1)}, u32[]{:S(2)}, u32[]{:S(2)}) collective-permute-start(bf16[1040,256]{1,0:T(8,128)(2,1)S(1)} %stack_rows.1.refs_4_), channel_id=1, source_target_pairs={{0,12},{1,13},{2,14},{3,15},{4,0},{5,1},{6,2},{7,3},{8,4},{9,5},{1... | collective-permute-start | bytes 1597448 | tf_op jit(solution)/shard_map/ppermute | solution.py:751
  18.0 14.2 %collective-permute-start.5 = (bf16[1040,256]{1,0:T(8,128)(2,1)S(1)}, bf16[1040,256]{1,0:T(8,128)(2,1)S(1)}, u32[]{:S(2)}, u32[]{:S(2)}) collective-permute-start(bf16[1040,256]{1,0:T(8,128)(2,1)S(1)} %stack_rows.1.refs_4_), channel_id=1, source_target_pairs={{0,8},{1,9},{2,10},{3,11},{4,12},{5,13},{6,14},{7,15},{8,0},{9,1},... | collective-permute-start | bytes 1597448 | tf_op jit(solution)/shard_map/ppermute | solution.py:751
  19.4 12.8 %collective-permute-start.6 = (bf16[16,1536]{1,0:T(8,128)(2,1)S(1)}, bf16[16,1536]{1,0:T(8,128)(2,1)S(1)}, u32[]{:S(2)}, u32[]{:S(2)}) collective-permute-start(bf16[16,1536]{1,0:T(8,128)(2,1)S(1)} %get-tuple-element.51.refs_4_), channel_id=1, source_target_pairs={{0,1},{1,2},{2,3},{3,4},{4,5},{5,6},{6,7},{7,8},{8,9},{9,10},{10,1... | collective-permute-start | bytes 147464 | tf_op jit(solution)/shard_map/ppermute | solution.py:746
  21.7 10.5 %collective-permute-start.7 = (bf16[16,1536]{1,0:T(8,128)(2,1)S(1)}, bf16[16,1536]{1,0:T(8,128)(2,1)S(1)}, u32[]{:S(2)}, u32[]{:S(2)}) collective-permute-start(bf16[16,1536]{1,0:T(8,128)(2,1)S(1)} %get-tuple-element.58), channel_id=1, source_target_pairs={{1,0},{2,1},{3,2},{4,3},{5,4},{6,5},{7,6},{8,7},{9,8},{10,9},{11,1... | collective-permute-start | bytes 147464 | tf_op jit(solution)/shard_map/ppermute | solution.py:747
  35.5 10.4 %collective-permute-start.8 = (bf16[400,128]{1,0:T(8,128)(2,1)S(1)}, bf16[400,128]{1,0:T(8,128)(2,1)S(1)}, u32[]{:S(2)}, u32[]{:S(2)}) collective-permute-start(bf16[400,128]{1,0:T(8,128)(2,1)S(1)} %get-tuple-element.60), channel_id=1, source_target_pairs={{0,3},{1,0},{2,1},{3,2},{4,7},{5,4},{6,5},{7,6},{8,11},{9,8},{10,9... | collective-permute-start | bytes 307208 | tf_op jit(solution)/shard_map/ppermute | solution.py:67
  39.8 6.1 %collective-permute-start.9 = (bf16[400,128]{1,0:T(8,128)(2,1)S(1)}, bf16[400,128]{1,0:T(8,128)(2,1)S(1)}, u32[]{:S(2)}, u32[]{:S(2)}) collective-permute-start(bf16[400,128]{1,0:T(8,128)(2,1)S(1)} %get-tuple-element.61), channel_id=1, source_target_pairs={{0,2},{1,3},{2,0},{3,1},{4,6},{5,7},{6,4},{7,5},{8,10},{9,11},{10,... | collective-permute-start | bytes 307208 | tf_op jit(solution)/shard_map/ppermute | solution.py:67
  40.8 5.4 %collective-permute-start.10 = (bf16[400,128]{1,0:T(8,128)(2,1)S(1)}, bf16[400,128]{1,0:T(8,128)(2,1)S(1)}, u32[]{:S(2)}, u32[]{:S(2)}) collective-permute-start(bf16[400,128]{1,0:T(8,128)(2,1)S(1)} %get-tuple-element.62), channel_id=1, source_target_pairs={{0,1},{1,2},{2,3},{3,0},{4,5},{5,6},{6,7},{7,4},{8,9},{9,10},{10,1... | collective-permute-start | bytes 307208 | tf_op jit(solution)/shard_map/ppermute | solution.py:67
  51.8 6.7 %collective-permute-start.11 = (bf16[4,384,768]{2,1,0:T(8,128)(2,1)S(1)}, bf16[4,384,768]{2,1,0:T(8,128)(2,1)S(1)}, u32[]{:S(2)}, u32[]{:S(2)}) collective-permute-start(bf16[4,384,768]{2,1,0:T(8,128)(2,1)S(1)} %get-tuple-element.67), channel_id=1, source_target_pairs={{0,16},{16,0},{1,17},{17,1},{2,18},{18,2},{3,19},{19,3},{4,20},{20... | collective-permute-start | bytes 7077896 | tf_op jit(solution)/shard_map/ppermute | solution.py:764
  59.8 20.4 %collective-permute-start.12 = (bf16[384,768]{1,0:T(8,128)(2,1)S(1)}, bf16[384,768]{1,0:T(8,128)(2,1)S(1)}, u32[]{:S(2)}, u32[]{:S(2)}) collective-permute-start(bf16[384,768]{1,0:T(8,128)(2,1)S(1)} %get-tuple-element.69), channel_id=1, source_target_pairs={{0,32},{1,33},{2,34},{3,35},{4,36},{5,37},{6,38},{7,39},{8,40},{9,... | collective-permute-start | bytes 1769480 | tf_op jit(solution)/shard_map/ppermute | solution.py:67
  60.8 19.4 %collective-permute-start.13 = (bf16[384,768]{1,0:T(8,128)(2,1)S(1)}, bf16[384,768]{1,0:T(8,128)(2,1)S(1)}, u32[]{:S(2)}, u32[]{:S(2)}) collective-permute-start(bf16[384,768]{1,0:T(8,128)(2,1)S(1)} %get-tuple-element.70), channel_id=1, source_target_pairs={{0,64},{1,65},{2,66},{3,67},{4,68},{5,69},{6,70},{7,71},{8,72},{9,... | collective-permute-start | bytes 1769480 | tf_op jit(solution)/shard_map/ppermute | solution.py:67
  64.0 16.2 %collective-permute-start.14 = (bf16[384,768]{1,0:T(8,128)(2,1)S(1)}, bf16[384,768]{1,0:T(8,128)(2,1)S(1)}, u32[]{:S(2)}, u32[]{:S(2)}) collective-permute-start(bf16[384,768]{1,0:T(8,128)(2,1)S(1)} %get-tuple-element.71), channel_id=1, source_target_pairs={{0,96},{1,97},{2,98},{3,99},{4,100},{5,101},{6,102},{7,103},{8,104... | collective-permute-start | bytes 1769480 | tf_op jit(solution)/shard_map/ppermute | solution.py:67
  77.7 9.9 %collective-permute-start.18 = (f32[3,768]{1,0:T(4,128)S(1)}, f32[3,768]{1,0:T(4,128)S(1)}, u32[]{:S(2)}, u32[]{:S(2)}) collective-permute-start(f32[3,768]{1,0:T(4,128)S(1)} %get-tuple-element.79), channel_id=1, source_target_pairs={{0,16},{16,0},{1,17},{17,1},{2,18},{18,2},{3,19},{19,3},{4,20},{20... | collective-permute-start | bytes 27656 | tf_op jit(solution)/shard_map/ppermute | solution.py:773
  81.1 6.5 %collective-permute-start.15 = (bf16[96,768]{1,0:T(8,128)(2,1)S(1)}, bf16[96,768]{1,0:T(8,128)(2,1)S(1)}, u32[]{:S(2)}, u32[]{:S(2)}) collective-permute-start(bf16[96,768]{1,0:T(8,128)(2,1)S(1)} %get-tuple-element.73), channel_id=1, source_target_pairs={{0,2},{1,3},{2,0},{3,1},{4,6},{5,7},{6,4},{7,5},{8,10},{9,11},{10,... | collective-permute-start | bytes 442376 | tf_op jit(solution)/shard_map/ppermute | solution.py:67
  84.9 5.2 %collective-permute-start.16 = (bf16[96,768]{1,0:T(8,128)(2,1)S(1)}, bf16[96,768]{1,0:T(8,128)(2,1)S(1)}, u32[]{:S(2)}, u32[]{:S(2)}) collective-permute-start(bf16[96,768]{1,0:T(8,128)(2,1)S(1)} %get-tuple-element.74), channel_id=1, source_target_pairs={{0,1},{1,2},{2,3},{3,0},{4,5},{5,6},{6,7},{7,4},{8,9},{9,10},{10,1... | collective-permute-start | bytes 442376 | tf_op jit(solution)/shard_map/ppermute | solution.py:67
  84.9 5.2 %collective-permute-start.17 = (bf16[96,768]{1,0:T(8,128)(2,1)S(1)}, bf16[96,768]{1,0:T(8,128)(2,1)S(1)}, u32[]{:S(2)}, u32[]{:S(2)}) collective-permute-start(bf16[96,768]{1,0:T(8,128)(2,1)S(1)} %get-tuple-element.75), channel_id=1, source_target_pairs={{0,3},{1,0},{2,1},{3,2},{4,7},{5,4},{6,5},{7,6},{8,11},{9,8},{10,9... | collective-permute-start | bytes 442376 | tf_op jit(solution)/shard_map/ppermute | solution.py:67
  90.2 7.7 %collective-permute-start.20 = (bf16[112,768]{1,0:T(8,128)(2,1)S(1)}, bf16[112,768]{1,0:T(8,128)(2,1)S(1)}, u32[]{:S(2)}, u32[]{:S(2)}) collective-permute-start(bf16[112,768]{1,0:T(8,128)(2,1)S(1)} %fusion.1), channel_id=1, source_target_pairs={{0,4},{1,5},{2,6},{3,7},{4,8},{5,9},{6,10},{7,11},{8,12},{9,13},{1... | collective-permute-start | bytes 516104 | tf_op jit(solution)/shard_map/ppermute | solution.py:67
  90.6 7.3 %collective-permute-start.19 = (bf16[112,768]{1,0:T(8,128)(2,1)S(1)}, bf16[112,768]{1,0:T(8,128)(2,1)S(1)}, u32[]{:S(2)}, u32[]{:S(2)}) collective-permute-start(bf16[112,768]{1,0:T(8,128)(2,1)S(1)} %fusion.1), channel_id=1, source_target_pairs={{0,8},{1,9},{2,10},{3,11},{4,12},{5,13},{6,14},{7,15},{8,0},{9,1},... | collective-permute-start | bytes 516104 | tf_op jit(solution)/shard_map/ppermute | solution.py:67
  92.2 6.3 %collective-permute-start.21 = (bf16[112,768]{1,0:T(8,128)(2,1)S(1)}, bf16[112,768]{1,0:T(8,128)(2,1)S(1)}, u32[]{:S(2)}, u32[]{:S(2)}) collective-permute-start(bf16[112,768]{1,0:T(8,128)(2,1)S(1)} %fusion.1), channel_id=1, source_target_pairs={{0,12},{1,13},{2,14},{3,15},{4,0},{5,1},{6,2},{7,3},{8,4},{9,5},{1... | collective-permute-start | bytes 516104 | tf_op jit(solution)/shard_map/ppermute | solution.py:67
  98.6 6.9 %collective-permute-start.24 = (bf16[112,768]{1,0:T(8,128)(2,1)S(1)}, bf16[112,768]{1,0:T(8,128)(2,1)S(1)}, u32[]{:S(2)}, u32[]{:S(2)}) collective-permute-start(bf16[112,768]{1,0:T(8,128)(2,1)S(1)} %multiply_convert_fusion.refs_0_), channel_id=1, source_target_pairs={{0,3},{1,0},{2,1},{3,2},{4,7},{5,4},{6,5},{7,6},{8,11},{9,8},{10,9... | collective-permute-start | bytes 516104 | tf_op jit(solution)/shard_map/ppermute | solution.py:67
  101.4 5.9 %collective-permute-start.23 = (bf16[112,768]{1,0:T(8,128)(2,1)S(1)}, bf16[112,768]{1,0:T(8,128)(2,1)S(1)}, u32[]{:S(2)}, u32[]{:S(2)}) collective-permute-start(bf16[112,768]{1,0:T(8,128)(2,1)S(1)} %multiply_convert_fusion.refs_0_), channel_id=1, source_target_pairs={{0,2},{1,3},{2,0},{3,1},{4,6},{5,7},{6,4},{7,5},{8,10},{9,11},{10,... | collective-permute-start | bytes 516104 | tf_op jit(solution)/shard_map/ppermute | solution.py:67
  101.4 7.6 %collective-permute-start.22 = (bf16[112,768]{1,0:T(8,128)(2,1)S(1)}, bf16[112,768]{1,0:T(8,128)(2,1)S(1)}, u32[]{:S(2)}, u32[]{:S(2)}) collective-permute-start(bf16[112,768]{1,0:T(8,128)(2,1)S(1)} %multiply_convert_fusion.refs_0_), channel_id=1, source_target_pairs={{0,1},{1,2},{2,3},{3,0},{4,5},{5,6},{6,7},{7,4},{8,9},{9,10},{10,1... | collective-permute-start | bytes 516104 | tf_op jit(solution)/shard_map/ppermute | solution.py:67
  109.8 9.2 %collective-permute-start.27 = (bf16[784,384]{1,0:T(8,128)(2,1)S(1)}, bf16[784,384]{1,0:T(8,128)(2,1)S(1)}, u32[]{:S(2)}, u32[]{:S(2)}) collective-permute-start(bf16[784,384]{1,0:T(8,128)(2,1)S(1)} %join_rows.1.refs_0_), channel_id=1, source_target_pairs={{0,96},{1,97},{2,98},{3,99},{4,100},{5,101},{6,102},{7,103},{8,104... | collective-permute-start | bytes 1806344 | tf_op jit(solution)/shard_map/ppermute | solution.py:67
  111.2 11.3 %collective-permute-start.26 = (bf16[784,384]{1,0:T(8,128)(2,1)S(1)}, bf16[784,384]{1,0:T(8,128)(2,1)S(1)}, u32[]{:S(2)}, u32[]{:S(2)}) collective-permute-start(bf16[784,384]{1,0:T(8,128)(2,1)S(1)} %join_rows.1.refs_0_), channel_id=1, source_target_pairs={{0,64},{1,65},{2,66},{3,67},{4,68},{5,69},{6,70},{7,71},{8,72},{9,... | collective-permute-start | bytes 1806344 | tf_op jit(solution)/shard_map/ppermute | solution.py:67
  112.4 16.0 %collective-permute-start.25 = (bf16[784,384]{1,0:T(8,128)(2,1)S(1)}, bf16[784,384]{1,0:T(8,128)(2,1)S(1)}, u32[]{:S(2)}, u32[]{:S(2)}) collective-permute-start(bf16[784,384]{1,0:T(8,128)(2,1)S(1)} %join_rows.1.refs_0_), channel_id=1, source_target_pairs={{0,32},{1,33},{2,34},{3,35},{4,36},{5,37},{6,38},{7,39},{8,40},{9,... | collective-permute-start | bytes 1806344 | tf_op jit(solution)/shard_map/ppermute | solution.py:67
  112.6 18.8 %collective-permute-start.28 = (bf16[784,384]{1,0:T(8,128)(2,1)S(1)}, bf16[784,384]{1,0:T(8,128)(2,1)S(1)}, u32[]{:S(2)}, u32[]{:S(2)}) collective-permute-start(bf16[784,384]{1,0:T(8,128)(2,1)S(1)} %join_rows.1.refs_0_), channel_id=1, source_target_pairs={{0,16},{16,0},{1,17},{17,1},{2,18},{18,2},{3,19},{19,3},{4,20},{20... | collective-permute-start | bytes 1806344 | tf_op jit(solution)/shard_map/ppermute | solution.py:784
  119.0 12.4 %collective-permute-start.31 = (bf16[784,384]{1,0:T(8,128)(2,1)S(1)}, bf16[784,384]{1,0:T(8,128)(2,1)S(1)}, u32[]{:S(2)}, u32[]{:S(2)}) collective-permute-start(bf16[784,384]{1,0:T(8,128)(2,1)S(1)} %collective-permute-done.27.refs_3_), channel_id=1, source_target_pairs={{0,16},{16,0},{1,17},{17,1},{2,18},{18,2},{3,19},{19,3},{4,20},{20... | collective-permute-start | bytes 1806344 | tf_op jit(solution)/shard_map/ppermute | solution.py:784
  122.5 8.9 %collective-permute-start.30 = (bf16[784,384]{1,0:T(8,128)(2,1)S(1)}, bf16[784,384]{1,0:T(8,128)(2,1)S(1)}, u32[]{:S(2)}, u32[]{:S(2)}) collective-permute-start(bf16[784,384]{1,0:T(8,128)(2,1)S(1)} %collective-permute-done.26.refs_2_), channel_id=1, source_target_pairs={{0,16},{16,0},{1,17},{17,1},{2,18},{18,2},{3,19},{19,3},{4,20},{20... | collective-permute-start | bytes 1806344 | tf_op jit(solution)/shard_map/ppermute | solution.py:784
  128.3 4.7 %collective-permute-start.29 = (bf16[784,384]{1,0:T(8,128)(2,1)S(1)}, bf16[784,384]{1,0:T(8,128)(2,1)S(1)}, u32[]{:S(2)}, u32[]{:S(2)}) collective-permute-start(bf16[784,384]{1,0:T(8,128)(2,1)S(1)} %collective-permute-done.25.refs_1_), channel_id=1, source_target_pairs={{0,16},{16,0},{1,17},{17,1},{2,18},{18,2},{3,19},{19,3},{4,20},{20... | collective-permute-start | bytes 1806344 | tf_op jit(solution)/shard_map/ppermute | solution.py:784
  (4 other events, 14.6 us)

commit v11 on v10

--- a/solution.py
+++ b/solution.py
@@ -504,7 +504,7 @@
     steps = half // WIDE
 
     def kernel(s_ref, theirs_ref, ours_ref, g_ref, low_ref, high_ref, pw_ref, dw_ref, behind_ref, *refs):
-        gs_ref, gd_theirs, gd_ours, grad, upper, ends, up_ref = refs
+        grad_ref, gd_theirs, gd_ours, upper, ends, up_ref = refs
         j = pl.program_id(0)
 
         @pl.when(j < steps)
@@ -536,13 +536,16 @@
             )
             return taps, (coming * rate).astype(BF).astype(F32)
 
-        _, grad[8:16, :] = grad_of(up_ref[:32, :].astype(F32), 8, 8, outer[:8])
-        _, grad[16 + fine : 24 + fine, :] = grad_of(up_ref[fine:, :].astype(F32), 16, 8, outer[8:])
+        blank = jnp.zeros((8, WIDE), F32)
+        _, edge = grad_of(up_ref[:32, :].astype(F32), 8, 8, outer[:8])
+        grad_ref[:TAIL, :] = jnp.concatenate([blank, edge], axis=0).astype(BF)
+        _, edge = grad_of(up_ref[fine:, :].astype(F32), 16, 8, outer[8:])
+        grad_ref[TAIL + fine :, :] = jnp.concatenate([edge, blank], axis=0).astype(BF)
         sums = [jnp.zeros((8, WIDE), F32)] * 3
         for k in range(0, fine, STRIP):
             near = up_ref[k : k + STRIP + 2 * TAIL, :].astype(F32)
             taps, mid = grad_of(near, TAIL, STRIP, upper[k : k + STRIP, :])
-            grad[16 + k : 16 + k + STRIP, :] = mid
+            grad_ref[TAIL + k : TAIL + k + STRIP, :] = mid.astype(BF)
             for t in range(3):
                 term = taps[t] * mid
                 for r in range(0, STRIP, 8):
@@ -555,12 +558,6 @@
                 for t in range(3):
                     ref[t : t + 1, :] = depth[t]
 
-        for k in range(0, fine, STRIP):
-            near = grad[8 + k : 24 + k + STRIP, :]
-            gs_ref[k : k + STRIP, :] = (
-                w[0] * near[9 : 9 + STRIP] + w[1] * near[8 : 8 + STRIP] + w[2] * near[7 : 7 + STRIP]
-            ).astype(BF)
-
     def block(j, s_ref):
         return jnp.where(j < steps, (1 - s_ref[1]) * steps + j, s_ref[1] * steps + j - steps)
 
@@ -579,7 +576,7 @@
     return pl.pallas_call(
         kernel,
         out_shape=[
-            jax.ShapeDtypeStruct((fine, columns), BF),
+            jax.ShapeDtypeStruct((fine + 2 * TAIL, columns), BF),
             jax.ShapeDtypeStruct((3, half), F32),
             jax.ShapeDtypeStruct((3, half), F32),
         ],
@@ -596,9 +593,8 @@
                 cols(3),
                 ANY,
             ],
-            out_specs=[cols(fine), early(3), late(3)],
+            out_specs=[cols(fine + 2 * TAIL), early(3), late(3)],
             scratch_shapes=[
-                pltpu.VMEM((fine + 2 * TAIL, WIDE), F32),
                 pltpu.VMEM((fine, WIDE), F32),
                 pltpu.VMEM((TAIL, columns), BF),
                 pltpu.VMEM((fine + 2 * TAIL, WIDE), BF),
@@ -612,6 +608,34 @@
     )(scalars, theirs, ours, upstream, before, after, point_weight, depth_weight, behind)
 
 
+def spread_back(grad_pre, depth_weight):
+    fine, columns = grad_pre.shape[0] - 2 * TAIL, grad_pre.shape[1]
+
+    def kernel(grad_ref, dw_ref, gs_ref, mark_ref):
+        mark_ref[...] = jnp.zeros((8, 128), F32)
+        w = [dw_ref[t : t + 1, :] for t in range(3)]
+        for k in range(0, fine, STRIP):
+            near = grad_ref[k : k + STRIP + 2 * TAIL, :].astype(F32)
+            gs_ref[k : k + STRIP, :] = (
+                w[0] * near[TAIL + 1 : TAIL + 1 + STRIP]
+                + w[1] * near[TAIL : TAIL + STRIP]
+                + w[2] * near[TAIL - 1 : TAIL - 1 + STRIP]
+            ).astype(BF)
+
+    def cols(count):
+        return pl.BlockSpec((count, WIDE), lambda j: (0, j))
+
+    return pl.pallas_call(
+        kernel,
+        grid=(columns // WIDE,),
+        out_shape=[jax.ShapeDtypeStruct((fine, columns), BF), jax.ShapeDtypeStruct((8, 128), F32)],
+        in_specs=[cols(fine + 2 * TAIL), cols(3)],
+        out_specs=[cols(fine), pl.BlockSpec((8, 128), lambda j: (0, 0))],
+        compiler_params=params(16),
+        name="spread_back",
+    )(grad_pre, depth_weight)
+
+
 def product(scalars, act, turned, steps, arrived):
     half, quarter = act.shape[1], turned.shape[0] // 4
 
@@ -654,12 +678,12 @@
     )(at, *got)
 
 
-def join_rows(at, got):
+def join_rows(at, got, behind):
     slim, columns = got[0].shape[0] - TAIL, got[0].shape[1]
     quarter = 4 * slim
 
     def kernel(at_ref, *refs):
-        ins, out, held = refs[:4], refs[4], refs[5]
+        ins, out, held = refs[:4], refs[5], refs[6]
         for d in range(4):
             put = pl.ds(pl.multiple_of((Spot(at_ref).second_at + 4 - d) % 4 * slim, 16), slim)
             held[put, :] = ins[d][:slim, :]
@@ -670,12 +694,12 @@
     return pl.pallas_call(
         kernel,
         out_shape=jax.ShapeDtypeStruct((columns + TAIL, quarter), BF),
-        in_specs=[SMEM] + [VMEM] * 4,
+        in_specs=[SMEM] + [VMEM] * 4 + [ANY],
         out_specs=VMEM,
         scratch_shapes=[pltpu.VMEM((quarter, columns), BF)],
         compiler_params=params(10),
         name="join_rows",
-    )(at, *got)
+    )(at, *got, behind)
 
 
 def lay_out(scalars, own, other):
@@ -767,7 +791,7 @@
     piece_3, piece_0 = product(scalars, act, turned, (3, 0), arrived)
     got = exchange([piece_0, piece_1, piece_2, piece_3], SUM_RINGS[0])
 
-    grad_skip, d_theirs, d_mine = backward(
+    grad_pre, d_theirs, d_mine = backward(
         scalars, up_theirs, up_ours, upstream, before, after, point_weight, depth_weight, piece_0
     )
     d_sum = d_mine + lax.ppermute(d_theirs, "c", swap)
@@ -778,7 +802,8 @@
     got = exchange([mixed] * 4, SUM_RINGS[2])
     norm_scale = 1.0 / math.sqrt(128 * fine)
     summed = (total_of(got) * norm_scale).astype(BF)
-    joined = join_rows(scalars, exchange([summed] * 4, SUM_RINGS[1]))
+    grad_skip, mark = spread_back(grad_pre, depth_weight)
+    joined = join_rows(scalars, exchange([summed] * 4, SUM_RINGS[1]), mark)
 
     own = exchange([joined] * 4, SUM_RINGS[0])
     other = [lax.ppermute(block, "c", swap) for block in own]

time: 137 us -> 137 us (level)
  waiting for transfers between devices: 28.4 us -> 25.3 us
  starting transfers between devices: 56 us -> 58.5 us
    ppermute x21, waiting for transfers between devices: 25 us -> 21.9 us  [exchange(): got[d] = lax.ppermute(pieces[d], AXES, turn(axes, sign * d))]
    ppermute x4, starting transfers between devices: 11.8 us -> 13.2 us  [local(): other = [lax.ppermute(block, 'c', swap) for block in own]]
    pallas_call x1 -> x2, Pallas kernels: 12.9 us -> 13.8 us  [the longest x1 10.8 us: backward(): pl.pallas_call(kernel, out_shape=[jax.ShapeDtypeStruct((fine + 2 * TAIL,...]
  transfers between devices with their start and end apart: 32 -> 32, of which waited for: 13 -> 14; matrix products, arithmetic and copies ran while one was open for 1% -> 1% of each run, Pallas kernels for 21% -> 22%
where the time goes in v11:
time: 137 us
  starting transfers between devices  58.5 us (43%)
  Pallas kernels  48.1 us (35%)
  waiting for transfers between devices  25.3 us (18%)
  local copies, waits for them, and re-layouts  3.21 us (2%)
  between operations  1.73 us (1%)
    ppermute x21, starting transfers between devices, exchange(): got[d] = lax.ppermute(pieces[d], AXES, turn(axes, sign * d))  32.4 us
    ppermute x21, waiting for transfers between devices, exchange(): got[d] = lax.ppermute(pieces[d], AXES, turn(axes, sign * d))  21.9 us
    ppermute x4, starting transfers between devices, local(): other = [lax.ppermute(block, 'c', swap) for block in own]  13.2 us
    pallas_call x1, Pallas kernels, backward(): pl.pallas_call(kernel, out_shape=[jax.ShapeDtypeStruct((fine + 2 * TAIL,...  10.8 us
    pallas_call x4, Pallas kernels, attend(): pl.pallas_call(kernel, out_shape=outs, in_specs=[SMEM] + [VMEM] * len(ins...  9.97 us
    pallas_call x2, Pallas kernels, forward(): pl.pallas_call(kernel, out_shape=outs, grid_spec=pltpu.PrefetchScalarGrid...  9.51 us
    ppermute x3, starting transfers between devices, local(): far = {d: lax.ppermute(own, AXES, turn(ROW_RING, d)) for d in (1, 3, 2)}  4.13 us
    pallas_call x1, Pallas kernels, project(): pl.pallas_call(kernel, out_shape=[jax.ShapeDtypeStruct((rows + rows // 4,...  3.92 us
  transfers between devices with their start and end apart: 32, of which 14 were waited for; matrix products, arithmetic and copies ran while one was open for 1% of the time, Pallas kernels for 22%

profile of v11, /device:TPU:1, one launch (start us, length us, event | category | flops | bytes accessed | tf_op | source)
XLA Modules:
  0.0 137.0 jit_solution(1584573400441874438)
XLA Ops:
  0.6 3.9 %project.1 = (bf16[320,256]{1,0:T(8,128)(2,1)S(1)}, bf16[320,256]{1,0:T(8,128)(2,1)S(1)}, bf16[320,256]{1,0:T(8,128)(2,1)S(1)}, bf16[320,256]{1,0:T(8,128)(2,1)S(1)}) custom-call(bf16[256,1536]{1,0:T(8,128)(2,1)} %bitcast.11, bf16[1536,256]{1,0:T(8,128)(2,1)} %wq_hbm.1, bf16[1536,256]{1,0:T(8,128)(2,1)} %wk_hbm.1, bf16[1536,768]{1,0:T(8,128)(2,1)} %wv_hbm.1), custom_call_target="tpu_custom_call" | custom-call | tf_op jit(solution)/shard_map/project/pallas_call | solution.py:112
  4.6 2.5 %collective-permute-start = (bf16[320,256]{1,0:T(8,128)(2,1)S(1)}, bf16[320,256]{1,0:T(8,128)(2,1)S(1)}, u32[]{:S(2)}, u32[]{:S(2)}) collective-permute-start(bf16[320,256]{1,0:T(8,128)(2,1)S(1)} %get-tuple-element.46), channel_id=1, source_target_pairs={{0,1},{1,2},{2,3},{3,0},{4,5},{5,6},{6,7},{7,4},{8,9},{9,10},{10,1... | collective-permute-start | bytes 491528 | tf_op jit(solution)/shard_map/ppermute | solution.py:67
  7.1 3.3 %collective-permute-start.1 = (bf16[320,256]{1,0:T(8,128)(2,1)S(1)}, bf16[320,256]{1,0:T(8,128)(2,1)S(1)}, u32[]{:S(2)}, u32[]{:S(2)}) collective-permute-start(bf16[320,256]{1,0:T(8,128)(2,1)S(1)} %get-tuple-element.47), channel_id=1, source_target_pairs={{0,2},{1,3},{2,0},{3,1},{4,6},{5,7},{6,4},{7,5},{8,10},{9,11},{10,... | collective-permute-start | bytes 491528 | tf_op jit(solution)/shard_map/ppermute | solution.py:67
  12.2 3.0 %collective-permute-done.1.refs_2_ = bf16[320,256]{1,0:T(8,128)(2,1)S(1)} collective-permute-done((bf16[320,256]{1,0:T(8,128)(2,1)S(1)}, bf16[320,256]{1,0:T(8,128)(2,1)S(1)}, u32[]{:S(2)}, u32[]{:S(2)}) %collective-permute-start.1) | collective-permute-done | bytes 163872 | tf_op jit(solution)/shard_map/ppermute | solution.py:67
  19.4 2.3 %collective-permute-start.6 = (bf16[16,1536]{1,0:T(8,128)(2,1)S(1)}, bf16[16,1536]{1,0:T(8,128)(2,1)S(1)}, u32[]{:S(2)}, u32[]{:S(2)}) collective-permute-start(bf16[16,1536]{1,0:T(8,128)(2,1)S(1)} %get-tuple-element.53.refs_4_), channel_id=1, source_target_pairs={{0,1},{1,2},{2,3},{3,4},{4,5},{5,6},{6,7},{7,8},{8,9},{9,10},{10,1... | collective-permute-start | bytes 147464 | tf_op jit(solution)/shard_map/ppermute | solution.py:770
  23.8 2.2 %attend.4 = (f32[1024,256]{1,0:T(8,128)S(1)}, f32[1024,128]{1,0:T(8,128)S(1)}) custom-call(s32[5]{0:T(128)S(1)} %concatenate.6.s_ref.at_ref, bf16[256,128]{1,0:T(8,128)(2,1)S(1)} %get-tuple-element.49.refs_0_, bf16[256,128]{1,0:T(8,128)(2,1)S(1)} %get-tuple-element.50.refs_1_, bf16[256,128]{1,0:T(8,128)(2,1)S(1)} %get-tuple-element.51.refs_2_, ...), custom_call_target="tpu_custom_call" | custom-call | flops 1073741824 | bytes 4194304 | tf_op jit(solution)/shard_map/attend/pallas_call | solution.py:283
  26.1 2.3 %attend.5 = (f32[1024,256]{1,0:T(8,128)S(1)}, f32[1024,128]{1,0:T(8,128)S(1)}) custom-call(s32[5]{0:T(128)S(1)} %concatenate.6.s_ref.at_ref, bf16[256,128]{1,0:T(8,128)(2,1)S(1)} %get-tuple-element.49.refs_0_, bf16[256,128]{1,0:T(8,128)(2,1)S(1)} %get-tuple-element.50.refs_1_, bf16[256,128]{1,0:T(8,128)(2,1)S(1)} %get-tuple-element.51.refs_2_, ...), custom_call_target="tpu_custom_call" | custom-call | flops 1073741824 | bytes 4194304 | tf_op jit(solution)/shard_map/attend/pallas_call | solution.py:283
  29.9 2.2 %attend.6 = (f32[1024,256]{1,0:T(8,128)S(1)}, f32[1024,128]{1,0:T(8,128)S(1)}) custom-call(s32[5]{0:T(128)S(1)} %concatenate.6.s_ref.at_ref, bf16[256,128]{1,0:T(8,128)(2,1)S(1)} %get-tuple-element.49.refs_0_, bf16[256,128]{1,0:T(8,128)(2,1)S(1)} %get-tuple-element.50.refs_1_, bf16[256,128]{1,0:T(8,128)(2,1)S(1)} %get-tuple-element.51.refs_2_, ...), custom_call_target="tpu_custom_call" | custom-call | flops 1073741824 | bytes 4194304 | tf_op jit(solution)/shard_map/attend/pallas_call | solution.py:283
  32.2 3.3 %attend.7 = (bf16[400,128]{1,0:T(8,128)(2,1)S(1)}, bf16[400,128]{1,0:T(8,128)(2,1)S(1)}, bf16[400,128]{1,0:T(8,128)(2,1)S(1)}, bf16[400,128]{1,0:T(8,128)(2,1)S(1)}) custom-call(s32[5]{0:T(128)S(1)} %concatenate.6.s_ref.at_ref, bf16[256,128]{1,0:T(8,128)(2,1)S(1)} %get-tuple-element.49.refs_0_, bf16[256,128]{1,0:T(8,128)(2,1)S(1)} %get-tuple-element.50.refs_1_, ...), custom_call_target="tpu_custom_call" | custom-call | flops 1073741824 | bytes 4194304 | tf_op jit(solution)/shard_map/attend/pallas_call | solution.py:283
  35.5 4.3 %collective-permute-start.8 = (bf16[400,128]{1,0:T(8,128)(2,1)S(1)}, bf16[400,128]{1,0:T(8,128)(2,1)S(1)}, u32[]{:S(2)}, u32[]{:S(2)}) collective-permute-start(bf16[400,128]{1,0:T(8,128)(2,1)S(1)} %get-tuple-element.62), channel_id=1, source_target_pairs={{0,3},{1,0},{2,1},{3,2},{4,7},{5,4},{6,5},{7,6},{8,11},{9,8},{10,9... | collective-permute-start | bytes 307208 | tf_op jit(solution)/shard_map/ppermute | solution.py:67
  44.0 1.8 %load.1 = (bf16[256,1536]{1,0:T(8,128)(2,1)S(1)}, bf16[512,1536]{1,0:T(8,128)(2,1)S(1)}, bf16[4,192,1536]{2,1,0:T(8,128)(2,1)S(1)}) custom-call(bf16[400,128]{1,0:T(8,128)(2,1)S(1)} %get-tuple-element.61.behind_ref.b0, bf16[256,1536]{1,0:T(8,128)(2,1)S(1)} %bitcast.13, bf16[512,1536]{1,0:T(8,128)(2,1)S(1)} %bitcast.18, bf16[4,192,1536]{2,1,0:T(8,128)(2,1)} %bitcast.19), custom_call_target="tpu_custom_call" | custom-call | tf_op jit(solution)/shard_map/load/pallas_call | solution.py:490
  46.2 5.5 %forward.3 = (bf16[544,768]{1,0:T(8,128)(2,1)S(1)}, bf16[4,384,768]{2,1,0:T(8,128)(2,1)S(1)}) custom-call(s32[5]{0:T(128)S(1)} %concatenate.6.s_ref.at_ref, bf16[400,128]{1,0:T(8,128)(2,1)S(1)} %get-tuple-element.61.behind_ref.b0, bf16[400,128]{1,0:T(8,128)(2,1)S(1)} %collective-permute-done.8.b1, bf16[400,128]{1,0:T(8,128)(2,1)S(1)} %collective-permute-done.9.b2, ...), custom_call_target="tpu_custom_call" | custom-call | flops 2415919104 | bytes 9437184 | tf_op jit(solution)/shard_map/forward/pallas_call | solution.py:459
  51.8 2.5 %collective-permute-start.11 = (bf16[4,384,768]{2,1,0:T(8,128)(2,1)S(1)}, bf16[4,384,768]{2,1,0:T(8,128)(2,1)S(1)}, u32[]{:S(2)}, u32[]{:S(2)}) collective-permute-start(bf16[4,384,768]{2,1,0:T(8,128)(2,1)S(1)} %get-tuple-element.69), channel_id=1, source_target_pairs={{0,16},{16,0},{1,17},{17,1},{2,18},{18,2},{3,19},{19,3},{4,20},{20... | collective-permute-start | bytes 7077896 | tf_op jit(solution)/shard_map/ppermute | solution.py:788
  54.3 4.0 %forward.2 = (bf16[544,768]{1,0:T(8,128)(2,1)S(1)}, bf16[512,768]{1,0:T(8,128)(2,1)S(1)}) custom-call(s32[5]{0:T(128)S(1)} %concatenate.6.s_ref.at_ref, bf16[400,128]{1,0:T(8,128)(2,1)S(1)} %get-tuple-element.61.behind_ref.b0, bf16[400,128]{1,0:T(8,128)(2,1)S(1)} %collective-permute-done.8.b1, bf16[400,128]{1,0:T(8,128)(2,1)S(1)} %collective-permute-done.9.b2, ...), custom_call_target="tpu_custom_call" | custom-call | flops 2415919104 | bytes 9437184 | tf_op jit(solution)/shard_map/forward/pallas_call | solution.py:459
  60.8 1.8 %collective-permute-start.13 = (bf16[384,768]{1,0:T(8,128)(2,1)S(1)}, bf16[384,768]{1,0:T(8,128)(2,1)S(1)}, u32[]{:S(2)}, u32[]{:S(2)}) collective-permute-start(bf16[384,768]{1,0:T(8,128)(2,1)S(1)} %get-tuple-element.72), channel_id=1, source_target_pairs={{0,64},{1,65},{2,66},{3,67},{4,68},{5,69},{6,70},{7,71},{8,72},{9,... | collective-permute-start | bytes 1769480 | tf_op jit(solution)/shard_map/ppermute | solution.py:67
  64.7 10.8 %backward.1 = (bf16[544,1536]{1,0:T(8,128)(2,1)S(1)}, f32[3,768]{1,0:T(4,128)S(1)}, f32[3,768]{1,0:T(4,128)S(1)}) custom-call(s32[5]{0:T(128)S(1)} %concatenate.6.s_ref.at_ref, bf16[544,768]{1,0:T(8,128)(2,1)S(1)} %get-tuple-element.78.theirs_ref, bf16[544,768]{1,0:T(8,128)(2,1)S(1)} %get-tuple-element.79.ours_ref, bf16[512,1536]{1,0:T(8,128)(2,1)S(1)} %bitcast.16, ...), custom_call_target="tpu_custom_call" | custom-call | flops 2415919104 | bytes 11534336 | tf_op jit(solution)/shard_map/backward/pallas_call | solution.py:576
  75.5 2.6 %collective-permute-start.18 = (f32[3,768]{1,0:T(4,128)S(1)}, f32[3,768]{1,0:T(4,128)S(1)}, u32[]{:S(2)}, u32[]{:S(2)}) collective-permute-start(f32[3,768]{1,0:T(4,128)S(1)} %get-tuple-element.81), channel_id=1, source_target_pairs={{0,16},{16,0},{1,17},{17,1},{2,18},{18,2},{3,19},{19,3},{4,20},{20... | collective-permute-start | bytes 27656 | tf_op jit(solution)/shard_map/ppermute | solution.py:797
  79.1 3.8 %collective-permute-start.15 = (bf16[96,768]{1,0:T(8,128)(2,1)S(1)}, bf16[96,768]{1,0:T(8,128)(2,1)S(1)}, u32[]{:S(2)}, u32[]{:S(2)}) collective-permute-start(bf16[96,768]{1,0:T(8,128)(2,1)S(1)} %get-tuple-element.75), channel_id=1, source_target_pairs={{0,2},{1,3},{2,0},{3,1},{4,6},{5,7},{6,4},{7,5},{8,10},{9,11},{10,... | collective-permute-start | bytes 442376 | tf_op jit(solution)/shard_map/ppermute | solution.py:67
  82.9 2.7 %collective-permute-start.17 = (bf16[96,768]{1,0:T(8,128)(2,1)S(1)}, bf16[96,768]{1,0:T(8,128)(2,1)S(1)}, u32[]{:S(2)}, u32[]{:S(2)}) collective-permute-start(bf16[96,768]{1,0:T(8,128)(2,1)S(1)} %get-tuple-element.77), channel_id=1, source_target_pairs={{0,3},{1,0},{2,1},{3,2},{4,7},{5,4},{6,5},{7,6},{8,11},{9,8},{10,9... | collective-permute-start | bytes 442376 | tf_op jit(solution)/shard_map/ppermute | solution.py:67
  85.7 2.4 %collective-permute-done.16 = bf16[96,768]{1,0:T(8,128)(2,1)S(1)} collective-permute-done((bf16[96,768]{1,0:T(8,128)(2,1)S(1)}, bf16[96,768]{1,0:T(8,128)(2,1)S(1)}, u32[]{:S(2)}, u32[]{:S(2)}) %collective-permute-start.16) | collective-permute-done | bytes 147488 | tf_op jit(solution)/shard_map/ppermute | solution.py:67
  88.9 2.1 %collective-permute-start.19 = (bf16[112,768]{1,0:T(8,128)(2,1)S(1)}, bf16[112,768]{1,0:T(8,128)(2,1)S(1)}, u32[]{:S(2)}, u32[]{:S(2)}) collective-permute-start(bf16[112,768]{1,0:T(8,128)(2,1)S(1)} %fusion.1), channel_id=1, source_target_pairs={{0,8},{1,9},{2,10},{3,11},{4,12},{5,13},{6,14},{7,15},{8,0},{9,1},... | collective-permute-start | bytes 516104 | tf_op jit(solution)/shard_map/ppermute | solution.py:67
  92.2 1.8 %collective-permute-done.20 = bf16[112,768]{1,0:T(8,128)(2,1)S(1)} collective-permute-done((bf16[112,768]{1,0:T(8,128)(2,1)S(1)}, bf16[112,768]{1,0:T(8,128)(2,1)S(1)}, u32[]{:S(2)}, u32[]{:S(2)}) %collective-permute-start.20) | collective-permute-done | bytes 172064 | tf_op jit(solution)/shard_map/ppermute | solution.py:67
  94.0 1.9 %collective-permute-done.19 = bf16[112,768]{1,0:T(8,128)(2,1)S(1)} collective-permute-done((bf16[112,768]{1,0:T(8,128)(2,1)S(1)}, bf16[112,768]{1,0:T(8,128)(2,1)S(1)}, u32[]{:S(2)}, u32[]{:S(2)}) %collective-permute-start.19) | collective-permute-done | bytes 172064 | tf_op jit(solution)/shard_map/ppermute | solution.py:67
  96.6 2.7 %collective-permute-start.24 = (bf16[112,768]{1,0:T(8,128)(2,1)S(1)}, bf16[112,768]{1,0:T(8,128)(2,1)S(1)}, u32[]{:S(2)}, u32[]{:S(2)}) collective-permute-start(bf16[112,768]{1,0:T(8,128)(2,1)S(1)} %multiply_convert_fusion.refs_0_), channel_id=1, source_target_pairs={{0,3},{1,0},{2,1},{3,2},{4,7},{5,4},{6,5},{7,6},{8,11},{9,8},{10,9... | collective-permute-start | bytes 516104 | tf_op jit(solution)/shard_map/ppermute | solution.py:67
  99.9 2.9 %spread_back.1 = (bf16[512,1536]{1,0:T(8,128)(2,1)}, f32[8,128]{1,0:T(8,128)S(1)}) custom-call(bf16[544,1536]{1,0:T(8,128)(2,1)S(1)} %get-tuple-element.82.grad_ref, f32[3,1536]{1,0:T(4,128)S(1)} %copy-done.3), custom_call_target="tpu_custom_call" | custom-call | tf_op jit(solution)/shard_map/spread_back/pallas_call | solution.py:628
  105.1 1.9 %collective-permute-done.22.refs_1_ = bf16[112,768]{1,0:T(8,128)(2,1)S(1)} collective-permute-done((bf16[112,768]{1,0:T(8,128)(2,1)S(1)}, bf16[112,768]{1,0:T(8,128)(2,1)S(1)}, u32[]{:S(2)}, u32[]{:S(2)}) %collective-permute-start.22) | collective-permute-done | bytes 172064 | tf_op jit(solution)/shard_map/ppermute | solution.py:67
  107.8 2.0 %collective-permute-start.27 = (bf16[784,384]{1,0:T(8,128)(2,1)S(1)}, bf16[784,384]{1,0:T(8,128)(2,1)S(1)}, u32[]{:S(2)}, u32[]{:S(2)}) collective-permute-start(bf16[784,384]{1,0:T(8,128)(2,1)S(1)} %join_rows.1.refs_0_), channel_id=1, source_target_pairs={{0,96},{1,97},{2,98},{3,99},{4,100},{5,101},{6,102},{7,103},{8,104... | collective-permute-start | bytes 1806344 | tf_op jit(solution)/shard_map/ppermute | solution.py:67
  110.7 4.7 %collective-permute-start.28 = (bf16[784,384]{1,0:T(8,128)(2,1)S(1)}, bf16[784,384]{1,0:T(8,128)(2,1)S(1)}, u32[]{:S(2)}, u32[]{:S(2)}) collective-permute-start(bf16[784,384]{1,0:T(8,128)(2,1)S(1)} %join_rows.1.refs_0_), channel_id=1, source_target_pairs={{0,16},{16,0},{1,17},{17,1},{2,18},{18,2},{3,19},{19,3},{4,20},{20... | collective-permute-start | bytes 1806344 | tf_op jit(solution)/shard_map/ppermute | solution.py:809
  115.5 7.7 %collective-permute-done.27.refs_3_ = bf16[784,384]{1,0:T(8,128)(2,1)S(1)} collective-permute-done((bf16[784,384]{1,0:T(8,128)(2,1)S(1)}, bf16[784,384]{1,0:T(8,128)(2,1)S(1)}, u32[]{:S(2)}, u32[]{:S(2)}) %collective-permute-start.27) | collective-permute-done | bytes 602144 | tf_op jit(solution)/shard_map/ppermute | solution.py:67
  123.2 4.5 %collective-permute-start.31 = (bf16[784,384]{1,0:T(8,128)(2,1)S(1)}, bf16[784,384]{1,0:T(8,128)(2,1)S(1)}, u32[]{:S(2)}, u32[]{:S(2)}) collective-permute-start(bf16[784,384]{1,0:T(8,128)(2,1)S(1)} %collective-permute-done.27.refs_3_), channel_id=1, source_target_pairs={{0,16},{16,0},{1,17},{17,1},{2,18},{18,2},{3,19},{19,3},{4,20},{20... | collective-permute-start | bytes 1806344 | tf_op jit(solution)/shard_map/ppermute | solution.py:809
  127.7 3.9 %collective-permute-start.29 = (bf16[784,384]{1,0:T(8,128)(2,1)S(1)}, bf16[784,384]{1,0:T(8,128)(2,1)S(1)}, u32[]{:S(2)}, u32[]{:S(2)}) collective-permute-start(bf16[784,384]{1,0:T(8,128)(2,1)S(1)} %collective-permute-done.25.refs_1_), channel_id=1, source_target_pairs={{0,16},{16,0},{1,17},{17,1},{2,18},{18,2},{3,19},{19,3},{4,20},{20... | collective-permute-start | bytes 1806344 | tf_op jit(solution)/shard_map/ppermute | solution.py:809
  133.3 3.6 %lay_out.1 = (bf16[1536,1536]{1,0:T(8,128)(2,1)}, f32[3,1536]{1,0:T(4,128)}) custom-call(s32[5]{0:T(128)S(1)} %concatenate.6.s_ref.at_ref, bf16[784,384]{1,0:T(8,128)(2,1)S(1)} %join_rows.1.refs_0_, bf16[784,384]{1,0:T(8,128)(2,1)S(1)} %collective-permute-done.25.refs_1_, bf16[784,384]{1,0:T(8,128)(2,1)S(1)} %collective-permute-done.26.refs_2_, ...), custom_call_target="tpu_custom_call" | custom-call | tf_op jit(solution)/shard_map/lay_out/pallas_call | solution.py:736
  (64 shorter events, 28.2 us)
Async XLA Ops:
  4.6 7.6 %collective-permute-start = (bf16[320,256]{1,0:T(8,128)(2,1)S(1)}, bf16[320,256]{1,0:T(8,128)(2,1)S(1)}, u32[]{:S(2)}, u32[]{:S(2)}) collective-permute-start(bf16[320,256]{1,0:T(8,128)(2,1)S(1)} %get-tuple-element.46), channel_id=1, source_target_pairs={{0,1},{1,2},{2,3},{3,0},{4,5},{5,6},{6,7},{7,4},{8,9},{9,10},{10,1... | collective-permute-start | bytes 491528 | tf_op jit(solution)/shard_map/ppermute | solution.py:67
  7.1 8.1 %collective-permute-start.1 = (bf16[320,256]{1,0:T(8,128)(2,1)S(1)}, bf16[320,256]{1,0:T(8,128)(2,1)S(1)}, u32[]{:S(2)}, u32[]{:S(2)}) collective-permute-start(bf16[320,256]{1,0:T(8,128)(2,1)S(1)} %get-tuple-element.47), channel_id=1, source_target_pairs={{0,2},{1,3},{2,0},{3,1},{4,6},{5,7},{6,4},{7,5},{8,10},{9,11},{10,... | collective-permute-start | bytes 491528 | tf_op jit(solution)/shard_map/ppermute | solution.py:67
  10.4 4.8 %collective-permute-start.2 = (bf16[320,256]{1,0:T(8,128)(2,1)S(1)}, bf16[320,256]{1,0:T(8,128)(2,1)S(1)}, u32[]{:S(2)}, u32[]{:S(2)}) collective-permute-start(bf16[320,256]{1,0:T(8,128)(2,1)S(1)} %get-tuple-element.48), channel_id=1, source_target_pairs={{0,3},{1,0},{2,1},{3,2},{4,7},{5,4},{6,5},{7,6},{8,11},{9,8},{10,9... | collective-permute-start | bytes 491528 | tf_op jit(solution)/shard_map/ppermute | solution.py:67
  15.3 10.8 %collective-permute-start.3 = (bf16[1040,256]{1,0:T(8,128)(2,1)S(1)}, bf16[1040,256]{1,0:T(8,128)(2,1)S(1)}, u32[]{:S(2)}, u32[]{:S(2)}) collective-permute-start(bf16[1040,256]{1,0:T(8,128)(2,1)S(1)} %stack_rows.1.refs_4_), channel_id=1, source_target_pairs={{0,4},{1,5},{2,6},{3,7},{4,8},{5,9},{6,10},{7,11},{8,12},{9,13},{1... | collective-permute-start | bytes 1597448 | tf_op jit(solution)/shard_map/ppermute | solution.py:775
  16.3 13.6 %collective-permute-start.4 = (bf16[1040,256]{1,0:T(8,128)(2,1)S(1)}, bf16[1040,256]{1,0:T(8,128)(2,1)S(1)}, u32[]{:S(2)}, u32[]{:S(2)}) collective-permute-start(bf16[1040,256]{1,0:T(8,128)(2,1)S(1)} %stack_rows.1.refs_4_), channel_id=1, source_target_pairs={{0,12},{1,13},{2,14},{3,15},{4,0},{5,1},{6,2},{7,3},{8,4},{9,5},{1... | collective-permute-start | bytes 1597448 | tf_op jit(solution)/shard_map/ppermute | solution.py:775
  18.0 14.2 %collective-permute-start.5 = (bf16[1040,256]{1,0:T(8,128)(2,1)S(1)}, bf16[1040,256]{1,0:T(8,128)(2,1)S(1)}, u32[]{:S(2)}, u32[]{:S(2)}) collective-permute-start(bf16[1040,256]{1,0:T(8,128)(2,1)S(1)} %stack_rows.1.refs_4_), channel_id=1, source_target_pairs={{0,8},{1,9},{2,10},{3,11},{4,12},{5,13},{6,14},{7,15},{8,0},{9,1},... | collective-permute-start | bytes 1597448 | tf_op jit(solution)/shard_map/ppermute | solution.py:775
  19.4 12.8 %collective-permute-start.6 = (bf16[16,1536]{1,0:T(8,128)(2,1)S(1)}, bf16[16,1536]{1,0:T(8,128)(2,1)S(1)}, u32[]{:S(2)}, u32[]{:S(2)}) collective-permute-start(bf16[16,1536]{1,0:T(8,128)(2,1)S(1)} %get-tuple-element.53.refs_4_), channel_id=1, source_target_pairs={{0,1},{1,2},{2,3},{3,4},{4,5},{5,6},{6,7},{7,8},{8,9},{9,10},{10,1... | collective-permute-start | bytes 147464 | tf_op jit(solution)/shard_map/ppermute | solution.py:770
  21.7 10.5 %collective-permute-start.7 = (bf16[16,1536]{1,0:T(8,128)(2,1)S(1)}, bf16[16,1536]{1,0:T(8,128)(2,1)S(1)}, u32[]{:S(2)}, u32[]{:S(2)}) collective-permute-start(bf16[16,1536]{1,0:T(8,128)(2,1)S(1)} %get-tuple-element.60), channel_id=1, source_target_pairs={{1,0},{2,1},{3,2},{4,3},{5,4},{6,5},{7,6},{8,7},{9,8},{10,9},{11,1... | collective-permute-start | bytes 147464 | tf_op jit(solution)/shard_map/ppermute | solution.py:771
  35.5 10.4 %collective-permute-start.8 = (bf16[400,128]{1,0:T(8,128)(2,1)S(1)}, bf16[400,128]{1,0:T(8,128)(2,1)S(1)}, u32[]{:S(2)}, u32[]{:S(2)}) collective-permute-start(bf16[400,128]{1,0:T(8,128)(2,1)S(1)} %get-tuple-element.62), channel_id=1, source_target_pairs={{0,3},{1,0},{2,1},{3,2},{4,7},{5,4},{6,5},{7,6},{8,11},{9,8},{10,9... | collective-permute-start | bytes 307208 | tf_op jit(solution)/shard_map/ppermute | solution.py:67
  39.8 6.1 %collective-permute-start.9 = (bf16[400,128]{1,0:T(8,128)(2,1)S(1)}, bf16[400,128]{1,0:T(8,128)(2,1)S(1)}, u32[]{:S(2)}, u32[]{:S(2)}) collective-permute-start(bf16[400,128]{1,0:T(8,128)(2,1)S(1)} %get-tuple-element.63), channel_id=1, source_target_pairs={{0,2},{1,3},{2,0},{3,1},{4,6},{5,7},{6,4},{7,5},{8,10},{9,11},{10,... | collective-permute-start | bytes 307208 | tf_op jit(solution)/shard_map/ppermute | solution.py:67
  40.8 5.4 %collective-permute-start.10 = (bf16[400,128]{1,0:T(8,128)(2,1)S(1)}, bf16[400,128]{1,0:T(8,128)(2,1)S(1)}, u32[]{:S(2)}, u32[]{:S(2)}) collective-permute-start(bf16[400,128]{1,0:T(8,128)(2,1)S(1)} %get-tuple-element.64), channel_id=1, source_target_pairs={{0,1},{1,2},{2,3},{3,0},{4,5},{5,6},{6,7},{7,4},{8,9},{9,10},{10,1... | collective-permute-start | bytes 307208 | tf_op jit(solution)/shard_map/ppermute | solution.py:67
  51.8 6.7 %collective-permute-start.11 = (bf16[4,384,768]{2,1,0:T(8,128)(2,1)S(1)}, bf16[4,384,768]{2,1,0:T(8,128)(2,1)S(1)}, u32[]{:S(2)}, u32[]{:S(2)}) collective-permute-start(bf16[4,384,768]{2,1,0:T(8,128)(2,1)S(1)} %get-tuple-element.69), channel_id=1, source_target_pairs={{0,16},{16,0},{1,17},{17,1},{2,18},{18,2},{3,19},{19,3},{4,20},{20... | collective-permute-start | bytes 7077896 | tf_op jit(solution)/shard_map/ppermute | solution.py:788
  59.8 18.4 %collective-permute-start.12 = (bf16[384,768]{1,0:T(8,128)(2,1)S(1)}, bf16[384,768]{1,0:T(8,128)(2,1)S(1)}, u32[]{:S(2)}, u32[]{:S(2)}) collective-permute-start(bf16[384,768]{1,0:T(8,128)(2,1)S(1)} %get-tuple-element.71), channel_id=1, source_target_pairs={{0,32},{1,33},{2,34},{3,35},{4,36},{5,37},{6,38},{7,39},{8,40},{9,... | collective-permute-start | bytes 1769480 | tf_op jit(solution)/shard_map/ppermute | solution.py:67
  60.8 17.3 %collective-permute-start.13 = (bf16[384,768]{1,0:T(8,128)(2,1)S(1)}, bf16[384,768]{1,0:T(8,128)(2,1)S(1)}, u32[]{:S(2)}, u32[]{:S(2)}) collective-permute-start(bf16[384,768]{1,0:T(8,128)(2,1)S(1)} %get-tuple-element.72), channel_id=1, source_target_pairs={{0,64},{1,65},{2,66},{3,67},{4,68},{5,69},{6,70},{7,71},{8,72},{9,... | collective-permute-start | bytes 1769480 | tf_op jit(solution)/shard_map/ppermute | solution.py:67
  64.0 14.2 %collective-permute-start.14 = (bf16[384,768]{1,0:T(8,128)(2,1)S(1)}, bf16[384,768]{1,0:T(8,128)(2,1)S(1)}, u32[]{:S(2)}, u32[]{:S(2)}) collective-permute-start(bf16[384,768]{1,0:T(8,128)(2,1)S(1)} %get-tuple-element.73), channel_id=1, source_target_pairs={{0,96},{1,97},{2,98},{3,99},{4,100},{5,101},{6,102},{7,103},{8,104... | collective-permute-start | bytes 1769480 | tf_op jit(solution)/shard_map/ppermute | solution.py:67
  75.5 10.0 %collective-permute-start.18 = (f32[3,768]{1,0:T(4,128)S(1)}, f32[3,768]{1,0:T(4,128)S(1)}, u32[]{:S(2)}, u32[]{:S(2)}) collective-permute-start(f32[3,768]{1,0:T(4,128)S(1)} %get-tuple-element.81), channel_id=1, source_target_pairs={{0,16},{16,0},{1,17},{17,1},{2,18},{18,2},{3,19},{19,3},{4,20},{20... | collective-permute-start | bytes 27656 | tf_op jit(solution)/shard_map/ppermute | solution.py:797
  79.1 6.7 %collective-permute-start.15 = (bf16[96,768]{1,0:T(8,128)(2,1)S(1)}, bf16[96,768]{1,0:T(8,128)(2,1)S(1)}, u32[]{:S(2)}, u32[]{:S(2)}) collective-permute-start(bf16[96,768]{1,0:T(8,128)(2,1)S(1)} %get-tuple-element.75), channel_id=1, source_target_pairs={{0,2},{1,3},{2,0},{3,1},{4,6},{5,7},{6,4},{7,5},{8,10},{9,11},{10,... | collective-permute-start | bytes 442376 | tf_op jit(solution)/shard_map/ppermute | solution.py:67
  82.9 5.2 %collective-permute-start.16 = (bf16[96,768]{1,0:T(8,128)(2,1)S(1)}, bf16[96,768]{1,0:T(8,128)(2,1)S(1)}, u32[]{:S(2)}, u32[]{:S(2)}) collective-permute-start(bf16[96,768]{1,0:T(8,128)(2,1)S(1)} %get-tuple-element.76), channel_id=1, source_target_pairs={{0,1},{1,2},{2,3},{3,0},{4,5},{5,6},{6,7},{7,4},{8,9},{9,10},{10,1... | collective-permute-start | bytes 442376 | tf_op jit(solution)/shard_map/ppermute | solution.py:67
  82.9 5.2 %collective-permute-start.17 = (bf16[96,768]{1,0:T(8,128)(2,1)S(1)}, bf16[96,768]{1,0:T(8,128)(2,1)S(1)}, u32[]{:S(2)}, u32[]{:S(2)}) collective-permute-start(bf16[96,768]{1,0:T(8,128)(2,1)S(1)} %get-tuple-element.77), channel_id=1, source_target_pairs={{0,3},{1,0},{2,1},{3,2},{4,7},{5,4},{6,5},{7,6},{8,11},{9,8},{10,9... | collective-permute-start | bytes 442376 | tf_op jit(solution)/shard_map/ppermute | solution.py:67
  88.2 5.8 %collective-permute-start.20 = (bf16[112,768]{1,0:T(8,128)(2,1)S(1)}, bf16[112,768]{1,0:T(8,128)(2,1)S(1)}, u32[]{:S(2)}, u32[]{:S(2)}) collective-permute-start(bf16[112,768]{1,0:T(8,128)(2,1)S(1)} %fusion.1), channel_id=1, source_target_pairs={{0,4},{1,5},{2,6},{3,7},{4,8},{5,9},{6,10},{7,11},{8,12},{9,13},{1... | collective-permute-start | bytes 516104 | tf_op jit(solution)/shard_map/ppermute | solution.py:67
  88.9 7.1 %collective-permute-start.19 = (bf16[112,768]{1,0:T(8,128)(2,1)S(1)}, bf16[112,768]{1,0:T(8,128)(2,1)S(1)}, u32[]{:S(2)}, u32[]{:S(2)}) collective-permute-start(bf16[112,768]{1,0:T(8,128)(2,1)S(1)} %fusion.1), channel_id=1, source_target_pairs={{0,8},{1,9},{2,10},{3,11},{4,12},{5,13},{6,14},{7,15},{8,0},{9,1},... | collective-permute-start | bytes 516104 | tf_op jit(solution)/shard_map/ppermute | solution.py:67
  91.0 5.4 %collective-permute-start.21 = (bf16[112,768]{1,0:T(8,128)(2,1)S(1)}, bf16[112,768]{1,0:T(8,128)(2,1)S(1)}, u32[]{:S(2)}, u32[]{:S(2)}) collective-permute-start(bf16[112,768]{1,0:T(8,128)(2,1)S(1)} %fusion.1), channel_id=1, source_target_pairs={{0,12},{1,13},{2,14},{3,15},{4,0},{5,1},{6,2},{7,3},{8,4},{9,5},{1... | collective-permute-start | bytes 516104 | tf_op jit(solution)/shard_map/ppermute | solution.py:67
  96.6 6.9 %collective-permute-start.24 = (bf16[112,768]{1,0:T(8,128)(2,1)S(1)}, bf16[112,768]{1,0:T(8,128)(2,1)S(1)}, u32[]{:S(2)}, u32[]{:S(2)}) collective-permute-start(bf16[112,768]{1,0:T(8,128)(2,1)S(1)} %multiply_convert_fusion.refs_0_), channel_id=1, source_target_pairs={{0,3},{1,0},{2,1},{3,2},{4,7},{5,4},{6,5},{7,6},{8,11},{9,8},{10,9... | collective-permute-start | bytes 516104 | tf_op jit(solution)/shard_map/ppermute | solution.py:67
  99.2 5.9 %collective-permute-start.23 = (bf16[112,768]{1,0:T(8,128)(2,1)S(1)}, bf16[112,768]{1,0:T(8,128)(2,1)S(1)}, u32[]{:S(2)}, u32[]{:S(2)}) collective-permute-start(bf16[112,768]{1,0:T(8,128)(2,1)S(1)} %multiply_convert_fusion.refs_0_), channel_id=1, source_target_pairs={{0,2},{1,3},{2,0},{3,1},{4,6},{5,7},{6,4},{7,5},{8,10},{9,11},{10,... | collective-permute-start | bytes 516104 | tf_op jit(solution)/shard_map/ppermute | solution.py:67
  99.4 7.6 %collective-permute-start.22 = (bf16[112,768]{1,0:T(8,128)(2,1)S(1)}, bf16[112,768]{1,0:T(8,128)(2,1)S(1)}, u32[]{:S(2)}, u32[]{:S(2)}) collective-permute-start(bf16[112,768]{1,0:T(8,128)(2,1)S(1)} %multiply_convert_fusion.refs_0_), channel_id=1, source_target_pairs={{0,1},{1,2},{2,3},{3,0},{4,5},{5,6},{6,7},{7,4},{8,9},{9,10},{10,1... | collective-permute-start | bytes 516104 | tf_op jit(solution)/shard_map/ppermute | solution.py:67
  107.8 15.4 %collective-permute-start.27 = (bf16[784,384]{1,0:T(8,128)(2,1)S(1)}, bf16[784,384]{1,0:T(8,128)(2,1)S(1)}, u32[]{:S(2)}, u32[]{:S(2)}) collective-permute-start(bf16[784,384]{1,0:T(8,128)(2,1)S(1)} %join_rows.1.refs_0_), channel_id=1, source_target_pairs={{0,96},{1,97},{2,98},{3,99},{4,100},{5,101},{6,102},{7,103},{8,104... | collective-permute-start | bytes 1806344 | tf_op jit(solution)/shard_map/ppermute | solution.py:67
  109.7 17.9 %collective-permute-start.26 = (bf16[784,384]{1,0:T(8,128)(2,1)S(1)}, bf16[784,384]{1,0:T(8,128)(2,1)S(1)}, u32[]{:S(2)}, u32[]{:S(2)}) collective-permute-start(bf16[784,384]{1,0:T(8,128)(2,1)S(1)} %join_rows.1.refs_0_), channel_id=1, source_target_pairs={{0,64},{1,65},{2,66},{3,67},{4,68},{5,69},{6,70},{7,71},{8,72},{9,... | collective-permute-start | bytes 1806344 | tf_op jit(solution)/shard_map/ppermute | solution.py:67
  110.5 17.2 %collective-permute-start.25 = (bf16[784,384]{1,0:T(8,128)(2,1)S(1)}, bf16[784,384]{1,0:T(8,128)(2,1)S(1)}, u32[]{:S(2)}, u32[]{:S(2)}) collective-permute-start(bf16[784,384]{1,0:T(8,128)(2,1)S(1)} %join_rows.1.refs_0_), channel_id=1, source_target_pairs={{0,32},{1,33},{2,34},{3,35},{4,36},{5,37},{6,38},{7,39},{8,40},{9,... | collective-permute-start | bytes 1806344 | tf_op jit(solution)/shard_map/ppermute | solution.py:67
  110.7 20.9 %collective-permute-start.28 = (bf16[784,384]{1,0:T(8,128)(2,1)S(1)}, bf16[784,384]{1,0:T(8,128)(2,1)S(1)}, u32[]{:S(2)}, u32[]{:S(2)}) collective-permute-start(bf16[784,384]{1,0:T(8,128)(2,1)S(1)} %join_rows.1.refs_0_), channel_id=1, source_target_pairs={{0,16},{16,0},{1,17},{17,1},{2,18},{18,2},{3,19},{19,3},{4,20},{20... | collective-permute-start | bytes 1806344 | tf_op jit(solution)/shard_map/ppermute | solution.py:809
  123.2 8.5 %collective-permute-start.31 = (bf16[784,384]{1,0:T(8,128)(2,1)S(1)}, bf16[784,384]{1,0:T(8,128)(2,1)S(1)}, u32[]{:S(2)}, u32[]{:S(2)}) collective-permute-start(bf16[784,384]{1,0:T(8,128)(2,1)S(1)} %collective-permute-done.27.refs_3_), channel_id=1, source_target_pairs={{0,16},{16,0},{1,17},{17,1},{2,18},{18,2},{3,19},{19,3},{4,20},{20... | collective-permute-start | bytes 1806344 | tf_op jit(solution)/shard_map/ppermute | solution.py:809
  127.7 4.0 %collective-permute-start.30 = (bf16[784,384]{1,0:T(8,128)(2,1)S(1)}, bf16[784,384]{1,0:T(8,128)(2,1)S(1)}, u32[]{:S(2)}, u32[]{:S(2)}) collective-permute-start(bf16[784,384]{1,0:T(8,128)(2,1)S(1)} %collective-permute-done.26.refs_2_), channel_id=1, source_target_pairs={{0,16},{16,0},{1,17},{17,1},{2,18},{18,2},{3,19},{19,3},{4,20},{20... | collective-permute-start | bytes 1806344 | tf_op jit(solution)/shard_map/ppermute | solution.py:809
  127.7 5.6 %collective-permute-start.29 = (bf16[784,384]{1,0:T(8,128)(2,1)S(1)}, bf16[784,384]{1,0:T(8,128)(2,1)S(1)}, u32[]{:S(2)}, u32[]{:S(2)}) collective-permute-start(bf16[784,384]{1,0:T(8,128)(2,1)S(1)} %collective-permute-done.25.refs_1_), channel_id=1, source_target_pairs={{0,16},{16,0},{1,17},{17,1},{2,18},{18,2},{3,19},{19,3},{4,20},{20... | collective-permute-start | bytes 1806344 | tf_op jit(solution)/shard_map/ppermute | solution.py:809
  (4 other events, 14.6 us)

commit v12 on v11

--- a/solution.py
+++ b/solution.py
@@ -704,7 +704,7 @@
 
 def lay_out(scalars, own, other):
     half, quarter = own[0].shape[0] - TAIL, own[0].shape[1]
-    parts = 4
+    parts = 2
     part = half // parts
 
     def kernel(s_ref, *refs):

time: 137 us -> 137 us (level)
  no operation moved by 1% of the time
where the time goes in v12:
time: 137 us
  starting transfers between devices  58.5 us (43%)
  Pallas kernels  48 us (35%)
  waiting for transfers between devices  25.3 us (18%)
  local copies, waits for them, and re-layouts  3.21 us (2%)
  between operations  1.73 us (1%)
    ppermute x21, starting transfers between devices, exchange(): got[d] = lax.ppermute(pieces[d], AXES, turn(axes, sign * d))  32.4 us
    ppermute x21, waiting for transfers between devices, exchange(): got[d] = lax.ppermute(pieces[d], AXES, turn(axes, sign * d))  21.9 us
    ppermute x4, starting transfers between devices, local(): other = [lax.ppermute(block, 'c', swap) for block in own]  13.2 us
    pallas_call x1, Pallas kernels, backward(): pl.pallas_call(kernel, out_shape=[jax.ShapeDtypeStruct((fine + 2 * TAIL,...  10.8 us
    pallas_call x4, Pallas kernels, attend(): pl.pallas_call(kernel, out_shape=outs, in_specs=[SMEM] + [VMEM] * len(ins...  9.97 us
    pallas_call x2, Pallas kernels, forward(): pl.pallas_call(kernel, out_shape=outs, grid_spec=pltpu.PrefetchScalarGrid...  9.51 us
    ppermute x3, starting transfers between devices, local(): far = {d: lax.ppermute(own, AXES, turn(ROW_RING, d)) for d in (1, 3, 2)}  4.13 us
    pallas_call x1, Pallas kernels, project(): pl.pallas_call(kernel, out_shape=[jax.ShapeDtypeStruct((rows + rows // 4,...  3.92 us
  transfers between devices with their start and end apart: 32, of which 14 were waited for; matrix products, arithmetic and copies ran while one was open for 1% of the time, Pallas kernels for 22%

profile of v12, /device:TPU:1, one launch (start us, length us, event | category | flops | bytes accessed | tf_op | source)
XLA Modules:
  0.0 136.9 jit_solution(883984469763805466)
XLA Ops:
  0.6 3.9 %project.1 = (bf16[320,256]{1,0:T(8,128)(2,1)S(1)}, bf16[320,256]{1,0:T(8,128)(2,1)S(1)}, bf16[320,256]{1,0:T(8,128)(2,1)S(1)}, bf16[320,256]{1,0:T(8,128)(2,1)S(1)}) custom-call(bf16[256,1536]{1,0:T(8,128)(2,1)} %bitcast.11, bf16[1536,256]{1,0:T(8,128)(2,1)} %wq_hbm.1, bf16[1536,256]{1,0:T(8,128)(2,1)} %wk_hbm.1, bf16[1536,768]{1,0:T(8,128)(2,1)} %wv_hbm.1), custom_call_target="tpu_custom_call" | custom-call | tf_op jit(solution)/shard_map/project/pallas_call | solution.py:112
  4.6 2.5 %collective-permute-start = (bf16[320,256]{1,0:T(8,128)(2,1)S(1)}, bf16[320,256]{1,0:T(8,128)(2,1)S(1)}, u32[]{:S(2)}, u32[]{:S(2)}) collective-permute-start(bf16[320,256]{1,0:T(8,128)(2,1)S(1)} %get-tuple-element.46), channel_id=1, source_target_pairs={{0,1},{1,2},{2,3},{3,0},{4,5},{5,6},{6,7},{7,4},{8,9},{9,10},{10,1... | collective-permute-start | bytes 491528 | tf_op jit(solution)/shard_map/ppermute | solution.py:67
  7.1 3.3 %collective-permute-start.1 = (bf16[320,256]{1,0:T(8,128)(2,1)S(1)}, bf16[320,256]{1,0:T(8,128)(2,1)S(1)}, u32[]{:S(2)}, u32[]{:S(2)}) collective-permute-start(bf16[320,256]{1,0:T(8,128)(2,1)S(1)} %get-tuple-element.47), channel_id=1, source_target_pairs={{0,2},{1,3},{2,0},{3,1},{4,6},{5,7},{6,4},{7,5},{8,10},{9,11},{10,... | collective-permute-start | bytes 491528 | tf_op jit(solution)/shard_map/ppermute | solution.py:67
  12.2 3.0 %collective-permute-done.1.refs_2_ = bf16[320,256]{1,0:T(8,128)(2,1)S(1)} collective-permute-done((bf16[320,256]{1,0:T(8,128)(2,1)S(1)}, bf16[320,256]{1,0:T(8,128)(2,1)S(1)}, u32[]{:S(2)}, u32[]{:S(2)}) %collective-permute-start.1) | collective-permute-done | bytes 163872 | tf_op jit(solution)/shard_map/ppermute | solution.py:67
  19.4 2.3 %collective-permute-start.6 = (bf16[16,1536]{1,0:T(8,128)(2,1)S(1)}, bf16[16,1536]{1,0:T(8,128)(2,1)S(1)}, u32[]{:S(2)}, u32[]{:S(2)}) collective-permute-start(bf16[16,1536]{1,0:T(8,128)(2,1)S(1)} %get-tuple-element.53.refs_4_), channel_id=1, source_target_pairs={{0,1},{1,2},{2,3},{3,4},{4,5},{5,6},{6,7},{7,8},{8,9},{9,10},{10,1... | collective-permute-start | bytes 147464 | tf_op jit(solution)/shard_map/ppermute | solution.py:770
  23.8 2.2 %attend.4 = (f32[1024,256]{1,0:T(8,128)S(1)}, f32[1024,128]{1,0:T(8,128)S(1)}) custom-call(s32[5]{0:T(128)S(1)} %concatenate.6.s_ref.at_ref, bf16[256,128]{1,0:T(8,128)(2,1)S(1)} %get-tuple-element.49.refs_0_, bf16[256,128]{1,0:T(8,128)(2,1)S(1)} %get-tuple-element.50.refs_1_, bf16[256,128]{1,0:T(8,128)(2,1)S(1)} %get-tuple-element.51.refs_2_, ...), custom_call_target="tpu_custom_call" | custom-call | flops 1073741824 | bytes 4194304 | tf_op jit(solution)/shard_map/attend/pallas_call | solution.py:283
  26.1 2.3 %attend.5 = (f32[1024,256]{1,0:T(8,128)S(1)}, f32[1024,128]{1,0:T(8,128)S(1)}) custom-call(s32[5]{0:T(128)S(1)} %concatenate.6.s_ref.at_ref, bf16[256,128]{1,0:T(8,128)(2,1)S(1)} %get-tuple-element.49.refs_0_, bf16[256,128]{1,0:T(8,128)(2,1)S(1)} %get-tuple-element.50.refs_1_, bf16[256,128]{1,0:T(8,128)(2,1)S(1)} %get-tuple-element.51.refs_2_, ...), custom_call_target="tpu_custom_call" | custom-call | flops 1073741824 | bytes 4194304 | tf_op jit(solution)/shard_map/attend/pallas_call | solution.py:283
  29.9 2.2 %attend.6 = (f32[1024,256]{1,0:T(8,128)S(1)}, f32[1024,128]{1,0:T(8,128)S(1)}) custom-call(s32[5]{0:T(128)S(1)} %concatenate.6.s_ref.at_ref, bf16[256,128]{1,0:T(8,128)(2,1)S(1)} %get-tuple-element.49.refs_0_, bf16[256,128]{1,0:T(8,128)(2,1)S(1)} %get-tuple-element.50.refs_1_, bf16[256,128]{1,0:T(8,128)(2,1)S(1)} %get-tuple-element.51.refs_2_, ...), custom_call_target="tpu_custom_call" | custom-call | flops 1073741824 | bytes 4194304 | tf_op jit(solution)/shard_map/attend/pallas_call | solution.py:283
  32.2 3.3 %attend.7 = (bf16[400,128]{1,0:T(8,128)(2,1)S(1)}, bf16[400,128]{1,0:T(8,128)(2,1)S(1)}, bf16[400,128]{1,0:T(8,128)(2,1)S(1)}, bf16[400,128]{1,0:T(8,128)(2,1)S(1)}) custom-call(s32[5]{0:T(128)S(1)} %concatenate.6.s_ref.at_ref, bf16[256,128]{1,0:T(8,128)(2,1)S(1)} %get-tuple-element.49.refs_0_, bf16[256,128]{1,0:T(8,128)(2,1)S(1)} %get-tuple-element.50.refs_1_, ...), custom_call_target="tpu_custom_call" | custom-call | flops 1073741824 | bytes 4194304 | tf_op jit(solution)/shard_map/attend/pallas_call | solution.py:283
  35.5 4.3 %collective-permute-start.8 = (bf16[400,128]{1,0:T(8,128)(2,1)S(1)}, bf16[400,128]{1,0:T(8,128)(2,1)S(1)}, u32[]{:S(2)}, u32[]{:S(2)}) collective-permute-start(bf16[400,128]{1,0:T(8,128)(2,1)S(1)} %get-tuple-element.62), channel_id=1, source_target_pairs={{0,3},{1,0},{2,1},{3,2},{4,7},{5,4},{6,5},{7,6},{8,11},{9,8},{10,9... | collective-permute-start | bytes 307208 | tf_op jit(solution)/shard_map/ppermute | solution.py:67
  44.0 1.8 %load.1 = (bf16[256,1536]{1,0:T(8,128)(2,1)S(1)}, bf16[512,1536]{1,0:T(8,128)(2,1)S(1)}, bf16[4,192,1536]{2,1,0:T(8,128)(2,1)S(1)}) custom-call(bf16[400,128]{1,0:T(8,128)(2,1)S(1)} %get-tuple-element.61.behind_ref.b0, bf16[256,1536]{1,0:T(8,128)(2,1)S(1)} %bitcast.13, bf16[512,1536]{1,0:T(8,128)(2,1)S(1)} %bitcast.18, bf16[4,192,1536]{2,1,0:T(8,128)(2,1)} %bitcast.19), custom_call_target="tpu_custom_call" | custom-call | tf_op jit(solution)/shard_map/load/pallas_call | solution.py:490
  46.2 5.5 %forward.3 = (bf16[544,768]{1,0:T(8,128)(2,1)S(1)}, bf16[4,384,768]{2,1,0:T(8,128)(2,1)S(1)}) custom-call(s32[5]{0:T(128)S(1)} %concatenate.6.s_ref.at_ref, bf16[400,128]{1,0:T(8,128)(2,1)S(1)} %get-tuple-element.61.behind_ref.b0, bf16[400,128]{1,0:T(8,128)(2,1)S(1)} %collective-permute-done.8.b1, bf16[400,128]{1,0:T(8,128)(2,1)S(1)} %collective-permute-done.9.b2, ...), custom_call_target="tpu_custom_call" | custom-call | flops 2415919104 | bytes 9437184 | tf_op jit(solution)/shard_map/forward/pallas_call | solution.py:459
  51.8 2.5 %collective-permute-start.11 = (bf16[4,384,768]{2,1,0:T(8,128)(2,1)S(1)}, bf16[4,384,768]{2,1,0:T(8,128)(2,1)S(1)}, u32[]{:S(2)}, u32[]{:S(2)}) collective-permute-start(bf16[4,384,768]{2,1,0:T(8,128)(2,1)S(1)} %get-tuple-element.69), channel_id=1, source_target_pairs={{0,16},{16,0},{1,17},{17,1},{2,18},{18,2},{3,19},{19,3},{4,20},{20... | collective-permute-start | bytes 7077896 | tf_op jit(solution)/shard_map/ppermute | solution.py:788
  54.3 4.0 %forward.2 = (bf16[544,768]{1,0:T(8,128)(2,1)S(1)}, bf16[512,768]{1,0:T(8,128)(2,1)S(1)}) custom-call(s32[5]{0:T(128)S(1)} %concatenate.6.s_ref.at_ref, bf16[400,128]{1,0:T(8,128)(2,1)S(1)} %get-tuple-element.61.behind_ref.b0, bf16[400,128]{1,0:T(8,128)(2,1)S(1)} %collective-permute-done.8.b1, bf16[400,128]{1,0:T(8,128)(2,1)S(1)} %collective-permute-done.9.b2, ...), custom_call_target="tpu_custom_call" | custom-call | flops 2415919104 | bytes 9437184 | tf_op jit(solution)/shard_map/forward/pallas_call | solution.py:459
  60.8 1.8 %collective-permute-start.13 = (bf16[384,768]{1,0:T(8,128)(2,1)S(1)}, bf16[384,768]{1,0:T(8,128)(2,1)S(1)}, u32[]{:S(2)}, u32[]{:S(2)}) collective-permute-start(bf16[384,768]{1,0:T(8,128)(2,1)S(1)} %get-tuple-element.72), channel_id=1, source_target_pairs={{0,64},{1,65},{2,66},{3,67},{4,68},{5,69},{6,70},{7,71},{8,72},{9,... | collective-permute-start | bytes 1769480 | tf_op jit(solution)/shard_map/ppermute | solution.py:67
  64.7 10.8 %backward.1 = (bf16[544,1536]{1,0:T(8,128)(2,1)S(1)}, f32[3,768]{1,0:T(4,128)S(1)}, f32[3,768]{1,0:T(4,128)S(1)}) custom-call(s32[5]{0:T(128)S(1)} %concatenate.6.s_ref.at_ref, bf16[544,768]{1,0:T(8,128)(2,1)S(1)} %get-tuple-element.78.theirs_ref, bf16[544,768]{1,0:T(8,128)(2,1)S(1)} %get-tuple-element.79.ours_ref, bf16[512,1536]{1,0:T(8,128)(2,1)S(1)} %bitcast.16, ...), custom_call_target="tpu_custom_call" | custom-call | flops 2415919104 | bytes 11534336 | tf_op jit(solution)/shard_map/backward/pallas_call | solution.py:576
  75.5 2.6 %collective-permute-start.18 = (f32[3,768]{1,0:T(4,128)S(1)}, f32[3,768]{1,0:T(4,128)S(1)}, u32[]{:S(2)}, u32[]{:S(2)}) collective-permute-start(f32[3,768]{1,0:T(4,128)S(1)} %get-tuple-element.81), channel_id=1, source_target_pairs={{0,16},{16,0},{1,17},{17,1},{2,18},{18,2},{3,19},{19,3},{4,20},{20... | collective-permute-start | bytes 27656 | tf_op jit(solution)/shard_map/ppermute | solution.py:797
  79.1 3.8 %collective-permute-start.15 = (bf16[96,768]{1,0:T(8,128)(2,1)S(1)}, bf16[96,768]{1,0:T(8,128)(2,1)S(1)}, u32[]{:S(2)}, u32[]{:S(2)}) collective-permute-start(bf16[96,768]{1,0:T(8,128)(2,1)S(1)} %get-tuple-element.75), channel_id=1, source_target_pairs={{0,2},{1,3},{2,0},{3,1},{4,6},{5,7},{6,4},{7,5},{8,10},{9,11},{10,... | collective-permute-start | bytes 442376 | tf_op jit(solution)/shard_map/ppermute | solution.py:67
  82.9 2.7 %collective-permute-start.17 = (bf16[96,768]{1,0:T(8,128)(2,1)S(1)}, bf16[96,768]{1,0:T(8,128)(2,1)S(1)}, u32[]{:S(2)}, u32[]{:S(2)}) collective-permute-start(bf16[96,768]{1,0:T(8,128)(2,1)S(1)} %get-tuple-element.77), channel_id=1, source_target_pairs={{0,3},{1,0},{2,1},{3,2},{4,7},{5,4},{6,5},{7,6},{8,11},{9,8},{10,9... | collective-permute-start | bytes 442376 | tf_op jit(solution)/shard_map/ppermute | solution.py:67
  85.7 2.4 %collective-permute-done.16 = bf16[96,768]{1,0:T(8,128)(2,1)S(1)} collective-permute-done((bf16[96,768]{1,0:T(8,128)(2,1)S(1)}, bf16[96,768]{1,0:T(8,128)(2,1)S(1)}, u32[]{:S(2)}, u32[]{:S(2)}) %collective-permute-start.16) | collective-permute-done | bytes 147488 | tf_op jit(solution)/shard_map/ppermute | solution.py:67
  88.9 2.1 %collective-permute-start.19 = (bf16[112,768]{1,0:T(8,128)(2,1)S(1)}, bf16[112,768]{1,0:T(8,128)(2,1)S(1)}, u32[]{:S(2)}, u32[]{:S(2)}) collective-permute-start(bf16[112,768]{1,0:T(8,128)(2,1)S(1)} %fusion.1), channel_id=1, source_target_pairs={{0,8},{1,9},{2,10},{3,11},{4,12},{5,13},{6,14},{7,15},{8,0},{9,1},... | collective-permute-start | bytes 516104 | tf_op jit(solution)/shard_map/ppermute | solution.py:67
  92.2 1.8 %collective-permute-done.20 = bf16[112,768]{1,0:T(8,128)(2,1)S(1)} collective-permute-done((bf16[112,768]{1,0:T(8,128)(2,1)S(1)}, bf16[112,768]{1,0:T(8,128)(2,1)S(1)}, u32[]{:S(2)}, u32[]{:S(2)}) %collective-permute-start.20) | collective-permute-done | bytes 172064 | tf_op jit(solution)/shard_map/ppermute | solution.py:67
  94.0 1.9 %collective-permute-done.19 = bf16[112,768]{1,0:T(8,128)(2,1)S(1)} collective-permute-done((bf16[112,768]{1,0:T(8,128)(2,1)S(1)}, bf16[112,768]{1,0:T(8,128)(2,1)S(1)}, u32[]{:S(2)}, u32[]{:S(2)}) %collective-permute-start.19) | collective-permute-done | bytes 172064 | tf_op jit(solution)/shard_map/ppermute | solution.py:67
  96.6 2.7 %collective-permute-start.24 = (bf16[112,768]{1,0:T(8,128)(2,1)S(1)}, bf16[112,768]{1,0:T(8,128)(2,1)S(1)}, u32[]{:S(2)}, u32[]{:S(2)}) collective-permute-start(bf16[112,768]{1,0:T(8,128)(2,1)S(1)} %multiply_convert_fusion.refs_0_), channel_id=1, source_target_pairs={{0,3},{1,0},{2,1},{3,2},{4,7},{5,4},{6,5},{7,6},{8,11},{9,8},{10,9... | collective-permute-start | bytes 516104 | tf_op jit(solution)/shard_map/ppermute | solution.py:67
  99.9 2.9 %spread_back.1 = (bf16[512,1536]{1,0:T(8,128)(2,1)}, f32[8,128]{1,0:T(8,128)S(1)}) custom-call(bf16[544,1536]{1,0:T(8,128)(2,1)S(1)} %get-tuple-element.82.grad_ref, f32[3,1536]{1,0:T(4,128)S(1)} %copy-done.3), custom_call_target="tpu_custom_call" | custom-call | tf_op jit(solution)/shard_map/spread_back/pallas_call | solution.py:628
  105.1 1.9 %collective-permute-done.22.refs_1_ = bf16[112,768]{1,0:T(8,128)(2,1)S(1)} collective-permute-done((bf16[112,768]{1,0:T(8,128)(2,1)S(1)}, bf16[112,768]{1,0:T(8,128)(2,1)S(1)}, u32[]{:S(2)}, u32[]{:S(2)}) %collective-permute-start.22) | collective-permute-done | bytes 172064 | tf_op jit(solution)/shard_map/ppermute | solution.py:67
  107.8 2.0 %collective-permute-start.27 = (bf16[784,384]{1,0:T(8,128)(2,1)S(1)}, bf16[784,384]{1,0:T(8,128)(2,1)S(1)}, u32[]{:S(2)}, u32[]{:S(2)}) collective-permute-start(bf16[784,384]{1,0:T(8,128)(2,1)S(1)} %join_rows.1.refs_0_), channel_id=1, source_target_pairs={{0,96},{1,97},{2,98},{3,99},{4,100},{5,101},{6,102},{7,103},{8,104... | collective-permute-start | bytes 1806344 | tf_op jit(solution)/shard_map/ppermute | solution.py:67
  110.7 4.7 %collective-permute-start.28 = (bf16[784,384]{1,0:T(8,128)(2,1)S(1)}, bf16[784,384]{1,0:T(8,128)(2,1)S(1)}, u32[]{:S(2)}, u32[]{:S(2)}) collective-permute-start(bf16[784,384]{1,0:T(8,128)(2,1)S(1)} %join_rows.1.refs_0_), channel_id=1, source_target_pairs={{0,16},{16,0},{1,17},{17,1},{2,18},{18,2},{3,19},{19,3},{4,20},{20... | collective-permute-start | bytes 1806344 | tf_op jit(solution)/shard_map/ppermute | solution.py:809
  115.5 7.7 %collective-permute-done.27.refs_3_ = bf16[784,384]{1,0:T(8,128)(2,1)S(1)} collective-permute-done((bf16[784,384]{1,0:T(8,128)(2,1)S(1)}, bf16[784,384]{1,0:T(8,128)(2,1)S(1)}, u32[]{:S(2)}, u32[]{:S(2)}) %collective-permute-start.27) | collective-permute-done | bytes 602144 | tf_op jit(solution)/shard_map/ppermute | solution.py:67
  123.2 4.5 %collective-permute-start.31 = (bf16[784,384]{1,0:T(8,128)(2,1)S(1)}, bf16[784,384]{1,0:T(8,128)(2,1)S(1)}, u32[]{:S(2)}, u32[]{:S(2)}) collective-permute-start(bf16[784,384]{1,0:T(8,128)(2,1)S(1)} %collective-permute-done.27.refs_3_), channel_id=1, source_target_pairs={{0,16},{16,0},{1,17},{17,1},{2,18},{18,2},{3,19},{19,3},{4,20},{20... | collective-permute-start | bytes 1806344 | tf_op jit(solution)/shard_map/ppermute | solution.py:809
  127.7 3.9 %collective-permute-start.29 = (bf16[784,384]{1,0:T(8,128)(2,1)S(1)}, bf16[784,384]{1,0:T(8,128)(2,1)S(1)}, u32[]{:S(2)}, u32[]{:S(2)}) collective-permute-start(bf16[784,384]{1,0:T(8,128)(2,1)S(1)} %collective-permute-done.25.refs_1_), channel_id=1, source_target_pairs={{0,16},{16,0},{1,17},{17,1},{2,18},{18,2},{3,19},{19,3},{4,20},{20... | collective-permute-start | bytes 1806344 | tf_op jit(solution)/shard_map/ppermute | solution.py:809
  133.3 3.5 %lay_out.1 = (bf16[1536,1536]{1,0:T(8,128)(2,1)}, f32[3,1536]{1,0:T(4,128)}) custom-call(s32[5]{0:T(128)S(1)} %concatenate.6.s_ref.at_ref, bf16[784,384]{1,0:T(8,128)(2,1)S(1)} %join_rows.1.refs_0_, bf16[784,384]{1,0:T(8,128)(2,1)S(1)} %collective-permute-done.25.refs_1_, bf16[784,384]{1,0:T(8,128)(2,1)S(1)} %collective-permute-done.26.refs_2_, ...), custom_call_target="tpu_custom_call" | custom-call | tf_op jit(solution)/shard_map/lay_out/pallas_call | solution.py:736
  (64 shorter events, 28.2 us)
Async XLA Ops:
  4.6 7.6 %collective-permute-start = (bf16[320,256]{1,0:T(8,128)(2,1)S(1)}, bf16[320,256]{1,0:T(8,128)(2,1)S(1)}, u32[]{:S(2)}, u32[]{:S(2)}) collective-permute-start(bf16[320,256]{1,0:T(8,128)(2,1)S(1)} %get-tuple-element.46), channel_id=1, source_target_pairs={{0,1},{1,2},{2,3},{3,0},{4,5},{5,6},{6,7},{7,4},{8,9},{9,10},{10,1... | collective-permute-start | bytes 491528 | tf_op jit(solution)/shard_map/ppermute | solution.py:67
  7.1 8.1 %collective-permute-start.1 = (bf16[320,256]{1,0:T(8,128)(2,1)S(1)}, bf16[320,256]{1,0:T(8,128)(2,1)S(1)}, u32[]{:S(2)}, u32[]{:S(2)}) collective-permute-start(bf16[320,256]{1,0:T(8,128)(2,1)S(1)} %get-tuple-element.47), channel_id=1, source_target_pairs={{0,2},{1,3},{2,0},{3,1},{4,6},{5,7},{6,4},{7,5},{8,10},{9,11},{10,... | collective-permute-start | bytes 491528 | tf_op jit(solution)/shard_map/ppermute | solution.py:67
  10.4 4.8 %collective-permute-start.2 = (bf16[320,256]{1,0:T(8,128)(2,1)S(1)}, bf16[320,256]{1,0:T(8,128)(2,1)S(1)}, u32[]{:S(2)}, u32[]{:S(2)}) collective-permute-start(bf16[320,256]{1,0:T(8,128)(2,1)S(1)} %get-tuple-element.48), channel_id=1, source_target_pairs={{0,3},{1,0},{2,1},{3,2},{4,7},{5,4},{6,5},{7,6},{8,11},{9,8},{10,9... | collective-permute-start | bytes 491528 | tf_op jit(solution)/shard_map/ppermute | solution.py:67
  15.3 10.8 %collective-permute-start.3 = (bf16[1040,256]{1,0:T(8,128)(2,1)S(1)}, bf16[1040,256]{1,0:T(8,128)(2,1)S(1)}, u32[]{:S(2)}, u32[]{:S(2)}) collective-permute-start(bf16[1040,256]{1,0:T(8,128)(2,1)S(1)} %stack_rows.1.refs_4_), channel_id=1, source_target_pairs={{0,4},{1,5},{2,6},{3,7},{4,8},{5,9},{6,10},{7,11},{8,12},{9,13},{1... | collective-permute-start | bytes 1597448 | tf_op jit(solution)/shard_map/ppermute | solution.py:775
  16.3 13.6 %collective-permute-start.4 = (bf16[1040,256]{1,0:T(8,128)(2,1)S(1)}, bf16[1040,256]{1,0:T(8,128)(2,1)S(1)}, u32[]{:S(2)}, u32[]{:S(2)}) collective-permute-start(bf16[1040,256]{1,0:T(8,128)(2,1)S(1)} %stack_rows.1.refs_4_), channel_id=1, source_target_pairs={{0,12},{1,13},{2,14},{3,15},{4,0},{5,1},{6,2},{7,3},{8,4},{9,5},{1... | collective-permute-start | bytes 1597448 | tf_op jit(solution)/shard_map/ppermute | solution.py:775
  18.0 14.2 %collective-permute-start.5 = (bf16[1040,256]{1,0:T(8,128)(2,1)S(1)}, bf16[1040,256]{1,0:T(8,128)(2,1)S(1)}, u32[]{:S(2)}, u32[]{:S(2)}) collective-permute-start(bf16[1040,256]{1,0:T(8,128)(2,1)S(1)} %stack_rows.1.refs_4_), channel_id=1, source_target_pairs={{0,8},{1,9},{2,10},{3,11},{4,12},{5,13},{6,14},{7,15},{8,0},{9,1},... | collective-permute-start | bytes 1597448 | tf_op jit(solution)/shard_map/ppermute | solution.py:775
  19.4 12.8 %collective-permute-start.6 = (bf16[16,1536]{1,0:T(8,128)(2,1)S(1)}, bf16[16,1536]{1,0:T(8,128)(2,1)S(1)}, u32[]{:S(2)}, u32[]{:S(2)}) collective-permute-start(bf16[16,1536]{1,0:T(8,128)(2,1)S(1)} %get-tuple-element.53.refs_4_), channel_id=1, source_target_pairs={{0,1},{1,2},{2,3},{3,4},{4,5},{5,6},{6,7},{7,8},{8,9},{9,10},{10,1... | collective-permute-start | bytes 147464 | tf_op jit(solution)/shard_map/ppermute | solution.py:770
  21.7 10.5 %collective-permute-start.7 = (bf16[16,1536]{1,0:T(8,128)(2,1)S(1)}, bf16[16,1536]{1,0:T(8,128)(2,1)S(1)}, u32[]{:S(2)}, u32[]{:S(2)}) collective-permute-start(bf16[16,1536]{1,0:T(8,128)(2,1)S(1)} %get-tuple-element.60), channel_id=1, source_target_pairs={{1,0},{2,1},{3,2},{4,3},{5,4},{6,5},{7,6},{8,7},{9,8},{10,9},{11,1... | collective-permute-start | bytes 147464 | tf_op jit(solution)/shard_map/ppermute | solution.py:771
  35.5 10.4 %collective-permute-start.8 = (bf16[400,128]{1,0:T(8,128)(2,1)S(1)}, bf16[400,128]{1,0:T(8,128)(2,1)S(1)}, u32[]{:S(2)}, u32[]{:S(2)}) collective-permute-start(bf16[400,128]{1,0:T(8,128)(2,1)S(1)} %get-tuple-element.62), channel_id=1, source_target_pairs={{0,3},{1,0},{2,1},{3,2},{4,7},{5,4},{6,5},{7,6},{8,11},{9,8},{10,9... | collective-permute-start | bytes 307208 | tf_op jit(solution)/shard_map/ppermute | solution.py:67
  39.8 6.1 %collective-permute-start.9 = (bf16[400,128]{1,0:T(8,128)(2,1)S(1)}, bf16[400,128]{1,0:T(8,128)(2,1)S(1)}, u32[]{:S(2)}, u32[]{:S(2)}) collective-permute-start(bf16[400,128]{1,0:T(8,128)(2,1)S(1)} %get-tuple-element.63), channel_id=1, source_target_pairs={{0,2},{1,3},{2,0},{3,1},{4,6},{5,7},{6,4},{7,5},{8,10},{9,11},{10,... | collective-permute-start | bytes 307208 | tf_op jit(solution)/shard_map/ppermute | solution.py:67
  40.8 5.4 %collective-permute-start.10 = (bf16[400,128]{1,0:T(8,128)(2,1)S(1)}, bf16[400,128]{1,0:T(8,128)(2,1)S(1)}, u32[]{:S(2)}, u32[]{:S(2)}) collective-permute-start(bf16[400,128]{1,0:T(8,128)(2,1)S(1)} %get-tuple-element.64), channel_id=1, source_target_pairs={{0,1},{1,2},{2,3},{3,0},{4,5},{5,6},{6,7},{7,4},{8,9},{9,10},{10,1... | collective-permute-start | bytes 307208 | tf_op jit(solution)/shard_map/ppermute | solution.py:67
  51.8 6.7 %collective-permute-start.11 = (bf16[4,384,768]{2,1,0:T(8,128)(2,1)S(1)}, bf16[4,384,768]{2,1,0:T(8,128)(2,1)S(1)}, u32[]{:S(2)}, u32[]{:S(2)}) collective-permute-start(bf16[4,384,768]{2,1,0:T(8,128)(2,1)S(1)} %get-tuple-element.69), channel_id=1, source_target_pairs={{0,16},{16,0},{1,17},{17,1},{2,18},{18,2},{3,19},{19,3},{4,20},{20... | collective-permute-start | bytes 7077896 | tf_op jit(solution)/shard_map/ppermute | solution.py:788
  59.8 18.4 %collective-permute-start.12 = (bf16[384,768]{1,0:T(8,128)(2,1)S(1)}, bf16[384,768]{1,0:T(8,128)(2,1)S(1)}, u32[]{:S(2)}, u32[]{:S(2)}) collective-permute-start(bf16[384,768]{1,0:T(8,128)(2,1)S(1)} %get-tuple-element.71), channel_id=1, source_target_pairs={{0,32},{1,33},{2,34},{3,35},{4,36},{5,37},{6,38},{7,39},{8,40},{9,... | collective-permute-start | bytes 1769480 | tf_op jit(solution)/shard_map/ppermute | solution.py:67
  60.8 17.3 %collective-permute-start.13 = (bf16[384,768]{1,0:T(8,128)(2,1)S(1)}, bf16[384,768]{1,0:T(8,128)(2,1)S(1)}, u32[]{:S(2)}, u32[]{:S(2)}) collective-permute-start(bf16[384,768]{1,0:T(8,128)(2,1)S(1)} %get-tuple-element.72), channel_id=1, source_target_pairs={{0,64},{1,65},{2,66},{3,67},{4,68},{5,69},{6,70},{7,71},{8,72},{9,... | collective-permute-start | bytes 1769480 | tf_op jit(solution)/shard_map/ppermute | solution.py:67
  64.0 14.2 %collective-permute-start.14 = (bf16[384,768]{1,0:T(8,128)(2,1)S(1)}, bf16[384,768]{1,0:T(8,128)(2,1)S(1)}, u32[]{:S(2)}, u32[]{:S(2)}) collective-permute-start(bf16[384,768]{1,0:T(8,128)(2,1)S(1)} %get-tuple-element.73), channel_id=1, source_target_pairs={{0,96},{1,97},{2,98},{3,99},{4,100},{5,101},{6,102},{7,103},{8,104... | collective-permute-start | bytes 1769480 | tf_op jit(solution)/shard_map/ppermute | solution.py:67
  75.5 10.0 %collective-permute-start.18 = (f32[3,768]{1,0:T(4,128)S(1)}, f32[3,768]{1,0:T(4,128)S(1)}, u32[]{:S(2)}, u32[]{:S(2)}) collective-permute-start(f32[3,768]{1,0:T(4,128)S(1)} %get-tuple-element.81), channel_id=1, source_target_pairs={{0,16},{16,0},{1,17},{17,1},{2,18},{18,2},{3,19},{19,3},{4,20},{20... | collective-permute-start | bytes 27656 | tf_op jit(solution)/shard_map/ppermute | solution.py:797
  79.1 6.7 %collective-permute-start.15 = (bf16[96,768]{1,0:T(8,128)(2,1)S(1)}, bf16[96,768]{1,0:T(8,128)(2,1)S(1)}, u32[]{:S(2)}, u32[]{:S(2)}) collective-permute-start(bf16[96,768]{1,0:T(8,128)(2,1)S(1)} %get-tuple-element.75), channel_id=1, source_target_pairs={{0,2},{1,3},{2,0},{3,1},{4,6},{5,7},{6,4},{7,5},{8,10},{9,11},{10,... | collective-permute-start | bytes 442376 | tf_op jit(solution)/shard_map/ppermute | solution.py:67
  82.9 5.2 %collective-permute-start.16 = (bf16[96,768]{1,0:T(8,128)(2,1)S(1)}, bf16[96,768]{1,0:T(8,128)(2,1)S(1)}, u32[]{:S(2)}, u32[]{:S(2)}) collective-permute-start(bf16[96,768]{1,0:T(8,128)(2,1)S(1)} %get-tuple-element.76), channel_id=1, source_target_pairs={{0,1},{1,2},{2,3},{3,0},{4,5},{5,6},{6,7},{7,4},{8,9},{9,10},{10,1... | collective-permute-start | bytes 442376 | tf_op jit(solution)/shard_map/ppermute | solution.py:67
  82.9 5.2 %collective-permute-start.17 = (bf16[96,768]{1,0:T(8,128)(2,1)S(1)}, bf16[96,768]{1,0:T(8,128)(2,1)S(1)}, u32[]{:S(2)}, u32[]{:S(2)}) collective-permute-start(bf16[96,768]{1,0:T(8,128)(2,1)S(1)} %get-tuple-element.77), channel_id=1, source_target_pairs={{0,3},{1,0},{2,1},{3,2},{4,7},{5,4},{6,5},{7,6},{8,11},{9,8},{10,9... | collective-permute-start | bytes 442376 | tf_op jit(solution)/shard_map/ppermute | solution.py:67
  88.2 5.8 %collective-permute-start.20 = (bf16[112,768]{1,0:T(8,128)(2,1)S(1)}, bf16[112,768]{1,0:T(8,128)(2,1)S(1)}, u32[]{:S(2)}, u32[]{:S(2)}) collective-permute-start(bf16[112,768]{1,0:T(8,128)(2,1)S(1)} %fusion.1), channel_id=1, source_target_pairs={{0,4},{1,5},{2,6},{3,7},{4,8},{5,9},{6,10},{7,11},{8,12},{9,13},{1... | collective-permute-start | bytes 516104 | tf_op jit(solution)/shard_map/ppermute | solution.py:67
  88.9 7.1 %collective-permute-start.19 = (bf16[112,768]{1,0:T(8,128)(2,1)S(1)}, bf16[112,768]{1,0:T(8,128)(2,1)S(1)}, u32[]{:S(2)}, u32[]{:S(2)}) collective-permute-start(bf16[112,768]{1,0:T(8,128)(2,1)S(1)} %fusion.1), channel_id=1, source_target_pairs={{0,8},{1,9},{2,10},{3,11},{4,12},{5,13},{6,14},{7,15},{8,0},{9,1},... | collective-permute-start | bytes 516104 | tf_op jit(solution)/shard_map/ppermute | solution.py:67
  91.0 5.4 %collective-permute-start.21 = (bf16[112,768]{1,0:T(8,128)(2,1)S(1)}, bf16[112,768]{1,0:T(8,128)(2,1)S(1)}, u32[]{:S(2)}, u32[]{:S(2)}) collective-permute-start(bf16[112,768]{1,0:T(8,128)(2,1)S(1)} %fusion.1), channel_id=1, source_target_pairs={{0,12},{1,13},{2,14},{3,15},{4,0},{5,1},{6,2},{7,3},{8,4},{9,5},{1... | collective-permute-start | bytes 516104 | tf_op jit(solution)/shard_map/ppermute | solution.py:67
  96.6 6.9 %collective-permute-start.24 = (bf16[112,768]{1,0:T(8,128)(2,1)S(1)}, bf16[112,768]{1,0:T(8,128)(2,1)S(1)}, u32[]{:S(2)}, u32[]{:S(2)}) collective-permute-start(bf16[112,768]{1,0:T(8,128)(2,1)S(1)} %multiply_convert_fusion.refs_0_), channel_id=1, source_target_pairs={{0,3},{1,0},{2,1},{3,2},{4,7},{5,4},{6,5},{7,6},{8,11},{9,8},{10,9... | collective-permute-start | bytes 516104 | tf_op jit(solution)/shard_map/ppermute | solution.py:67
  99.2 5.9 %collective-permute-start.23 = (bf16[112,768]{1,0:T(8,128)(2,1)S(1)}, bf16[112,768]{1,0:T(8,128)(2,1)S(1)}, u32[]{:S(2)}, u32[]{:S(2)}) collective-permute-start(bf16[112,768]{1,0:T(8,128)(2,1)S(1)} %multiply_convert_fusion.refs_0_), channel_id=1, source_target_pairs={{0,2},{1,3},{2,0},{3,1},{4,6},{5,7},{6,4},{7,5},{8,10},{9,11},{10,... | collective-permute-start | bytes 516104 | tf_op jit(solution)/shard_map/ppermute | solution.py:67
  99.4 7.6 %collective-permute-start.22 = (bf16[112,768]{1,0:T(8,128)(2,1)S(1)}, bf16[112,768]{1,0:T(8,128)(2,1)S(1)}, u32[]{:S(2)}, u32[]{:S(2)}) collective-permute-start(bf16[112,768]{1,0:T(8,128)(2,1)S(1)} %multiply_convert_fusion.refs_0_), channel_id=1, source_target_pairs={{0,1},{1,2},{2,3},{3,0},{4,5},{5,6},{6,7},{7,4},{8,9},{9,10},{10,1... | collective-permute-start | bytes 516104 | tf_op jit(solution)/shard_map/ppermute | solution.py:67
  107.8 15.4 %collective-permute-start.27 = (bf16[784,384]{1,0:T(8,128)(2,1)S(1)}, bf16[784,384]{1,0:T(8,128)(2,1)S(1)}, u32[]{:S(2)}, u32[]{:S(2)}) collective-permute-start(bf16[784,384]{1,0:T(8,128)(2,1)S(1)} %join_rows.1.refs_0_), channel_id=1, source_target_pairs={{0,96},{1,97},{2,98},{3,99},{4,100},{5,101},{6,102},{7,103},{8,104... | collective-permute-start | bytes 1806344 | tf_op jit(solution)/shard_map/ppermute | solution.py:67
  109.7 17.9 %collective-permute-start.26 = (bf16[784,384]{1,0:T(8,128)(2,1)S(1)}, bf16[784,384]{1,0:T(8,128)(2,1)S(1)}, u32[]{:S(2)}, u32[]{:S(2)}) collective-permute-start(bf16[784,384]{1,0:T(8,128)(2,1)S(1)} %join_rows.1.refs_0_), channel_id=1, source_target_pairs={{0,64},{1,65},{2,66},{3,67},{4,68},{5,69},{6,70},{7,71},{8,72},{9,... | collective-permute-start | bytes 1806344 | tf_op jit(solution)/shard_map/ppermute | solution.py:67
  110.5 17.2 %collective-permute-start.25 = (bf16[784,384]{1,0:T(8,128)(2,1)S(1)}, bf16[784,384]{1,0:T(8,128)(2,1)S(1)}, u32[]{:S(2)}, u32[]{:S(2)}) collective-permute-start(bf16[784,384]{1,0:T(8,128)(2,1)S(1)} %join_rows.1.refs_0_), channel_id=1, source_target_pairs={{0,32},{1,33},{2,34},{3,35},{4,36},{5,37},{6,38},{7,39},{8,40},{9,... | collective-permute-start | bytes 1806344 | tf_op jit(solution)/shard_map/ppermute | solution.py:67
  110.7 20.9 %collective-permute-start.28 = (bf16[784,384]{1,0:T(8,128)(2,1)S(1)}, bf16[784,384]{1,0:T(8,128)(2,1)S(1)}, u32[]{:S(2)}, u32[]{:S(2)}) collective-permute-start(bf16[784,384]{1,0:T(8,128)(2,1)S(1)} %join_rows.1.refs_0_), channel_id=1, source_target_pairs={{0,16},{16,0},{1,17},{17,1},{2,18},{18,2},{3,19},{19,3},{4,20},{20... | collective-permute-start | bytes 1806344 | tf_op jit(solution)/shard_map/ppermute | solution.py:809
  123.2 8.5 %collective-permute-start.31 = (bf16[784,384]{1,0:T(8,128)(2,1)S(1)}, bf16[784,384]{1,0:T(8,128)(2,1)S(1)}, u32[]{:S(2)}, u32[]{:S(2)}) collective-permute-start(bf16[784,384]{1,0:T(8,128)(2,1)S(1)} %collective-permute-done.27.refs_3_), channel_id=1, source_target_pairs={{0,16},{16,0},{1,17},{17,1},{2,18},{18,2},{3,19},{19,3},{4,20},{20... | collective-permute-start | bytes 1806344 | tf_op jit(solution)/shard_map/ppermute | solution.py:809
  127.7 4.0 %collective-permute-start.30 = (bf16[784,384]{1,0:T(8,128)(2,1)S(1)}, bf16[784,384]{1,0:T(8,128)(2,1)S(1)}, u32[]{:S(2)}, u32[]{:S(2)}) collective-permute-start(bf16[784,384]{1,0:T(8,128)(2,1)S(1)} %collective-permute-done.26.refs_2_), channel_id=1, source_target_pairs={{0,16},{16,0},{1,17},{17,1},{2,18},{18,2},{3,19},{19,3},{4,20},{20... | collective-permute-start | bytes 1806344 | tf_op jit(solution)/shard_map/ppermute | solution.py:809
  127.7 5.6 %collective-permute-start.29 = (bf16[784,384]{1,0:T(8,128)(2,1)S(1)}, bf16[784,384]{1,0:T(8,128)(2,1)S(1)}, u32[]{:S(2)}, u32[]{:S(2)}) collective-permute-start(bf16[784,384]{1,0:T(8,128)(2,1)S(1)} %collective-permute-done.25.refs_1_), channel_id=1, source_target_pairs={{0,16},{16,0},{1,17},{17,1},{2,18},{18,2},{3,19},{19,3},{4,20},{20... | collective-permute-start | bytes 1806344 | tf_op jit(solution)/shard_map/ppermute | solution.py:809
  (4 other events, 14.6 us)
